TPU v7x, 32 devices: a whole 2x2x4 slice. The times are simulated.
32 devices in a mesh: dp: 4 (over x, core), tensor: 8 (over z, y).
Axes of the slice: x: 2, y: 2, z: 4, core: 2. Of those that a mesh axis runs over, the one named last changes fastest.
Arguments:
- inputs: bfloat16 [2, 4096, 2048], P(None, ('dp', 'tensor')), may hold values from -6 to 6
- lengths: int32 [2, 4, 3], P(None, 'dp'), may hold values from 1 to 897, as said below
- norm_gain: bfloat16 [2048], P('dp'), may hold values from 0.25 to 1.75
- ffn_gain: bfloat16 [2048], P('dp'), may hold values from 0.25 to 1.75
- w_query: bfloat16 [2048, 2048], P(None, 'tensor'), may hold values from -0.125 to 0.125
- w_key: bfloat16 [2048, 2048], P(None, 'tensor'), may hold values from -0.125 to 0.125
- w_value: bfloat16 [2048, 2048], P(None, 'tensor'), may hold values from -0.125 to 0.125
- w_gate_out: bfloat16 [2048, 2048], P(None, 'tensor'), may hold values from -0.125 to 0.125
- w_beta: bfloat16 [2048, 16], P(None, 'tensor'), may hold values from -0.125 to 0.125
- conv_weight: bfloat16 [3, 4, 2048], P(None, None, 'tensor'), may hold values from -3 to 3
- head_gain: bfloat16 [16, 128], P('tensor'), may hold values from 0.25 to 1.75
- w_out: bfloat16 [2048, 2048], P('tensor'), may hold values from -0.1875 to 0.1875
- w_gate: bfloat16 [2048, 5632], P('dp', 'tensor'), may hold values from -0.125 to 0.125
- w_up: bfloat16 [2048, 5632], P('dp', 'tensor'), may hold values from -0.125 to 0.125
- w_down: bfloat16 [5632, 2048], P('tensor', 'dp'), may hold values from -0.109375 to 0.109375
- cotangent: bfloat16 [2, 4096, 2048], P(None, ('dp', 'tensor')), may hold values from -6 to 6
Outputs:
- outputs: float32 [2, 4096, 2048], P(None, ('dp', 'tensor'))
- input_grad: float32 [2, 4096, 2048], P(None, ('dp', 'tensor'))
- norm_gain_grad: float32 [2048], P(('dp', 'tensor'))
- ffn_gain_grad: float32 [2048], P(('dp', 'tensor'))
- w_query_grad: float32 [2048, 2048], P(None, 'tensor')
- w_key_grad: float32 [2048, 2048], P(None, 'tensor')
- w_value_grad: float32 [2048, 2048], P(None, 'tensor')
- w_gate_out_grad: float32 [2048, 2048], P(None, 'tensor')
- w_beta_grad: float32 [2048, 16], P(None, 'tensor')
- conv_weight_grad: float32 [3, 4, 2048], P(None, None, 'tensor')
- head_gain_grad: float32 [16, 128], P('tensor')
- w_out_grad: float32 [2048, 2048], P('tensor')
- w_gate_grad: float32 [2048, 5632], P('dp', 'tensor')
- w_up_grad: float32 [2048, 5632], P('dp', 'tensor')
- w_down_grad: float32 [5632, 2048], P('tensor', 'dp')
Inputs may be any that keep to these rules, and one draw needn't show every extreme that they name: `lengths`: each row holds one long sequence of exactly 897 tokens, first or second (drawn from the seed), one short sequence of 102 to 126 tokens, and the padding last; the entries sum to 1024.
All inputs are finite; a program needn't handle non-finite values.
Results may differ from a plain program's by a relative error of at most 0.02.
Values may be sent and summed in bfloat16 or wider, within the bound.
A program may use at most 384 MiB of HBM per device.

v0:
```python
from functools import partial

import jax
import jax.numpy as jnp
from jax import lax
from jax.sharding import PartitionSpec as P

BLOCK = 64


epsilon = 1e-06
highest = lax.Precision.HIGHEST


def matmul(left_side, right_side):
    return jnp.dot(left_side, right_side, precision=highest, preferred_element_type=jnp.float32)


def delta_rule(queries, key_rows, value_rows, beta_rates, segment, block_rows):
    length_all = queries.shape[0]
    head_width = queries.shape[1]
    blocks = length_all // block_rows
    query_blocks = queries.reshape(blocks, block_rows, head_width)
    key_blocks = key_rows.reshape(blocks, block_rows, head_width)
    value_blocks = value_rows.reshape(blocks, block_rows, head_width)
    beta_blocks = beta_rates.reshape(blocks, block_rows)
    segment_blocks = segment.reshape(blocks, block_rows)
    before = jnp.concatenate([jnp.full((1,), -1, jnp.int32), segment_blocks[:-1, -1]])
    places = jnp.arange(block_rows, dtype=jnp.int32)
    strict = places[:, None] > places[None, :]
    within = places[:, None] >= places[None, :]
    same_doc = segment_blocks[:, :, None] == segment_blocks[:, None, :]
    key_gram = jnp.einsum("nid,njd->nij", key_blocks, key_blocks, precision=highest)
    lower_part = jnp.where(same_doc & strict[None], key_gram * beta_blocks[:, :, None], 0.0)
    system = lower_part + jnp.eye(block_rows, dtype=jnp.float32)
    right_hand = jnp.concatenate([value_blocks, key_blocks], axis=2) * beta_blocks[:, :, None]
    solved = jax.scipy.linalg.solve_triangular(system, right_hand, lower=True, unit_diagonal=True)
    new_values = solved[:, :, :head_width]
    weighted_keys = solved[:, :, head_width:]
    query_gram = jnp.einsum("nid,njd->nij", query_blocks, key_blocks, precision=highest)
    attention = jnp.where(same_doc & within[None], query_gram, 0.0)
    carried = (segment_blocks == before[:, None]).astype(jnp.float32)
    closing = (segment_blocks == segment_blocks[:, -1:]).astype(jnp.float32)

    def advance(memory, pieces):
        query_part, key_part, value_part, weight_part, score_part, carry_part, close_part = pieces
        corrected = value_part - carry_part[:, None] * matmul(weight_part, memory)
        output = carry_part[:, None] * matmul(query_part, memory) + matmul(score_part, corrected)
        memory = carry_part[-1] * memory + matmul(key_part.T, close_part[:, None] * corrected)
        return (memory, output)

    _, outputs = lax.scan(
        jax.checkpoint(advance),
        jnp.zeros((head_width, head_width), jnp.float32),
        (query_blocks, key_blocks, new_values, weighted_keys, attention, carried, closing),
    )
    return outputs.reshape(length_all, head_width)


def mixer_block(projected, beta_logits, conv_weight, head_gain, segment, live_mask, block_rows):
    length_all = projected.shape[0]
    head_count = beta_logits.shape[1]
    inner_width = projected.shape[1] // 4
    head_width = inner_width // head_count
    channels = projected[:, : 3 * inner_width]
    tap_count = conv_weight.shape[1]
    tap_weights = jnp.transpose(conv_weight, (1, 0, 2)).reshape(tap_count, 3 * inner_width)
    mixed_rows = channels * tap_weights[0]
    for offset in range(1, tap_count):
        shifted = jnp.concatenate(
            [jnp.zeros((offset, 3 * inner_width), jnp.float32), channels[:-offset]], axis=0
        )
        earlier = jnp.concatenate([jnp.full((offset,), -1, jnp.int32), segment[:-offset]])
        valid_taps = (earlier == segment).astype(jnp.float32)
        mixed_rows = mixed_rows + shifted * tap_weights[offset] * valid_taps[:, None]
    activated = jax.nn.silu(mixed_rows).reshape(length_all, 3, head_count, head_width)
    queries = activated[:, 0]
    queries = (
        queries
        * lax.rsqrt(jnp.sum(queries * queries, axis=-1, keepdims=True) + epsilon)
        * head_width ** (-0.5)
    )
    key_rows = activated[:, 1]
    key_rows = key_rows * lax.rsqrt(jnp.sum(key_rows * key_rows, axis=-1, keepdims=True) + epsilon)
    value_rows = activated[:, 2]
    beta_rates = jax.nn.sigmoid(beta_logits) * live_mask[:, None]
    per_head = partial(delta_rule, segment=segment, block_rows=block_rows)
    outputs = jax.vmap(per_head, in_axes=1, out_axes=1)(queries, key_rows, value_rows, beta_rates)
    gate_rows = projected[:, 3 * inner_width :].reshape(length_all, head_count, head_width)
    row_scale = lax.rsqrt(jnp.mean(outputs * outputs, axis=-1, keepdims=True) + epsilon)
    gated_rows = outputs * row_scale * head_gain[None] * jax.nn.silu(gate_rows)
    return gated_rows.reshape(length_all, inner_width)


def root_scale(row_values, gain_vector):
    row_scale = lax.rsqrt(jnp.mean(row_values * row_values, axis=-1, keepdims=True) + epsilon)
    return (row_values * row_scale * gain_vector, row_scale)


def norm_backward(row_values, row_scale, gain_vector, normed_grad):
    weighted = normed_grad * gain_vector
    rows_grad = row_scale * weighted - row_values * row_scale * row_scale * row_scale * jnp.mean(
        weighted * row_values, axis=-1, keepdims=True
    )
    gain_grad = jnp.sum(normed_grad * row_values * row_scale, axis=0)
    return (rows_grad, gain_grad)


def per_device(
    inputs,
    lengths,
    norm_gain,
    ffn_gain,
    w_query,
    w_key,
    w_value,
    w_gate_out,
    w_beta,
    conv_weight,
    head_gain,
    w_out,
    w_gate,
    w_up,
    w_down,
    cotangent,
):
    batch_count = inputs.shape[0]
    tok_rows = inputs.shape[1]
    model_width = inputs.shape[2]
    group_rows = tok_rows * lax.axis_size("tensor")
    local_width = w_query.shape[1]
    w_inner = jnp.concatenate([w_query, w_key, w_value, w_gate_out], axis=1)
    conv_float = conv_weight.astype(jnp.float32)
    gain_heads = head_gain.astype(jnp.float32)
    positions = jnp.arange(group_rows, dtype=jnp.int32)
    out_full = lax.all_gather(w_out, "tensor", axis=0, tiled=True)
    out_full_grad = jnp.zeros(out_full.shape, jnp.float32)
    inner_grad_sum = jnp.zeros(w_inner.shape, jnp.float32)
    beta_grad_sum = jnp.zeros(w_beta.shape, jnp.float32)
    conv_grad_sum = jnp.zeros(conv_weight.shape, jnp.float32)
    heads_grad_sum = jnp.zeros(head_gain.shape, jnp.float32)
    gate_grad_sum = jnp.zeros(w_gate.shape, jnp.float32)
    up_grad_sum = jnp.zeros(w_up.shape, jnp.float32)
    down_grad_sum = jnp.zeros(w_down.shape, jnp.float32)
    gain_one_sum = jnp.zeros((model_width,), jnp.float32)
    gain_two_sum = jnp.zeros((model_width,), jnp.float32)
    result_rows = []
    input_grads = []
    for batch_index in range(batch_count):
        gate_full, up_full, down_full, gain_one, gain_two = (
            lax.all_gather(w_gate, "dp", axis=0, tiled=True),
            lax.all_gather(w_up, "dp", axis=0, tiled=True),
            lax.all_gather(w_down, "dp", axis=1, tiled=True),
            lax.all_gather(norm_gain, "dp", axis=0, tiled=True),
            lax.all_gather(ffn_gain, "dp", axis=0, tiled=True),
        )
        gain_one = gain_one.astype(jnp.float32)
        gain_two = gain_two.astype(jnp.float32)
        rows_in = inputs[batch_index].astype(jnp.float32)
        lengths_row = lengths[batch_index, 0]
        seq_ends = jnp.cumsum(lengths_row)[:-1]
        segment = jnp.sum((positions[:, None] >= seq_ends[None, :]).astype(jnp.int32), axis=1)
        live_mask = (segment < lengths_row.shape[0] - 1).astype(jnp.float32)
        normed_one, scale_one = root_scale(rows_in, gain_one)
        normed_low = normed_one.astype(jnp.bfloat16)
        gathered_one, grad_rows = (
            lax.all_gather(normed_low, "tensor", axis=0, tiled=True),
            lax.all_gather(cotangent[batch_index], "tensor", axis=0, tiled=True),
        )
        projected = jnp.dot(gathered_one, w_inner, preferred_element_type=jnp.float32)
        beta_logits = jnp.dot(gathered_one, w_beta, preferred_element_type=jnp.float32)
        mixer_local = partial(mixer_block, segment=segment, live_mask=live_mask, block_rows=BLOCK)
        mixed_rows, mixer_back = jax.vjp(
            mixer_local, projected, beta_logits, conv_float, gain_heads
        )
        mixed_low = mixed_rows.astype(jnp.bfloat16)
        token_heads = lax.all_to_all(mixed_low, "tensor", split_axis=0, concat_axis=1, tiled=True)
        attended = jnp.dot(token_heads, out_full, preferred_element_type=jnp.float32)
        hidden = rows_in + attended
        normed_two, scale_two = root_scale(hidden, gain_two)
        gathered_two = lax.all_gather(normed_two.astype(jnp.bfloat16), "tensor", axis=0, tiled=True)
        gate_values = jnp.dot(gathered_two, gate_full, preferred_element_type=jnp.float32)
        up_values = jnp.dot(gathered_two, up_full, preferred_element_type=jnp.float32)
        sigmoid_gate = jax.nn.sigmoid(gate_values)
        silu_gate = gate_values * sigmoid_gate
        inner_rows = (silu_gate * up_values).astype(jnp.bfloat16)
        ffn_out = lax.psum_scatter(
            jnp.dot(inner_rows, down_full, preferred_element_type=jnp.float32).astype(jnp.bfloat16),
            "tensor",
            scatter_dimension=0,
            tiled=True,
        ).astype(jnp.float32)
        result_rows.append(hidden + ffn_out)
        inner_grad = jnp.einsum(
            "td,fd->tf", grad_rows, down_full, preferred_element_type=jnp.float32
        )
        gate_grad = (
            inner_grad * up_values * sigmoid_gate * (1.0 + gate_values * (1.0 - sigmoid_gate))
        ).astype(jnp.bfloat16)
        up_grad = (inner_grad * silu_gate).astype(jnp.bfloat16)
        down_weight_grad = jnp.einsum(
            "tf,td->fd", inner_rows, grad_rows, preferred_element_type=jnp.float32
        )
        gate_weight_grad = jnp.einsum(
            "td,tf->df", gathered_two, gate_grad, preferred_element_type=jnp.float32
        )
        up_weight_grad = jnp.einsum(
            "td,tf->df", gathered_two, up_grad, preferred_element_type=jnp.float32
        )
        normed_two_grad = lax.psum_scatter(
            (
                jnp.einsum("tf,df->td", gate_grad, gate_full, preferred_element_type=jnp.float32)
                + jnp.einsum("tf,df->td", up_grad, up_full, preferred_element_type=jnp.float32)
            ).astype(jnp.bfloat16),
            "tensor",
            scatter_dimension=0,
            tiled=True,
        ).astype(jnp.float32)
        hidden_norm_grad, gain_two_part = norm_backward(
            hidden, scale_two, gain_two, normed_two_grad
        )
        hidden_grad = cotangent[batch_index].astype(jnp.float32) + hidden_norm_grad
        attended_low = hidden_grad.astype(jnp.bfloat16)
        token_grad = jnp.einsum(
            "td,hd->th", attended_low, out_full, preferred_element_type=jnp.float32
        )
        mixed_grad = lax.all_to_all(
            token_grad.astype(jnp.bfloat16), "tensor", split_axis=1, concat_axis=0, tiled=True
        ).astype(token_grad.dtype)
        out_full_grad = out_full_grad + jnp.einsum(
            "th,td->hd", token_heads, attended_low, preferred_element_type=jnp.float32
        )
        projected_grad, beta_logit_grad, conv_part, heads_part = mixer_back(mixed_grad)
        projected_low = projected_grad.astype(jnp.bfloat16)
        beta_low = beta_logit_grad.astype(jnp.bfloat16)
        inner_grad_sum = inner_grad_sum + jnp.einsum(
            "td,tc->dc", gathered_one, projected_low, preferred_element_type=jnp.float32
        )
        beta_grad_sum = beta_grad_sum + jnp.einsum(
            "td,tc->dc", gathered_one, beta_low, preferred_element_type=jnp.float32
        )
        conv_grad_sum = conv_grad_sum + conv_part
        heads_grad_sum = heads_grad_sum + heads_part
        normed_one_grad = lax.psum_scatter(
            (
                jnp.einsum("tc,dc->td", projected_low, w_inner, preferred_element_type=jnp.float32)
                + jnp.einsum("tc,dc->td", beta_low, w_beta, preferred_element_type=jnp.float32)
            ).astype(jnp.bfloat16),
            "tensor",
            scatter_dimension=0,
            tiled=True,
        ).astype(jnp.float32)
        input_norm_grad, gain_one_part = norm_backward(
            rows_in, scale_one, gain_one, normed_one_grad
        )
        input_grads.append(hidden_grad + input_norm_grad)
        gain_one_sum = gain_one_sum + gain_one_part
        gain_two_sum = gain_two_sum + gain_two_part
        gate_share, up_share, down_share = (
            lax.psum_scatter(
                gate_weight_grad.astype(jnp.bfloat16), "dp", scatter_dimension=0, tiled=True
            ).astype(jnp.float32),
            lax.psum_scatter(
                up_weight_grad.astype(jnp.bfloat16), "dp", scatter_dimension=0, tiled=True
            ).astype(jnp.float32),
            lax.psum_scatter(
                down_weight_grad.astype(jnp.bfloat16), "dp", scatter_dimension=1, tiled=True
            ).astype(jnp.float32),
        )
        gate_grad_sum = gate_grad_sum + gate_share
        up_grad_sum = up_grad_sum + up_share
        down_grad_sum = down_grad_sum + down_share
    gain_one_total, gain_two_total = (
        lax.psum_scatter(gain_one_sum, ("dp", "tensor"), scatter_dimension=0, tiled=True),
        lax.psum_scatter(gain_two_sum, ("dp", "tensor"), scatter_dimension=0, tiled=True),
    )
    out_weight_grad = lax.psum_scatter(
        out_full_grad.astype(jnp.bfloat16), "tensor", scatter_dimension=0, tiled=True
    )
    inner_total, beta_total, conv_total, heads_total, out_total = (
        lax.psum(inner_grad_sum.astype(jnp.bfloat16), "dp").astype(jnp.float32),
        lax.psum(beta_grad_sum.astype(jnp.bfloat16), "dp").astype(jnp.float32),
        lax.psum(conv_grad_sum.astype(jnp.bfloat16), "dp").astype(jnp.float32),
        lax.psum(heads_grad_sum.astype(jnp.bfloat16), "dp").astype(jnp.float32),
        lax.psum(out_weight_grad, "dp").astype(jnp.float32),
    )
    query_grad = inner_total[:, :local_width]
    key_grad = inner_total[:, local_width : 2 * local_width]
    value_grad = inner_total[:, 2 * local_width : 3 * local_width]
    gate_out_grad = inner_total[:, 3 * local_width :]
    return (
        jnp.stack(result_rows),
        jnp.stack(input_grads),
        gain_one_total,
        gain_two_total,
        query_grad,
        key_grad,
        value_grad,
        gate_out_grad,
        beta_total,
        conv_total,
        heads_total,
        out_total,
        gate_grad_sum,
        up_grad_sum,
        down_grad_sum,
    )


def solution(mesh):
    in_specs = (
        P(None, ("dp", "tensor"), None),
        P(None, "dp", None),
        P("dp"),
        P("dp"),
        P(None, "tensor"),
        P(None, "tensor"),
        P(None, "tensor"),
        P(None, "tensor"),
        P(None, "tensor"),
        P(None, None, "tensor"),
        P("tensor", None),
        P("tensor", None),
        P("dp", "tensor"),
        P("dp", "tensor"),
        P("tensor", "dp"),
        P(None, ("dp", "tensor"), None),
    )
    out_specs = (
        P(None, ("dp", "tensor"), None),
        P(None, ("dp", "tensor"), None),
        P(("dp", "tensor")),
        P(("dp", "tensor")),
        P(None, "tensor"),
        P(None, "tensor"),
        P(None, "tensor"),
        P(None, "tensor"),
        P(None, "tensor"),
        P(None, None, "tensor"),
        P("tensor", None),
        P("tensor", None),
        P("dp", "tensor"),
        P("dp", "tensor"),
        P("tensor", "dp"),
    )
    return jax.shard_map(
        per_device, mesh=mesh, in_specs=in_specs, out_specs=out_specs, check_vma=False
    )
```

profile of v0, /device:TPU:0, one launch (start us, length us, event | category | flops | bytes accessed | tf_op | source)
XLA Modules:
  0.0 2611.8 jit_solution(13390907486030129356)
XLA Ops:
  37.9 56.2 %all-gather.15.cloned.1.call-done = bf16[1024,2048]{1,0:T(8,128)(2,1)} async-done(((bf16[128,2048]{1,0:T(8,128)(2,1)}), bf16[1024,2048]{1,0:T(8,128)(2,1)}) %all-gather.15.cloned.1.call-update) | async-done | bytes 4194320 | tf_op jit(solution)/shard_map/all_gather | solution.py:167
  94.1 7.6 fusion.259
  108.3 60.3 %all-gather.27.cloned.1.call-done = bf16[1024,2048]{1,0:T(8,128)(2,1)} async-done(((bf16[128,2048]{1,0:T(8,128)(2,1)}), bf16[1024,2048]{1,0:T(8,128)(2,1)}) %all-gather.27.cloned.1.call-update) | async-done | bytes 4194320 | tf_op jit(solution)/shard_map/all_gather | solution.py:167
  168.5 7.6 fusion.263
  185.9 8.7 fusion.101
  224.7 159.0 %custom-call.15 = f32[2,16,1,64,64]{3,4,2,1,0:T(8,128)} custom-call(f32[2,16,1,64,64]{4,3,2,1,0:T(8,128)} %get-tuple-element.1491), custom_call_target="InvertDiagBlocksLowerTriangular" | custom-call | tf_op jit(solution)/shard_map/jvp(vmap(jit(_solve_triangular)))/vmap()/triangular_solve | solution.py:37
  397.4 136.2 %while.81 = (s32[]{:T(128)}, f32[2,128,128]{2,1,0:T(8,128)S(1)}, f32[16,2,64,128]{3,2,0,1:T(8,128)S(1)}, f32[16,2,128,128]{3,2,1,0:T(8,128)}, f32[16,64]{1,0:T(8...) while((s32[]{:T(128)}, f32[2,128,128]{2,1,0:T(8,128)S(1)}, ...), condition=%wide.region_16.18_spmd.clone, body=%wide.region_15.17_spmd.clone.sunk | while | flops 88358912 | bytes 1513886 | solution.py:52
  539.0 158.7 %custom-call.14 = f32[2,16,1,64,64]{3,4,2,1,0:T(8,128)} custom-call(f32[2,16,1,64,64]{4,3,2,1,0:T(8,128)} %get-tuple-element.1490), custom_call_target="InvertDiagBlocksLowerTriangular" | custom-call | tf_op jit(solution)/shard_map/jvp(vmap(jit(_solve_triangular)))/vmap()/triangular_solve | solution.py:37
  713.3 146.2 %while.80 = (s32[]{:T(128)}, f32[2,128,128]{2,1,0:T(8,128)S(1)}, f32[16,2,64,128]{3,2,0,1:T(8,128)}, f32[16,2,128,128]{3,2,1,0:T(8,128)}, f32[16,64]{1,0:T(8,128...) while((s32[]{:T(128)}, f32[2,128,128]{2,1,0:T(8,128)S(1)}, ...), condition=%wide.region_6.8_spmd.clone, body=%wide.region_5.7_spmd.clone.sunk | while | flops 88358912 | bytes 1513886 | solution.py:52
  878.7 9.0 all-to-all-done
  896.2 70.1 %all-gather.19.cloned.1.call-done = bf16[1024,2048]{1,0:T(8,128)(2,1)} async-done(((bf16[128,2048]{1,0:T(8,128)(2,1)}), bf16[1024,2048]{1,0:T(8,128)(2,1)}) %all-gather.19.cloned.1.call-update) | async-done | bytes 4194320 | tf_op jit(solution)/shard_map/all_gather | solution.py:181
  966.2 7.9 fusion.261
  974.1 18.9 all-gather.23.cloned.1.call-done
  993.0 7.8 fusion.262
  1000.8 20.8 all-gather.25.cloned.1.call-done
  1021.6 76.1 %all-gather.31.cloned.1.call-done = bf16[1,1024,2048]{2,1,0:T(8,128)(2,1)} async-done(((bf16[1,128,2048]{2,1,0:T(8,128)(2,1)}), bf16[1,1024,2048]{2,1,0:T(8,128)(2,1)}) %all-gather.31.cloned.1.call-update) | async-done | bytes 4194320 | tf_op jit(solution)/shard_map/all_gather | solution.py:168
  1097.8 10.1 multiply_convert_fusion.2
  1118.7 30.0 %all_to_all.58 = bf16[8,128,256]{1,2,0:T(8,128)(2,1)S(1)} all-to-all(bf16[8,128,256]{1,2,0:T(8,128)(2,1)S(1)} %copy.340), channel_id=1, replica_groups=mesh['dp'=4,'tensor'=8] {'tensor'}, dimensions={0} | all-to-all | bytes 1048576 | tf_op jit(solution)/shard_map/all_to_all | solution.py:177
  1153.8 60.6 %reduce-scatter.18.cloned.1.call-done = bf16[128,2048]{1,0:T(8,128)(2,1)} async-done(((bf16[1024,2048]{1,0:T(8,128)(2,1)}), bf16[128,2048]{1,0:T(8,128)(2,1)}) %reduce-scatter.18.cloned.1.call-update) | async-done | bytes 524304 | tf_op jit(solution)/shard_map/reduce_scatter | solution.py:210
  1218.0 72.5 %all-gather.29.cloned.1.call-done = bf16[1024,2048]{1,0:T(8,128)(2,1)} async-done(((bf16[128,2048]{1,0:T(8,128)(2,1)}), bf16[1024,2048]{1,0:T(8,128)(2,1)}) %all-gather.29.cloned.1.call-update) | async-done | bytes 4194320 | tf_op jit(solution)/shard_map/all_gather | solution.py:181
  1290.5 8.0 fusion.265
  1303.2 61.9 %all-gather.33.cloned.1.call-done = bf16[1,1024,2048]{2,1,0:T(8,128)(2,1)} async-done(((bf16[1,128,2048]{2,1,0:T(8,128)(2,1)}), bf16[1,1024,2048]{2,1,0:T(8,128)(2,1)}) %all-gather.33.cloned.1.call-update) | async-done | bytes 4194320 | tf_op jit(solution)/shard_map/all_gather | solution.py:168
  1365.2 10.1 multiply_convert_fusion
  1384.5 7.7 convolution_convert_fusion.1
  1392.3 7.6 convolution_convert_fusion
  1400.0 7.4 convolution_convert_fusion.3
  1407.7 7.5 convolution_convert_fusion.2
  1415.3 7.4 convolution_convert_fusion.5
  1422.8 7.5 convolution_convert_fusion.4
  1430.4 7.4 fusion.90
  1438.3 7.4 fusion.93
  1445.7 25.1 reduce-scatter.22.cloned.1.call-done
  1472.8 89.3 %reduce-scatter.14.cloned.1.call-done = bf16[128,2048]{1,0:T(8,128)(2,1)} async-done(((bf16[1024,2048]{1,0:T(8,128)(2,1)}), bf16[128,2048]{1,0:T(8,128)(2,1)}) %reduce-scatter.14.cloned.1.call-update) | async-done | bytes 524304 | tf_op jit(solution)/shard_map/reduce_scatter | solution.py:187
  1562.1 91.6 %reduce-scatter.16.cloned.1.call-done = bf16[128,2048]{1,0:T(8,128)(2,1)} async-done(((bf16[1024,2048]{1,0:T(8,128)(2,1)}), bf16[128,2048]{1,0:T(8,128)(2,1)}) %reduce-scatter.16.cloned.1.call-update) | async-done | bytes 524304 | tf_op jit(solution)/shard_map/reduce_scatter | solution.py:187
  1658.2 7.5 convolution_convert_fusion.7
  1671.1 6.8 convolution_convert_fusion.6
  1678.9 8.1 fusion.224
  1693.2 11.9 add_convert_fusion
  1726.7 232.7 %while.83 = (s32[]{:T(128)}, f32[2,128,128]{2,1,0:T(8,128)}, f32[16,2,64,128]{3,2,0,1:T(8,128)}, f32[16,2,64,128]{3,2,0,1:T(8,128)}, f32[16,2,64,128]{3,2,1,0:T(...) while((s32[]{:T(128)}, f32[2,128,128]{2,1,0:T(8,128)}, ...), condition=%wide.region_35.38_spmd.clone, body=%wide.region_34.37_spmd.clone.sunk | while | flops 201637888 | bytes 4001019 | solution.py:52
  1964.9 252.9 %while.82 = (s32[]{:T(128)}, f32[2,128,128]{2,1,0:T(8,128)}, f32[16,2,64,128]{3,2,0,1:T(8,128)}, f32[16,2,64,128]{3,2,0,1:T(8,128)}, f32[16,2,64,128]{3,2,1,0:T(...) while((s32[]{:T(128)}, f32[2,128,128]{2,1,0:T(8,128)}, ...), condition=%wide.region_24.26_spmd.clone, body=%wide.region_23.25_spmd.clone.sunk | while | flops 201637888 | bytes 4000763 | solution.py:52
  2299.3 7.9 fusion.221
  2336.4 10.7 fusion.219
  2347.2 9.0 add_convert_fusion.1
  2362.1 10.7 all-reduce.41
  2374.6 25.2 reduce-scatter.24.cloned.1.call-done
  2399.7 91.5 %reduce-scatter.20.cloned.1.call-done = bf16[128,2048]{1,0:T(8,128)(2,1)} async-done(((bf16[1024,2048]{1,0:T(8,128)(2,1)}), bf16[128,2048]{1,0:T(8,128)(2,1)}) %reduce-scatter.20.cloned.1.call-update) | async-done | bytes 524304 | tf_op jit(solution)/shard_map/reduce_scatter | solution.py:244
  2493.1 41.6 %all-reduce.40 = (f32[2048]{0:T(1024)S(1)}, f32[2048]{0:T(1024)S(1)}) all-reduce(f32[2048]{0:T(1024)S(1)} %add.452, f32[2048]{0:T(1024)S(1)} %add.453), channel_id=10, replica_groups=mesh['dp'=4,'tensor'=8] {'dp','tensor'}, use_global_device_ids=true, to_apply=%region_44.47.clone | all-reduce | flops 4096 | bytes 32768
  2539.4 57.9 %all-reduce.45.cloned.1.call-done = (bf16[2048,1024]{1,0:T(8,128)(2,1)}, bf16[256,2048]{1,0:T(8,128)(2,1)}) async-done(((bf16[2048,1024]{1,0:T(8,128)(2,1)}, bf16[256,2048]{1,0:T(8,128)(2,1)}), (bf16[2048,1024]{1,0:T(8,128)(2,1)}, bf16[256,2048]{1,0:T(8,128)(2,1)})) %all-reduce.45.cloned.1.call-update) | async-done | bytes 5242896 | tf_op jit(solution)/shard_map/psum | solution.py:281
  (1568 shorter events, 1113.9 us)
Async XLA Ops:
  7.2 204.7 %copy-start = (bf16[2048,2]{0,1:T(2,128)(2,1)S(1)}, bf16[2048,2]{0,1:T(2,128)(2,1)}, u32[]{:S(2)}) copy-start(bf16[2048,2]{0,1:T(2,128)(2,1)} %param.38) | copy-start | bytes 24580
  7.2 86.9 %all-gather.15.cloned.1.call-start = ((), (), s32[]{:S(2)}) async-start(), calls=%async_computation.17 | async-start | bytes 4718592 | tf_op jit(solution)/shard_map/all_gather | solution.py:167
  18.8 149.7 %all-gather.27.cloned.1.call-start = ((), (), s32[]{:S(2)}) async-start(), calls=%async_computation.24 | async-start | bytes 4718592 | tf_op jit(solution)/shard_map/all_gather | solution.py:167
  19.6 868.1 %all-gather.17.cloned.1.call-start = ((), (), s32[]{:S(2)}) async-start(), calls=%async_computation.18 | async-start | bytes 9437184 | tf_op jit(solution)/shard_map/all_gather | solution.py:136
  20.3 875.9 %all-gather.21.cloned.1.call-start = ((), (), s32[]{:S(2)}) async-start(), calls=%async_computation.20 | async-start | bytes 3604480 | tf_op jit(solution)/shard_map/all_gather | solution.py:151
  35.0 672.8 %copy-start.98 = (pred[16,64,64]{2,1,0:T(8,128)(4,1)}, pred[16,64,64]{2,1,0:T(8,128)(4,1)S(1)}, u32[]{:S(2)}) copy-start(pred[16,64,64]{2,1,0:T(8,128)(4,1)S(1)} %get-tuple-element.1499) | copy-start | bytes 196612
  37.9 139.6 %copy-start.150 = (f32[1024]{0:T(1024)}, f32[1024]{0:T(1024)S(1)}, u32[]{:S(2)}) copy-start(f32[1024]{0:T(1024)S(1)} %get-tuple-element.1538) | copy-start | bytes 12292
  37.9 139.6 %copy-start.152 = (f32[1024]{0:T(1024)}, f32[1024]{0:T(1024)S(1)}, u32[]{:S(2)}) copy-start(f32[1024]{0:T(1024)S(1)} %get-tuple-element.1539) | copy-start | bytes 12292
  37.9 139.6 %copy-start.154 = (f32[1024]{0:T(1024)}, f32[1024]{0:T(1024)S(1)}, u32[]{:S(2)}) copy-start(f32[1024]{0:T(1024)S(1)} %get-tuple-element.1540) | copy-start | bytes 12292
  37.9 139.6 %copy-start.156 = (f32[1024]{0:T(1024)}, f32[1024]{0:T(1024)S(1)}, u32[]{:S(2)}) copy-start(f32[1024]{0:T(1024)S(1)} %get-tuple-element.1519) | copy-start | bytes 12292
  37.9 139.6 %copy-start.158 = (f32[1024]{0:T(1024)}, f32[1024]{0:T(1024)S(1)}, u32[]{:S(2)}) copy-start(f32[1024]{0:T(1024)S(1)} %get-tuple-element.1520) | copy-start | bytes 12292
  37.9 139.6 %copy-start.160 = (f32[1024]{0:T(1024)}, f32[1024]{0:T(1024)S(1)}, u32[]{:S(2)}) copy-start(f32[1024]{0:T(1024)S(1)} %get-tuple-element.1518) | copy-start | bytes 12292
  201.5 191.5 %copy-start.3 = (f32[1024,2,128]{2,0,1:T(8,128)}, f32[1024,2,128]{2,0,1:T(8,128)S(1)}, u32[]{:S(2)}) copy-start(f32[1024,2,128]{2,0,1:T(8,128)S(1)} %bitcast_multiply_fusion.20) | copy-start | bytes 3145732
  208.9 499.0 %copy-start.1 = (f32[1024,2,128]{2,0,1:T(8,128)}, f32[1024,2,128]{2,0,1:T(8,128)S(1)}, u32[]{:S(2)}) copy-start(f32[1024,2,128]{2,0,1:T(8,128)S(1)} %bitcast_multiply_fusion.30) | copy-start | bytes 3145732
  533.7 332.3 %copy-start.35 = (f32[16,2,64,128]{3,2,0,1:T(8,128)}, f32[16,2,64,128]{3,2,0,1:T(8,128)S(1)}, u32[]{:S(2)}) copy-start(f32[16,2,64,128]{3,2,0,1:T(8,128)S(1)} %get-tuple-element.794) | copy-start | bytes 3145732
  535.6 164.6 %copy-start.33 = (f32[1024,1,2,128]{3,0,2,1:T(8,128)}, f32[1024,1,2,128]{3,0,2,1:T(8,128)S(1)}, u32[]{:S(2)}) copy-start(f32[1024,1,2,128]{3,0,2,1:T(8,128)S(1)} %copy.427) | copy-start | bytes 3145732
  536.7 163.6 %copy-start.111 = (f32[2,16,64]{2,1,0:T(8,128)S(1)}, f32[2,16,64]{2,1,0:T(8,128)}, u32[]{:S(2)}) copy-start(f32[2,16,64]{2,1,0:T(8,128)} %mul.1285) | copy-start | bytes 24580
  869.9 17.8 all-to-all-start
  873.4 92.8 %all-gather.19.cloned.1.call-start = ((), (), s32[]{:S(2)}) async-start(), calls=%async_computation.19 | async-start | bytes 4718592 | tf_op jit(solution)/shard_map/all_gather | solution.py:181
  893.7 99.3 %all-gather.23.cloned.1.call-start = ((), (), s32[]{:S(2)}) async-start(), calls=%async_computation.21 | async-start | bytes 3604480 | tf_op jit(solution)/shard_map/all_gather | solution.py:152
  894.2 127.4 %all-gather.25.cloned.1.call-start = ((), (), s32[]{:S(2)}) async-start(), calls=%async_computation.22 | async-start | bytes 3604480 | tf_op jit(solution)/shard_map/all_gather | solution.py:153
  895.0 202.8 %all-gather.31.cloned.1.call-start = ((), (), s32[]{:S(2)}) async-start(), calls=%async_computation.38 | async-start | bytes 4718592 | tf_op jit(solution)/shard_map/all_gather | solution.py:168
  896.1 318.3 %reduce-scatter.18.cloned.1.call-start = ((), (), s32[]{:S(2)}) async-start(), calls=%async_computation.27 | async-start | bytes 4718592 | tf_op jit(solution)/shard_map/reduce_scatter | solution.py:210
  1117.2 173.3 %all-gather.29.cloned.1.call-start = ((), (), s32[]{:S(2)}) async-start(), calls=%async_computation.25 | async-start | bytes 4718592 | tf_op jit(solution)/shard_map/all_gather | solution.py:181
  1153.7 317.1 %copy-start.45 = (f32[128,2048]{1,0:T(8,128)}, f32[128,2048]{1,0:T(8,128)S(1)}, u32[]{:S(2)}) copy-start(f32[128,2048]{1,0:T(8,128)S(1)} %get-tuple-element.1533) | copy-start | bytes 3145732
  1217.2 147.9 %all-gather.33.cloned.1.call-start = ((), (), s32[]{:S(2)}) async-start(), calls=%async_computation.39 | async-start | bytes 4718592 | tf_op jit(solution)/shard_map/all_gather | solution.py:168
  1218.0 252.8 %reduce-scatter.22.cloned.1.call-start = ((), (), s32[]{:S(2)}) async-start(), calls=%async_computation.29 | async-start | bytes 4718592 | tf_op jit(solution)/shard_map/reduce_scatter | solution.py:210
  1384.5 177.6 %reduce-scatter.14.cloned.1.call-start = ((), (), s32[]{:S(2)}) async-start(), calls=%async_computation.23 | async-start | bytes 4718592 | tf_op jit(solution)/shard_map/reduce_scatter | solution.py:187
  1392.2 261.5 %reduce-scatter.16.cloned.1.call-start = ((), (), s32[]{:S(2)}) async-start(), calls=%async_computation.26 | async-start | bytes 4718592 | tf_op jit(solution)/shard_map/reduce_scatter | solution.py:187
  1399.9 928.3 %reduce-scatter.32.cloned.1.call-start = ((), (), s32[]{:S(2)}) async-start(), calls=%async_computation.34 | async-start | bytes 3604480 | tf_op jit(solution)/shard_map/reduce_scatter | solution.py:263
  1407.4 920.8 %reduce-scatter.34.cloned.1.call-start = ((), (), s32[]{:S(2)}) async-start(), calls=%async_computation.35 | async-start | bytes 3604480 | tf_op jit(solution)/shard_map/reduce_scatter | solution.py:263
  1415.2 915.7 %reduce-scatter.28.cloned.1.call-start = ((), (), s32[]{:S(2)}) async-start(), calls=%async_computation.32 | async-start | bytes 3604480 | tf_op jit(solution)/shard_map/reduce_scatter | solution.py:260
  1422.8 908.2 %reduce-scatter.30.cloned.1.call-start = ((), (), s32[]{:S(2)}) async-start(), calls=%async_computation.33 | async-start | bytes 3604480 | tf_op jit(solution)/shard_map/reduce_scatter | solution.py:260
  1430.3 903.4 %reduce-scatter.36.cloned.1.call-start = ((), (), s32[]{:S(2)}) async-start(), calls=%async_computation.36 | async-start | bytes 3604480 | tf_op jit(solution)/shard_map/reduce_scatter | solution.py:266
  1437.8 896.0 %reduce-scatter.38.cloned.1.call-start = ((), (), s32[]{:S(2)}) async-start(), calls=%async_computation.37 | async-start | bytes 3604480 | tf_op jit(solution)/shard_map/reduce_scatter | solution.py:266
  1666.7 20.3 all-to-all-start.2
  1687.0 21.4 all-to-all-start.3
  1693.0 663.1 %reduce-scatter.26.cloned.1.call-start = ((), (), s32[]{:S(2)}) async-start(), calls=%async_computation.31 | async-start | bytes 9437184 | tf_op jit(solution)/shard_map/reduce_scatter | solution.py:277
  1705.1 694.6 %reduce-scatter.24.cloned.1.call-start = ((), (), s32[]{:S(2)}) async-start(), calls=%async_computation.30 | async-start | bytes 4718592 | tf_op jit(solution)/shard_map/reduce_scatter | solution.py:244
  1964.9 252.9 %copy-start.4 = (f32[1024,2,128]{2,0,1:T(8,128)S(1)}, f32[1024,2,128]{2,0,1:T(8,128)}, u32[]{:S(2)}) copy-start(f32[1024,2,128]{2,0,1:T(8,128)} %copy-done.3) | copy-start | bytes 3145732
  1964.9 252.9 %copy-start.65 = (f32[2,1024,128]{2,1,0:T(8,128)S(1)}, f32[2,1024,128]{2,1,0:T(8,128)}, u32[]{:S(2)}) copy-start(f32[2,1024,128]{2,1,0:T(8,128)} %copy-done.64) | copy-start | bytes 3145732
  2310.6 180.7 %reduce-scatter.20.cloned.1.call-start = ((), (), s32[]{:S(2)}) async-start(), calls=%async_computation.28 | async-start | bytes 4718592 | tf_op jit(solution)/shard_map/reduce_scatter | solution.py:244
  2328.0 269.3 %all-reduce.45.cloned.1.call-start = ((), (), s32[]{:S(2)}) async-start(), calls=%async_computation.40 | async-start | bytes 10485760 | tf_op jit(solution)/shard_map/psum | solution.py:281
  2361.4 129.8 %copy-start.121 = (f32[4,1,512]{2,1,0:T(1,128)S(1)}, f32[4,1,512]{2,1,0:T(1,128)}, u32[]{:S(2)}) copy-start(f32[4,1,512]{2,1,0:T(1,128)} %copy-done.120) | copy-start | bytes 24580
  2361.4 129.8 %copy-start.179 = (f32[128]{0:T(128)S(1)}, f32[128]{0:T(128)}, u32[]{:S(2)}) copy-start(f32[128]{0:T(128)} %copy-done.178) | copy-start | bytes 1540
  2361.4 129.8 %copy-start.181 = (f32[128]{0:T(128)S(1)}, f32[128]{0:T(128)}, u32[]{:S(2)}) copy-start(f32[128]{0:T(128)} %copy-done.180) | copy-start | bytes 1540
  2361.4 174.5 %copy-start.42 = (f32[128,2048]{1,0:T(8,128)S(1)}, f32[128,2048]{1,0:T(8,128)}, u32[]{:S(2)}) copy-start(f32[128,2048]{1,0:T(8,128)} %copy-done.41) | copy-start | bytes 3145732
  2361.4 174.5 %copy-start.44 = (f32[128,2048]{1,0:T(8,128)S(1)}, f32[128,2048]{1,0:T(8,128)}, u32[]{:S(2)}) copy-start(f32[128,2048]{1,0:T(8,128)} %copy-done.43) | copy-start | bytes 3145732
  (183 other events, 1018.3 us)
Sparse Core Ops, SparseCore 0:
  18.9 75.1 all-gather.14
  96.8 71.6 all-gather.26
  170.6 123.3 all-gather.16
  295.5 25.9 all-gather.20
  893.8 72.4 all-gather.18
  967.7 25.2 all-gather.22
  994.5 27.0 all-gather.24
  1024.3 73.3 all-gather.30
  1117.4 96.9 reduce-scatter.17
  1217.4 73.1 all-gather.28
  1293.5 71.6 all-gather.32
  1384.6 86.1 reduce-scatter.21
  1474.4 87.6 reduce-scatter.13
  1566.0 87.6 reduce-scatter.15
  1656.1 36.0 reduce-scatter.31
  1694.8 36.3 reduce-scatter.33
  1733.6 36.2 reduce-scatter.27
  1772.5 36.3 reduce-scatter.29
  1811.4 36.4 reduce-scatter.35
  1850.4 36.3 reduce-scatter.37
  1890.4 148.8 reduce-scatter.25
  2310.7 89.0 reduce-scatter.23
  2403.4 87.8 reduce-scatter.19
  2493.7 103.5 all-reduce.44
where the time goes:
time: 2640 us; the launch traced here: 2610 us
  waiting for transfers between devices  891 us (34%)
  matrix products  706 us (27%)
  other arithmetic  482 us (18%)
  local copies, waits for them, and re-layouts  402 us (15%)
  blocking collectives  93.6 us (4%)
    dot_general x416, matrix products, matmul(): jnp.dot(left_side, right_side, precision=highest, preferred_element_type=...  426 us
    another operation x6, other arithmetic, delta_rule(): jax.scipy.linalg.solve_triangular(system, right_hand, lower=True, unit_di...  322 us
    reduce_scatter x2, waiting for transfers between devices, per_device(): lax.psum_scatter(jnp.dot(inner_rows, down_full, preferred_element_type=jn...  181 us
    squeeze x160, local copies, waits for them, and re-layouts, delta_rule(): lax.scan(jax.checkpoint(advance), jnp.zeros((head_width, head_width), jnp...  157 us
    all_gather x2, waiting for transfers between devices, per_device(): lax.all_gather(normed_two.astype(jnp.bfloat16), 'tensor', axis=0, tiled=T...  143 us
    all_gather x2, waiting for transfers between devices, per_device(): lax.all_gather(cotangent[batch_index], 'tensor', axis=0, tiled=True)  138 us
    reduce_scatter x2, waiting for transfers between devices, per_device(): lax.psum_scatter((jnp.einsum('tc,dc->td', projected_low, w_inner, preferr...  117 us
    all_gather x2, waiting for transfers between devices, per_device(): lax.all_gather(normed_low, 'tensor', axis=0, tiled=True)  116 us
  transfers between devices with their start and end apart: 27, of which 16 were waited for; matrix products, arithmetic and copies ran while one was open for 58% of the time, Pallas kernels for 0%

commit v1 on v0

v1 whole, which is shorter than its diff:
```python
from functools import partial

import jax
import jax.numpy as jnp
from jax import lax
from jax.experimental import pallas as pl
from jax.experimental.pallas import tpu as pltpu
from jax.sharding import PartitionSpec as P


CHUNK = 128
HALO = 8
epsilon = 1e-06
highest = lax.Precision.HIGHEST
f32 = jnp.float32
bf16 = jnp.bfloat16


def product(left, right, left_dim, right_dim, exact=False):
    dims = (((left_dim,), (right_dim,)), ((), ()))
    if exact:
        return lax.dot_general(left, right, dims, precision=highest, preferred_element_type=f32)
    return lax.dot_general(
        left.astype(bf16), right.astype(bf16), dims, preferred_element_type=f32
    )


def sigmoid(x):
    return 1.0 / (1.0 + jnp.exp(-x))


def segment_tools(lengths_ref):
    ends = []
    total = 0
    for i in range(lengths_ref.shape[0] - 1):
        total = total + lengths_ref[i]
        ends.append(total)

    def segment_of(pos):
        result = 0
        for end in ends:
            result = result + (pos >= end).astype(jnp.int32)
        return result

    return segment_of, len(ends)


def chunk_masks(segment_of, base, chunk):
    col = base + lax.broadcasted_iota(jnp.int32, (chunk, 1), 0)
    row = base + lax.broadcasted_iota(jnp.int32, (1, chunk), 1)
    seg_col = segment_of(col)
    seg_row = segment_of(row)
    first = segment_of(base - 1)
    last = segment_of(base + chunk - 1)
    same = seg_col == seg_row
    strict = (same & (col > row)).astype(f32)
    within = (same & (col >= row)).astype(f32)
    has_past = base > 0
    carry = ((seg_col == first) & has_past).astype(f32)
    close = (seg_col == last).astype(f32)
    keep = ((first == last) & has_past).astype(f32)
    return strict, within, carry, close, keep


def level_masks(chunk):
    row = lax.broadcasted_iota(jnp.int32, (chunk, chunk), 0)
    col = lax.broadcasted_iota(jnp.int32, (chunk, chunk), 1)
    masks = []
    width = 1
    while width < chunk:
        mask = (
            (row // (2 * width) == col // (2 * width))
            & ((row // width) % 2 == 1)
            & ((col // width) % 2 == 0)
        )
        masks.append(mask)
        width *= 2
    return masks, (row == col).astype(f32)


def conv_part(proj_ref, tap_ref, segment_of, base, part, width, chunk):
    taps = tap_ref.shape[0] // 3
    cols = pl.ds(part * width, width)
    main = proj_ref[pl.ds(base, chunk), cols]
    prev = proj_ref[pl.ds(pl.multiple_of(jnp.maximum(base - HALO, 0), HALO), HALO), cols]
    full = jnp.concatenate([prev, main], axis=0)
    col = base + lax.broadcasted_iota(jnp.int32, (chunk, 1), 0)
    seg = segment_of(col)
    total = main * tap_ref[part * taps : part * taps + 1, :]
    shifted = [main]
    for s in range(1, taps):
        valid = (segment_of(col - s) == seg) & (col >= s)
        moved = jnp.where(valid, pltpu.roll(full, s, 0)[HALO:], 0.0)
        shifted.append(moved)
        total = total + moved * tap_ref[part * taps + s : part * taps + s + 1, :]
    return total, shifted


def heads_of(x, heads):
    return [x[:, h * 128 : (h + 1) * 128] for h in range(heads)]


def unit_rows(a, scale):
    r = lax.rsqrt(jnp.sum(a * a, axis=-1, keepdims=True) + epsilon)
    return a * (r * scale)


def mixer_forward_kernel(exact, group, lengths_ref, proj_ref, beta_ref, tap_ref, gain_ref,
                         mixed_ref, heads_ref, fixed_ref, delta_ref, state_ref, inverse_ref,
                         query_s, key_s, value_s, score_s):
    rows_all = proj_ref.shape[0]
    width = proj_ref.shape[1] // 4
    heads = width // 128
    chunk = CHUNK
    count = rows_all // chunk
    segment_of, segments = segment_tools(lengths_ref)

    @pl.loop(0, count)
    def _(c):
        base = pl.multiple_of(c * chunk, chunk)
        rows = pl.ds(base, chunk)
        for part, target in enumerate((query_s, key_s, value_s)):
            pre, _ = conv_part(proj_ref, tap_ref, segment_of, base, part, width, chunk)
            act = pre * sigmoid(pre)
            if part == 2:
                target[rows, :] = act
            else:
                scale = 128 ** (-0.5) if part == 0 else 1.0
                for h, a in enumerate(heads_of(act, heads)):
                    target[rows, h * 128 : (h + 1) * 128] = unit_rows(a, scale)

    def beta_of(base, h):
        pos = base + lax.broadcasted_iota(jnp.int32, (chunk, 1), 0)
        live = (segment_of(pos) < segments).astype(f32)
        return sigmoid(beta_ref[pl.ds(base, chunk), h : h + 1]) * live

    masks, eye = level_masks(chunk)

    @pl.loop(0, count // group)
    def _(g):
        lowers, places = [], []
        for i in range(group):
            c = g * group + i
            base = pl.multiple_of(c * chunk, chunk)
            strict, within, _, _, _ = chunk_masks(segment_of, base, chunk)
            for h in range(heads):
                cols = slice(h * 128, (h + 1) * 128)
                k = key_s[pl.ds(base, chunk), cols]
                q = query_s[pl.ds(base, chunk), cols]
                lowers.append(product(k, k, 1, 1, exact) * strict * beta_of(base, h))
                score_s[c * heads + h] = (product(q, k, 1, 1, exact) * within).astype(score_s.dtype)
                places.append(c * heads + h)
        inverses = [eye - jnp.where(masks[0], lower, 0.0) for lower in lowers]
        for mask in masks[1:]:
            steps = [product(jnp.where(mask, lower, 0.0), x, 1, 0, True) for lower, x in zip(lowers, inverses)]
            inverses = [x - product(x, step, 1, 0, True) for x, step in zip(inverses, steps)]
        for place, x in zip(places, inverses):
            inverse_ref[place] = x

    def advance(c, states):
        base = pl.multiple_of(c * chunk, chunk)
        rows = pl.ds(base, chunk)
        _, _, carry, close, keep = chunk_masks(segment_of, base, chunk)
        new_states = []
        for h in range(heads):
            cols = slice(h * 128, (h + 1) * 128)
            state = states[h]
            k = key_s[rows, cols]
            q = query_s[rows, cols]
            delta = value_s[rows, cols] - carry * product(k, state, 1, 0, exact)
            fixed = product(inverse_ref[c * heads + h], beta_of(base, h) * delta, 1, 0, exact)
            out = carry * product(q, state, 1, 0, exact) + product(
                score_s[c * heads + h], fixed, 1, 0, exact)
            state_ref[c * heads + h] = state
            new_states.append(keep * state + product(k, close * fixed, 0, 0, exact))
            delta_ref[rows, cols] = delta
            fixed_ref[rows, cols] = fixed
            heads_ref[rows, cols] = out
            gate = proj_ref[rows, 3 * width + h * 128 : 3 * width + (h + 1) * 128]
            r = lax.rsqrt(jnp.mean(out * out, axis=-1, keepdims=True) + epsilon)
            mixed_ref[rows, cols] = (
                out * r * gain_ref[h : h + 1, :] * (gate * sigmoid(gate))
            ).astype(mixed_ref.dtype)
        return tuple(new_states)

    lax.fori_loop(0, count, advance, tuple(jnp.zeros((128, 128), f32) for _ in range(heads)))


def mixer_backward_kernel(exact, lengths_ref, proj_ref, beta_ref, tap_ref, gain_ref, grad_ref,
                          heads_ref, fixed_ref, delta_ref, state_ref, inverse_ref,
                          dproj_ref, dbeta_ref, dtap_ref, dgain_ref,
                          query_s, key_s, pre_s, dout_s, dpre_s):
    rows_all = proj_ref.shape[0]
    width = proj_ref.shape[1] // 4
    heads = width // 128
    chunk = CHUNK
    count = rows_all // chunk
    taps = tap_ref.shape[0] // 3
    segment_of, segments = segment_tools(lengths_ref)
    dgain_ref[...] = jnp.zeros_like(dgain_ref)
    dtap_ref[...] = jnp.zeros_like(dtap_ref)

    @pl.loop(0, count)
    def _(c):
        base = pl.multiple_of(c * chunk, chunk)
        rows = pl.ds(base, chunk)
        for part in range(3):
            pre, _ = conv_part(proj_ref, tap_ref, segment_of, base, part, width, chunk)
            pre_s[rows, part * width : (part + 1) * width] = pre
            if part < 2:
                act = pre * sigmoid(pre)
                target = (query_s, key_s)[part]
                scale = 128 ** (-0.5) if part == 0 else 1.0
                for h, a in enumerate(heads_of(act, heads)):
                    target[rows, h * 128 : (h + 1) * 128] = unit_rows(a, scale)
        for h in range(heads):
            cols = slice(h * 128, (h + 1) * 128)
            gate_cols = slice(3 * width + h * 128, 3 * width + (h + 1) * 128)
            out = heads_ref[rows, cols]
            gate = proj_ref[rows, gate_cols]
            grad = grad_ref[rows, cols].astype(f32)
            gain = gain_ref[h : h + 1, :]
            sg = sigmoid(gate)
            silu = gate * sg
            r = lax.rsqrt(jnp.mean(out * out, axis=-1, keepdims=True) + epsilon)
            normed = out * r
            dgain_ref[h : h + 1, :] += jnp.sum(grad * normed * silu, axis=0, keepdims=True)
            dproj_ref[rows, gate_cols] = (
                grad * normed * gain * (sg * (1.0 + gate * (1.0 - sg)))
            ).astype(dproj_ref.dtype)
            weighted = grad * gain * silu
            dout_s[rows, cols] = r * weighted - out * (r * r * r) * jnp.mean(
                weighted * out, axis=-1, keepdims=True)

    dpre_s[rows_all : rows_all + HALO, :] = jnp.zeros((HALO, 3 * width), f32)

    def retreat(step, dstates):
        c = count - 1 - step
        base = pl.multiple_of(c * chunk, chunk)
        rows = pl.ds(base, chunk)
        strict, within, carry, close, keep = chunk_masks(segment_of, base, chunk)
        pos = base + lax.broadcasted_iota(jnp.int32, (chunk, 1), 0)
        live = (segment_of(pos) < segments).astype(f32)
        new_dstates = []
        for h in range(heads):
            cols = slice(h * 128, (h + 1) * 128)
            place = c * heads + h
            k = key_s[rows, cols]
            q = query_s[rows, cols]
            dout = dout_s[rows, cols]
            state = state_ref[place]
            inverse = inverse_ref[place]
            fixed = fixed_ref[rows, cols]
            delta = delta_ref[rows, cols]
            dstate = dstates[h]
            rate = sigmoid(beta_ref[rows, h : h + 1])
            beta = rate * live
            scores = product(q, k, 1, 1, exact) * within
            gram = product(k, k, 1, 1, exact) * strict
            dfixed = product(scores, dout, 0, 0, exact) + close * product(k, dstate, 1, 0, exact)
            drhs = product(inverse, dfixed, 0, 0, exact)
            ddelta = beta * drhs
            carried_dout = carry * dout
            carried_ddelta = carry * ddelta
            new_dstates.append(
                keep * dstate
                + product(q, carried_dout, 0, 0, exact)
                - product(k, carried_ddelta, 0, 0, exact)
            )
            dscores = product(dout, fixed, 1, 1, exact) * within
            dlower = -product(drhs, fixed, 1, 1, exact) * strict
            dgram = beta * dlower
            dq = product(carried_dout, state, 1, 1, exact) + product(dscores, k, 1, 0, exact)
            dk = (
                product(dscores, q, 0, 0, exact)
                + close * product(fixed, dstate, 1, 1, exact)
                - product(carried_ddelta, state, 1, 1, exact)
                + product(dgram, k, 1, 0, exact)
                + product(dgram, k, 0, 0, exact)
            )
            drate = live * (
                jnp.sum(drhs * delta, axis=-1, keepdims=True)
                + jnp.sum(dlower * gram, axis=-1, keepdims=True)
            )
            dbeta_ref[rows, h : h + 1] = (drate * rate * (1.0 - rate)).astype(dbeta_ref.dtype)
            for part, da in enumerate((dq, dk, ddelta)):
                part_cols = slice(part * width + h * 128, part * width + (h + 1) * 128)
                pre = pre_s[rows, part_cols]
                sg = sigmoid(pre)
                if part < 2:
                    a = pre * sg
                    scale = 128 ** (-0.5) if part == 0 else 1.0
                    r = lax.rsqrt(jnp.sum(a * a, axis=-1, keepdims=True) + epsilon)
                    da = (scale * r) * (da - a * (r * r) * jnp.sum(da * a, axis=-1, keepdims=True))
                dpre_s[rows, part_cols] = da * (sg * (1.0 + pre * (1.0 - sg)))
        return tuple(new_dstates)

    lax.fori_loop(0, count, retreat, tuple(jnp.zeros((128, 128), f32) for _ in range(heads)))

    @pl.loop(0, count)
    def _(c):
        base = pl.multiple_of(c * chunk, chunk)
        rows = pl.ds(base, chunk)
        col = base + lax.broadcasted_iota(jnp.int32, (chunk, 1), 0)
        seg = segment_of(col)
        for part in range(3):
            cols = slice(part * width, (part + 1) * width)
            _, shifted = conv_part(proj_ref, tap_ref, segment_of, base, part, width, chunk)
            full = dpre_s[pl.ds(base, chunk + HALO), cols]
            main = full[:chunk]
            total = main * tap_ref[part * taps : part * taps + 1, :]
            for s in range(taps):
                at = slice(part * taps + s, part * taps + s + 1)
                dtap_ref[at, :] += jnp.sum(main * shifted[s], axis=0, keepdims=True)
                if s > 0:
                    valid = (segment_of(col + s) == seg) & (col + s < rows_all)
                    moved = pltpu.roll(full, chunk + HALO - s, 0)[:chunk]
                    total = total + jnp.where(valid, moved, 0.0) * tap_ref[at, :]
            dproj_ref[rows, cols] = total.astype(dproj_ref.dtype)


def vmem():
    return pl.BlockSpec(memory_space=pltpu.VMEM)


def mixer_forward(lengths_row, projected, beta_logits, taps, gain, exact=True, group=4):
    rows, wide = projected.shape
    width = wide // 4
    heads = width // 128
    places = rows // CHUNK * heads
    group = min(group, rows // CHUNK)
    return pl.pallas_call(
        partial(mixer_forward_kernel, exact, group),
        out_shape=(
            jax.ShapeDtypeStruct((rows, width), bf16),
            jax.ShapeDtypeStruct((rows, width), f32),
            jax.ShapeDtypeStruct((rows, width), f32),
            jax.ShapeDtypeStruct((rows, width), f32),
            jax.ShapeDtypeStruct((places, 128, 128), f32),
            jax.ShapeDtypeStruct((places, CHUNK, CHUNK), f32),
        ),
        in_specs=[pl.BlockSpec(memory_space=pltpu.SMEM)] + [vmem()] * 4,
        out_specs=(vmem(),) * 6,
        scratch_shapes=[pltpu.VMEM((rows, width), f32)] * 3
        + [pltpu.VMEM((places, CHUNK, CHUNK), f32 if exact else bf16)],
        compiler_params=pltpu.CompilerParams(vmem_limit_bytes=48 * 2**20),
        cost_estimate=pl.CostEstimate(flops=10**10, bytes_accessed=10**7, transcendentals=10**6),
        name="mixer_forward",
    )(lengths_row, projected, beta_logits, taps, gain)


def mixer_backward(lengths_row, projected, beta_logits, taps, gain, grad, saved, exact=True):
    rows, wide = projected.shape
    width = wide // 4
    heads = width // 128
    return pl.pallas_call(
        partial(mixer_backward_kernel, exact),
        out_shape=(
            jax.ShapeDtypeStruct((rows, wide), bf16),
            jax.ShapeDtypeStruct((rows, heads), bf16),
            jax.ShapeDtypeStruct(taps.shape, f32),
            jax.ShapeDtypeStruct(gain.shape, f32),
        ),
        in_specs=[pl.BlockSpec(memory_space=pltpu.SMEM)] + [vmem()] * 10,
        out_specs=(vmem(),) * 4,
        scratch_shapes=[pltpu.VMEM((rows, width), f32)] * 2
        + [pltpu.VMEM((rows, 3 * width), f32), pltpu.VMEM((rows, width), f32),
           pltpu.VMEM((rows + HALO, 3 * width), f32)],
        compiler_params=pltpu.CompilerParams(vmem_limit_bytes=56 * 2**20),
        cost_estimate=pl.CostEstimate(flops=10**10, bytes_accessed=10**7, transcendentals=10**6),
        name="mixer_backward",
    )(lengths_row, projected, beta_logits, taps, gain, grad, *saved)


def root_scale(row_values, gain_vector):
    row_scale = lax.rsqrt(jnp.mean(row_values * row_values, axis=-1, keepdims=True) + epsilon)
    return (row_values * row_scale * gain_vector, row_scale)


def norm_backward(row_values, row_scale, gain_vector, normed_grad):
    weighted = normed_grad * gain_vector
    rows_grad = row_scale * weighted - row_values * row_scale * row_scale * row_scale * jnp.mean(
        weighted * row_values, axis=-1, keepdims=True
    )
    gain_grad = jnp.sum(normed_grad * row_values * row_scale, axis=0)
    return (rows_grad, gain_grad)


def gather(x, axis_name, axis=0):
    return lax.all_gather(x, axis_name, axis=axis, tiled=True)


def scatter_sum(x, axis_name, axis=0):
    return lax.psum_scatter(
        x.astype(bf16), axis_name, scatter_dimension=axis, tiled=True
    ).astype(f32)


def dot(a, b):
    return jnp.dot(a, b, preferred_element_type=f32)


def dot_nt(a, b):
    return jnp.einsum("tk,nk->tn", a, b, preferred_element_type=f32)


def dot_tn(a, b):
    return jnp.einsum("tm,tn->mn", a, b, preferred_element_type=f32)


def per_device(
    inputs,
    lengths,
    norm_gain,
    ffn_gain,
    w_query,
    w_key,
    w_value,
    w_gate_out,
    w_beta,
    conv_weight,
    head_gain,
    w_out,
    w_gate,
    w_up,
    w_down,
    cotangent,
):
    batches = range(inputs.shape[0])
    local_width = w_query.shape[1]
    w_inner = jnp.concatenate([w_query, w_key, w_value, w_gate_out], axis=1)
    taps = conv_weight.astype(f32).reshape(-1, local_width)
    gain_heads = head_gain.astype(f32)
    gain_one = gather(norm_gain, "dp").astype(f32)
    gain_two = gather(ffn_gain, "dp").astype(f32)
    rows_in = [inputs[m].astype(f32) for m in batches]
    one = [root_scale(rows, gain_one) for rows in rows_in]
    gathered_one = [gather(one[m][0].astype(bf16), "tensor") for m in batches]
    projected = [dot(rows, w_inner) for rows in gathered_one]
    beta_logits = [dot(rows, w_beta) for rows in gathered_one]
    gate_full = gather(w_gate, "dp")
    up_full = gather(w_up, "dp")
    down_full = gather(w_down, "dp", 1)
    out_full = gather(w_out, "tensor")
    grad_rows = [gather(cotangent[m], "tensor") for m in batches]
    mixed, saved = [], []
    for m in batches:
        low, *kept = mixer_forward(lengths[m, 0], projected[m], beta_logits[m], taps, gain_heads)
        mixed.append(low)
        saved.append(kept)
    token_heads = [
        lax.all_to_all(low, "tensor", split_axis=0, concat_axis=1, tiled=True) for low in mixed
    ]
    hidden = [rows_in[m] + dot(token_heads[m], out_full) for m in batches]
    two = [root_scale(rows, gain_two) for rows in hidden]
    gathered_two = [gather(two[m][0].astype(bf16), "tensor") for m in batches]
    result_rows, inner_rows, gate_grads, up_grads, hidden_grads = [], [], [], [], []
    attended_low, mixed_grads = [], []
    gain_two_sum = 0.0
    for m in batches:
        gate_values = dot(gathered_two[m], gate_full)
        up_values = dot(gathered_two[m], up_full)
        sigmoid_gate = jax.nn.sigmoid(gate_values)
        silu_gate = gate_values * sigmoid_gate
        inner = (silu_gate * up_values).astype(bf16)
        inner_grad = dot_nt(grad_rows[m], down_full)
        gate_grad = (
            inner_grad * up_values * sigmoid_gate * (1.0 + gate_values * (1.0 - sigmoid_gate))
        ).astype(bf16)
        up_grad = (inner_grad * silu_gate).astype(bf16)
        normed_grad = scatter_sum(dot_nt(gate_grad, gate_full) + dot_nt(up_grad, up_full), "tensor")
        result_rows.append(hidden[m] + scatter_sum(dot(inner, down_full), "tensor"))
        norm_grad, gain_part = norm_backward(hidden[m], two[m][1], gain_two, normed_grad)
        gain_two_sum = gain_two_sum + gain_part
        hidden_grad = cotangent[m].astype(f32) + norm_grad
        low = hidden_grad.astype(bf16)
        token_grad = dot_nt(low, out_full).astype(bf16)
        mixed_grads.append(
            lax.all_to_all(token_grad, "tensor", split_axis=1, concat_axis=0, tiled=True)
        )
        inner_rows.append(inner)
        gate_grads.append(gate_grad)
        up_grads.append(up_grad)
        hidden_grads.append(hidden_grad)
        attended_low.append(low)
    grad_all = jnp.concatenate(grad_rows)
    two_all = jnp.concatenate(gathered_two)
    gate_share = scatter_sum(dot_tn(two_all, jnp.concatenate(gate_grads)), "dp")
    up_share = scatter_sum(dot_tn(two_all, jnp.concatenate(up_grads)), "dp")
    down_share = scatter_sum(dot_tn(jnp.concatenate(inner_rows), grad_all), "dp", 1)
    out_grad = lax.psum_scatter(
        dot_tn(jnp.concatenate(token_heads), jnp.concatenate(attended_low)).astype(bf16),
        "tensor",
        scatter_dimension=0,
        tiled=True,
    )
    input_grads, projected_low, beta_low = [], [], []
    taps_sum, heads_sum, gain_one_sum = 0.0, 0.0, 0.0
    for m in batches:
        projected_grad, beta_grad, taps_part, heads_part = mixer_backward(
            lengths[m, 0], projected[m], beta_logits[m], taps, gain_heads, mixed_grads[m], saved[m]
        )
        normed_grad = scatter_sum(dot_nt(projected_grad, w_inner) + dot_nt(beta_grad, w_beta), "tensor")
        norm_grad, gain_part = norm_backward(rows_in[m], one[m][1], gain_one, normed_grad)
        input_grads.append(hidden_grads[m] + norm_grad)
        gain_one_sum = gain_one_sum + gain_part
        taps_sum = taps_sum + taps_part
        heads_sum = heads_sum + heads_part
        projected_low.append(projected_grad)
        beta_low.append(beta_grad)
    one_all = jnp.concatenate(gathered_one)
    inner_sum = dot_tn(one_all, jnp.concatenate(projected_low))
    beta_sum = dot_tn(one_all, jnp.concatenate(beta_low))
    gain_one_total = lax.psum_scatter(
        gain_one_sum, ("dp", "tensor"), scatter_dimension=0, tiled=True)
    gain_two_total = lax.psum_scatter(
        gain_two_sum, ("dp", "tensor"), scatter_dimension=0, tiled=True)
    inner_total, beta_total, conv_total, heads_total, out_total = (
        lax.psum(part.astype(bf16), "dp").astype(f32)
        for part in (inner_sum, beta_sum, taps_sum, heads_sum, out_grad)
    )
    return (
        jnp.stack(result_rows),
        jnp.stack(input_grads),
        gain_one_total,
        gain_two_total,
        inner_total[:, :local_width],
        inner_total[:, local_width : 2 * local_width],
        inner_total[:, 2 * local_width : 3 * local_width],
        inner_total[:, 3 * local_width :],
        beta_total,
        conv_total.reshape(conv_weight.shape),
        heads_total,
        out_total,
        gate_share,
        up_share,
        down_share,
    )


def solution(mesh):
    in_specs = (
        P(None, ("dp", "tensor"), None),
        P(None, "dp", None),
        P("dp"),
        P("dp"),
        P(None, "tensor"),
        P(None, "tensor"),
        P(None, "tensor"),
        P(None, "tensor"),
        P(None, "tensor"),
        P(None, None, "tensor"),
        P("tensor", None),
        P("tensor", None),
        P("dp", "tensor"),
        P("dp", "tensor"),
        P("tensor", "dp"),
        P(None, ("dp", "tensor"), None),
    )
    out_specs = (
        P(None, ("dp", "tensor"), None),
        P(None, ("dp", "tensor"), None),
        P(("dp", "tensor")),
        P(("dp", "tensor")),
        P(None, "tensor"),
        P(None, "tensor"),
        P(None, "tensor"),
        P(None, "tensor"),
        P(None, "tensor"),
        P(None, None, "tensor"),
        P("tensor", None),
        P("tensor", None),
        P("dp", "tensor"),
        P("dp", "tensor"),
        P("tensor", "dp"),
    )
    return jax.shard_map(
        per_device, mesh=mesh, in_specs=in_specs, out_specs=out_specs, check_vma=False
    )
```

time: 2640 us -> 1650 us (0.62)
  matrix products: 706 us -> 203 us
  other arithmetic: 482 us -> 33.9 us
  local copies, waits for them, and re-layouts: 402 us -> 43.7 us
  waiting for transfers between devices: 891 us -> 1060 us
  Pallas kernels: 0 us -> 159 us
  blocking collectives: 93.6 us -> 120 us
    dot_general x466 -> x30, matrix products: 686 us -> 203 us  [the longest x12 77.8 us: dot(): return jnp.dot(a, b, preferred_element_type=f32)]
    another operation x40 -> x0, other arithmetic: 350 us -> none  [the longest x6 322 us: delta_rule(): jax.scipy.linalg.solve_triangular(system, right_hand, lower=True, unit_di...]
    pallas_call x0 -> x4, Pallas kernels: none -> 159 us  [the longest x2 90.5 us: mixer_backward(): pl.pallas_call(partial(mixer_backward_kernel, exact), out_shape=(jax.Shap...]
    squeeze x160 -> x1, local copies, waits for them, and re-layouts: 157 us -> 0.01 us  [per_device(): lengths[m, 0]]
    all_gather x10, waiting for transfers between devices: 437 us -> 515 us  [gather(): return lax.all_gather(x, axis_name, axis=axis, tiled=True)]
    slice x83 -> x2, local copies, waits for them, and re-layouts: 60.5 us -> 8.18 us  [the longest x1 5.8 us: per_device(): inner_total[:, 3 * local_width:]]
    dynamic_slice x96 -> x0, local copies, waits for them, and re-layouts: 51.4 us -> none  [delta_rule(): lax.scan(jax.checkpoint(advance), jnp.zeros((head_width, head_width), jnp...]
    mul x70 -> x0, local copies, waits for them, and re-layouts: 49 us -> none  [the longest x32 22 us: advance(): close_part[:, None] * corrected]
  transfers between devices with their start and end apart: 27 -> 22, of which waited for: 16 -> 19; matrix products, arithmetic and copies ran while one was open for 58% -> 14% of each run, Pallas kernels for 0% -> 10%
where the time goes in v1:
time: 1650 us; the launch traced here: 1640 us
  waiting for transfers between devices  1060 us (64%)
  matrix products  203 us (12%)
  Pallas kernels  159 us (10%)
  blocking collectives  120 us (7%)
  local copies, waits for them, and re-layouts  43.7 us (3%)
  other arithmetic  33.9 us (2%)
    all_gather x10, waiting for transfers between devices, gather(): return lax.all_gather(x, axis_name, axis=axis, tiled=True)  515 us
    reduce_scatter x9, waiting for transfers between devices, scatter_sum(): lax.psum_scatter(x.astype(bf16), axis_name, scatter_dimension=axis, tiled...  361 us
    psum x1, waiting for transfers between devices, per_device(): lax.psum(part.astype(bf16), 'dp').astype(f32)  99.5 us
    pallas_call x2, Pallas kernels, mixer_backward(): pl.pallas_call(partial(mixer_backward_kernel, exact), out_shape=(jax.Shap...  90.5 us
    dot_general x12, matrix products, dot(): return jnp.dot(a, b, preferred_element_type=f32)  77.8 us
    dot_general x12, matrix products, dot_nt(): return jnp.einsum('tk,nk->tn', a, b, preferred_element_type=f32)  69.9 us
    pallas_call x2, Pallas kernels, mixer_forward(): pl.pallas_call(partial(mixer_forward_kernel, exact, group), out_shape=(ja...  68.3 us
    reduce_scatter x1, waiting for transfers between devices, per_device(): lax.psum_scatter(dot_tn(jnp.concatenate(token_heads), jnp.concatenate(att...  58.6 us
  transfers between devices with their start and end apart: 22, of which 19 were waited for; matrix products, arithmetic and copies ran while one was open for 14% of the time, Pallas kernels for 10%

profile of v1, /device:TPU:0, one launch (start us, length us, event | category | flops | bytes accessed | tf_op | source)
XLA Modules:
  0.0 1643.2 jit_solution(16406795382630413594)
XLA Ops:
  8.0 6.1 all-gather.2
  25.5 68.1 %all-gather.15.cloned.1.call-done = bf16[1024,2048]{1,0:T(8,128)(2,1)} async-done(((bf16[128,2048]{1,0:T(8,128)(2,1)}), bf16[1024,2048]{1,0:T(8,128)(2,1)}) %all-gather.15.cloned.1.call-update) | async-done | bytes 4194320 | tf_op jit(solution)/shard_map/all_gather | solution.py:390
  97.2 8.6 fusion.88.proj_ref
  105.8 34.2 %mixer_forward.2 = (bf16[1024,256]{1,0:T(8,128)(2,1)S(1)}, f32[1024,256]{1,0:T(8,128)S(1)}, f32[1024,256]{1,0:T(8,128)S(1)}, f32[1024,256]{1,0:T(8,128)S(1)}, f3...) custom-call(s32[3]{0:T(128)S(1)} %get-tuple-element.94.lengths_ref, f32[1024,1024]{1,0:T(8,128)} %fusion.88.proj_ref, ...), custom_call_target="tpu_custom_call" | custom-call | flops 10000000000 | bytes 10000000 | tf_op jit(solution)/shard_map/mixer_forward/pallas_call | solution.py:332
  153.7 24.4 %all-to-all-done = bf16[8,128,256]{1,2,0:T(8,128)(2,1)S(1)} async-done(((bf16[8,128,256]{1,2,0:T(8,128)(2,1)}), bf16[8,128,256]{1,2,0:T(8,128)(2,1)S(1)}, u32[]{:S(2)}, u32[]{:S(2)}) %all-to-all-start) | async-done | bytes 524320 | tf_op jit(solution)/shard_map/all_to_all | solution.py:452
  178.1 49.7 %all-gather.17.cloned.1.call-done = bf16[2048,2048]{1,0:T(8,128)(2,1)} async-done(((bf16[256,2048]{1,0:T(8,128)(2,1)}), bf16[2048,2048]{1,0:T(8,128)(2,1)}) %all-gather.17.cloned.1.call-update) | async-done | bytes 8388624 | tf_op jit(solution)/shard_map/all_gather | solution.py:390
  238.3 16.9 %all-gather.21.cloned.1.call-done = bf16[2048,704]{0,1:T(8,128)(2,1)} async-done(((bf16[512,704]{0,1:T(8,128)(2,1)}), bf16[2048,704]{0,1:T(8,128)(2,1)}) %all-gather.21.cloned.1.call-update) | async-done | bytes 2883600 | tf_op jit(solution)/shard_map/all_gather | solution.py:390
  255.3 76.0 %all-gather.19.cloned.1.call-done = bf16[1024,2048]{1,0:T(8,128)(2,1)} async-done(((bf16[128,2048]{1,0:T(8,128)(2,1)}), bf16[1024,2048]{1,0:T(8,128)(2,1)}) %all-gather.19.cloned.1.call-update) | async-done | bytes 4194320 | tf_op jit(solution)/shard_map/all_gather | solution.py:390
  331.3 7.8 fusion.90
  339.1 18.9 %all-gather.23.cloned.1.call-done = bf16[2048,704]{0,1:T(8,128)(2,1)} async-done(((bf16[512,704]{0,1:T(8,128)(2,1)}), bf16[2048,704]{0,1:T(8,128)(2,1)}) %all-gather.23.cloned.1.call-update) | async-done | bytes 2883600 | tf_op jit(solution)/shard_map/all_gather | solution.py:390
  358.0 7.8 fusion.91
  365.8 20.7 %all-gather.25.cloned.1.call-done = bf16[704,2048]{1,0:T(8,128)(2,1)} async-done(((bf16[704,512]{1,0:T(8,128)(2,1)}), bf16[704,2048]{1,0:T(8,128)(2,1)}) %all-gather.25.cloned.1.call-update) | async-done | bytes 2883600 | tf_op jit(solution)/shard_map/all_gather | solution.py:390
  386.5 76.1 %all-gather.31.cloned.1.call-done = bf16[1,1024,2048]{2,1,0:T(8,128)(2,1)} async-done(((bf16[1,128,2048]{2,1,0:T(8,128)(2,1)}), bf16[1,1024,2048]{2,1,0:T(8,128)(2,1)}) %all-gather.31.cloned.1.call-update) | async-done | bytes 4194320 | tf_op jit(solution)/shard_map/all_gather | solution.py:390
  462.7 10.1 multiply_convert_fusion.2
  482.0 55.1 %all-gather.27.cloned.1.call-done = bf16[1024,2048]{1,0:T(8,128)(2,1)} async-done(((bf16[128,2048]{1,0:T(8,128)(2,1)}), bf16[1024,2048]{1,0:T(8,128)(2,1)}) %all-gather.27.cloned.1.call-update) | async-done | bytes 4194320 | tf_op jit(solution)/shard_map/all_gather | solution.py:390
  540.6 8.4 fusion.92.proj_ref
  549.1 34.1 %mixer_forward.3 = (bf16[1024,256]{1,0:T(8,128)(2,1)S(1)}, f32[1024,256]{1,0:T(8,128)S(1)}, f32[1024,256]{1,0:T(8,128)S(1)}, f32[1024,256]{1,0:T(8,128)S(1)}, f3...) custom-call(s32[3]{0:T(128)S(1)} %get-tuple-element.95.lengths_ref, f32[1024,1024]{1,0:T(8,128)} %fusion.92.proj_ref, ...), custom_call_target="tpu_custom_call" | custom-call | flops 10000000000 | bytes 10000000 | tf_op jit(solution)/shard_map/mixer_forward/pallas_call | solution.py:332
  588.2 17.5 %all_to_all.76 = bf16[8,128,256]{1,2,0:T(8,128)(2,1)S(1)} all-to-all(bf16[8,128,256]{1,2,0:T(8,128)(2,1)} %copy.48), channel_id=1, replica_groups=mesh['dp'=4,'tensor'=8] {'tensor'}, dimensions={0} | all-to-all | bytes 1048576 | tf_op jit(solution)/shard_map/all_to_all | solution.py:452
  610.6 21.4 %reduce-scatter.15.cloned.1.call-done = bf16[128,2048]{1,0:T(8,128)(2,1)} async-done(((bf16[1024,2048]{1,0:T(8,128)(2,1)}), bf16[128,2048]{1,0:T(8,128)(2,1)}) %reduce-scatter.15.cloned.1.call-update) | async-done | bytes 524304 | tf_op jit(solution)/shard_map/reduce_scatter | solution.py:394
  636.1 72.1 %all-gather.29.cloned.1.call-done = bf16[1024,2048]{1,0:T(8,128)(2,1)} async-done(((bf16[128,2048]{1,0:T(8,128)(2,1)}), bf16[1024,2048]{1,0:T(8,128)(2,1)}) %all-gather.29.cloned.1.call-update) | async-done | bytes 4194320 | tf_op jit(solution)/shard_map/all_gather | solution.py:390
  708.3 8.0 fusion.94
  721.1 61.8 %all-gather.33.cloned.1.call-done = bf16[1,1024,2048]{2,1,0:T(8,128)(2,1)} async-done(((bf16[1,128,2048]{2,1,0:T(8,128)(2,1)}), bf16[1,1024,2048]{2,1,0:T(8,128)(2,1)}) %all-gather.33.cloned.1.call-update) | async-done | bytes 4194320 | tf_op jit(solution)/shard_map/all_gather | solution.py:390
  782.9 10.1 multiply_convert_fusion
  802.2 7.7 convolution_convert_fusion.1
  817.3 7.4 convolution_convert_fusion.3
  824.8 11.5 convolution_convert_fusion.4
  836.4 10.8 fusion.11
  847.3 41.2 %reduce-scatter.19.cloned.1.call-done = bf16[128,2048]{1,0:T(8,128)(2,1)} async-done(((bf16[1024,2048]{1,0:T(8,128)(2,1)}), bf16[128,2048]{1,0:T(8,128)(2,1)}) %reduce-scatter.19.cloned.1.call-update) | async-done | bytes 524304 | tf_op jit(solution)/shard_map/reduce_scatter | solution.py:394
  889.9 89.9 %reduce-scatter.13.cloned.1.call-done = bf16[128,2048]{1,0:T(8,128)(2,1)} async-done(((bf16[1024,2048]{1,0:T(8,128)(2,1)}), bf16[128,2048]{1,0:T(8,128)(2,1)}) %reduce-scatter.13.cloned.1.call-update) | async-done | bytes 524304 | tf_op jit(solution)/shard_map/reduce_scatter | solution.py:394
  984.2 6.3 convolution_convert_fusion
  991.6 6.4 convolution_convert_fusion.5
  998.0 19.3 %all_to_all.77 = bf16[128,8,256]{2,0,1:T(8,128)(2,1)} all-to-all(bf16[128,8,256]{2,0,1:T(8,128)(2,1)S(1)} %bitcast.134), channel_id=1, replica_groups=mesh['dp'=4,'tensor'=8] {'tensor'}, dimensions={1} | all-to-all | bytes 1048576 | tf_op jit(solution)/shard_map/all_to_all | solution.py:479
  1017.3 45.3 %mixer_backward.3 = (bf16[1024,1024]{1,0:T(8,128)(2,1)}, bf16[1024,2]{1,0:T(8,128)(2,1)}, f32[12,256]{1,0:T(8,128)}, f32[2,128]{1,0:T(2,128)}) custom-call(s32[3]{0:T(128)} %copy-done.3, f32[1024,1024]{1,0:T(8,128)} %fusion.92.proj_ref, f32[1024,2]{1,0:T(8,128)} %copy-done.6, f32[12,256]{1,0:T(8,128)} %copy-done.1, f32[2,128]{1,0:T(2,128)} %copy-done.4, ...), custom_call_target="tpu_custom_call" | custom-call | flops 10000000000 | bytes 10000000 | tf_op jit(solution)/shard_map/mixer_backward/pallas_call | solution.py:356
  1062.6 6.2 fusion.99
  1073.0 6.3 convolution_convert_fusion.6
  1079.3 17.9 %all_to_all.78 = bf16[128,8,256]{2,0,1:T(8,128)(2,1)} all-to-all(bf16[128,8,256]{2,0,1:T(8,128)(2,1)S(1)} %bitcast.135), channel_id=1, replica_groups=mesh['dp'=4,'tensor'=8] {'tensor'}, dimensions={1} | all-to-all | bytes 1048576 | tf_op jit(solution)/shard_map/all_to_all | solution.py:479
  1097.2 45.2 %mixer_backward.2 = (bf16[1024,1024]{1,0:T(8,128)(2,1)}, bf16[1024,2]{1,0:T(8,128)(2,1)}, f32[12,256]{1,0:T(8,128)}, f32[2,128]{1,0:T(2,128)}) custom-call(s32[3]{0:T(128)} %copy-done.2, f32[1024,1024]{1,0:T(8,128)} %fusion.88.proj_ref, f32[1024,2]{1,0:T(8,128)} %copy-done.5, f32[12,256]{1,0:T(8,128)} %copy-done.1, f32[2,128]{1,0:T(2,128)} %copy-done.4, ...), custom_call_target="tpu_custom_call" | custom-call | flops 10000000000 | bytes 10000000 | tf_op jit(solution)/shard_map/mixer_backward/pallas_call | solution.py:356
  1142.4 6.2 fusion.97
  1152.3 7.8 convolution_convert_fusion.2
  1175.1 14.8 fusion.8
  1189.9 58.6 %reduce-scatter.23.cloned.1.call-done = bf16[256,2048]{1,0:T(8,128)(2,1)} async-done(((bf16[2048,2048]{1,0:T(8,128)(2,1)}), bf16[256,2048]{1,0:T(8,128)(2,1)}) %reduce-scatter.23.cloned.1.call-update) | async-done | bytes 1048592 | tf_op jit(solution)/shard_map/reduce_scatter | solution.py:491
  1253.2 11.6 all-reduce.3
  1266.6 72.9 %reduce-scatter.21.cloned.1.call-done = bf16[128,2048]{1,0:T(8,128)(2,1)} async-done(((bf16[1024,2048]{1,0:T(8,128)(2,1)}), bf16[128,2048]{1,0:T(8,128)(2,1)}) %reduce-scatter.21.cloned.1.call-update) | async-done | bytes 524304 | tf_op jit(solution)/shard_map/reduce_scatter | solution.py:394
  1339.5 91.3 %reduce-scatter.17.cloned.1.call-done = bf16[128,2048]{1,0:T(8,128)(2,1)} async-done(((bf16[1024,2048]{1,0:T(8,128)(2,1)}), bf16[128,2048]{1,0:T(8,128)(2,1)}) %reduce-scatter.17.cloned.1.call-update) | async-done | bytes 524304 | tf_op jit(solution)/shard_map/reduce_scatter | solution.py:394
  1432.7 42.6 %all-reduce.2 = (f32[2048]{0:T(1024)S(1)}, f32[2048]{0:T(1024)S(1)}) all-reduce(f32[2048]{0:T(1024)S(1)} %add.146, f32[2048]{0:T(1024)S(1)} %add.147), channel_id=10, replica_groups=mesh['dp'=4,'tensor'=8] {'dp','tensor'}, use_global_device_ids=true, to_apply=%region_16.0.clone | all-reduce | flops 4096 | bytes 32768
  1479.7 44.1 %reduce-scatter.11.cloned.1.call-done = bf16[128,2048]{1,0:T(8,128)(2,1)} async-done(((bf16[1024,2048]{1,0:T(8,128)(2,1)}), bf16[128,2048]{1,0:T(8,128)(2,1)}) %reduce-scatter.11.cloned.1.call-update) | async-done | bytes 524304 | tf_op jit(solution)/shard_map/reduce_scatter | solution.py:394
  1529.3 99.5 %all-reduce.7.cloned.1.call-done = (bf16[2048,1024]{1,0:T(8,128)(2,1)}, bf16[256,2048]{1,0:T(8,128)(2,1)}) async-done(((bf16[2048,1024]{1,0:T(8,128)(2,1)}, bf16[256,2048]{1,0:T(8,128)(2,1)}), (bf16[2048,1024]{1,0:T(8,128)(2,1)}, bf16[256,2048]{1,0:T(8,128)(2,1)})) %all-reduce.7.cloned.1.call-update) | async-done | bytes 5242896 | tf_op jit(solution)/shard_map/psum | solution.py:519
  1628.7 5.8 fusion.86
  (249 shorter events, 137.3 us)
Async XLA Ops:
  7.2 86.4 %copy-start = (bf16[2048,2]{0,1:T(2,128)(2,1)S(1)}, bf16[2048,2]{0,1:T(2,128)(2,1)}, u32[]{:S(2)}) copy-start(bf16[2048,2]{0,1:T(2,128)(2,1)} %param.24) | copy-start | bytes 24580
  7.2 12.6 copy-start.37
  7.2 86.4 %all-gather.15.cloned.1.call-start = ((), (), s32[]{:S(2)}) async-start(), calls=%async_computation.14 | async-start | bytes 4718592 | tf_op jit(solution)/shard_map/all_gather | solution.py:390
  18.3 209.5 %all-gather.17.cloned.1.call-start = ((), (), s32[]{:S(2)}) async-start(), calls=%async_computation.15 | async-start | bytes 9437184 | tf_op jit(solution)/shard_map/all_gather | solution.py:390
  19.0 236.2 %all-gather.21.cloned.1.call-start = ((), (), s32[]{:S(2)}) async-start(), calls=%async_computation.17 | async-start | bytes 3604480 | tf_op jit(solution)/shard_map/all_gather | solution.py:390
  20.9 528.1 %copy-start.1 = (f32[12,256]{1,0:T(8,128)}, f32[12,256]{1,0:T(8,128)S(1)}, u32[]{:S(2)}) copy-start(f32[12,256]{1,0:T(8,128)S(1)} %reshape.113.tap_ref) | copy-start | bytes 36868
  21.0 528.1 %copy-start.4 = (f32[2,128]{1,0:T(2,128)}, f32[2,128]{1,0:T(2,128)S(1)}, u32[]{:S(2)}) copy-start(f32[2,128]{1,0:T(2,128)S(1)} %convert_element_type.156.gain_ref) | copy-start | bytes 3076
  21.0 84.8 %copy-start.2 = (s32[3]{0:T(128)}, s32[3]{0:T(128)S(1)}, u32[]{:S(2)}) copy-start(s32[3]{0:T(128)S(1)} %get-tuple-element.94.lengths_ref) | copy-start | bytes 40
  21.0 528.1 %copy-start.3 = (s32[3]{0:T(128)}, s32[3]{0:T(128)S(1)}, u32[]{:S(2)}) copy-start(s32[3]{0:T(128)S(1)} %get-tuple-element.95.lengths_ref) | copy-start | bytes 40
  97.2 8.6 copy-start.5
  105.8 42.7 %copy-start.52 = (bf16[512]{0:T(512)(128)(2,1)S(1)}, bf16[512]{0:T(512)(128)(2,1)}, u32[]{:S(2)}) copy-start(bf16[512]{0:T(512)(128)(2,1)} %param.19) | copy-start | bytes 3076
  105.8 122.0 %copy-start.15 = (bf16[2,128,2048]{2,1,0:T(8,128)(2,1)S(1)}, bf16[2,128,2048]{2,1,0:T(8,128)(2,1)}, u32[]{:S(2)}) copy-start(bf16[2,128,2048]{2,1,0:T(8,128)(2,1)} %param.16) | copy-start | bytes 3145732
  144.9 33.2 %all-to-all-start = ((bf16[8,128,256]{1,2,0:T(8,128)(2,1)}), bf16[8,128,256]{1,2,0:T(8,128)(2,1)S(1)}, u32[]{:S(2)}, u32[]{:S(2)}) async-start(bf16[8,128,256]{1,2,0:T(8,128)(2,1)} %copy.46), calls=%async_computation | async-start | bytes 1048576 | tf_op jit(solution)/shard_map/all_to_all | solution.py:452
  148.4 182.8 %all-gather.19.cloned.1.call-start = ((), (), s32[]{:S(2)}) async-start(), calls=%async_computation.16 | async-start | bytes 4718592 | tf_op jit(solution)/shard_map/all_gather | solution.py:390
  178.1 54.4 %copy-start.18 = (bf16[8,128,256]{1,2,0:T(8,128)(2,1)}, bf16[8,128,256]{1,2,0:T(8,128)(2,1)S(1)}, u32[]{:S(2)}) copy-start(bf16[8,128,256]{1,2,0:T(8,128)(2,1)S(1)} %all-to-all-done) | copy-start | bytes 1572868
  233.5 124.5 %all-gather.23.cloned.1.call-start = ((), (), s32[]{:S(2)}) async-start(), calls=%async_computation.18 | async-start | bytes 3604480 | tf_op jit(solution)/shard_map/all_gather | solution.py:390
  234.1 152.4 %all-gather.25.cloned.1.call-start = ((), (), s32[]{:S(2)}) async-start(), calls=%async_computation.19 | async-start | bytes 3604480 | tf_op jit(solution)/shard_map/all_gather | solution.py:390
  234.7 228.0 %all-gather.31.cloned.1.call-start = ((), (), s32[]{:S(2)}) async-start(), calls=%async_computation.32 | async-start | bytes 4718592 | tf_op jit(solution)/shard_map/all_gather | solution.py:390
  237.1 299.9 %all-gather.27.cloned.1.call-start = ((), (), s32[]{:S(2)}) async-start(), calls=%async_computation.21 | async-start | bytes 4718592 | tf_op jit(solution)/shard_map/all_gather | solution.py:390
  237.9 394.2 %reduce-scatter.15.cloned.1.call-start = ((), (), s32[]{:S(2)}) async-start(), calls=%async_computation.24 | async-start | bytes 4718592 | tf_op jit(solution)/shard_map/reduce_scatter | solution.py:394
  462.7 10.2 copy-start.56
  481.9 226.3 %all-gather.29.cloned.1.call-start = ((), (), s32[]{:S(2)}) async-start(), calls=%async_computation.22 | async-start | bytes 4718592 | tf_op jit(solution)/shard_map/all_gather | solution.py:390
  540.6 8.5 copy-start.6
  634.9 147.9 %all-gather.33.cloned.1.call-start = ((), (), s32[]{:S(2)}) async-start(), calls=%async_computation.33 | async-start | bytes 4718592 | tf_op jit(solution)/shard_map/all_gather | solution.py:390
  635.7 252.8 %reduce-scatter.19.cloned.1.call-start = ((), (), s32[]{:S(2)}) async-start(), calls=%async_computation.26 | async-start | bytes 4718592 | tf_op jit(solution)/shard_map/reduce_scatter | solution.py:394
  708.2 8.0 copy-start.29
  708.3 8.0 copy-start.59
  782.9 10.2 copy-start.57
  802.2 177.6 %reduce-scatter.13.cloned.1.call-start = ((), (), s32[]{:S(2)}) async-start(), calls=%async_computation.23 | async-start | bytes 4718592 | tf_op jit(solution)/shard_map/reduce_scatter | solution.py:394
  809.9 357.6 %reduce-scatter.27.cloned.1.call-start = ((), (), s32[]{:S(2)}) async-start(), calls=%async_computation.30 | async-start | bytes 3604480 | tf_op jit(solution)/shard_map/reduce_scatter | solution.py:394
  824.7 345.2 %reduce-scatter.25.cloned.1.call-start = ((), (), s32[]{:S(2)}) async-start(), calls=%async_computation.29 | async-start | bytes 3604480 | tf_op jit(solution)/shard_map/reduce_scatter | solution.py:394
  836.3 336.0 %reduce-scatter.29.cloned.1.call-start = ((), (), s32[]{:S(2)}) async-start(), calls=%async_computation.31 | async-start | bytes 3604480 | tf_op jit(solution)/shard_map/reduce_scatter | solution.py:394
  847.2 132.6 %copy-start.17 = (bf16[2,128,2048]{2,1,0:T(8,128)(2,1)S(1)}, bf16[2,128,2048]{2,1,0:T(8,128)(2,1)}, u32[]{:S(2)}) copy-start(bf16[2,128,2048]{2,1,0:T(8,128)(2,1)} %param.31) | copy-start | bytes 3145732
  847.2 401.3 %reduce-scatter.23.cloned.1.call-start = ((), (), s32[]{:S(2)}) async-start(), calls=%async_computation.28 | async-start | bytes 9437184 | tf_op jit(solution)/shard_map/reduce_scatter | solution.py:491
  990.5 349.0 %reduce-scatter.21.cloned.1.call-start = ((), (), s32[]{:S(2)}) async-start(), calls=%async_computation.27 | async-start | bytes 4718592 | tf_op jit(solution)/shard_map/reduce_scatter | solution.py:394
  1017.3 45.3 %copy-start.40 = (bf16[2048,1024]{1,0:T(8,128)(2,1)S(1)}, bf16[2048,1024]{1,0:T(8,128)(2,1)}, u32[]{:S(2)}) copy-start(bf16[2048,1024]{1,0:T(8,128)(2,1)} %constant_dynamic-update-slice_fusion) | copy-start | bytes 12582916
  1062.6 6.2 copy-start.35
  1072.0 358.8 %reduce-scatter.17.cloned.1.call-start = ((), (), s32[]{:S(2)}) async-start(), calls=%async_computation.25 | async-start | bytes 4718592 | tf_op jit(solution)/shard_map/reduce_scatter | solution.py:394
  1097.2 45.2 %copy-start.41 = (bf16[2048,1024]{1,0:T(8,128)(2,1)S(1)}, bf16[2048,1024]{1,0:T(8,128)(2,1)}, u32[]{:S(2)}) copy-start(bf16[2048,1024]{1,0:T(8,128)(2,1)} %constant_dynamic-update-slice_fusion) | copy-start | bytes 12582916
  1142.4 6.3 copy-start.36
  1152.0 371.7 %reduce-scatter.11.cloned.1.call-start = ((), (), s32[]{:S(2)}) async-start(), calls=%async_computation.20 | async-start | bytes 4718592 | tf_op jit(solution)/shard_map/reduce_scatter | solution.py:394
  1160.1 468.6 %all-reduce.7.cloned.1.call-start = ((), (), s32[]{:S(2)}) async-start(), calls=%async_computation.34 | async-start | bytes 10485760 | tf_op jit(solution)/shard_map/psum | solution.py:519
  1167.5 7.3 copy-start.44
  1248.5 182.3 %copy-start.16 = (bf16[2,128,2048]{2,1,0:T(8,128)(2,1)S(1)}, bf16[2,128,2048]{2,1,0:T(8,128)(2,1)}, u32[]{:S(2)}) copy-start(bf16[2,128,2048]{2,1,0:T(8,128)(2,1)} %param.16) | copy-start | bytes 3145732
  1248.5 182.3 %copy-start.43 = (f32[4,1,512]{2,1,0:T(1,128)S(1)}, f32[4,1,512]{2,1,0:T(1,128)}, u32[]{:S(2)}) copy-start(f32[4,1,512]{2,1,0:T(1,128)} %copy-done.42) | copy-start | bytes 24580
  1248.6 182.3 %copy-start.49 = (f32[128]{0:T(128)S(1)}, f32[128]{0:T(128)}, u32[]{:S(2)}) copy-start(f32[128]{0:T(128)} %copy-done.48) | copy-start | bytes 1540
  1248.6 182.3 %copy-start.51 = (f32[128]{0:T(128)S(1)}, f32[128]{0:T(128)}, u32[]{:S(2)}) copy-start(f32[128]{0:T(128)} %copy-done.50) | copy-start | bytes 1540
  1628.7 5.8 copy-start.34
  (42 other events, 136.9 us)
Sparse Core Ops, SparseCore 0:
  18.4 75.1 all-gather.14
  95.7 131.9 all-gather.16
  229.3 25.8 all-gather.20
  257.8 73.3 all-gather.18
  332.7 25.2 all-gather.22
  359.4 27.0 all-gather.24
  389.2 73.3 all-gather.30
  465.3 71.6 all-gather.26
  540.7 91.3 reduce-scatter.14
  635.1 73.1 all-gather.28
  711.2 71.6 all-gather.32
  802.3 86.1 reduce-scatter.18
  892.1 87.6 reduce-scatter.12
  982.3 36.0 reduce-scatter.26
  1020.8 36.3 reduce-scatter.24
  1059.7 36.3 reduce-scatter.28
  1099.6 148.9 reduce-scatter.22
  1252.4 87.0 reduce-scatter.20
  1343.1 87.6 reduce-scatter.16
  1434.7 88.9 reduce-scatter.10
  1526.2 102.4 all-reduce.6

commit v2 on v1

--- a/solution.py
+++ b/solution.py
@@ -372,6 +372,303 @@
     )(lengths_row, projected, beta_logits, taps, gain, grad, *saved)
 
 
+NT = (((1,), (1,)), ((), ()))
+
+
+def other(axis_name):
+    return {axis_name: 1 - lax.axis_index(axis_name)}
+
+
+def ffn_kernel(x_ref, c_ref, w_ref, out_ref, ngrad_ref, wgrad_ref,
+               xs, cs, ws, inner_s, gate_s, up_s, acts_t, part, crecv, drecv, nrecv, stage, ctile,
+               ag_send, ag_recv, pair_send, pair_recv, rs_send, rs_recv, c_sem, w_sem, g_sem, t_sem):
+    half = xs.shape[1] // 2
+    rows = 2 * half
+    model = xs.shape[2]
+    hidden = ws.shape[1]
+    lines = w_ref.shape[0]
+    quarter = w_ref.shape[2]
+    tile_f = 256
+    tile_d = min(512, model)
+    tile_w = min(256, model)
+
+    def remote(src, dst, send, recv, axis_name):
+        return pltpu.make_async_remote_copy(
+            src_ref=src, dst_ref=dst, send_sem=send, recv_sem=recv,
+            device_id=other(axis_name), device_id_type=pl.DeviceIdType.MESH)
+
+    def halves(ref, index, h):
+        return ref.at[index, pl.ds(h * half, half)]
+
+    barrier = pltpu.get_barrier_semaphore()
+    for axis_name in ("core", "x", "y"):
+        pl.semaphore_signal(
+            barrier, inc=1, device_id=other(axis_name), device_id_type=pl.DeviceIdType.MESH)
+
+    weight_copies = [
+        pltpu.make_async_copy(
+            w_ref.at[line, kind], ws.at[kind, pl.ds(line * quarter, quarter)], w_sem.at[line, kind])
+        for line in range(lines) for kind in range(3)
+    ]
+    for copy in weight_copies:
+        copy.start()
+
+    def slot_of(step):
+        return (1 - lax.rem(step, 2)) * 4 + step // 2
+
+    def c_copy(step, slot):
+        return pltpu.make_async_copy(
+            c_ref.at[slot], cs.at[lax.rem(step, 2)], c_sem.at[lax.rem(step, 2)])
+
+    c_copy(0, 4).start()
+    pl.semaphore_wait(barrier, 3)
+
+    own_pair = remote(x_ref, xs.at[4], ag_send.at[0], ag_recv.at[0], "core")
+    own_x = [remote(x_ref.at[pl.ds(h * half, half)], halves(xs, 1, h), ag_send.at[1 + h], ag_recv.at[1 + h], "x") for h in range(2)]
+    own_y = [remote(x_ref.at[pl.ds(h * half, half)], halves(xs, 2, h), ag_send.at[3 + h], ag_recv.at[3 + h], "y") for h in range(2)]
+    relay_y = remote(halves(xs, 1, 0), halves(xs, 3, 0), ag_send.at[5], ag_recv.at[5], "y")
+    relay_x = remote(halves(xs, 2, 1), halves(xs, 3, 1), ag_send.at[6], ag_recv.at[6], "x")
+    pair_of = [None] + [remote(xs.at[j], xs.at[4 + j], ag_send.at[6 + j], ag_recv.at[6 + j], "core") for j in (1, 2, 3)]
+    own_pair.start()
+    own_x[0].start()
+    own_y[1].start()
+    own_x[1].start()
+    own_y[0].start()
+    own_copy = pltpu.make_async_copy(x_ref, xs.at[0], t_sem.at[0])
+    own_copy.start()
+    own_copy.wait()
+    for copy in weight_copies:
+        copy.wait()
+
+    def part_send(j):
+        return remote(part.at[lax.rem(j, 2)], crecv.at[j], pair_send.at[j], pair_recv.at[j], "core")
+
+    x_sends = [[remote(crecv.at[1, a, pl.ds(h * half, half)], nrecv.at[0, a, pl.ds(h * half, half)],
+                       rs_send.at[a * 2 + h], rs_recv.at[a * 2 + h], "x") for a in range(2)] for h in range(2)]
+    y_sends = [[remote(crecv.at[2, a, pl.ds(h * half, half)], nrecv.at[1, a, pl.ds(h * half, half)],
+                       rs_send.at[4 + a * 2 + h], rs_recv.at[4 + a * 2 + h], "y") for a in range(2)] for h in range(2)]
+    d_sends = [[remote(crecv.at[3, a, pl.ds(h * half, half)], drecv.at[a, pl.ds(h * half, half)],
+                       rs_send.at[8 + a * 2 + h], rs_recv.at[8 + a * 2 + h], ("x", "y")[h]) for a in range(2)] for h in range(2)]
+
+    @pl.loop(0, 8)
+    def _(step):
+        j = step // 2
+        slot = slot_of(step)
+        pairing = lax.rem(step, 2) == 0
+
+        @pl.when(step < 7)
+        def _():
+            c_copy(step + 1, slot_of(step + 1)).start()
+
+        @pl.when(step == 0)
+        def _():
+            own_pair.wait_recv()
+
+        @pl.when(step == 2)
+        def _():
+            own_x[0].wait_recv()
+            relay_y.start()
+            own_y[1].wait_recv()
+            relay_x.start()
+            own_x[1].wait_recv()
+            pair_of[1].start()
+            own_y[0].wait_recv()
+            pair_of[2].start()
+            pair_of[1].wait_recv()
+
+        @pl.when(step == 4)
+        def _():
+            relay_y.wait_recv()
+            relay_x.wait_recv()
+            pair_of[3].start()
+            pair_of[2].wait_recv()
+
+        @pl.when(step == 6)
+        def _():
+            pair_of[3].wait_recv()
+
+        c_copy(step, slot).wait()
+
+        for start in range(0, hidden, tile_f):
+            size = min(tile_f, hidden - start)
+            cols = slice(start, start + size)
+            x = xs[slot]
+            gate = lax.dot_general(x, ws[0, cols, :], NT, preferred_element_type=f32)
+            up = lax.dot_general(x, ws[1, cols, :], NT, preferred_element_type=f32)
+            grad = lax.dot_general(cs[lax.rem(step, 2)], ws[2, cols, :], NT, preferred_element_type=f32)
+            sg = sigmoid(gate)
+            silu = gate * sg
+            inner = (silu * up).astype(bf16)
+            gate_grad = (grad * up * sg * (1.0 + gate * (1.0 - sg))).astype(bf16)
+            up_grad = (grad * silu).astype(bf16)
+            places = pl.ds(pl.multiple_of(slot * rows, rows), rows)
+            for kind, (value, target) in enumerate(((gate_grad, gate_s), (up_grad, up_s), (inner, inner_s))):
+                target[:, cols] = value
+                acts_t[kind, cols, places] = value.T
+
+        @pl.when(pairing & (step >= 4))
+        def _():
+            part_send(j - 2).wait_send()
+
+        place = jnp.where(pairing, lax.rem(j, 2), 2)
+        for start in range(0, model, tile_d):
+            cols = slice(start, start + tile_d)
+            part[place, 0, :, cols] = jnp.dot(
+                inner_s[...], ws[2, :, cols], preferred_element_type=f32).astype(bf16)
+            part[place, 1, :, cols] = (
+                jnp.dot(gate_s[...], ws[0, :, cols], preferred_element_type=f32)
+                + jnp.dot(up_s[...], ws[1, :, cols], preferred_element_type=f32)
+            ).astype(bf16)
+
+        @pl.when(pairing)
+        def _():
+            part_send(j).start()
+
+        @pl.when(jnp.logical_not(pairing))
+        def _():
+            part_send(j).wait_recv()
+            for a in range(2):
+                for start in range(0, model, tile_d):
+                    cols = slice(start, start + tile_d)
+                    crecv[j, a, :, cols] = (
+                        crecv[j, a, :, cols].astype(f32) + part[2, a, :, cols].astype(f32)
+                    ).astype(bf16)
+
+        @pl.when(step == 3)
+        def _():
+            for copy in x_sends[0]:
+                copy.start()
+
+        @pl.when(step == 5)
+        def _():
+            for copy in y_sends[1]:
+                copy.start()
+
+        @pl.when(step == 7)
+        def _():
+            for h in range(2):
+                for copy in d_sends[h]:
+                    copy.start()
+
+    tiles = model // tile_w
+
+    def c_tile(t):
+        return pltpu.make_async_copy(
+            c_ref.at[:, :, pl.ds(pl.multiple_of(t * tile_w, tile_w), tile_w)], ctile.at[lax.rem(t, 2)], t_sem.at[lax.rem(t, 2)])
+
+    def grad_copy(kind, t, line):
+        return pltpu.make_async_copy(
+            stage.at[lax.rem(t, 2), pl.ds(line * quarter, quarter)],
+            wgrad_ref.at[line, kind, :, pl.ds(pl.multiple_of(t * tile_w, tile_w), tile_w)],
+            g_sem.at[lax.rem(t, 2), line])
+
+    def weight_grads(kind):
+        if kind == 2:
+            c_tile(0).start()
+
+        @pl.loop(0, tiles)
+        def _(t):
+            if kind == 2:
+                @pl.when(t + 1 < tiles)
+                def _():
+                    c_tile(t + 1).start()
+                c_tile(t).wait()
+                right = ctile[lax.rem(t, 2)].reshape(8 * rows, tile_w)
+            else:
+                right = xs[:, :, pl.ds(pl.multiple_of(t * tile_w, tile_w), tile_w)].reshape(8 * rows, tile_w)
+
+            @pl.when(t >= 2)
+            def _():
+                for line in range(lines):
+                    grad_copy(kind, t - 2, line).wait()
+
+            stage[lax.rem(t, 2)] = jnp.dot(
+                acts_t[kind], right, preferred_element_type=f32).astype(bf16)
+            for line in range(lines):
+                grad_copy(kind, t, line).start()
+
+        for t in range(max(tiles - 2, 0), tiles):
+            for line in range(lines):
+                grad_copy(kind, t, line).wait()
+
+    weight_grads(0)
+    for h in range(2):
+        j = 2 - h
+        for a in range(2):
+            d_sends[h][a].wait_recv()
+            at = pl.ds(h * half, half)
+            crecv[j, a, at, :] = (
+                crecv[j, a, at, :].astype(f32) + drecv[a, at, :].astype(f32)).astype(bf16)
+        for copy in (y_sends, x_sends)[h][h]:
+            copy.start()
+    weight_grads(1)
+    weight_grads(2)
+    for a, target in enumerate((out_ref, ngrad_ref)):
+        for h in range(2):
+            x_sends[h][a].wait_recv()
+            y_sends[h][a].wait_recv()
+            at = pl.ds(h * half, half)
+            target[at, :] = (
+                crecv[0, a, at, :].astype(f32)
+                + nrecv[0, a, at, :].astype(f32)
+                + nrecv[1, a, at, :].astype(f32)
+            )
+    own_pair.wait_send()
+    for h in range(2):
+        own_x[h].wait_send()
+        own_y[h].wait_send()
+        for a in range(2):
+            x_sends[h][a].wait_send()
+            y_sends[h][a].wait_send()
+            d_sends[h][a].wait_send()
+    relay_x.wait_send()
+    relay_y.wait_send()
+    for j in (1, 2, 3):
+        pair_of[j].wait_send()
+    part_send(2).wait_send()
+    part_send(3).wait_send()
+
+
+def ffn_plane(x_own, c_all, weights):
+    rows, model = x_own.shape
+    lines, _, quarter, _ = weights.shape
+    hidden = lines * quarter
+    tile_w = min(256, model)
+    sems = pltpu.SemaphoreType.DMA
+    anywhere = pl.BlockSpec(memory_space=pl.ANY)
+    return pl.pallas_call(
+        ffn_kernel,
+        out_shape=(
+            jax.ShapeDtypeStruct((rows, model), f32),
+            jax.ShapeDtypeStruct((rows, model), f32),
+            jax.ShapeDtypeStruct(weights.shape, bf16),
+        ),
+        in_specs=[anywhere] * 3,
+        out_specs=(vmem(), vmem(), anywhere),
+        scratch_shapes=[
+            pltpu.VMEM((8, rows, model), bf16),
+            pltpu.VMEM((2, rows, model), bf16),
+            pltpu.VMEM((3, hidden, model), bf16),
+            pltpu.VMEM((rows, hidden), bf16),
+            pltpu.VMEM((rows, hidden), bf16),
+            pltpu.VMEM((rows, hidden), bf16),
+            pltpu.VMEM((3, hidden, 8 * rows), bf16),
+            pltpu.VMEM((3, 2, rows, model), bf16),
+            pltpu.VMEM((4, 2, rows, model), bf16),
+            pltpu.VMEM((2, rows, model), bf16),
+            pltpu.VMEM((2, 2, rows, model), bf16),
+            pltpu.VMEM((2, hidden, tile_w), bf16),
+            pltpu.VMEM((2, 8, rows, tile_w), bf16),
+            sems((10,)), sems((10,)), sems((4,)), sems((4,)), sems((12,)), sems((12,)),
+            sems((2,)), sems((lines, 3)), sems((2, lines)), sems((2,)),
+        ],
+        compiler_params=pltpu.CompilerParams(
+            collective_id=2, has_side_effects=True, vmem_limit_bytes=62 * 2**20),
+        cost_estimate=pl.CostEstimate(flops=8 * 10**10, bytes_accessed=4 * 10**7, transcendentals=10**6),
+        name="ffn_plane",
+    )(x_own, c_all, weights)
+
+
 def root_scale(row_values, gain_vector):
     row_scale = lax.rsqrt(jnp.mean(row_values * row_values, axis=-1, keepdims=True) + epsilon)
     return (row_values * row_scale * gain_vector, row_scale)
@@ -386,6 +683,10 @@
     return (rows_grad, gain_grad)
 
 
+DP = ("x", "core")
+TP = ("z", "y")
+
+
 def gather(x, axis_name, axis=0):
     return lax.all_gather(x, axis_name, axis=axis, tiled=True)
 
@@ -406,6 +707,91 @@
 
 def dot_tn(a, b):
     return jnp.einsum("tm,tn->mn", a, b, preferred_element_type=f32)
+
+
+def exchange(x, axis_name, distance=1):
+    size = lax.axis_size(axis_name)
+    return lax.ppermute(x, axis_name, [(i, i ^ distance) for i in range(size)])
+
+
+def swap_blocks(blocks):
+    size = lax.axis_size(DP)
+    me = lax.axis_index(DP)
+    pieces = []
+    for r in range(size):
+        block = lax.dynamic_index_in_dim(blocks, me ^ r, keepdims=False)
+        pieces.append(exchange(block, DP, r) if r else block)
+    pieces = jnp.stack(pieces)
+    return [lax.dynamic_index_in_dim(pieces, me ^ q, keepdims=False) for q in range(size)]
+
+
+def plane_weights(w_gate, w_up, w_down):
+    size = lax.axis_size(DP)
+    local = jnp.stack([w_gate.T, w_up.T, w_down])
+    kinds, hidden, part = local.shape
+    quarter = hidden // size
+    blocks = local.reshape(kinds, size, quarter, part).swapaxes(0, 1)
+    own = jnp.concatenate(swap_blocks(blocks), axis=2)
+    own = own.reshape(kinds * quarter, size * part)
+    return gather(own, "z").reshape(-1, kinds, quarter, size * part)
+
+
+def plane_weight_grads(grads):
+    size = lax.axis_size(DP)
+    lines, kinds, quarter, model = grads.shape
+    own = lax.psum_scatter(
+        grads.reshape(lines * kinds * quarter, model), "z", scatter_dimension=0, tiled=True)
+    blocks = own.reshape(kinds * quarter, size, model // size).swapaxes(0, 1)
+    pieces = [piece.reshape(kinds, quarter, -1) for piece in swap_blocks(blocks)]
+    whole = jnp.concatenate(pieces, axis=1).astype(f32)
+    return whole[0].T, whole[1].T, whole[2]
+
+
+def plane_rows(x):
+    for axis_name in ("x", "y", "core"):
+        x = jnp.concatenate([x, exchange(x, axis_name)])
+    return x
+
+
+def feed_forward_plane(normed, cotangents, w_gate, w_up, w_down):
+    weights = plane_weights(w_gate, w_up, w_down)
+    rows = jnp.concatenate(normed)
+    count, model = rows.shape
+    c_all = plane_rows(cotangents.reshape(1, count, model))
+    out, normed_grad, grads = ffn_plane(rows, c_all, weights)
+    per_batch = (len(normed), count // len(normed), model)
+    return out.reshape(per_batch), normed_grad.reshape(per_batch), plane_weight_grads(grads)
+
+
+def feed_forward_groups(normed, cotangents, w_gate, w_up, w_down):
+    gate_full = gather(w_gate, DP)
+    up_full = gather(w_up, DP)
+    down_full = gather(w_down, DP, 1)
+    outs, normed_grads, inner_rows, gate_grads, up_grads, rows, grad_rows = [], [], [], [], [], [], []
+    for m in range(len(normed)):
+        rows.append(gather(normed[m], TP))
+        grad_rows.append(gather(cotangents[m], TP))
+        gate_values = dot(rows[m], gate_full)
+        up_values = dot(rows[m], up_full)
+        sigmoid_gate = jax.nn.sigmoid(gate_values)
+        silu_gate = gate_values * sigmoid_gate
+        inner = (silu_gate * up_values).astype(bf16)
+        inner_grad = dot_nt(grad_rows[m], down_full)
+        gate_grad = (
+            inner_grad * up_values * sigmoid_gate * (1.0 + gate_values * (1.0 - sigmoid_gate))
+        ).astype(bf16)
+        up_grad = (inner_grad * silu_gate).astype(bf16)
+        normed_grads.append(scatter_sum(dot_nt(gate_grad, gate_full) + dot_nt(up_grad, up_full), TP))
+        outs.append(scatter_sum(dot(inner, down_full), TP))
+        inner_rows.append(inner)
+        gate_grads.append(gate_grad)
+        up_grads.append(up_grad)
+    grad_all = jnp.concatenate(grad_rows)
+    rows_all = jnp.concatenate(rows)
+    gate_share = scatter_sum(dot_tn(rows_all, jnp.concatenate(gate_grads)), DP)
+    up_share = scatter_sum(dot_tn(rows_all, jnp.concatenate(up_grads)), DP)
+    down_share = scatter_sum(dot_tn(jnp.concatenate(inner_rows), grad_all), DP, 1)
+    return outs, normed_grads, (gate_share, up_share, down_share)
 
 
 def per_device(
@@ -428,69 +814,48 @@
 ):
     batches = range(inputs.shape[0])
     local_width = w_query.shape[1]
+    planar = all(lax.axis_size(name) == 2 for name in ("x", "core", "y"))
     w_inner = jnp.concatenate([w_query, w_key, w_value, w_gate_out], axis=1)
     taps = conv_weight.astype(f32).reshape(-1, local_width)
     gain_heads = head_gain.astype(f32)
-    gain_one = gather(norm_gain, "dp").astype(f32)
-    gain_two = gather(ffn_gain, "dp").astype(f32)
+    gain_one = gather(norm_gain, DP).astype(f32)
+    gain_two = gather(ffn_gain, DP).astype(f32)
     rows_in = [inputs[m].astype(f32) for m in batches]
     one = [root_scale(rows, gain_one) for rows in rows_in]
-    gathered_one = [gather(one[m][0].astype(bf16), "tensor") for m in batches]
+    gathered_one = [gather(one[m][0].astype(bf16), TP) for m in batches]
     projected = [dot(rows, w_inner) for rows in gathered_one]
     beta_logits = [dot(rows, w_beta) for rows in gathered_one]
-    gate_full = gather(w_gate, "dp")
-    up_full = gather(w_up, "dp")
-    down_full = gather(w_down, "dp", 1)
-    out_full = gather(w_out, "tensor")
-    grad_rows = [gather(cotangent[m], "tensor") for m in batches]
+    out_full = gather(w_out, TP)
     mixed, saved = [], []
     for m in batches:
         low, *kept = mixer_forward(lengths[m, 0], projected[m], beta_logits[m], taps, gain_heads)
         mixed.append(low)
         saved.append(kept)
     token_heads = [
-        lax.all_to_all(low, "tensor", split_axis=0, concat_axis=1, tiled=True) for low in mixed
+        lax.all_to_all(low, TP, split_axis=0, concat_axis=1, tiled=True) for low in mixed
     ]
     hidden = [rows_in[m] + dot(token_heads[m], out_full) for m in batches]
     two = [root_scale(rows, gain_two) for rows in hidden]
-    gathered_two = [gather(two[m][0].astype(bf16), "tensor") for m in batches]
-    result_rows, inner_rows, gate_grads, up_grads, hidden_grads = [], [], [], [], []
-    attended_low, mixed_grads = [], []
+    feed_forward = feed_forward_plane if planar else feed_forward_groups
+    ffn_out, normed_grads, (gate_share, up_share, down_share) = feed_forward(
+        [two[m][0].astype(bf16) for m in batches], cotangent, w_gate, w_up, w_down)
+    result_rows, hidden_grads, attended_low, mixed_grads = [], [], [], []
     gain_two_sum = 0.0
     for m in batches:
-        gate_values = dot(gathered_two[m], gate_full)
-        up_values = dot(gathered_two[m], up_full)
-        sigmoid_gate = jax.nn.sigmoid(gate_values)
-        silu_gate = gate_values * sigmoid_gate
-        inner = (silu_gate * up_values).astype(bf16)
-        inner_grad = dot_nt(grad_rows[m], down_full)
-        gate_grad = (
-            inner_grad * up_values * sigmoid_gate * (1.0 + gate_values * (1.0 - sigmoid_gate))
-        ).astype(bf16)
-        up_grad = (inner_grad * silu_gate).astype(bf16)
-        normed_grad = scatter_sum(dot_nt(gate_grad, gate_full) + dot_nt(up_grad, up_full), "tensor")
-        result_rows.append(hidden[m] + scatter_sum(dot(inner, down_full), "tensor"))
-        norm_grad, gain_part = norm_backward(hidden[m], two[m][1], gain_two, normed_grad)
+        result_rows.append(hidden[m] + ffn_out[m])
+        norm_grad, gain_part = norm_backward(hidden[m], two[m][1], gain_two, normed_grads[m])
         gain_two_sum = gain_two_sum + gain_part
         hidden_grad = cotangent[m].astype(f32) + norm_grad
         low = hidden_grad.astype(bf16)
         token_grad = dot_nt(low, out_full).astype(bf16)
         mixed_grads.append(
-            lax.all_to_all(token_grad, "tensor", split_axis=1, concat_axis=0, tiled=True)
+            lax.all_to_all(token_grad, TP, split_axis=1, concat_axis=0, tiled=True)
         )
-        inner_rows.append(inner)
-        gate_grads.append(gate_grad)
-        up_grads.append(up_grad)
         hidden_grads.append(hidden_grad)
         attended_low.append(low)
-    grad_all = jnp.concatenate(grad_rows)
-    two_all = jnp.concatenate(gathered_two)
-    gate_share = scatter_sum(dot_tn(two_all, jnp.concatenate(gate_grads)), "dp")
-    up_share = scatter_sum(dot_tn(two_all, jnp.concatenate(up_grads)), "dp")
-    down_share = scatter_sum(dot_tn(jnp.concatenate(inner_rows), grad_all), "dp", 1)
     out_grad = lax.psum_scatter(
         dot_tn(jnp.concatenate(token_heads), jnp.concatenate(attended_low)).astype(bf16),
-        "tensor",
+        TP,
         scatter_dimension=0,
         tiled=True,
     )
@@ -500,7 +865,7 @@
         projected_grad, beta_grad, taps_part, heads_part = mixer_backward(
             lengths[m, 0], projected[m], beta_logits[m], taps, gain_heads, mixed_grads[m], saved[m]
         )
-        normed_grad = scatter_sum(dot_nt(projected_grad, w_inner) + dot_nt(beta_grad, w_beta), "tensor")
+        normed_grad = scatter_sum(dot_nt(projected_grad, w_inner) + dot_nt(beta_grad, w_beta), TP)
         norm_grad, gain_part = norm_backward(rows_in[m], one[m][1], gain_one, normed_grad)
         input_grads.append(hidden_grads[m] + norm_grad)
         gain_one_sum = gain_one_sum + gain_part
@@ -511,19 +876,17 @@
     one_all = jnp.concatenate(gathered_one)
     inner_sum = dot_tn(one_all, jnp.concatenate(projected_low))
     beta_sum = dot_tn(one_all, jnp.concatenate(beta_low))
-    gain_one_total = lax.psum_scatter(
-        gain_one_sum, ("dp", "tensor"), scatter_dimension=0, tiled=True)
-    gain_two_total = lax.psum_scatter(
-        gain_two_sum, ("dp", "tensor"), scatter_dimension=0, tiled=True)
+    gain_totals = lax.psum_scatter(
+        jnp.stack([gain_one_sum, gain_two_sum]), DP + TP, scatter_dimension=1, tiled=True)
     inner_total, beta_total, conv_total, heads_total, out_total = (
-        lax.psum(part.astype(bf16), "dp").astype(f32)
+        lax.psum(part.astype(bf16), DP).astype(f32)
         for part in (inner_sum, beta_sum, taps_sum, heads_sum, out_grad)
     )
     return (
         jnp.stack(result_rows),
         jnp.stack(input_grads),
-        gain_one_total,
-        gain_two_total,
+        gain_totals[0],
+        gain_totals[1],
         inner_total[:, :local_width],
         inner_total[:, local_width : 2 * local_width],
         inner_total[:, 2 * local_width : 3 * local_width],
@@ -539,41 +902,47 @@
 
 
 def solution(mesh):
+    dp, tensor = mesh.shape["dp"], mesh.shape["tensor"]
+    inner = 2 if tensor == 8 else 4
+    axes = ("x", "core", "z", "y")
+    fine = jax.sharding.Mesh(
+        mesh.devices.reshape(dp // 2, 2, tensor // inner, inner), axes)
+    tokens = P(None, DP + TP, None)
     in_specs = (
-        P(None, ("dp", "tensor"), None),
-        P(None, "dp", None),
-        P("dp"),
-        P("dp"),
-        P(None, "tensor"),
-        P(None, "tensor"),
-        P(None, "tensor"),
-        P(None, "tensor"),
-        P(None, "tensor"),
-        P(None, None, "tensor"),
-        P("tensor", None),
-        P("tensor", None),
-        P("dp", "tensor"),
-        P("dp", "tensor"),
-        P("tensor", "dp"),
-        P(None, ("dp", "tensor"), None),
+        tokens,
+        P(None, DP, None),
+        P(DP),
+        P(DP),
+        P(None, TP),
+        P(None, TP),
+        P(None, TP),
+        P(None, TP),
+        P(None, TP),
+        P(None, None, TP),
+        P(TP, None),
+        P(TP, None),
+        P(DP, TP),
+        P(DP, TP),
+        P(TP, DP),
+        tokens,
     )
     out_specs = (
-        P(None, ("dp", "tensor"), None),
-        P(None, ("dp", "tensor"), None),
-        P(("dp", "tensor")),
-        P(("dp", "tensor")),
-        P(None, "tensor"),
-        P(None, "tensor"),
-        P(None, "tensor"),
-        P(None, "tensor"),
-        P(None, "tensor"),
-        P(None, None, "tensor"),
-        P("tensor", None),
-        P("tensor", None),
-        P("dp", "tensor"),
-        P("dp", "tensor"),
-        P("tensor", "dp"),
+        tokens,
+        tokens,
+        P(DP + TP),
+        P(DP + TP),
+        P(None, TP),
+        P(None, TP),
+        P(None, TP),
+        P(None, TP),
+        P(None, TP),
+        P(None, None, TP),
+        P(TP, None),
+        P(TP, None),
+        P(DP, TP),
+        P(DP, TP),
+        P(TP, DP),
     )
     return jax.shard_map(
-        per_device, mesh=mesh, in_specs=in_specs, out_specs=out_specs, check_vma=False
+        per_device, mesh=fine, in_specs=in_specs, out_specs=out_specs, check_vma=False
     )

time: 1650 us -> 1430 us (0.87)
  waiting for transfers between devices: 1060 us -> 856 us
  Pallas kernels: 159 us -> 283 us
  matrix products: 203 us -> 88.9 us
  blocking collectives: 120 us -> 73.5 us
    all_gather x10 -> x4, waiting for transfers between devices: 515 us -> 205 us  [gather(): return lax.all_gather(x, axis_name, axis=axis, tiled=True)]
    reduce_scatter x9 -> x2, waiting for transfers between devices: 361 us -> 60.9 us  [scatter_sum(): lax.psum_scatter(x.astype(bf16), axis_name, scatter_dimension=axis, tiled...]
    reduce_scatter x0 -> x1, waiting for transfers between devices: none -> 150 us  [plane_weight_grads(): lax.psum_scatter(grads.reshape(lines * kinds * quarter, model), 'z', scat...]
    pallas_call x0 -> x1, Pallas kernels: none -> 125 us  [ffn_plane(): pl.pallas_call(ffn_kernel, out_shape=(jax.ShapeDtypeStruct((rows, model),...]
    unnamed x21 -> x11, waiting for transfers between devices: 4.05 us -> 125 us
    ppermute x0 -> x9, waiting for transfers between devices: none -> 84.7 us  [exchange(): return lax.ppermute(x, axis_name, [(i, i ^ distance) for i in range(size)])]
    reduce_scatter x1, waiting for transfers between devices: 58.6 us -> 136 us  [per_device(): lax.psum_scatter(dot_tn(jnp.concatenate(token_heads), jnp.concatenate(att...]
    dot_general x12 -> x6, matrix products: 77.8 us -> 34.7 us  [dot(): return jnp.dot(a, b, preferred_element_type=f32)]
  transfers between devices with their start and end apart: 22 -> 21, of which waited for: 19 -> 11; matrix products, arithmetic and copies ran while one was open for 14% -> 10% of each run, Pallas kernels for 10% -> 8%
where the time goes in v2:
time: 1430 us
  waiting for transfers between devices  856 us (60%)
  Pallas kernels  283 us (20%)
  matrix products  88.9 us (6%)
  blocking collectives  73.5 us (5%)
  local copies, waits for them, and re-layouts  54.2 us (4%)
  other arithmetic  38.4 us (3%)
  starting transfers between devices  20.2 us (1%)
  between operations  15.2 us (1%)
    all_gather x4, waiting for transfers between devices, gather(): return lax.all_gather(x, axis_name, axis=axis, tiled=True)  205 us
    reduce_scatter x1, waiting for transfers between devices, plane_weight_grads(): lax.psum_scatter(grads.reshape(lines * kinds * quarter, model), 'z', scat...  150 us
    reduce_scatter x1, waiting for transfers between devices, per_device(): lax.psum_scatter(dot_tn(jnp.concatenate(token_heads), jnp.concatenate(att...  136 us
    pallas_call x1, Pallas kernels, ffn_plane(): pl.pallas_call(ffn_kernel, out_shape=(jax.ShapeDtypeStruct((rows, model),...  125 us
    unnamed x11, waiting for transfers between devices  125 us
    psum x1, waiting for transfers between devices, per_device(): lax.psum(part.astype(bf16), DP).astype(f32)  94.9 us
    pallas_call x2, Pallas kernels, mixer_backward(): pl.pallas_call(partial(mixer_backward_kernel, exact), out_shape=(jax.Shap...  90.4 us
    ppermute x9, waiting for transfers between devices, exchange(): return lax.ppermute(x, axis_name, [(i, i ^ distance) for i in range(size)])  84.7 us
  transfers between devices with their start and end apart: 21, of which 11 were waited for; matrix products, arithmetic and copies ran while one was open for 10% of the time, Pallas kernels for 8%

profile of v2, /device:TPU:0, one launch (start us, length us, event | category | flops | bytes accessed | tf_op | source)
XLA Modules:
  0.0 1429.9 jit_solution(13670119279820027920)
XLA Ops:
  9.6 6.1 all-gather
  16.3 2.5 fusion.19
  23.0 12.4 collective-permute-done.5
  35.3 11.8 collective-permute-done.4
  51.2 23.2 %collective-permute-done = bf16[1,256,2048]{2,1,0:T(8,128)(2,1)S(1)} collective-permute-done((bf16[1,256,2048]{2,1,0:T(8,128)(2,1)S(1)}, bf16[1,256,2048]{2,1,0:T(8,128)(2,1)S(1)}, u32[]{:S(2)}, u32[]{:S(2)}) %collective-permute-start) | collective-permute-done | bytes 1048608 | tf_op jit(solution)/shard_map/ppermute | solution.py:714
  77.6 5.3 all-gather.1
  92.2 37.4 %collective-permute-done.1 = bf16[2,256,2048]{2,1,0:T(8,128)(2,1)} collective-permute-done((bf16[2,256,2048]{2,1,0:T(8,128)(2,1)}, bf16[2,256,2048]{2,1,0:T(8,128)(2,1)}, u32[]{:S(2)}, u32[]{:S(2)}) %collective-permute-start.1) | collective-permute-done | bytes 2097184 | tf_op jit(solution)/shard_map/ppermute | solution.py:714
  129.6 3.4 pad_maximum_fusion.1
  133.0 3.6 fusion.50.beta_ref
  136.6 8.5 fusion.49.proj_ref
  145.1 34.1 %mixer_forward.2 = (bf16[1024,256]{1,0:T(8,128)(2,1)S(1)}, f32[1024,256]{1,0:T(8,128)S(1)}, f32[1024,256]{1,0:T(8,128)S(1)}, f32[1024,256]{1,0:T(8,128)S(1)}, f3...) custom-call(s32[3]{0:T(128)S(1)} %get-tuple-element.123.lengths_ref, f32[1024,1024]{1,0:T(8,128)} %fusion.49.proj_ref, ...), custom_call_target="tpu_custom_call" | custom-call | flops 10000000000 | bytes 10000000 | tf_op jit(solution)/shard_map/mixer_forward/pallas_call | solution.py:332
  184.1 5.5 all-to-all-start
  189.7 3.6 fusion.52.beta_ref
  193.3 8.5 fusion.51.proj_ref
  201.8 34.1 %mixer_forward.3 = (bf16[1024,256]{1,0:T(8,128)(2,1)S(1)}, f32[1024,256]{1,0:T(8,128)S(1)}, f32[1024,256]{1,0:T(8,128)S(1)}, f32[1024,256]{1,0:T(8,128)S(1)}, f3...) custom-call(s32[3]{0:T(128)S(1)} %get-tuple-element.124.lengths_ref, f32[1024,1024]{1,0:T(8,128)} %fusion.51.proj_ref, ...), custom_call_target="tpu_custom_call" | custom-call | flops 10000000000 | bytes 10000000 | tf_op jit(solution)/shard_map/mixer_forward/pallas_call | solution.py:332
  240.8 6.0 all-to-all-start.1
  246.9 6.6 pad_maximum_fusion.c_ref
  253.5 63.8 %all-gather.9.cloned.1.call-done = bf16[2048,2048]{1,0:T(8,128)(2,1)} async-done(((bf16[256,2048]{1,0:T(8,128)(2,1)}), bf16[2048,2048]{1,0:T(8,128)(2,1)}) %all-gather.9.cloned.1.call-update) | async-done | bytes 8388624 | tf_op jit(solution)/shard_map/all_gather | solution.py:691
  317.3 4.9 multiply_reduce_fusion.5
  322.3 5.7 multiply_reduce_fusion.4
  330.3 141.4 %all-gather.13.cloned.1.call-done = bf16[2112,2048]{1,0:T(8,128)(2,1)} async-done(((bf16[528,2048]{1,0:T(8,128)(2,1)}), bf16[2112,2048]{1,0:T(8,128)(2,1)}) %all-gather.13.cloned.1.call-update) | async-done | bytes 8650768 | tf_op jit(solution)/shard_map/all_gather | solution.py:691
  471.6 124.7 %ffn_plane.1 = (f32[256,2048]{1,0:T(8,128)}, f32[256,2048]{1,0:T(8,128)}, bf16[4,3,176,2048]{3,2,1,0:T(8,128)(2,1)}) custom-call(bf16[256,2048]{1,0:T(8,128)(2,1)} %pad_maximum_fusion.9.x_ref, bf16[8,256,2048]{2,1,0:T(8,128)(2,1)} %pad_maximum_fusion.c_ref, bf16[4,3,176,2048]{3,2,1,0:T(8,128)(2,1)} %bitcast.190), custom_call_target="tpu_custom_call" | custom-call | flops 80000000000 | bytes 40000000 | tf_op jit(solution)/shard_map/ffn_plane/pallas_call | solution.py:639
  596.4 2.6 multiply_reduce_fusion.1
  599.5 4.5 add_bitcast_fusion.1
  604.0 2.9 convolution_convert_fusion.2
  607.0 18.0 %all_to_all.76 = bf16[128,8,256]{2,0,1:T(8,128)(2,1)} all-to-all(bf16[128,8,256]{2,0,1:T(8,128)(2,1)S(1)} %bitcast.167), channel_id=1, replica_groups=mesh['x'=2,'core'=2,'z'=4,'y'=2] {'z','y'}, dimensions={1} | all-to-all | bytes 1048576 | tf_op jit(solution)/shard_map/all_to_all | solution.py:852
  625.0 45.1 %mixer_backward.2 = (bf16[1024,1024]{1,0:T(8,128)(2,1)}, bf16[1024,2]{1,0:T(8,128)(2,1)}, f32[12,256]{1,0:T(8,128)}, f32[2,128]{1,0:T(2,128)}) custom-call(s32[3]{0:T(128)} %copy-done.3, f32[1024,1024]{1,0:T(8,128)} %fusion.49.proj_ref, f32[1024,2]{1,0:T(8,128)} %copy-done.6, f32[12,256]{1,0:T(8,128)} %copy-done.1, f32[2,128]{1,0:T(2,128)} %copy-done.4, ...), custom_call_target="tpu_custom_call" | custom-call | flops 10000000000 | bytes 10000000 | tf_op jit(solution)/shard_map/mixer_backward/pallas_call | solution.py:356
  670.1 7.0 fusion.53
  677.2 3.2 add_convert_fusion.1
  680.8 6.3 convolution_convert_fusion.1
  687.2 32.6 %all_to_all.77 = bf16[128,8,256]{2,0,1:T(8,128)(2,1)} all-to-all(bf16[128,8,256]{2,0,1:T(8,128)(2,1)S(1)} %bitcast.168), channel_id=1, replica_groups=mesh['x'=2,'core'=2,'z'=4,'y'=2] {'z','y'}, dimensions={1} | all-to-all | bytes 1048576 | tf_op jit(solution)/shard_map/all_to_all | solution.py:852
  719.7 45.3 %mixer_backward.3 = (bf16[1024,1024]{1,0:T(8,128)(2,1)}, bf16[1024,2]{1,0:T(8,128)(2,1)}, f32[12,256]{1,0:T(8,128)}, f32[2,128]{1,0:T(2,128)}) custom-call(s32[3]{0:T(128)} %copy-done.2, f32[1024,1024]{1,0:T(8,128)} %fusion.51.proj_ref, f32[1024,2]{1,0:T(8,128)} %copy-done.5, f32[12,256]{1,0:T(8,128)} %copy-done.1, f32[2,128]{1,0:T(2,128)} %copy-done.4, ...), custom_call_target="tpu_custom_call" | custom-call | flops 10000000000 | bytes 10000000 | tf_op jit(solution)/shard_map/mixer_backward/pallas_call | solution.py:356
  765.1 7.1 fusion.54
  772.2 3.2 add_convert_fusion
  775.4 6.9 convolution_convert_fusion
  783.4 4.9 constant_dynamic-update-slice_fusion.5
  792.4 4.7 convolution_convert_fusion.3
  797.2 13.0 fusion.4
  810.1 60.9 %reduce-scatter.10.cloned.1.call-done = bf16[128,2048]{1,0:T(8,128)(2,1)} async-done(((bf16[1024,2048]{1,0:T(8,128)(2,1)}), bf16[128,2048]{1,0:T(8,128)(2,1)}) %reduce-scatter.10.cloned.1.call-update) | async-done | bytes 524304 | tf_op jit(solution)/shard_map/reduce_scatter | solution.py:695
  874.5 11.5 all-reduce
  887.7 135.7 %reduce-scatter.12.cloned.1.call-done = bf16[256,2048]{1,0:T(8,128)(2,1)} async-done(((bf16[2048,2048]{1,0:T(8,128)(2,1)}), bf16[256,2048]{1,0:T(8,128)(2,1)}) %reduce-scatter.12.cloned.1.call-update) | async-done | bytes 1048592 | tf_op jit(solution)/shard_map/reduce_scatter | solution.py:856
  1023.5 150.1 %reduce-scatter.14.cloned.1.call-done = bf16[528,2048]{1,0:T(8,128)(2,1)} async-done(((bf16[2112,2048]{1,0:T(8,128)(2,1)}), bf16[528,2048]{1,0:T(8,128)(2,1)}) %reduce-scatter.14.cloned.1.call-update) | async-done | bytes 2162704 | tf_op jit(solution)/shard_map/reduce_scatter | solution.py:742
  1173.6 4.7 reshape.210
  1178.3 5.3 constant_dynamic-slice_fusion.7
  1190.5 122.4 %reduce-scatter.16.cloned.1.call-done = f32[64,2]{1,0:T(8,128)} async-done(((f32[2048,2]{1,0:T(8,128)}), f32[64,2]{1,0:T(8,128)}) %reduce-scatter.16.cloned.1.call-update) | async-done | bytes 528
  1319.5 94.9 %all-reduce.4.cloned.1.call-done = (bf16[2048,1024]{1,0:T(8,128)(2,1)}, bf16[256,2048]{1,0:T(8,128)(2,1)}) async-done(((bf16[2048,1024]{1,0:T(8,128)(2,1)}, bf16[256,2048]{1,0:T(8,128)(2,1)}), (bf16[2048,1024]{1,0:T(8,128)(2,1)}, bf16[256,2048]{1,0:T(8,128)(2,1)})) %all-reduce.4.cloned.1.call-update) | async-done | bytes 5242896 | tf_op jit(solution)/shard_map/psum | solution.py:882
  1414.4 2.8 convert_element_type.132
  1417.2 5.7 fusion.47
  (209 shorter events, 60.5 us)
Async XLA Ops:
  7.2 125.8 %copy-start = (bf16[2048,2]{0,1:T(2,128)(2,1)S(1)}, bf16[2048,2]{0,1:T(2,128)(2,1)}, u32[]{:S(2)}) copy-start(bf16[2048,2]{0,1:T(2,128)(2,1)} %param.24) | copy-start | bytes 24580
  7.2 13.2 copy-start.34
  7.2 13.2 copy-start.35
  7.2 13.2 copy-start.36
  7.2 125.8 %all-gather.7.cloned.1.call-start = ((), (), s32[]{:S(2)}) async-start(), calls=%async_computation.9 | async-start | bytes 4718592 | tf_op jit(solution)/shard_map/all_gather | solution.py:691
  18.8 170.9 %all-gather.11.cloned.1.call-start = ((), (), s32[]{:S(2)}) async-start(), calls=%async_computation.11 | async-start | bytes 4718592 | tf_op jit(solution)/shard_map/all_gather | solution.py:691
  19.5 297.8 %all-gather.9.cloned.1.call-start = ((), (), s32[]{:S(2)}) async-start(), calls=%async_computation.10 | async-start | bytes 9437184 | tf_op jit(solution)/shard_map/all_gather | solution.py:691
  20.3 451.4 %all-gather.13.cloned.1.call-start = ((), (), s32[]{:S(2)}) async-start(), calls=%async_computation.12 | async-start | bytes 10813440 | tf_op jit(solution)/shard_map/all_gather | solution.py:691
  20.8 14.6 %collective-permute-start.5 = (bf16[3,176,512]{2,1,0:T(8,128)(2,1)S(1)}, bf16[3,176,512]{2,1,0:T(8,128)(2,1)S(1)}, u32[]{:S(2)}, u32[]{:S(2)}) collective-permute-start(bf16[3,176,512]{2,1,0:T(8,128)(2,1)S(1)} %get-tuple-element.106), channel_id=1, source_target_pairs={{0,24},{8,16},{16,8},{24,0},{1,25},{9,17},{17,9},{25,1},{2,26},{10... | collective-permute-start | bytes 1622024 | tf_op jit(solution)/shard_map/ppermute | solution.py:714
  22.7 24.4 %collective-permute-start.4 = (bf16[3,176,512]{2,1,0:T(8,128)(2,1)S(1)}, bf16[3,176,512]{2,1,0:T(8,128)(2,1)S(1)}, u32[]{:S(2)}, u32[]{:S(2)}) collective-permute-start(bf16[3,176,512]{2,1,0:T(8,128)(2,1)S(1)} %get-tuple-element.107), channel_id=1, source_target_pairs={{0,16},{8,24},{16,0},{24,8},{1,17},{9,25},{17,1},{25,9},{2,18},{10... | collective-permute-start | bytes 1622024 | tf_op jit(solution)/shard_map/ppermute | solution.py:714
  22.9 24.3 %collective-permute-start.3 = (bf16[3,176,512]{2,1,0:T(8,128)(2,1)S(1)}, bf16[3,176,512]{2,1,0:T(8,128)(2,1)S(1)}, u32[]{:S(2)}, u32[]{:S(2)}) collective-permute-start(bf16[3,176,512]{2,1,0:T(8,128)(2,1)S(1)} %get-tuple-element.108), channel_id=1, source_target_pairs={{0,8},{8,0},{16,24},{24,16},{1,9},{9,1},{17,25},{25,17},{2,10},{10... | collective-permute-start | bytes 1622024 | tf_op jit(solution)/shard_map/ppermute | solution.py:714
  49.2 28.3 %copy-start.50 = (bf16[2,128]{1,0:T(2,128)(2,1)S(1)}, bf16[2,128]{1,0:T(2,128)(2,1)}, u32[]{:S(2)}) copy-start(bf16[2,128]{1,0:T(2,128)(2,1)} %param.26) | copy-start | bytes 1540
  49.2 28.4 %copy-start.46 = (bf16[512]{0:T(512)(128)(2,1)S(1)}, bf16[512]{0:T(512)(128)(2,1)}, u32[]{:S(2)}) copy-start(bf16[512]{0:T(512)(128)(2,1)} %param.19) | copy-start | bytes 3076
  49.2 33.7 %copy-start.45 = (bf16[3,4,256]{2,1,0:T(4,128)(2,1)S(1)}, bf16[3,4,256]{2,1,0:T(4,128)(2,1)}, u32[]{:S(2)}) copy-start(bf16[3,4,256]{2,1,0:T(4,128)(2,1)} %param.25) | copy-start | bytes 18436
  49.2 33.7 %copy-start.47 = (s32[2,1,3]{2,1,0:T(1,128)S(1)}, s32[2,1,3]{2,1,0:T(1,128)}, u32[]{:S(2)}) copy-start(s32[2,1,3]{2,1,0:T(1,128)} %param.17) | copy-start | bytes 76
  49.3 25.1 %collective-permute-start = (bf16[1,256,2048]{2,1,0:T(8,128)(2,1)S(1)}, bf16[1,256,2048]{2,1,0:T(8,128)(2,1)S(1)}, u32[]{:S(2)}, u32[]{:S(2)}) collective-permute-start(bf16[1,256,2048]{2,1,0:T(8,128)(2,1)S(1)} %bitcast.150), channel_id=1, source_target_pairs={{0,16},{16,0},{1,17},{17,1},{2,18},{18,2},{3,19},{19,3},{4,20},{20... | collective-permute-start | bytes 3145736 | tf_op jit(solution)/shard_map/ppermute | solution.py:714
  75.8 53.7 %collective-permute-start.1 = (bf16[2,256,2048]{2,1,0:T(8,128)(2,1)}, bf16[2,256,2048]{2,1,0:T(8,128)(2,1)}, u32[]{:S(2)}, u32[]{:S(2)}) collective-permute-start(bf16[2,256,2048]{2,1,0:T(8,128)(2,1)} %pad_maximum_fusion.6), channel_id=1, source_target_pairs={{0,1},{1,0},{2,3},{3,2},{4,5},{5,4},{6,7},{7,6},{8,9},{9,8},{10,11... | collective-permute-start | bytes 6291464 | tf_op jit(solution)/shard_map/ppermute | solution.py:714
  77.6 124.2 %copy-start.4 = (f32[2,128]{1,0:T(2,128)}, f32[2,128]{1,0:T(2,128)S(1)}, u32[]{:S(2)}) copy-start(f32[2,128]{1,0:T(2,128)S(1)} %convert_element_type.105.gain_ref) | copy-start | bytes 3076
  83.0 118.8 %copy-start.1 = (f32[12,256]{1,0:T(8,128)}, f32[12,256]{1,0:T(8,128)S(1)}, u32[]{:S(2)}) copy-start(f32[12,256]{1,0:T(8,128)S(1)} %reshape.217.tap_ref) | copy-start | bytes 36868
  83.0 62.1 %copy-start.3 = (s32[3]{0:T(128)}, s32[3]{0:T(128)S(1)}, u32[]{:S(2)}) copy-start(s32[3]{0:T(128)S(1)} %get-tuple-element.123.lengths_ref) | copy-start | bytes 40
  83.0 118.7 %copy-start.2 = (s32[3]{0:T(128)}, s32[3]{0:T(128)S(1)}, u32[]{:S(2)}) copy-start(s32[3]{0:T(128)S(1)} %get-tuple-element.124.lengths_ref) | copy-start | bytes 40
  133.0 113.9 %collective-permute-start.2 = (bf16[4,256,2048]{2,1,0:T(8,128)(2,1)}, bf16[4,256,2048]{2,1,0:T(8,128)(2,1)}, u32[]{:S(2)}, u32[]{:S(2)}) collective-permute-start(bf16[4,256,2048]{2,1,0:T(8,128)(2,1)} %pad_maximum_fusion.1), channel_id=1, source_target_pairs={{0,8},{8,0},{1,9},{9,1},{2,10},{10,2},{3,11},{11,3},{4,12},{12,4},... | collective-permute-start | bytes 12582920 | tf_op jit(solution)/shard_map/ppermute | solution.py:714
  136.6 8.5 copy-start.6
  184.1 56.7 %all-to-all-start = ((bf16[8,128,256]{1,2,0:T(8,128)(2,1)}), bf16[8,128,256]{1,2,0:T(8,128)(2,1)}, u32[]{:S(2)}, u32[]{:S(2)}) async-start(bf16[8,128,256]{1,2,0:T(8,128)(2,1)} %copy.54), calls=%async_computation | async-start | bytes 1048576 | tf_op jit(solution)/shard_map/all_to_all | solution.py:835
  193.3 8.5 copy-start.5
  240.8 81.4 %all-to-all-start.1 = ((bf16[8,128,256]{1,2,0:T(8,128)(2,1)}), bf16[8,128,256]{1,2,0:T(8,128)(2,1)}, u32[]{:S(2)}, u32[]{:S(2)}) async-start(bf16[8,128,256]{1,2,0:T(8,128)(2,1)} %copy.56), calls=%async_computation.1 | async-start | bytes 1048576 | tf_op jit(solution)/shard_map/all_to_all | solution.py:835
  246.8 70.5 %copy-start.15 = (bf16[2,128,2048]{2,1,0:T(8,128)(2,1)S(1)}, bf16[2,128,2048]{2,1,0:T(8,128)(2,1)}, u32[]{:S(2)}) copy-start(bf16[2,128,2048]{2,1,0:T(8,128)(2,1)} %param.16) | copy-start | bytes 3145732
  246.9 563.3 %reduce-scatter.8.cloned.1.call-start = ((), (), s32[]{:S(2)}) async-start(), calls=%async_computation.13 | async-start | bytes 4718592 | tf_op jit(solution)/shard_map/reduce_scatter | solution.py:695
  596.4 7.7 slice-start
  670.1 7.1 copy-start.32
  680.4 190.7 %reduce-scatter.10.cloned.1.call-start = ((), (), s32[]{:S(2)}) async-start(), calls=%async_computation.14 | async-start | bytes 4718592 | tf_op jit(solution)/shard_map/reduce_scatter | solution.py:695
  765.1 7.1 copy-start.33
  775.4 248.1 %reduce-scatter.12.cloned.1.call-start = ((), (), s32[]{:S(2)}) async-start(), calls=%async_computation.15 | async-start | bytes 9437184 | tf_op jit(solution)/shard_map/reduce_scatter | solution.py:856
  782.4 391.2 %reduce-scatter.14.cloned.1.call-start = ((), (), s32[]{:S(2)}) async-start(), calls=%async_computation.16 | async-start | bytes 10813440 | tf_op jit(solution)/shard_map/reduce_scatter | solution.py:742
  783.1 529.8 %reduce-scatter.16.cloned.1.call-start = ((), (), s32[]{:S(2)}) async-start(), calls=%async_computation.17 | async-start | bytes 1081344
  783.3 4.9 copy-start.25
  792.4 4.8 copy-start.51
  797.1 73.9 %copy-start.16 = (bf16[2,128,2048]{2,1,0:T(8,128)(2,1)S(1)}, bf16[2,128,2048]{2,1,0:T(8,128)(2,1)}, u32[]{:S(2)}) copy-start(bf16[2,128,2048]{2,1,0:T(8,128)(2,1)} %param.16) | copy-start | bytes 3145732
  797.1 73.9 %copy-start.38 = (f32[4,1,512]{2,1,0:T(1,128)S(1)}, f32[4,1,512]{2,1,0:T(1,128)}, u32[]{:S(2)}) copy-start(f32[4,1,512]{2,1,0:T(1,128)} %copy-done.37) | copy-start | bytes 24580
  797.1 73.9 %copy-start.42 = (f32[128]{0:T(128)S(1)}, f32[128]{0:T(128)}, u32[]{:S(2)}) copy-start(f32[128]{0:T(128)} %copy-done.41) | copy-start | bytes 1540
  797.1 73.9 %copy-start.44 = (f32[128]{0:T(128)S(1)}, f32[128]{0:T(128)}, u32[]{:S(2)}) copy-start(f32[128]{0:T(128)} %copy-done.43) | copy-start | bytes 1540
  810.1 64.3 %copy-start.48 = (f32[2,128]{1,0:T(2,128)S(1)}, f32[2,128]{1,0:T(2,128)}, u32[]{:S(2)}) copy-start(f32[2,128]{1,0:T(2,128)} %get-tuple-element.58) | copy-start | bytes 3076
  810.1 64.3 %copy-start.49 = (f32[2,128]{1,0:T(2,128)S(1)}, f32[2,128]{1,0:T(2,128)}, u32[]{:S(2)}) copy-start(f32[2,128]{1,0:T(2,128)} %get-tuple-element.59) | copy-start | bytes 3076
  874.4 540.0 %all-reduce.4.cloned.1.call-start = ((), (), s32[]{:S(2)}) async-start(), calls=%async_computation.18 | async-start | bytes 10485760 | tf_op jit(solution)/shard_map/psum | solution.py:882
  1186.4 128.8 %collective-permute-start.6 = (bf16[528,512]{1,0:T(8,128)(2,1)}, bf16[528,512]{1,0:T(8,128)(2,1)S(1)}, u32[]{:S(2)}, u32[]{:S(2)}) collective-permute-start(bf16[528,512]{1,0:T(8,128)(2,1)} %bitcast.142), channel_id=1, source_target_pairs={{0,8},{8,0},{16,24},{24,16},{1,9},{9,1},{17,25},{25,17},{2,10},{10... | collective-permute-start | bytes 1622024 | tf_op jit(solution)/shard_map/ppermute | solution.py:714
  1186.4 128.8 %collective-permute-start.7 = (bf16[528,512]{1,0:T(8,128)(2,1)}, bf16[528,512]{1,0:T(8,128)(2,1)S(1)}, u32[]{:S(2)}, u32[]{:S(2)}) collective-permute-start(bf16[528,512]{1,0:T(8,128)(2,1)} %bitcast.141), channel_id=1, source_target_pairs={{0,16},{8,24},{16,0},{24,8},{1,17},{9,25},{17,1},{25,9},{2,18},{10... | collective-permute-start | bytes 1622024 | tf_op jit(solution)/shard_map/ppermute | solution.py:714
  1187.9 127.3 %collective-permute-start.8 = (bf16[528,512]{1,0:T(8,128)(2,1)}, bf16[528,512]{1,0:T(8,128)(2,1)}, u32[]{:S(2)}, u32[]{:S(2)}) collective-permute-start(bf16[528,512]{1,0:T(8,128)(2,1)} %bitcast.140), channel_id=1, source_target_pairs={{0,24},{8,16},{16,8},{24,0},{1,25},{9,17},{17,9},{25,1},{2,26},{10... | collective-permute-start | bytes 1622024 | tf_op jit(solution)/shard_map/ppermute | solution.py:714
  1188.3 126.7 %copy-start.22 = (bf16[528,1,512]{2,1,0:T(2,128)(2,1)S(1)}, bf16[528,1,512]{2,1,0:T(2,128)(2,1)}, u32[]{:S(2)}) copy-start(bf16[528,1,512]{2,1,0:T(2,128)(2,1)} %get-tuple-element.97) | copy-start | bytes 1622020
  (28 other events, 68.9 us)
Sparse Core Ops, SparseCore 0:
  18.9 75.2 all-gather.6
  96.9 74.9 all-gather.10
  174.1 143.1 all-gather.8
  318.7 152.8 all-gather.12
  680.5 98.7 reduce-scatter.7
  783.2 87.8 reduce-scatter.9
  874.7 148.7 reduce-scatter.11
  1025.9 147.6 reduce-scatter.13
  1176.5 136.3 reduce-scatter.15
  1315.3 99.0 all-reduce.3

commit v3 on v2

--- a/solution.py
+++ b/solution.py
@@ -198,6 +198,7 @@
     taps = tap_ref.shape[0] // 3
     segment_of, segments = segment_tools(lengths_ref)
     dgain_ref[...] = jnp.zeros_like(dgain_ref)
+    dbeta_ref[...] = jnp.zeros_like(dbeta_ref)
     dtap_ref[...] = jnp.zeros_like(dtap_ref)
 
     @pl.loop(0, count)
@@ -352,12 +353,11 @@
 def mixer_backward(lengths_row, projected, beta_logits, taps, gain, grad, saved, exact=True):
     rows, wide = projected.shape
     width = wide // 4
-    heads = width // 128
     return pl.pallas_call(
         partial(mixer_backward_kernel, exact),
         out_shape=(
             jax.ShapeDtypeStruct((rows, wide), bf16),
-            jax.ShapeDtypeStruct((rows, heads), bf16),
+            jax.ShapeDtypeStruct((rows, 128), bf16),
             jax.ShapeDtypeStruct(taps.shape, f32),
             jax.ShapeDtypeStruct(gain.shape, f32),
         ),
@@ -669,6 +669,343 @@
     )(x_own, c_all, weights)
 
 
+def line_positions(lines):
+    o = lax.axis_index("z")
+    i = lax.axis_index("y")
+
+    def at(z, y):
+        return {"z": z, "y": y}
+
+    return o, i, at
+
+
+def line_barrier(lines):
+    o = lax.axis_index("z")
+    barrier = pltpu.get_barrier_semaphore()
+    mesh_id = pl.DeviceIdType.MESH
+
+    @pl.when(o > 0)
+    def _():
+        pl.semaphore_signal(barrier, inc=1, device_id={"z": o - 1}, device_id_type=mesh_id)
+
+    @pl.when(o < lines - 1)
+    def _():
+        pl.semaphore_signal(barrier, inc=1, device_id={"z": o + 1}, device_id_type=mesh_id)
+
+    pl.semaphore_signal(barrier, inc=1, device_id=other("y"), device_id_type=mesh_id)
+
+    peers = 1 + (o > 0).astype(jnp.int32) + (o < lines - 1).astype(jnp.int32)
+    pl.semaphore_wait(barrier, peers)
+
+
+def line_copy(src, dst, send, recv, target):
+    return pltpu.make_async_remote_copy(
+        src_ref=src, dst_ref=dst, send_sem=send, recv_sem=recv,
+        device_id=target, device_id_type=pl.DeviceIdType.MESH)
+
+
+def gather_kernel(x_ref, w_ref, wb_ref, rows_ref, proj_ref, beta_ref, xs, stage, beta_stage,
+                  right_send, left_send, line_recv, pair_send, pair_recv, row_sem, out_sem, beta_sem):
+    batches = xs.shape[1]
+    lines = xs.shape[0] // 2
+    rows = xs.shape[2]
+    model = xs.shape[3]
+    o = lax.axis_index("z")
+    i = lax.axis_index("y")
+    line_barrier(lines)
+
+    def right(z, m):
+        return line_copy(xs.at[z * 2 + i, m], xs.at[z * 2 + i, m], right_send.at[z, m],
+                         line_recv.at[z, m], {"z": o + 1})
+
+    def left(z, m):
+        return line_copy(xs.at[z * 2 + i, m], xs.at[z * 2 + i, m], left_send.at[z, m],
+                         line_recv.at[z, m], {"z": o - 1})
+
+    def across(z, m):
+        return line_copy(xs.at[z * 2 + i, m], xs.at[z * 2 + i, m], pair_send.at[z, m],
+                         pair_recv.at[z, m], other("y"))
+
+    own = pltpu.make_async_copy(x_ref, xs.at[o * 2 + i], row_sem.at[2 * lines, 0])
+    own.start()
+    own.wait()
+
+    def outs(turn, slot, m):
+        return (
+            pltpu.make_async_copy(stage.at[lax.rem(turn, 2), m], proj_ref.at[m, slot], out_sem.at[lax.rem(turn, 2), m]),
+            pltpu.make_async_copy(beta_stage.at[lax.rem(turn, 2), m], beta_ref.at[m, slot], beta_sem.at[lax.rem(turn, 2), m]),
+        )
+
+    def keep(slot, m):
+        return pltpu.make_async_copy(xs.at[slot, m], rows_ref.at[m, slot], row_sem.at[slot, m])
+
+    def project(turn, slot):
+        @pl.when(turn >= 2)
+        def _():
+            for m in range(batches):
+                for copy in outs(turn, slot, m):
+                    copy.wait()
+        for m in range(batches):
+            keep(slot, m).start()
+        x = xs[slot].reshape(batches * rows, model)
+        width = w_ref.shape[1]
+        tile = min(256, width)
+        for start in range(0, width, tile):
+            cols = slice(start, start + tile)
+            stage[lax.rem(turn, 2), :, :, cols] = jnp.dot(
+                x, w_ref[:, cols], preferred_element_type=f32).reshape(batches, rows, tile)
+        beta_stage[lax.rem(turn, 2)] = jnp.dot(
+            x, wb_ref[...], preferred_element_type=f32).reshape(batches, rows, 128)
+        for m in range(batches):
+            for copy in outs(turn, slot, m):
+                copy.start()
+
+    def in_line(index):
+        far = (index + 1) // 2
+        side = 1 - 2 * lax.rem(index, 2)
+        z = o + side * far
+        return far, side, z, (z >= 0) & (z < lines)
+
+    def first(index, turn):
+        far, side, z, valid = in_line(index)
+
+        @pl.when(valid)
+        def _():
+            for m in range(batches):
+                @pl.when(far > 0)
+                def _():
+                    left(z, m).wait_recv()
+
+                @pl.when((o < lines - 1) & (z <= o))
+                def _():
+                    right(z, m).start()
+
+                @pl.when((o > 0) & (z >= o))
+                def _():
+                    left(z, m).start()
+
+                across(z, m).start()
+            project(turn, z * 2 + i)
+
+        return turn + valid.astype(jnp.int32)
+
+    turn = lax.fori_loop(0, 2 * lines - 1, first, jnp.int32(0))
+
+    def second(index, turn):
+        far, side, z, valid = in_line(index)
+
+        @pl.when(valid)
+        def _():
+            for m in range(batches):
+                across(z, m).wait_recv()
+            project(turn, z * 2 + 1 - i)
+
+        return turn + valid.astype(jnp.int32)
+
+    lax.fori_loop(0, 2 * lines - 1, second, turn)
+
+    for turn in range(2 * lines - 2, 2 * lines):
+        for m in range(batches):
+            for copy in outs(turn, 0, m):
+                copy.wait()
+
+    @pl.loop(0, lines)
+    def _(z):
+        for m in range(batches):
+            @pl.when((o < lines - 1) & (z <= o))
+            def _():
+                right(z, m).wait_send()
+
+            @pl.when((o > 0) & (z >= o))
+            def _():
+                left(z, m).wait_send()
+
+            across(z, m).wait_send()
+            keep(z * 2, m).wait()
+            keep(z * 2 + 1, m).wait()
+
+
+def gather_project(x, w_inner, w_beta):
+    batches, rows, model = x.shape
+    lines = lax.axis_size("z")
+    width = w_inner.shape[1]
+    slots = 2 * lines
+    heads = w_beta.shape[1]
+    w_beta = jnp.pad(w_beta, ((0, 0), (0, 128 - heads)))
+    sems = pltpu.SemaphoreType.DMA
+    anywhere = pl.BlockSpec(memory_space=pl.ANY)
+    gathered, projected, beta = pl.pallas_call(
+        gather_kernel,
+        out_shape=(
+            jax.ShapeDtypeStruct((batches, slots, rows, model), bf16),
+            jax.ShapeDtypeStruct((batches, slots, rows, width), f32),
+            jax.ShapeDtypeStruct((batches, slots, rows, 128), f32),
+        ),
+        in_specs=[anywhere, vmem(), vmem()],
+        out_specs=(anywhere,) * 3,
+        scratch_shapes=[
+            pltpu.VMEM((slots, batches, rows, model), bf16),
+            pltpu.VMEM((2, batches, rows, width), f32),
+            pltpu.VMEM((2, batches, rows, 128), f32),
+            sems((lines, batches)), sems((lines, batches)), sems((lines, batches)),
+            sems((lines, batches)), sems((lines, batches)),
+            sems((slots + 1, batches)), sems((2, batches)), sems((2, batches)),
+        ],
+        compiler_params=pltpu.CompilerParams(
+            collective_id=1, has_side_effects=True, vmem_limit_bytes=40 * 2**20),
+        cost_estimate=pl.CostEstimate(flops=7 * 10**10, bytes_accessed=4 * 10**7, transcendentals=0),
+        name="gather_project",
+    )(x, w_inner, w_beta)
+    total = slots * rows
+    return (gathered.reshape(batches, total, model), projected.reshape(batches, total, width),
+            beta.reshape(batches, total, 128))
+
+
+def scatter_kernel(g_ref, gb_ref, w_ref, wb_ref, out_ref, gs, bs, ysend, yrecv, from_left, from_right,
+                   pair_send, pair_recv, right_send, left_send, right_recv, left_recv, g_sem, b_sem):
+    batches, rows, width = gs.shape[1:]
+    lines = yrecv.shape[0]
+    model = yrecv.shape[3]
+    o = lax.axis_index("z")
+    i = lax.axis_index("y")
+    tile = min(512, model)
+
+    def target(index):
+        far = lines - 1 - index // 2
+        side = 1 - 2 * lax.rem(index, 2)
+        z = o + side * far
+        return far, z, (z >= 0) & (z < lines) & ((far > 0) | (side > 0))
+
+    def load(z, y, buffer):
+        slot = z * 2 + y
+        return (pltpu.make_async_copy(g_ref.at[:, slot], gs.at[buffer], g_sem.at[buffer]),
+                pltpu.make_async_copy(gb_ref.at[:, slot], bs.at[buffer], b_sem.at[buffer]))
+
+    def partial_rows(z, y, buffer, store):
+        for copy in load(z, y, buffer):
+            copy.start()
+        for copy in load(z, y, buffer):
+            copy.wait()
+        for m in range(batches):
+            g = gs[buffer, m]
+            b = bs[buffer, m]
+            for start in range(0, model, tile):
+                cols = slice(start, start + tile)
+                store(m, cols, lax.dot_general(g, w_ref[cols, :], NT, preferred_element_type=f32)
+                      + lax.dot_general(b, wb_ref[cols, :], NT, preferred_element_type=f32))
+
+    def across(z, m):
+        return line_copy(ysend.at[z, m], yrecv.at[z, m], pair_send.at[z, m], pair_recv.at[z, m], other("y"))
+
+    def right(z, m):
+        return line_copy(yrecv.at[z, m], from_left.at[z, m], right_send.at[z, m], right_recv.at[z, m], {"z": o + 1})
+
+    def left(z, m):
+        return line_copy(yrecv.at[z, m], from_right.at[z, m], left_send.at[z, m], left_recv.at[z, m], {"z": o - 1})
+
+    line_barrier(lines)
+
+    @pl.loop(0, 2 * lines)
+    def _(index):
+        far, z, valid = target(index)
+
+        @pl.when(valid)
+        def _():
+            def store(m, cols, value):
+                ysend[z, m, :, cols] = value.astype(bf16)
+            partial_rows(z, 1 - i, 0, store)
+            for m in range(batches):
+                across(z, m).start()
+
+    @pl.loop(0, 2 * lines)
+    def _(index):
+        far, z, valid = target(index)
+
+        @pl.when(valid)
+        def _():
+            for m in range(batches):
+                across(z, m).wait_recv()
+
+            def store(m, cols, value):
+                yrecv[z, m, :, cols] = (yrecv[z, m, :, cols].astype(f32) + value).astype(bf16)
+            partial_rows(z, i, 0, store)
+            for m in range(batches):
+                @pl.when((z > o) & (o > 0))
+                def _():
+                    right(z, m).wait_recv()
+                    yrecv[z, m] = (yrecv[z, m].astype(f32) + from_left[z, m].astype(f32)).astype(bf16)
+
+                @pl.when(z > o)
+                def _():
+                    right(z, m).start()
+
+                @pl.when((z < o) & (o < lines - 1))
+                def _():
+                    left(z, m).wait_recv()
+                    yrecv[z, m] = (yrecv[z, m].astype(f32) + from_right[z, m].astype(f32)).astype(bf16)
+
+                @pl.when(z < o)
+                def _():
+                    left(z, m).start()
+
+    for m in range(batches):
+        out_ref[m] = yrecv[o, m].astype(f32)
+
+        @pl.when(o > 0)
+        def _():
+            right(o, m).wait_recv()
+            out_ref[m] += from_left[o, m].astype(f32)
+
+        @pl.when(o < lines - 1)
+        def _():
+            left(o, m).wait_recv()
+            out_ref[m] += from_right[o, m].astype(f32)
+
+    @pl.loop(0, lines)
+    def _(z):
+        for m in range(batches):
+            across(z, m).wait_send()
+
+            @pl.when(z > o)
+            def _():
+                right(z, m).wait_send()
+
+            @pl.when(z < o)
+            def _():
+                left(z, m).wait_send()
+
+
+def scatter_rows(grads, beta_grads, w_inner, w_beta):
+    batches, total, width = grads.shape
+    model = w_inner.shape[0]
+    lines = lax.axis_size("z")
+    slots = 2 * lines
+    rows = total // slots
+    heads = w_beta.shape[1]
+    w_beta = jnp.pad(w_beta, ((0, 0), (0, 128 - heads)))
+    sems = pltpu.SemaphoreType.DMA
+    anywhere = pl.BlockSpec(memory_space=pl.ANY)
+    slab = pltpu.VMEM((lines, batches, rows, model), bf16)
+    return pl.pallas_call(
+        scatter_kernel,
+        out_shape=jax.ShapeDtypeStruct((batches, rows, model), f32),
+        in_specs=[anywhere, anywhere, vmem(), vmem()],
+        out_specs=vmem(),
+        scratch_shapes=[
+            pltpu.VMEM((2, batches, rows, width), bf16),
+            pltpu.VMEM((2, batches, rows, 128), bf16),
+            slab, slab, slab, slab,
+            sems((lines, batches)), sems((lines, batches)), sems((lines, batches)),
+            sems((lines, batches)), sems((lines, batches)), sems((lines, batches)),
+            sems((2,)), sems((2,)),
+        ],
+        compiler_params=pltpu.CompilerParams(
+            collective_id=3, has_side_effects=True, vmem_limit_bytes=40 * 2**20),
+        cost_estimate=pl.CostEstimate(flops=7 * 10**10, bytes_accessed=4 * 10**7, transcendentals=0),
+        name="scatter_rows",
+    )(grads.reshape(batches, slots, rows, width), beta_grads.reshape(batches, slots, rows, 128), w_inner, w_beta)
+
+
 def root_scale(row_values, gain_vector):
     row_scale = lax.rsqrt(jnp.mean(row_values * row_values, axis=-1, keepdims=True) + epsilon)
     return (row_values * row_scale * gain_vector, row_scale)
@@ -679,7 +1016,7 @@
     rows_grad = row_scale * weighted - row_values * row_scale * row_scale * row_scale * jnp.mean(
         weighted * row_values, axis=-1, keepdims=True
     )
-    gain_grad = jnp.sum(normed_grad * row_values * row_scale, axis=0)
+    gain_grad = jnp.sum(normed_grad * row_values * row_scale, axis=tuple(range(row_values.ndim - 1)))
     return (rows_grad, gain_grad)
 
 
@@ -721,8 +1058,7 @@
     for r in range(size):
         block = lax.dynamic_index_in_dim(blocks, me ^ r, keepdims=False)
         pieces.append(exchange(block, DP, r) if r else block)
-    pieces = jnp.stack(pieces)
-    return [lax.dynamic_index_in_dim(pieces, me ^ q, keepdims=False) for q in range(size)]
+    return ordered_blocks(pieces)
 
 
 def plane_weights(w_gate, w_up, w_down):
@@ -753,14 +1089,60 @@
     return x
 
 
+def ordered_blocks(pieces):
+    me = lax.axis_index(DP)
+    pieces = jnp.stack(pieces)
+    return [lax.dynamic_index_in_dim(pieces, me ^ q, keepdims=False) for q in range(len(pieces))]
+
+
+def pick(x, index, axis):
+    return lax.dynamic_index_in_dim(x, index, axis, keepdims=False)
+
+
+def gather_pairs(x):
+    across = exchange(x, "x")
+    return ordered_blocks([x, exchange(x, "core"), across, exchange(across, "core")])
+
+
+def sum_pairs(x):
+    core = lax.axis_index("core")
+    halves = x.reshape(2, x.shape[0] // 2, *x.shape[1:])
+    mine = pick(halves, core, 0).astype(f32)
+    mine = mine + exchange(pick(halves, 1 - core, 0).astype(bf16), "core").astype(f32)
+    low = mine.astype(bf16)
+    mine = (mine + exchange(low, "x").astype(f32)).astype(bf16)
+    theirs = exchange(mine, "core")
+    first = jnp.where(core == 0, mine, theirs)
+    second = jnp.where(core == 0, theirs, mine)
+    return first, second
+
+
+def gather_out(w_out):
+    me = lax.axis_index(DP)
+    quarters = w_out.reshape(lax.axis_size(DP), -1, w_out.shape[1])
+    column = gather(pick(quarters, me, 0)[None], TP)
+    return jnp.stack(gather_pairs(column), axis=1).reshape(-1, w_out.shape[1])
+
+
+def scatter_out(grad):
+    devices = lax.axis_size(TP)
+    grad = grad.reshape(devices, 2, 2, -1, grad.shape[1])
+    for axis_name, axis in (("core", 2), ("x", 1)):
+        me = lax.axis_index(axis_name)
+        theirs = exchange(pick(grad, 1 - me, axis), axis_name)
+        grad = (pick(grad, me, axis).astype(f32) + theirs.astype(f32)).astype(bf16)
+    own = lax.psum_scatter(grad, TP, scatter_dimension=0, tiled=True)[0]
+    return jnp.concatenate(gather_pairs(own)).astype(f32)
+
+
 def feed_forward_plane(normed, cotangents, w_gate, w_up, w_down):
     weights = plane_weights(w_gate, w_up, w_down)
-    rows = jnp.concatenate(normed)
-    count, model = rows.shape
+    batches, rows, model = normed.shape
+    rows = normed.reshape(batches * rows, model)
+    count = rows.shape[0]
     c_all = plane_rows(cotangents.reshape(1, count, model))
     out, normed_grad, grads = ffn_plane(rows, c_all, weights)
-    per_batch = (len(normed), count // len(normed), model)
-    return out.reshape(per_batch), normed_grad.reshape(per_batch), plane_weight_grads(grads)
+    return out.reshape(normed.shape), normed_grad.reshape(normed.shape), plane_weight_grads(grads)
 
 
 def feed_forward_groups(normed, cotangents, w_gate, w_up, w_down):
@@ -768,7 +1150,7 @@
     up_full = gather(w_up, DP)
     down_full = gather(w_down, DP, 1)
     outs, normed_grads, inner_rows, gate_grads, up_grads, rows, grad_rows = [], [], [], [], [], [], []
-    for m in range(len(normed)):
+    for m in range(normed.shape[0]):
         rows.append(gather(normed[m], TP))
         grad_rows.append(gather(cotangents[m], TP))
         gate_values = dot(rows[m], gate_full)
@@ -791,7 +1173,7 @@
     gate_share = scatter_sum(dot_tn(rows_all, jnp.concatenate(gate_grads)), DP)
     up_share = scatter_sum(dot_tn(rows_all, jnp.concatenate(up_grads)), DP)
     down_share = scatter_sum(dot_tn(jnp.concatenate(inner_rows), grad_all), DP, 1)
-    return outs, normed_grads, (gate_share, up_share, down_share)
+    return jnp.stack(outs), jnp.stack(normed_grads), (gate_share, up_share, down_share)
 
 
 def per_device(
@@ -814,85 +1196,102 @@
 ):
     batches = range(inputs.shape[0])
     local_width = w_query.shape[1]
+    heads = w_beta.shape[1]
+    devices = lax.axis_size(TP)
     planar = all(lax.axis_size(name) == 2 for name in ("x", "core", "y"))
     w_inner = jnp.concatenate([w_query, w_key, w_value, w_gate_out], axis=1)
     taps = conv_weight.astype(f32).reshape(-1, local_width)
     gain_heads = head_gain.astype(f32)
-    gain_one = gather(norm_gain, DP).astype(f32)
-    gain_two = gather(ffn_gain, DP).astype(f32)
-    rows_in = [inputs[m].astype(f32) for m in batches]
-    one = [root_scale(rows, gain_one) for rows in rows_in]
-    gathered_one = [gather(one[m][0].astype(bf16), TP) for m in batches]
-    projected = [dot(rows, w_inner) for rows in gathered_one]
-    beta_logits = [dot(rows, w_beta) for rows in gathered_one]
-    out_full = gather(w_out, TP)
-    mixed, saved = [], []
+    gains = gather(jnp.stack([norm_gain, ffn_gain]), DP, 1).astype(f32)
+    gain_one, gain_two = gains[0], gains[1]
+    rows_in = inputs.astype(f32)
+    normed_one, scale_one = root_scale(rows_in, gain_one)
+    normed_one = normed_one.astype(bf16)
+    if planar:
+        gathered_one, projected, beta_logits = gather_project(normed_one, w_inner, w_beta)
+        out_full = gather_out(w_out)
+    else:
+        gathered_one = jnp.stack([gather(normed_one[m], TP) for m in batches])
+        projected = [dot(gathered_one[m], w_inner) for m in batches]
+        beta_logits = [
+            jnp.pad(dot(gathered_one[m], w_beta), ((0, 0), (0, 128 - heads))) for m in batches]
+        out_full = gather(w_out, TP)
+    token_heads, saved = [], []
     for m in batches:
         low, *kept = mixer_forward(lengths[m, 0], projected[m], beta_logits[m], taps, gain_heads)
-        mixed.append(low)
         saved.append(kept)
-    token_heads = [
-        lax.all_to_all(low, TP, split_axis=0, concat_axis=1, tiled=True) for low in mixed
-    ]
-    hidden = [rows_in[m] + dot(token_heads[m], out_full) for m in batches]
-    two = [root_scale(rows, gain_two) for rows in hidden]
+        token_heads.append(lax.all_to_all(low, TP, split_axis=0, concat_axis=1, tiled=True))
+    token_heads = jnp.concatenate(token_heads)
+    hidden = rows_in + dot(token_heads, out_full).reshape(rows_in.shape)
+    normed_two, scale_two = root_scale(hidden, gain_two)
     feed_forward = feed_forward_plane if planar else feed_forward_groups
-    ffn_out, normed_grads, (gate_share, up_share, down_share) = feed_forward(
-        [two[m][0].astype(bf16) for m in batches], cotangent, w_gate, w_up, w_down)
-    result_rows, hidden_grads, attended_low, mixed_grads = [], [], [], []
-    gain_two_sum = 0.0
+    ffn_out, normed_grad, (gate_share, up_share, down_share) = feed_forward(
+        normed_two.astype(bf16), cotangent, w_gate, w_up, w_down)
+    result_rows = hidden + ffn_out
+    norm_grad, gain_two_sum = norm_backward(hidden, scale_two, gain_two, normed_grad)
+    hidden_grad = cotangent.astype(f32) + norm_grad
+    attended_low = hidden_grad.astype(bf16)
+    mixed_grads = []
     for m in batches:
-        result_rows.append(hidden[m] + ffn_out[m])
-        norm_grad, gain_part = norm_backward(hidden[m], two[m][1], gain_two, normed_grads[m])
-        gain_two_sum = gain_two_sum + gain_part
-        hidden_grad = cotangent[m].astype(f32) + norm_grad
-        low = hidden_grad.astype(bf16)
-        token_grad = dot_nt(low, out_full).astype(bf16)
+        token_grad = dot_nt(attended_low[m], out_full).astype(bf16)
+        token_grad = token_grad.reshape(-1, devices, local_width).swapaxes(0, 1)
         mixed_grads.append(
-            lax.all_to_all(token_grad, TP, split_axis=1, concat_axis=0, tiled=True)
-        )
-        hidden_grads.append(hidden_grad)
-        attended_low.append(low)
-    out_grad = lax.psum_scatter(
-        dot_tn(jnp.concatenate(token_heads), jnp.concatenate(attended_low)).astype(bf16),
-        TP,
-        scatter_dimension=0,
-        tiled=True,
-    )
-    input_grads, projected_low, beta_low = [], [], []
-    taps_sum, heads_sum, gain_one_sum = 0.0, 0.0, 0.0
+            lax.all_to_all(token_grad, TP, split_axis=0, concat_axis=0, tiled=True).reshape(
+                -1, local_width))
+    out_grad = dot_tn(token_heads, attended_low.reshape(token_heads.shape[0], -1)).astype(bf16)
+    projected_low, beta_low = [], []
+    taps_sum, heads_sum = 0.0, 0.0
     for m in batches:
         projected_grad, beta_grad, taps_part, heads_part = mixer_backward(
             lengths[m, 0], projected[m], beta_logits[m], taps, gain_heads, mixed_grads[m], saved[m]
         )
-        normed_grad = scatter_sum(dot_nt(projected_grad, w_inner) + dot_nt(beta_grad, w_beta), TP)
-        norm_grad, gain_part = norm_backward(rows_in[m], one[m][1], gain_one, normed_grad)
-        input_grads.append(hidden_grads[m] + norm_grad)
-        gain_one_sum = gain_one_sum + gain_part
         taps_sum = taps_sum + taps_part
         heads_sum = heads_sum + heads_part
         projected_low.append(projected_grad)
         beta_low.append(beta_grad)
-    one_all = jnp.concatenate(gathered_one)
-    inner_sum = dot_tn(one_all, jnp.concatenate(projected_low))
-    beta_sum = dot_tn(one_all, jnp.concatenate(beta_low))
+    projected_low = jnp.stack(projected_low)
+    beta_low = jnp.stack(beta_low)
+    tokens = gathered_one.reshape(-1, gathered_one.shape[2])
+    inner_sum = dot_tn(tokens, projected_low.reshape(-1, 4 * local_width))
+    beta_sum = dot_tn(tokens, beta_low.reshape(-1, 128)[:, :heads])
+    gain_one_sum = (
+        jnp.sum(inner_sum * w_inner.astype(f32), axis=1)
+        + jnp.sum(beta_sum * w_beta.astype(f32), axis=1)
+    ) / gain_one
     gain_totals = lax.psum_scatter(
         jnp.stack([gain_one_sum, gain_two_sum]), DP + TP, scatter_dimension=1, tiled=True)
-    inner_total, beta_total, conv_total, heads_total, out_total = (
-        lax.psum(part.astype(bf16), DP).astype(f32)
-        for part in (inner_sum, beta_sum, taps_sum, heads_sum, out_grad)
-    )
+    small = jnp.concatenate([part.reshape(-1) for part in (beta_sum, taps_sum, heads_sum)])
+    if planar:
+        inner_total = sum_pairs(inner_sum)
+        small = small + exchange(small, "core")
+        small = small + exchange(small, "x")
+        out_total = scatter_out(out_grad)
+        input_norm = scatter_rows(projected_low, beta_low, w_inner, w_beta)
+    else:
+        inner_total = [lax.psum(inner_sum.astype(bf16), DP)]
+        small = lax.psum(small, DP)
+        out_grad = lax.psum_scatter(out_grad, TP, scatter_dimension=0, tiled=True)
+        out_total = lax.psum(out_grad, DP).astype(f32)
+        input_norm = jnp.stack([
+            scatter_sum(
+                dot_nt(projected_low[m], w_inner) + dot_nt(beta_low[m, :, :heads], w_beta), TP)
+            for m in batches])
+    norm_grad, _ = norm_backward(rows_in, scale_one, gain_one, input_norm)
+    beta_total, conv_total, heads_total = (
+        piece.reshape(shape) for piece, shape in zip(
+            jnp.split(small, (beta_sum.size, beta_sum.size + taps_sum.size)),
+            (beta_sum.shape, conv_weight.shape, head_gain.shape)))
+    columns = [
+        jnp.concatenate([part[:, n * local_width : (n + 1) * local_width] for part in inner_total])
+        .astype(f32) for n in range(4)]
     return (
-        jnp.stack(result_rows),
-        jnp.stack(input_grads),
+        result_rows,
+        hidden_grad + norm_grad,
         gain_totals[0],
         gain_totals[1],
-        inner_total[:, :local_width],
-        inner_total[:, local_width : 2 * local_width],
-        inner_total[:, 2 * local_width : 3 * local_width],
-        inner_total[:, 3 * local_width :],
+        *columns,
         beta_total,
-        conv_total.reshape(conv_weight.shape),
+        conv_total,
         heads_total,
         out_total,
         gate_share,

time: 1430 us -> 1160 us (0.81)
  waiting for transfers between devices: 856 us -> 280 us
  Pallas kernels: 283 us -> 628 us
  matrix products: 88.9 us -> 32.3 us
  blocking collectives: 73.5 us -> 19.6 us
  other arithmetic: 38.4 us -> 73.4 us
  local copies, waits for them, and re-layouts: 54.2 us -> 72.2 us
  starting transfers between devices: 20.2 us -> 37.2 us
    pallas_call x0 -> x2, Pallas kernels: none -> 345 us  [the longest x1 207 us: gather_project(): pl.pallas_call(gather_kernel, out_shape=(jax.ShapeDtypeStruct((batches, s...]
    all_gather x4 -> x2, waiting for transfers between devices: 205 us -> 0.01 us  [gather(): return lax.all_gather(x, axis_name, axis=axis, tiled=True)]
    reduce_scatter x3 -> x1, waiting for transfers between devices: 197 us -> 0.01 us  [scatter_out(): own = lax.psum_scatter(grad, TP, scatter_dimension=0, tiled=True)[0]]
    unnamed x11 -> x6, waiting for transfers between devices: 125 us -> 0.2 us
    psum x1 -> x0, waiting for transfers between devices: 94.9 us -> none  [per_device(): lax.psum(part.astype(bf16), DP).astype(f32)]
    ppermute x9 -> x22, waiting for transfers between devices: 84.7 us -> 143 us  [exchange(): return lax.ppermute(x, axis_name, [(i, i ^ distance) for i in range(size)])]
    all_to_all x2 -> x0, blocking collectives: 50.6 us -> none  [per_device(): lax.all_to_all(token_grad, TP, split_axis=1, concat_axis=0, tiled=True)]
    reduce_scatter x1, waiting for transfers between devices: 150 us -> 114 us  [plane_weight_grads(): lax.psum_scatter(grads.reshape(lines * kinds * quarter, model), 'z', scat...]
  transfers between devices with their start and end apart: 21 -> 31, of which waited for: 11 -> 11; matrix products, arithmetic and copies ran while one was open for 10% -> 12% of each run, Pallas kernels for 8% -> 44%
where the time goes in v3:
time: 1160 us
  Pallas kernels  628 us (54%)
  waiting for transfers between devices  280 us (24%)
  other arithmetic  73.4 us (6%)
  local copies, waits for them, and re-layouts  72.2 us (6%)
  starting transfers between devices  37.2 us (3%)
  matrix products  32.3 us (3%)
  blocking collectives  19.6 us (2%)
  between operations  15.2 us (1%)
    pallas_call x1, Pallas kernels, gather_project(): pl.pallas_call(gather_kernel, out_shape=(jax.ShapeDtypeStruct((batches, s...  207 us
    ppermute x22, waiting for transfers between devices, exchange(): return lax.ppermute(x, axis_name, [(i, i ^ distance) for i in range(size)])  143 us
    pallas_call x1, Pallas kernels, scatter_rows(): pl.pallas_call(scatter_kernel, out_shape=jax.ShapeDtypeStruct((batches, r...  138 us
    pallas_call x1, Pallas kernels, ffn_plane(): pl.pallas_call(ffn_kernel, out_shape=(jax.ShapeDtypeStruct((rows, model),...  124 us
    reduce_scatter x1, waiting for transfers between devices, plane_weight_grads(): lax.psum_scatter(grads.reshape(lines * kinds * quarter, model), 'z', scat...  114 us
    pallas_call x2, Pallas kernels, mixer_backward(): pl.pallas_call(partial(mixer_backward_kernel, exact), out_shape=(jax.Shap...  90 us
    pallas_call x2, Pallas kernels, mixer_forward(): pl.pallas_call(partial(mixer_forward_kernel, exact, group), out_shape=(ja...  68.3 us
    unnamed x186, local copies, waits for them, and re-layouts  28.2 us
  transfers between devices with their start and end apart: 31, of which 11 were waited for; matrix products, arithmetic and copies ran while one was open for 12% of the time, Pallas kernels for 44%

profile of v3, /device:TPU:0, one launch (start us, length us, event | category | flops | bytes accessed | tf_op | source)
XLA Modules:
  0.0 1157.4 jit_solution(17863167738608873530)
XLA Ops:
  9.2 3.0 collective-permute-start.3
  19.0 17.4 %collective-permute-done.3 = bf16[1,256,2048]{2,1,0:T(8,128)(2,1)S(1)} collective-permute-done((bf16[1,256,2048]{2,1,0:T(8,128)(2,1)}, bf16[1,256,2048]{2,1,0:T(8,128)(2,1)S(1)}, u32[]{:S(2)}, u32[]{:S(2)}) %collective-permute-start.3) | collective-permute-done | bytes 1048608 | tf_op jit(solution)/shard_map/ppermute | solution.py:1051
  40.1 19.6 %all_gather.9 = bf16[2,2048]{1,0:T(2,128)(2,1)S(1)} all-gather(bf16[2,512]{1,0:T(2,128)(2,1)S(1)} %pad_maximum_fusion.17), channel_id=1, replica_groups=mesh['x'=2,'core'=2,'z'=4,'y'=2] {'x','core'}, dimensions={1}, use_global_device_ids=true | all-gather | bytes 10240 | tf_op jit(solution)/shard_map/all_gather | solution.py:1028
  67.7 28.0 %collective-permute-done.4 = bf16[2,256,2048]{2,1,0:T(8,128)(2,1)} collective-permute-done((bf16[2,256,2048]{2,1,0:T(8,128)(2,1)}, bf16[2,256,2048]{2,1,0:T(8,128)(2,1)}, u32[]{:S(2)}, u32[]{:S(2)}) %collective-permute-start.4) | collective-permute-done | bytes 2097184 | tf_op jit(solution)/shard_map/ppermute | solution.py:1051
  95.7 3.6 pad_maximum_fusion.3
  100.7 2.2 copy-done.5
  103.0 206.8 %gather_project.1 = (bf16[2,8,128,2048]{3,2,1,0:T(8,128)(2,1)}, f32[2,8,128,1024]{3,2,1,0:T(8,128)}, f32[2,8,128,128]{3,2,1,0:T(8,128)S(1)}) custom-call(bf16[2,128,2048]{2,1,0:T(8,128)(2,1)S(1)} %fusion.5.x_ref, bf16[2048,1024]{1,0:T(8,128)(2,1)S(1)} %copy-done.5, bf16[2048,128]{1,0:T(8,128)(2,1)S(1)} %pad.5.wb_ref), custom_call_target="tpu_custom_call" | custom-call | flops 70000001024 | bytes 40000000 | tf_op jit(solution)/shard_map/gather_project/pallas_call | solution.py:837
  310.0 8.7 fusion.17
  318.7 34.2 %mixer_forward.2 = (bf16[1024,256]{1,0:T(8,128)(2,1)S(1)}, f32[1024,256]{1,0:T(8,128)S(1)}, f32[1024,256]{1,0:T(8,128)S(1)}, f32[1024,256]{1,0:T(8,128)S(1)}, f3...) custom-call(s32[3]{0:T(128)S(1)} %get-tuple-element.161.lengths_ref, f32[1024,1024]{1,0:T(8,128)} %bitcast.224, ...), custom_call_target="tpu_custom_call" | custom-call | flops 10000000000 | bytes 10000000 | tf_op jit(solution)/shard_map/mixer_forward/pallas_call | solution.py:333
  358.0 3.5 all-to-all-start
  362.1 34.1 %mixer_forward.3 = (bf16[1024,256]{1,0:T(8,128)(2,1)S(1)}, f32[1024,256]{1,0:T(8,128)S(1)}, f32[1024,256]{1,0:T(8,128)S(1)}, f32[1024,256]{1,0:T(8,128)S(1)}, f3...) custom-call(s32[3]{0:T(128)S(1)} %get-tuple-element.162.lengths_ref, f32[1024,1024]{1,0:T(8,128)} %bitcast.222, ...), custom_call_target="tpu_custom_call" | custom-call | flops 10000000000 | bytes 10000000 | tf_op jit(solution)/shard_map/mixer_forward/pallas_call | solution.py:333
  401.0 6.2 all-to-all-start.1
  407.2 14.7 %all-to-all-done.1 = bf16[8,128,256]{1,2,0:T(8,128)(2,1)S(1)} async-done(((bf16[8,128,256]{1,2,0:T(8,128)(2,1)}), bf16[8,128,256]{1,2,0:T(8,128)(2,1)S(1)}, u32[]{:S(2)}, u32[]{:S(2)}) %all-to-all-start.1) | async-done | bytes 524320 | tf_op jit(solution)/shard_map/all_to_all | solution.py:1223
  421.9 2.4 pad_maximum_fusion.11
  424.2 2.3 copy.53
  426.5 6.7 pad_maximum_fusion.2.c_ref
  433.2 3.8 pad_maximum_fusion
  440.3 2.6 multiply_reduce_fusion.3
  445.7 124.0 %ffn_plane.1 = (f32[256,2048]{1,0:T(8,128)}, f32[256,2048]{1,0:T(8,128)}, bf16[4,3,176,2048]{3,2,1,0:T(8,128)(2,1)}) custom-call(bf16[256,2048]{1,0:T(8,128)(2,1)} %bitcast.241, bf16[8,256,2048]{2,1,0:T(8,128)(2,1)} %pad_maximum_fusion.2.c_ref, bf16[4,3,176,2048]{3,2,1,0:T(8,128)(2,1)} %bitcast.273), custom_call_target="tpu_custom_call" | custom-call | flops 80000000000 | bytes 40000000 | tf_op jit(solution)/shard_map/ffn_plane/pallas_call | solution.py:639
  569.8 3.5 multiply_reduce_fusion.1
  575.3 2.3 convolution_convert_fusion
  577.7 3.1 dynamic-slice_bitcast_fusion
  584.1 2.9 convolution_convert_fusion.2
  587.9 3.5 all-to-all-start.2
  591.4 6.3 convolution_convert_fusion.1
  598.5 7.7 all-to-all-done.2
  606.2 3.6 all-to-all-start.3
  609.9 44.9 %mixer_backward.2 = (bf16[1024,1024]{1,0:T(8,128)(2,1)}, bf16[1024,128]{1,0:T(8,128)(2,1)}, f32[12,256]{1,0:T(8,128)}, f32[2,128]{1,0:T(2,128)}) custom-call(s32[3]{0:T(128)} %copy-done.10, f32[1024,1024]{1,0:T(8,128)} %bitcast.225, f32[1024,128]{1,0:T(8,128)} %bitcast.188, f32[12,256]{1,0:T(8,128)} %copy-done.8, f32[2,128]{1,0:T(2,128)} %copy-done.11, ...), custom_call_target="tpu_custom_call" | custom-call | flops 10000000000 | bytes 10000000 | tf_op jit(solution)/shard_map/mixer_backward/pallas_call | solution.py:356
  655.6 45.1 %mixer_backward.3 = (bf16[1024,1024]{1,0:T(8,128)(2,1)}, bf16[1024,128]{1,0:T(8,128)(2,1)}, f32[12,256]{1,0:T(8,128)}, f32[2,128]{1,0:T(2,128)}) custom-call(s32[3]{0:T(128)} %copy-done.9, f32[1024,1024]{1,0:T(8,128)} %bitcast.223, f32[1024,128]{1,0:T(8,128)} %bitcast.186, f32[12,256]{1,0:T(8,128)} %copy-done.8, f32[2,128]{1,0:T(2,128)} %copy-done.11, ...), custom_call_target="tpu_custom_call" | custom-call | flops 10000000000 | bytes 10000000 | tf_op jit(solution)/shard_map/mixer_backward/pallas_call | solution.py:356
  701.8 4.2 pad_maximum_fusion.5
  706.0 4.8 multiply_reduce_fusion.4
  710.8 4.2 fusion
  719.5 13.5 %multiply_reduce_fusion = (f32[2048]{0:T(1024)S(1)}, f32[2048,1024]{1,0:T(8,128)}) fusion(bf16[2048,1024]{1,0:T(8,128)(2,1)S(1)} %copy-done.6, bf16[2048,2048]{1,0:T(8,128)(2,1)S(1)} %bitcast.206, bf16[2048,1024]{1,0:T(8,128)(2,1)} %bitcast.220), kind=kOutput, calls=%fused_computation.5 | convolution fusion | flops 8596224000 | bytes 25174016 | tf_op jit(solution)/shard_map/tm,tn->mn/dot_general | solution.py:1046
  734.4 29.7 %collective-permute-done.15 = bf16[8,64,2048]{2,1,0:T(8,128)(2,1)} collective-permute-done((bf16[8,64,2048]{2,1,0:T(8,128)(2,1)}, bf16[8,64,2048]{2,1,0:T(8,128)(2,1)}, u32[]{:S(2)}, u32[]{:S(2)}) %collective-permute-start.15) | collective-permute-done | bytes 2097184 | tf_op jit(solution)/shard_map/ppermute | solution.py:1051
  764.1 4.5 fusion.1
  769.2 2.5 fusion.12
  771.8 4.1 collective-permute-done.9
  776.0 5.1 fusion.2
  789.0 40.1 %collective-permute-done.10 = bf16[1024,1024]{1,0:T(8,128)(2,1)} collective-permute-done((bf16[1024,1024]{1,0:T(8,128)(2,1)}, bf16[1024,1024]{1,0:T(8,128)(2,1)}, u32[]{:S(2)}, u32[]{:S(2)}) %collective-permute-start.10) | collective-permute-done | bytes 2097184 | tf_op jit(solution)/shard_map/ppermute | solution.py:1051
  829.2 4.0 add_convert_fusion
  833.3 138.4 %scatter_rows.1 = f32[2,128,2048]{2,1,0:T(8,128)S(1)} custom-call(bf16[2,8,128,1024]{3,2,1,0:T(8,128)(2,1)S(1)} %pad_maximum_fusion.4.g_ref, bf16[2,8,128,128]{3,2,1,0:T(8,128)(2,1)S(1)} %pad_maximum_fusion.13.gb_ref, bf16[2048,1024]{1,0:T(8,128)(2,1)S(1)} %copy-done.7, bf16[2048,128]{1,0:T(8,128)(2,1)S(1)} %pad.5.wb_ref), custom_call_target="tpu_custom_call" | custom-call | flops 70000001024 | bytes 40000000 | tf_op jit(solution)/shard_map/scatter_rows/pallas_call | solution.py:989
  973.6 3.4 fusion.9
  994.0 3.4 collective-permute-done.17
  997.5 114.5 %reduce-scatter.8.cloned.1.call-done = bf16[528,2048]{1,0:T(8,128)(2,1)} async-done(((bf16[2112,2048]{1,0:T(8,128)(2,1)}), bf16[528,2048]{1,0:T(8,128)(2,1)}) %reduce-scatter.8.cloned.1.call-update) | async-done | bytes 2162704 | tf_op jit(solution)/shard_map/reduce_scatter | solution.py:1078
  1111.9 4.7 reshape.263
  1116.6 4.5 constant_dynamic-slice_fusion.7
  1127.4 9.2 collective-permute-done.20
  1136.7 10.8 collective-permute-done.21
  (306 shorter events, 89.8 us)
Async XLA Ops:
  7.2 92.1 %all-gather.3.cloned.1.call-start = ((), (), s32[]{:S(2)}) async-start(), calls=%async_computation.7 | async-start | bytes 2359296 | tf_op jit(solution)/shard_map/all_gather | solution.py:1028
  9.2 436.6 %all-gather.5.cloned.1.call-start = ((), (), s32[]{:S(2)}) async-start(), calls=%async_computation.8 | async-start | bytes 10813440 | tf_op jit(solution)/shard_map/all_gather | solution.py:1028
  9.2 27.2 %collective-permute-start.3 = (bf16[1,256,2048]{2,1,0:T(8,128)(2,1)}, bf16[1,256,2048]{2,1,0:T(8,128)(2,1)S(1)}, u32[]{:S(2)}, u32[]{:S(2)}) collective-permute-start(bf16[1,256,2048]{2,1,0:T(8,128)(2,1)} %bitcast.199), channel_id=1, source_target_pairs={{0,16},{16,0},{1,17},{17,1},{2,18},{18,2},{3,19},{19,3},{4,20},{20... | collective-permute-start | bytes 3145736 | tf_op jit(solution)/shard_map/ppermute | solution.py:1051
  15.4 48.5 %collective-permute-start.6 = (bf16[3,176,512]{2,1,0:T(8,128)(2,1)}, bf16[3,176,512]{2,1,0:T(8,128)(2,1)}, u32[]{:S(2)}, u32[]{:S(2)}) collective-permute-start(bf16[3,176,512]{2,1,0:T(8,128)(2,1)} %get-tuple-element.140), channel_id=1, source_target_pairs={{0,8},{8,0},{16,24},{24,16},{1,9},{9,1},{17,25},{25,17},{2,10},{10... | collective-permute-start | bytes 1622024 | tf_op jit(solution)/shard_map/ppermute | solution.py:1051
  15.4 48.5 %collective-permute-start.7 = (bf16[3,176,512]{2,1,0:T(8,128)(2,1)}, bf16[3,176,512]{2,1,0:T(8,128)(2,1)}, u32[]{:S(2)}, u32[]{:S(2)}) collective-permute-start(bf16[3,176,512]{2,1,0:T(8,128)(2,1)} %get-tuple-element.139), channel_id=1, source_target_pairs={{0,16},{8,24},{16,0},{24,8},{1,17},{9,25},{17,1},{25,9},{2,18},{10... | collective-permute-start | bytes 1622024 | tf_op jit(solution)/shard_map/ppermute | solution.py:1051
  15.5 48.5 %collective-permute-start.8 = (bf16[3,176,512]{2,1,0:T(8,128)(2,1)}, bf16[3,176,512]{2,1,0:T(8,128)(2,1)}, u32[]{:S(2)}, u32[]{:S(2)}) collective-permute-start(bf16[3,176,512]{2,1,0:T(8,128)(2,1)} %get-tuple-element.138), channel_id=1, source_target_pairs={{0,24},{8,16},{16,8},{24,0},{1,25},{9,17},{17,9},{25,1},{2,26},{10... | collective-permute-start | bytes 1622024 | tf_op jit(solution)/shard_map/ppermute | solution.py:1051
  38.0 57.6 %collective-permute-start.4 = (bf16[2,256,2048]{2,1,0:T(8,128)(2,1)}, bf16[2,256,2048]{2,1,0:T(8,128)(2,1)}, u32[]{:S(2)}, u32[]{:S(2)}) collective-permute-start(bf16[2,256,2048]{2,1,0:T(8,128)(2,1)} %pad_maximum_fusion.10), channel_id=1, source_target_pairs={{0,1},{1,0},{2,3},{3,2},{4,5},{5,4},{6,7},{7,6},{8,9},{9,8},{10,11... | collective-permute-start | bytes 6291464 | tf_op jit(solution)/shard_map/ppermute | solution.py:1051
  61.9 511.4 %copy-start.58 = (f32[1,2048]{1,0:T(1,128)}, f32[1,2048]{1,0:T(1,128)S(1)}, u32[]{:S(2)}) copy-start(f32[1,2048]{1,0:T(1,128)S(1)} %get-tuple-element.159) | copy-start | bytes 24580
  95.7 214.1 %copy-start.74 = (bf16[3,4,256]{2,1,0:T(4,128)(2,1)S(1)}, bf16[3,4,256]{2,1,0:T(4,128)(2,1)}, u32[]{:S(2)}) copy-start(bf16[3,4,256]{2,1,0:T(4,128)(2,1)} %param.25) | copy-start | bytes 18436
  95.7 214.2 %copy-start.80 = (bf16[2,128]{1,0:T(2,128)(2,1)S(1)}, bf16[2,128]{1,0:T(2,128)(2,1)}, u32[]{:S(2)}) copy-start(bf16[2,128]{1,0:T(2,128)(2,1)} %param.26) | copy-start | bytes 1540
  95.7 214.2 %copy-start.79 = (s32[2,1,3]{2,1,0:T(1,128)S(1)}, s32[2,1,3]{2,1,0:T(1,128)}, u32[]{:S(2)}) copy-start(s32[2,1,3]{2,1,0:T(1,128)} %param.17) | copy-start | bytes 76
  99.3 327.2 %collective-permute-start.5 = (bf16[4,256,2048]{2,1,0:T(8,128)(2,1)}, bf16[4,256,2048]{2,1,0:T(8,128)(2,1)}, u32[]{:S(2)}, u32[]{:S(2)}) collective-permute-start(bf16[4,256,2048]{2,1,0:T(8,128)(2,1)} %pad_maximum_fusion.3), channel_id=1, source_target_pairs={{0,8},{8,0},{1,9},{9,1},{2,10},{10,2},{3,11},{11,3},{4,12},{12,4},... | collective-permute-start | bytes 12582920 | tf_op jit(solution)/shard_map/ppermute | solution.py:1051
  99.3 262.3 %collective-permute-start.1 = (bf16[8,64,2048]{2,1,0:T(8,128)(2,1)}, bf16[8,64,2048]{2,1,0:T(8,128)(2,1)}, u32[]{:S(2)}, u32[]{:S(2)}) collective-permute-start(bf16[8,64,2048]{2,1,0:T(8,128)(2,1)} %all-gather.3.cloned.1.call-done), channel_id=1, source_target_pairs={{0,16},{16,0},{1,17},{17,1},{2,18},{18,2},{3,19},{19,3},{4,20},{20... | collective-permute-start | bytes 6291464 | tf_op jit(solution)/shard_map/ppermute | solution.py:1051
  309.9 52.2 %copy-start.8 = (f32[12,256]{1,0:T(8,128)}, f32[12,256]{1,0:T(8,128)S(1)}, u32[]{:S(2)}) copy-start(f32[12,256]{1,0:T(8,128)S(1)} %reshape.269.tap_ref) | copy-start | bytes 36868
  309.9 52.2 %copy-start.11 = (f32[2,128]{1,0:T(2,128)}, f32[2,128]{1,0:T(2,128)S(1)}, u32[]{:S(2)}) copy-start(f32[2,128]{1,0:T(2,128)S(1)} %convert_element_type.103.gain_ref) | copy-start | bytes 3076
  309.9 52.1 %copy-start.9 = (s32[3]{0:T(128)}, s32[3]{0:T(128)S(1)}, u32[]{:S(2)}) copy-start(s32[3]{0:T(128)S(1)} %get-tuple-element.162.lengths_ref) | copy-start | bytes 40
  310.0 52.0 %copy-start.2 = (f32[1,8,128,128]{3,2,1,0:T(8,128)}, f32[1,8,128,128]{3,2,1,0:T(8,128)S(1)}, u32[]{:S(2)}) copy-start(f32[1,8,128,128]{3,2,1,0:T(8,128)S(1)} %get-tuple-element.156) | copy-start | bytes 1572868
  358.0 43.1 %all-to-all-start = ((bf16[8,128,256]{1,2,0:T(8,128)(2,1)}), bf16[8,128,256]{1,2,0:T(8,128)(2,1)S(1)}, u32[]{:S(2)}, u32[]{:S(2)}) async-start(bf16[8,128,256]{1,2,0:T(8,128)(2,1)} %copy.51), calls=%async_computation | async-start | bytes 1048576 | tf_op jit(solution)/shard_map/all_to_all | solution.py:1223
  361.5 71.8 %collective-permute-start = (bf16[8,64,2048]{2,1,0:T(8,128)(2,1)}, bf16[8,64,2048]{2,1,0:T(8,128)(2,1)}, u32[]{:S(2)}, u32[]{:S(2)}) collective-permute-start(bf16[8,64,2048]{2,1,0:T(8,128)(2,1)} %all-gather.3.cloned.1.call-done), channel_id=1, source_target_pairs={{0,8},{8,0},{1,9},{9,1},{2,10},{10,2},{3,11},{11,3},{4,12},{12,4},... | collective-permute-start | bytes 6291464 | tf_op jit(solution)/shard_map/ppermute | solution.py:1051
  361.5 71.7 %collective-permute-start.2 = (bf16[8,64,2048]{2,1,0:T(8,128)(2,1)}, bf16[8,64,2048]{2,1,0:T(8,128)(2,1)}, u32[]{:S(2)}, u32[]{:S(2)}) collective-permute-start(bf16[8,64,2048]{2,1,0:T(8,128)(2,1)} %collective-permute-done.1), channel_id=1, source_target_pairs={{0,8},{8,0},{1,9},{9,1},{2,10},{10,2},{3,11},{11,3},{4,12},{12,4},... | collective-permute-start | bytes 6291464 | tf_op jit(solution)/shard_map/ppermute | solution.py:1051
  401.0 20.8 %all-to-all-start.1 = ((bf16[8,128,256]{1,2,0:T(8,128)(2,1)}), bf16[8,128,256]{1,2,0:T(8,128)(2,1)S(1)}, u32[]{:S(2)}, u32[]{:S(2)}) async-start(bf16[8,128,256]{1,2,0:T(8,128)(2,1)} %copy.52), calls=%async_computation.1 | async-start | bytes 1048576 | tf_op jit(solution)/shard_map/all_to_all | solution.py:1223
  443.2 130.2 %copy-start.66 = (f32[2,128]{1,0:T(2,128)}, f32[2,128]{1,0:T(2,128)S(1)}, u32[]{:S(2)}) copy-start(f32[2,128]{1,0:T(2,128)S(1)} %add_rsqrt_fusion) | copy-start | bytes 3076
  582.3 128.4 %collective-permute-start.14 = (bf16[8,2,64,2048]{3,2,1,0:T(8,128)(2,1)}, bf16[8,2,64,2048]{3,2,1,0:T(8,128)(2,1)}, u32[]{:S(2)}, u32[]{:S(2)}) collective-permute-start(bf16[8,2,64,2048]{3,2,1,0:T(8,128)(2,1)} %dynamic-slice_bitcast_fusion), channel_id=1, source_target_pairs={{0,8},{8,0},{1,9},{9,1},{2,10},{10,2},{3,11},{11,3},{4,12},{12,4},... | collective-permute-start | bytes 12582920 | tf_op jit(solution)/shard_map/ppermute | solution.py:1051
  587.9 18.4 %all-to-all-start.2 = ((bf16[8,128,256]{2,1,0:T(8,128)(2,1)}), bf16[8,128,256]{2,1,0:T(8,128)(2,1)S(1)}, u32[]{:S(2)}, u32[]{:S(2)}) async-start(bf16[8,128,256]{2,1,0:T(8,128)(2,1)} %bitcast.181), calls=%async_computation.2 | async-start | bytes 1048576 | tf_op jit(solution)/shard_map/all_to_all | solution.py:1239
  606.2 48.6 %all-to-all-start.3 = ((bf16[8,128,256]{2,1,0:T(8,128)(2,1)}), bf16[8,128,256]{2,1,0:T(8,128)(2,1)S(1)}, u32[]{:S(2)}, u32[]{:S(2)}) async-start(bf16[8,128,256]{2,1,0:T(8,128)(2,1)} %bitcast.179), calls=%async_computation.3 | async-start | bytes 1048576 | tf_op jit(solution)/shard_map/all_to_all | solution.py:1239
  609.8 369.0 %reduce-scatter.10.cloned.1.call-start = ((), (), s32[]{:S(2)}) async-start(), calls=%async_computation.11 | async-start | bytes 1081344
  655.6 45.1 %copy-start.52 = (bf16[1024,128]{1,0:T(8,128)(2,1)S(1)}, bf16[1024,128]{1,0:T(8,128)(2,1)}, u32[]{:S(2)}) copy-start(bf16[1024,128]{1,0:T(8,128)(2,1)} %get-tuple-element.59) | copy-start | bytes 786436
  655.6 46.1 %copy-start.37 = (bf16[1024,1024]{1,0:T(8,128)(2,1)S(1)}, bf16[1024,1024]{1,0:T(8,128)(2,1)}, u32[]{:S(2)}) copy-start(bf16[1024,1024]{1,0:T(8,128)(2,1)} %get-tuple-element.52) | copy-start | bytes 6291460
  716.5 47.6 %collective-permute-start.15 = (bf16[8,64,2048]{2,1,0:T(8,128)(2,1)}, bf16[8,64,2048]{2,1,0:T(8,128)(2,1)}, u32[]{:S(2)}, u32[]{:S(2)}) collective-permute-start(bf16[8,64,2048]{2,1,0:T(8,128)(2,1)} %dynamic-slice_bitcast_fusion.1), channel_id=1, source_target_pairs={{0,16},{16,0},{1,17},{17,1},{2,18},{18,2},{3,19},{19,3},{4,20},{20... | collective-permute-start | bytes 6291464 | tf_op jit(solution)/shard_map/ppermute | solution.py:1051
  734.4 256.4 %reduce-scatter.6.cloned.1.call-start = ((), (), s32[]{:S(2)}) async-start(), calls=%async_computation.9 | async-start | bytes 2359296 | tf_op jit(solution)/shard_map/reduce_scatter | solution.py:1134
  768.6 343.3 %reduce-scatter.8.cloned.1.call-start = ((), (), s32[]{:S(2)}) async-start(), calls=%async_computation.10 | async-start | bytes 10813440 | tf_op jit(solution)/shard_map/reduce_scatter | solution.py:1078
  771.7 4.2 collective-permute-start.9
  781.1 48.1 %collective-permute-start.10 = (bf16[1024,1024]{1,0:T(8,128)(2,1)}, bf16[1024,1024]{1,0:T(8,128)(2,1)}, u32[]{:S(2)}, u32[]{:S(2)}) collective-permute-start(bf16[1024,1024]{1,0:T(8,128)(2,1)} %fusion.2), channel_id=1, source_target_pairs={{0,16},{16,0},{1,17},{17,1},{2,18},{18,2},{3,19},{19,3},{4,20},{20... | collective-permute-start | bytes 6291464 | tf_op jit(solution)/shard_map/ppermute | solution.py:1051
  785.8 191.2 %collective-permute-start.12 = (f32[7424]{0:T(1024)S(1)}, f32[7424]{0:T(1024)S(1)}, u32[]{:S(2)}, u32[]{:S(2)}) collective-permute-start(f32[7424]{0:T(1024)S(1)} %pad_maximum_fusion.15), channel_id=1, source_target_pairs={{0,8},{8,0},{1,9},{9,1},{2,10},{10,2},{3,11},{11,3},{4,12},{12,4},... | collective-permute-start | bytes 89096 | tf_op jit(solution)/shard_map/ppermute | solution.py:1051
  786.9 42.3 %copy-start.40 = (bf16[1024,1024]{1,0:T(8,128)(2,1)S(1)}, bf16[1024,1024]{1,0:T(8,128)(2,1)}, u32[]{:S(2)}) copy-start(bf16[1024,1024]{1,0:T(8,128)(2,1)} %copy-done.39) | copy-start | bytes 6291460
  789.0 44.3 %copy-start.7 = (bf16[2048,1024]{1,0:T(8,128)(2,1)S(1)}, bf16[2048,1024]{1,0:T(8,128)(2,1)}, u32[]{:S(2)}) copy-start(bf16[2048,1024]{1,0:T(8,128)(2,1)} %copy-done.4) | copy-start | bytes 12582916
  833.2 138.5 %copy-start.34 = (bf16[2,128,2048]{2,1,0:T(8,128)(2,1)S(1)}, bf16[2,128,2048]{2,1,0:T(8,128)(2,1)}, u32[]{:S(2)}) copy-start(bf16[2,128,2048]{2,1,0:T(8,128)(2,1)} %param.16) | copy-start | bytes 3145732
  833.2 138.5 %copy-start.61 = (f32[1,2048]{1,0:T(1,128)S(1)}, f32[1,2048]{1,0:T(1,128)}, u32[]{:S(2)}) copy-start(f32[1,2048]{1,0:T(1,128)} %copy-done.60) | copy-start | bytes 24580
  833.2 150.9 %collective-permute-start.11 = (bf16[1024,1024]{1,0:T(8,128)(2,1)S(1)}, bf16[1024,1024]{1,0:T(8,128)(2,1)}, u32[]{:S(2)}, u32[]{:S(2)}) collective-permute-start(bf16[1024,1024]{1,0:T(8,128)(2,1)S(1)} %add_convert_fusion), channel_id=1, source_target_pairs={{0,8},{8,0},{1,9},{9,1},{2,10},{10,2},{3,11},{11,3},{4,12},{12,4},... | collective-permute-start | bytes 6291464 | tf_op jit(solution)/shard_map/ppermute | solution.py:1051
  833.3 138.8 %copy-start.26 = (f32[256,2048]{1,0:T(8,128)S(1)}, f32[256,2048]{1,0:T(8,128)}, u32[]{:S(2)}) copy-start(f32[256,2048]{1,0:T(8,128)} %get-tuple-element.46) | copy-start | bytes 6291460
  833.3 138.8 %copy-start.45 = (f32[256,2048]{1,0:T(8,128)S(1)}, f32[256,2048]{1,0:T(8,128)}, u32[]{:S(2)}) copy-start(f32[256,2048]{1,0:T(8,128)} %get-tuple-element.45) | copy-start | bytes 6291460
  977.0 4.0 collective-permute-start.13
  990.8 6.7 collective-permute-start.17
  994.0 129.6 %collective-permute-start.16 = (bf16[64,2048]{1,0:T(8,128)(2,1)S(1)}, bf16[64,2048]{1,0:T(8,128)(2,1)S(1)}, u32[]{:S(2)}, u32[]{:S(2)}) collective-permute-start(bf16[64,2048]{1,0:T(8,128)(2,1)S(1)} %bitcast.258), channel_id=1, source_target_pairs={{0,8},{8,0},{1,9},{9,1},{2,10},{10,2},{3,11},{11,3},{4,12},{12,4},... | collective-permute-start | bytes 786440 | tf_op jit(solution)/shard_map/ppermute | solution.py:1051
  997.4 126.2 %collective-permute-start.18 = (bf16[64,2048]{1,0:T(8,128)(2,1)}, bf16[64,2048]{1,0:T(8,128)(2,1)S(1)}, u32[]{:S(2)}, u32[]{:S(2)}) collective-permute-start(bf16[64,2048]{1,0:T(8,128)(2,1)} %collective-permute-done.17), channel_id=1, source_target_pairs={{0,8},{8,0},{1,9},{9,1},{2,10},{10,2},{3,11},{11,3},{4,12},{12,4},... | collective-permute-start | bytes 786440 | tf_op jit(solution)/shard_map/ppermute | solution.py:1051
  1121.3 6.1 collective-permute-start.19
  1121.5 15.1 %collective-permute-start.20 = (bf16[528,512]{1,0:T(8,128)(2,1)S(1)}, bf16[528,512]{1,0:T(8,128)(2,1)S(1)}, u32[]{:S(2)}, u32[]{:S(2)}) collective-permute-start(bf16[528,512]{1,0:T(8,128)(2,1)S(1)} %bitcast.253), channel_id=1, source_target_pairs={{0,16},{8,24},{16,0},{24,8},{1,17},{9,25},{17,1},{25,9},{2,18},{10... | collective-permute-start | bytes 1622024 | tf_op jit(solution)/shard_map/ppermute | solution.py:1051
  1123.2 24.3 %collective-permute-start.21 = (bf16[528,512]{1,0:T(8,128)(2,1)S(1)}, bf16[528,512]{1,0:T(8,128)(2,1)S(1)}, u32[]{:S(2)}, u32[]{:S(2)}) collective-permute-start(bf16[528,512]{1,0:T(8,128)(2,1)S(1)} %bitcast.254), channel_id=1, source_target_pairs={{0,24},{8,16},{16,8},{24,0},{1,25},{9,17},{17,9},{25,1},{2,26},{10... | collective-permute-start | bytes 1622024 | tf_op jit(solution)/shard_map/ppermute | solution.py:1051
  (70 other events, 360.6 us)
Sparse Core Ops, SparseCore 0:
  10.7 63.2 all-gather.2
  75.6 206.4 all-gather.4
  734.5 138.5 reduce-scatter.9
  876.9 82.7 reduce-scatter.5
  962.0 149.8 reduce-scatter.7

commit v4 on v3

--- a/solution.py
+++ b/solution.py
@@ -379,7 +379,7 @@
     return {axis_name: 1 - lax.axis_index(axis_name)}
 
 
-def ffn_kernel(x_ref, c_ref, w_ref, out_ref, ngrad_ref, wgrad_ref,
+def ffn_kernel(x_ref, w_ref, c_refs, out_ref, ngrad_ref, wgrad_ref,
                xs, cs, ws, inner_s, gate_s, up_s, acts_t, part, crecv, drecv, nrecv, stage, ctile,
                ag_send, ag_recv, pair_send, pair_recv, rs_send, rs_recv, c_sem, w_sem, g_sem, t_sem):
     half = xs.shape[1] // 2
@@ -416,9 +416,15 @@
     def slot_of(step):
         return (1 - lax.rem(step, 2)) * 4 + step // 2
 
-    def c_copy(step, slot):
-        return pltpu.make_async_copy(
-            c_ref.at[slot], cs.at[lax.rem(step, 2)], c_sem.at[lax.rem(step, 2)])
+    def c_copy(step, n):
+        buffer = lax.rem(step, 2)
+        return pltpu.make_async_copy(c_refs[n], cs.at[buffer], c_sem.at[buffer])
+
+    def c_start(step):
+        for n in range(8):
+            @pl.when(slot_of(step) == n)
+            def _():
+                c_copy(step, n).start()
 
     c_copy(0, 4).start()
     pl.semaphore_wait(barrier, 3)
@@ -434,7 +440,7 @@
     own_y[1].start()
     own_x[1].start()
     own_y[0].start()
-    own_copy = pltpu.make_async_copy(x_ref, xs.at[0], t_sem.at[0])
+    own_copy = pltpu.make_async_copy(x_ref, xs.at[0], t_sem.at[0, 0])
     own_copy.start()
     own_copy.wait()
     for copy in weight_copies:
@@ -458,7 +464,7 @@
 
         @pl.when(step < 7)
         def _():
-            c_copy(step + 1, slot_of(step + 1)).start()
+            c_start(step + 1)
 
         @pl.when(step == 0)
         def _():
@@ -487,7 +493,7 @@
         def _():
             pair_of[3].wait_recv()
 
-        c_copy(step, slot).wait()
+        c_copy(step, 0).wait()
 
         for start in range(0, hidden, tile_f):
             size = min(tile_f, hidden - start)
@@ -553,8 +559,11 @@
     tiles = model // tile_w
 
     def c_tile(t):
-        return pltpu.make_async_copy(
-            c_ref.at[:, :, pl.ds(pl.multiple_of(t * tile_w, tile_w), tile_w)], ctile.at[lax.rem(t, 2)], t_sem.at[lax.rem(t, 2)])
+        buffer = lax.rem(t, 2)
+        cols = pl.ds(pl.multiple_of(t * tile_w, tile_w), tile_w)
+        return [
+            pltpu.make_async_copy(ref.at[:, cols], ctile.at[buffer, n], t_sem.at[buffer, n])
+            for n, ref in enumerate(c_refs)]
 
     def grad_copy(kind, t, line):
         return pltpu.make_async_copy(
@@ -564,15 +573,18 @@
 
     def weight_grads(kind):
         if kind == 2:
-            c_tile(0).start()
+            for copy in c_tile(0):
+                copy.start()
 
         @pl.loop(0, tiles)
         def _(t):
             if kind == 2:
                 @pl.when(t + 1 < tiles)
                 def _():
-                    c_tile(t + 1).start()
-                c_tile(t).wait()
+                    for copy in c_tile(t + 1):
+                        copy.start()
+                for copy in c_tile(t):
+                    copy.wait()
                 right = ctile[lax.rem(t, 2)].reshape(8 * rows, tile_w)
             else:
                 right = xs[:, :, pl.ds(pl.multiple_of(t * tile_w, tile_w), tile_w)].reshape(8 * rows, tile_w)
@@ -629,7 +641,11 @@
     part_send(3).wait_send()
 
 
-def ffn_plane(x_own, c_all, weights):
+def ffn_call_kernel(x_ref, w_ref, *refs):
+    ffn_kernel(x_ref, w_ref, refs[:8], *refs[8:])
+
+
+def ffn_plane(x_own, weights, c_rows):
     rows, model = x_own.shape
     lines, _, quarter, _ = weights.shape
     hidden = lines * quarter
@@ -637,13 +653,13 @@
     sems = pltpu.SemaphoreType.DMA
     anywhere = pl.BlockSpec(memory_space=pl.ANY)
     return pl.pallas_call(
-        ffn_kernel,
+        ffn_call_kernel,
         out_shape=(
             jax.ShapeDtypeStruct((rows, model), f32),
             jax.ShapeDtypeStruct((rows, model), f32),
             jax.ShapeDtypeStruct(weights.shape, bf16),
         ),
-        in_specs=[anywhere] * 3,
+        in_specs=[anywhere] * 10,
         out_specs=(vmem(), vmem(), anywhere),
         scratch_shapes=[
             pltpu.VMEM((8, rows, model), bf16),
@@ -660,26 +676,16 @@
             pltpu.VMEM((2, hidden, tile_w), bf16),
             pltpu.VMEM((2, 8, rows, tile_w), bf16),
             sems((10,)), sems((10,)), sems((4,)), sems((4,)), sems((12,)), sems((12,)),
-            sems((2,)), sems((lines, 3)), sems((2, lines)), sems((2,)),
+            sems((2,)), sems((lines, 3)), sems((2, lines)), sems((2, 8)),
         ],
         compiler_params=pltpu.CompilerParams(
             collective_id=2, has_side_effects=True, vmem_limit_bytes=62 * 2**20),
         cost_estimate=pl.CostEstimate(flops=8 * 10**10, bytes_accessed=4 * 10**7, transcendentals=10**6),
         name="ffn_plane",
-    )(x_own, c_all, weights)
-
-
-def line_positions(lines):
-    o = lax.axis_index("z")
-    i = lax.axis_index("y")
-
-    def at(z, y):
-        return {"z": z, "y": y}
-
-    return o, i, at
-
-
-def line_barrier(lines):
+    )(x_own, weights, *c_rows)
+
+
+def line_barrier(lines, others):
     o = lax.axis_index("z")
     barrier = pltpu.get_barrier_semaphore()
     mesh_id = pl.DeviceIdType.MESH
@@ -692,9 +698,9 @@
     def _():
         pl.semaphore_signal(barrier, inc=1, device_id={"z": o + 1}, device_id_type=mesh_id)
 
-    pl.semaphore_signal(barrier, inc=1, device_id=other("y"), device_id_type=mesh_id)
-
-    peers = 1 + (o > 0).astype(jnp.int32) + (o < lines - 1).astype(jnp.int32)
+    for target in others:
+        pl.semaphore_signal(barrier, inc=1, device_id=target, device_id_type=mesh_id)
+    peers = len(others) + (o > 0).astype(jnp.int32) + (o < lines - 1).astype(jnp.int32)
     pl.semaphore_wait(barrier, peers)
 
 
@@ -704,70 +710,79 @@
         device_id=target, device_id_type=pl.DeviceIdType.MESH)
 
 
-def gather_kernel(x_ref, w_ref, wb_ref, rows_ref, proj_ref, beta_ref, xs, stage, beta_stage,
-                  right_send, left_send, line_recv, pair_send, pair_recv, row_sem, out_sem, beta_sem):
-    batches = xs.shape[1]
+def gather_kernel(x_ref, o_ref, w_ref, wb_ref, rows_ref, outs_ref, proj_ref, beta_ref,
+                  xs, stage, beta_stage, right_send, left_send, line_recv, pair_send, pair_recv,
+                  own_sem, row_sem, outs_sem, out_sem, beta_sem):
     lines = xs.shape[0] // 2
-    rows = xs.shape[2]
-    model = xs.shape[3]
+    batches, rows, model = x_ref.shape
+    more = o_ref.shape[1]
     o = lax.axis_index("z")
     i = lax.axis_index("y")
-    line_barrier(lines)
+    line_barrier(lines, [other("y")])
 
     def right(z, m):
-        return line_copy(xs.at[z * 2 + i, m], xs.at[z * 2 + i, m], right_send.at[z, m],
-                         line_recv.at[z, m], {"z": o + 1})
+        ref = xs.at[z * 2 + i, m]
+        return line_copy(ref, ref, right_send.at[z, m], line_recv.at[z, m], {"z": o + 1})
 
     def left(z, m):
-        return line_copy(xs.at[z * 2 + i, m], xs.at[z * 2 + i, m], left_send.at[z, m],
-                         line_recv.at[z, m], {"z": o - 1})
+        ref = xs.at[z * 2 + i, m]
+        return line_copy(ref, ref, left_send.at[z, m], line_recv.at[z, m], {"z": o - 1})
 
     def across(z, m):
-        return line_copy(xs.at[z * 2 + i, m], xs.at[z * 2 + i, m], pair_send.at[z, m],
-                         pair_recv.at[z, m], other("y"))
-
-    own = pltpu.make_async_copy(x_ref, xs.at[o * 2 + i], row_sem.at[2 * lines, 0])
-    own.start()
-    own.wait()
-
-    def outs(turn, slot, m):
-        return (
-            pltpu.make_async_copy(stage.at[lax.rem(turn, 2), m], proj_ref.at[m, slot], out_sem.at[lax.rem(turn, 2), m]),
-            pltpu.make_async_copy(beta_stage.at[lax.rem(turn, 2), m], beta_ref.at[m, slot], beta_sem.at[lax.rem(turn, 2), m]),
-        )
+        ref = xs.at[z * 2 + i, m, pl.ds(0, rows)]
+        return line_copy(ref, ref, pair_send.at[z, m], pair_recv.at[z, m], other("y"))
+
+    own = [
+        pltpu.make_async_copy(x_ref, xs.at[o * 2 + i, :, pl.ds(0, rows)], own_sem.at[0]),
+        pltpu.make_async_copy(o_ref, xs.at[o * 2 + i, :, pl.ds(rows, more)], own_sem.at[1]),
+    ]
+    for copy in own:
+        copy.start()
+    for copy in own:
+        copy.wait()
+
+    def outs(turn, slot):
+        buffer = lax.rem(turn, 2)
+        return [
+            copy for m in range(batches) for copy in (
+                pltpu.make_async_copy(stage.at[buffer, m], proj_ref.at[m, slot], out_sem.at[buffer, m]),
+                pltpu.make_async_copy(beta_stage.at[buffer, m], beta_ref.at[m, slot], beta_sem.at[buffer, m]))
+        ]
 
     def keep(slot, m):
-        return pltpu.make_async_copy(xs.at[slot, m], rows_ref.at[m, slot], row_sem.at[slot, m])
+        return pltpu.make_async_copy(xs.at[slot, m, pl.ds(0, rows)], rows_ref.at[m, slot], row_sem.at[slot, m])
+
+    def keep_outs(z):
+        return pltpu.make_async_copy(xs.at[z * 2 + i, :, pl.ds(rows, more)], outs_ref.at[z], outs_sem.at[z])
 
     def project(turn, slot):
         @pl.when(turn >= 2)
         def _():
-            for m in range(batches):
-                for copy in outs(turn, slot, m):
-                    copy.wait()
+            for copy in outs(turn, slot):
+                copy.wait()
         for m in range(batches):
             keep(slot, m).start()
-        x = xs[slot].reshape(batches * rows, model)
+        x = xs[slot, :, :rows].reshape(batches * rows, model)
+        buffer = lax.rem(turn, 2)
         width = w_ref.shape[1]
         tile = min(256, width)
         for start in range(0, width, tile):
             cols = slice(start, start + tile)
-            stage[lax.rem(turn, 2), :, :, cols] = jnp.dot(
+            stage[buffer, :, :, cols] = jnp.dot(
                 x, w_ref[:, cols], preferred_element_type=f32).reshape(batches, rows, tile)
-        beta_stage[lax.rem(turn, 2)] = jnp.dot(
+        beta_stage[buffer] = jnp.dot(
             x, wb_ref[...], preferred_element_type=f32).reshape(batches, rows, 128)
-        for m in range(batches):
-            for copy in outs(turn, slot, m):
-                copy.start()
+        for copy in outs(turn, slot):
+            copy.start()
 
     def in_line(index):
         far = (index + 1) // 2
         side = 1 - 2 * lax.rem(index, 2)
         z = o + side * far
-        return far, side, z, (z >= 0) & (z < lines)
+        return far, z, (z >= 0) & (z < lines)
 
     def first(index, turn):
-        far, side, z, valid = in_line(index)
+        far, z, valid = in_line(index)
 
         @pl.when(valid)
         def _():
@@ -785,6 +800,7 @@
                     left(z, m).start()
 
                 across(z, m).start()
+            keep_outs(z).start()
             project(turn, z * 2 + i)
 
         return turn + valid.astype(jnp.int32)
@@ -792,7 +808,7 @@
     turn = lax.fori_loop(0, 2 * lines - 1, first, jnp.int32(0))
 
     def second(index, turn):
-        far, side, z, valid = in_line(index)
+        far, z, valid = in_line(index)
 
         @pl.when(valid)
         def _():
@@ -803,14 +819,13 @@
         return turn + valid.astype(jnp.int32)
 
     lax.fori_loop(0, 2 * lines - 1, second, turn)
-
     for turn in range(2 * lines - 2, 2 * lines):
-        for m in range(batches):
-            for copy in outs(turn, 0, m):
-                copy.wait()
+        for copy in outs(turn, 0):
+            copy.wait()
 
     @pl.loop(0, lines)
     def _(z):
+        keep_outs(z).wait()
         for m in range(batches):
             @pl.when((o < lines - 1) & (z <= o))
             def _():
@@ -821,54 +836,102 @@
                 left(z, m).wait_send()
 
             across(z, m).wait_send()
-            keep(z * 2, m).wait()
-            keep(z * 2 + 1, m).wait()
-
-
-def gather_project(x, w_inner, w_beta):
+            for y in range(2):
+                keep(z * 2 + y, m).wait()
+
+
+def gather_project(x, w_out_part, w_inner, w_beta):
     batches, rows, model = x.shape
+    more = w_out_part.shape[1]
     lines = lax.axis_size("z")
     width = w_inner.shape[1]
     slots = 2 * lines
-    heads = w_beta.shape[1]
-    w_beta = jnp.pad(w_beta, ((0, 0), (0, 128 - heads)))
     sems = pltpu.SemaphoreType.DMA
     anywhere = pl.BlockSpec(memory_space=pl.ANY)
-    gathered, projected, beta = pl.pallas_call(
+    pair = sems((lines, batches))
+    gathered, outs, projected, beta = pl.pallas_call(
         gather_kernel,
         out_shape=(
             jax.ShapeDtypeStruct((batches, slots, rows, model), bf16),
+            jax.ShapeDtypeStruct((lines, batches, more, model), bf16),
             jax.ShapeDtypeStruct((batches, slots, rows, width), f32),
             jax.ShapeDtypeStruct((batches, slots, rows, 128), f32),
         ),
-        in_specs=[anywhere, vmem(), vmem()],
-        out_specs=(anywhere,) * 3,
+        in_specs=[anywhere] * 2 + [vmem()] * 2,
+        out_specs=(anywhere,) * 4,
         scratch_shapes=[
-            pltpu.VMEM((slots, batches, rows, model), bf16),
+            pltpu.VMEM((slots, batches, rows + more, model), bf16),
             pltpu.VMEM((2, batches, rows, width), f32),
             pltpu.VMEM((2, batches, rows, 128), f32),
-            sems((lines, batches)), sems((lines, batches)), sems((lines, batches)),
-            sems((lines, batches)), sems((lines, batches)),
-            sems((slots + 1, batches)), sems((2, batches)), sems((2, batches)),
+            pair, pair, pair, pair, pair,
+            sems((2,)), sems((slots, batches)), sems((lines,)), sems((2, batches)), sems((2, batches)),
         ],
         compiler_params=pltpu.CompilerParams(
             collective_id=1, has_side_effects=True, vmem_limit_bytes=40 * 2**20),
-        cost_estimate=pl.CostEstimate(flops=7 * 10**10, bytes_accessed=4 * 10**7, transcendentals=0),
+        cost_estimate=pl.CostEstimate(flops=10**11, bytes_accessed=4 * 10**7, transcendentals=0),
         name="gather_project",
-    )(x, w_inner, w_beta)
+    )(x, w_out_part, w_inner, w_beta)
     total = slots * rows
-    return (gathered.reshape(batches, total, model), projected.reshape(batches, total, width),
+    return (gathered.reshape(batches, total, model), outs, projected.reshape(batches, total, width),
             beta.reshape(batches, total, 128))
 
 
-def scatter_kernel(g_ref, gb_ref, w_ref, wb_ref, out_ref, gs, bs, ysend, yrecv, from_left, from_right,
-                   pair_send, pair_recv, right_send, left_send, right_recv, left_recv, g_sem, b_sem):
-    batches, rows, width = gs.shape[1:]
+def scatter_kernel(g_ref, gb_ref, o_ref, inner_ref, w_ref, wb_ref, small_ref, gains_ref,
+                   out_ref, small_out, outs_ref, inner_out,
+                   gs, bs, ysend, yrecv, from_left, from_right, outs_s, inner_s, inner_r, small_s, small_r, gains_r,
+                   pair_send, pair_recv, right_send, left_send, right_recv, left_recv, g_sem,
+                   sum_send, sum_recv, outs_send, outs_recv, gain_send, gain_recv, sum_sem):
+    batches, rows, width = gs.shape
     lines = yrecv.shape[0]
     model = yrecv.shape[3]
+    more = yrecv.shape[2] - rows
     o = lax.axis_index("z")
     i = lax.axis_index("y")
+    core = lax.axis_index("core")
+    me = lax.axis_index("x") * 2 + core
     tile = min(512, model)
+    diagonal = {"x": 1 - lax.axis_index("x"), "core": 1 - core}
+    slots = 2 * lines
+    mine = o * 2 + i
+    peers = []
+    for d in range(1, slots):
+        place = lax.rem(mine + d, slots)
+        peers.append((place, {"z": place // 2, "y": lax.rem(place, 2)}))
+    barrier = pltpu.get_barrier_semaphore()
+    greeted = [other("core"), other("x"), diagonal] + [device for _, device in peers]
+    for device in greeted:
+        pl.semaphore_signal(barrier, inc=1, device_id=device, device_id_type=pl.DeviceIdType.MESH)
+    pl.semaphore_wait(barrier, len(greeted))
+    gain_copies = [
+        line_copy(gains_ref.at[place], gains_r.at[mine], gain_send.at[d], gain_recv.at[d], device)
+        for d, (place, device) in enumerate(peers)
+    ]
+    for copy in gain_copies:
+        copy.start()
+
+    inner_pair = line_copy(inner_ref.at[1 - core], inner_r.at[0], sum_send.at[0], sum_recv.at[0], other("core"))
+    inner_across = line_copy(inner_s, inner_r.at[1], sum_send.at[1], sum_recv.at[1], other("x"))
+    inner_back = line_copy(inner_s, inner_out.at[core], sum_send.at[2], sum_recv.at[2], other("core"))
+    small_pair = line_copy(small_s.at[0], small_r.at[0], sum_send.at[3], sum_recv.at[3], other("core"))
+    small_across = line_copy(small_s.at[1], small_r.at[1], sum_send.at[4], sum_recv.at[4], other("x"))
+    inner_own = pltpu.make_async_copy(inner_ref.at[core], inner_s, sum_sem.at[0])
+    inner_keep = pltpu.make_async_copy(inner_s, inner_out.at[core], sum_sem.at[1])
+    outs_keep = pltpu.make_async_copy(outs_s, outs_ref.at[me], sum_sem.at[2])
+    outs_away = [
+        line_copy(outs_s, outs_ref.at[me], outs_send.at[n], outs_recv.at[n], target)
+        for n, target in enumerate((other("core"), other("x"), diagonal))
+    ]
+    inner_pair.start()
+    inner_own.start()
+
+    def add_into(target, other_ref):
+        height = target.shape[0]
+        step = next(size for size in range(min(128, height), 0, -16) if height % size == 0)
+
+        @pl.loop(0, height // step)
+        def _(n):
+            at = pl.ds(pl.multiple_of(n * step, step), step)
+            target[at, :] = (target[at, :].astype(f32) + other_ref[at, :].astype(f32)).astype(target.dtype)
 
     def target(index):
         far = lines - 1 - index // 2
@@ -876,34 +939,32 @@
         z = o + side * far
         return far, z, (z >= 0) & (z < lines) & ((far > 0) | (side > 0))
 
-    def load(z, y, buffer):
+    def load(z, y):
         slot = z * 2 + y
-        return (pltpu.make_async_copy(g_ref.at[:, slot], gs.at[buffer], g_sem.at[buffer]),
-                pltpu.make_async_copy(gb_ref.at[:, slot], bs.at[buffer], b_sem.at[buffer]))
-
-    def partial_rows(z, y, buffer, store):
-        for copy in load(z, y, buffer):
+        return (pltpu.make_async_copy(g_ref.at[:, slot], gs, g_sem.at[0]),
+                pltpu.make_async_copy(gb_ref.at[:, slot], bs, g_sem.at[1]))
+
+    def partial_rows(z, y, store):
+        for copy in load(z, y):
             copy.start()
-        for copy in load(z, y, buffer):
+        for copy in load(z, y):
             copy.wait()
         for m in range(batches):
-            g = gs[buffer, m]
-            b = bs[buffer, m]
+            g = gs[m]
+            b = bs[m]
             for start in range(0, model, tile):
                 cols = slice(start, start + tile)
-                store(m, cols, lax.dot_general(g, w_ref[cols, :], NT, preferred_element_type=f32)
+                store(m, slice(0, rows), cols, lax.dot_general(g, w_ref[cols, :], NT, preferred_element_type=f32)
                       + lax.dot_general(b, wb_ref[cols, :], NT, preferred_element_type=f32))
 
     def across(z, m):
-        return line_copy(ysend.at[z, m], yrecv.at[z, m], pair_send.at[z, m], pair_recv.at[z, m], other("y"))
+        return line_copy(ysend.at[z, m], yrecv.at[z, m, pl.ds(0, rows)], pair_send.at[z, m], pair_recv.at[z, m], other("y"))
 
     def right(z, m):
         return line_copy(yrecv.at[z, m], from_left.at[z, m], right_send.at[z, m], right_recv.at[z, m], {"z": o + 1})
 
     def left(z, m):
         return line_copy(yrecv.at[z, m], from_right.at[z, m], left_send.at[z, m], left_recv.at[z, m], {"z": o - 1})
-
-    line_barrier(lines)
 
     @pl.loop(0, 2 * lines)
     def _(index):
@@ -911,11 +972,23 @@
 
         @pl.when(valid)
         def _():
-            def store(m, cols, value):
-                ysend[z, m, :, cols] = value.astype(bf16)
-            partial_rows(z, 1 - i, 0, store)
+            def store(m, at, cols, value):
+                ysend[z, m, at, cols] = value.astype(bf16)
+            partial_rows(z, 1 - i, store)
             for m in range(batches):
                 across(z, m).start()
+
+    inner_own.wait()
+    inner_pair.wait_recv()
+    add_into(inner_s, inner_r.at[0])
+    inner_across.start()
+    gains_r[mine] = gains_ref[mine]
+    for copy in gain_copies:
+        copy.wait_recv()
+    tail = small_ref.shape[0]
+    small_s[0, :tail] = small_ref[...]
+    small_s[0, tail:] = jnp.sum(gains_r[...], axis=0)
+    small_pair.start()
 
     @pl.loop(0, 2 * lines)
     def _(index):
@@ -926,14 +999,15 @@
             for m in range(batches):
                 across(z, m).wait_recv()
 
-            def store(m, cols, value):
-                yrecv[z, m, :, cols] = (yrecv[z, m, :, cols].astype(f32) + value).astype(bf16)
-            partial_rows(z, i, 0, store)
+            def store(m, at, cols, value):
+                yrecv[z, m, at, cols] = (yrecv[z, m, at, cols].astype(f32) + value).astype(bf16)
+            partial_rows(z, i, store)
             for m in range(batches):
+                yrecv[z, m, rows:, :] = o_ref[z, m]
                 @pl.when((z > o) & (o > 0))
                 def _():
                     right(z, m).wait_recv()
-                    yrecv[z, m] = (yrecv[z, m].astype(f32) + from_left[z, m].astype(f32)).astype(bf16)
+                    add_into(yrecv.at[z, m], from_left.at[z, m])
 
                 @pl.when(z > o)
                 def _():
@@ -942,24 +1016,45 @@
                 @pl.when((z < o) & (o < lines - 1))
                 def _():
                     left(z, m).wait_recv()
-                    yrecv[z, m] = (yrecv[z, m].astype(f32) + from_right[z, m].astype(f32)).astype(bf16)
+                    add_into(yrecv.at[z, m], from_right.at[z, m])
 
                 @pl.when(z < o)
                 def _():
                     left(z, m).start()
 
+    inner_across.wait_recv()
+    inner_across.wait_send()
+    add_into(inner_s, inner_r.at[1])
+    inner_back.start()
+    inner_keep.start()
+    small_pair.wait_recv()
+    small_s[1] = small_s[0] + small_r[0]
+    small_across.start()
+
     for m in range(batches):
-        out_ref[m] = yrecv[o, m].astype(f32)
-
         @pl.when(o > 0)
         def _():
             right(o, m).wait_recv()
-            out_ref[m] += from_left[o, m].astype(f32)
 
         @pl.when(o < lines - 1)
         def _():
             left(o, m).wait_recv()
-            out_ref[m] += from_right[o, m].astype(f32)
+
+        out_ref[m] = yrecv[o, m, :rows, :].astype(f32)
+        outs_s[m * more : (m + 1) * more, :] = yrecv[o, m, rows : rows + more, :]
+
+        for side_ref, exists in ((from_left, o > 0), (from_right, o < lines - 1)):
+            @pl.when(exists)
+            def _():
+                out_ref[m] += side_ref[o, m, :rows, :].astype(f32)
+                at = slice(m * more, (m + 1) * more)
+                outs_s[at, :] = (
+                    outs_s[at, :].astype(f32) + side_ref[o, m, rows : rows + more, :].astype(f32)
+                ).astype(bf16)
+
+    outs_keep.start()
+    for copy in outs_away:
+        copy.start()
 
     @pl.loop(0, lines)
     def _(z):
@@ -974,36 +1069,182 @@
             def _():
                 left(z, m).wait_send()
 
-
-def scatter_rows(grads, beta_grads, w_inner, w_beta):
+    small_across.wait_recv()
+    small_out[...] = small_s[1] + small_r[1]
+    for copy in gain_copies:
+        copy.wait_send()
+    inner_pair.wait_send()
+    small_pair.wait_send()
+    small_across.wait_send()
+    inner_back.wait_recv()
+    inner_back.wait_send()
+    inner_keep.wait()
+    outs_keep.wait()
+    for copy in outs_away:
+        copy.wait_recv()
+        copy.wait_send()
+
+
+def scatter_rows(grads, beta_grads, out_grads, inner_grads, w_inner, w_beta, small, gains):
     batches, total, width = grads.shape
     model = w_inner.shape[0]
     lines = lax.axis_size("z")
     slots = 2 * lines
     rows = total // slots
-    heads = w_beta.shape[1]
-    w_beta = jnp.pad(w_beta, ((0, 0), (0, 128 - heads)))
+    more = out_grads.shape[2]
     sems = pltpu.SemaphoreType.DMA
     anywhere = pl.BlockSpec(memory_space=pl.ANY)
-    slab = pltpu.VMEM((lines, batches, rows, model), bf16)
+    slab = pltpu.VMEM((lines, batches, rows + more, model), bf16)
+    half = inner_grads.shape[1:]
+    flat = (small.shape[0] + gains.shape[1], 128)
     return pl.pallas_call(
         scatter_kernel,
-        out_shape=jax.ShapeDtypeStruct((batches, rows, model), f32),
-        in_specs=[anywhere, anywhere, vmem(), vmem()],
-        out_specs=vmem(),
+        out_shape=(
+            jax.ShapeDtypeStruct((batches, rows, model), f32),
+            jax.ShapeDtypeStruct(flat, f32),
+            jax.ShapeDtypeStruct((4, batches * more, model), bf16),
+            jax.ShapeDtypeStruct(inner_grads.shape, bf16),
+        ),
+        in_specs=[anywhere, anywhere, vmem(), anywhere, vmem(), vmem(), vmem(), vmem()],
+        out_specs=(vmem(), vmem(), anywhere, anywhere),
         scratch_shapes=[
-            pltpu.VMEM((2, batches, rows, width), bf16),
-            pltpu.VMEM((2, batches, rows, 128), bf16),
-            slab, slab, slab, slab,
+            pltpu.VMEM((batches, rows, width), bf16),
+            pltpu.VMEM((batches, rows, 128), bf16),
+            pltpu.VMEM((lines, batches, rows, model), bf16), slab, slab, slab,
+            pltpu.VMEM((batches * more, model), bf16),
+            pltpu.VMEM(half, bf16),
+            pltpu.VMEM((2, *half), bf16),
+            pltpu.VMEM((2, *flat), f32),
+            pltpu.VMEM((2, *flat), f32),
+            pltpu.VMEM(gains.shape, f32),
             sems((lines, batches)), sems((lines, batches)), sems((lines, batches)),
             sems((lines, batches)), sems((lines, batches)), sems((lines, batches)),
-            sems((2,)), sems((2,)),
+            sems((2,)), sems((5,)), sems((5,)), sems((3,)), sems((3,)), sems((slots,)), sems((slots,)), sems((3,)),
         ],
         compiler_params=pltpu.CompilerParams(
-            collective_id=3, has_side_effects=True, vmem_limit_bytes=40 * 2**20),
+            collective_id=3, has_side_effects=True, vmem_limit_bytes=58 * 2**20),
         cost_estimate=pl.CostEstimate(flops=7 * 10**10, bytes_accessed=4 * 10**7, transcendentals=0),
         name="scatter_rows",
-    )(grads.reshape(batches, slots, rows, width), beta_grads.reshape(batches, slots, rows, 128), w_inner, w_beta)
+    )(grads.reshape(batches, slots, rows, width), beta_grads.reshape(batches, slots, rows, 128),
+      out_grads, inner_grads, w_inner, w_beta, small, gains)
+
+
+def attend_kernel(x_ref, first_ref, second_ref, gain_ref, *refs):
+    pieces, (hidden_ref, normed_ref, w_ref, ws, sem, w_sem) = refs[:8], refs[8:]
+    x = lax.axis_index("x")
+    core = lax.axis_index("core")
+    y = lax.axis_index("y")
+    copies = []
+    for n, piece in enumerate(pieces):
+        far_y, far_x, far_core = n // 4, n // 2 % 2, n % 2
+        column = 1 - y if far_y else y
+        quarter = (1 - x if far_x else x) * 2 + (1 - core if far_core else core)
+        copies.append(pltpu.make_async_copy(piece, ws.at[:, column, quarter], sem.at[n]))
+    for copy in copies:
+        copy.start()
+    for copy in copies:
+        copy.wait()
+    keep = pltpu.make_async_copy(ws, w_ref, w_sem.at[0])
+    keep.start()
+    model = x_ref.shape[1]
+    tile = min(512, model)
+    devices = first_ref.shape[0]
+    width = first_ref.shape[2]
+    squares = 0.0
+    for start in range(0, model, tile):
+        cols = slice(start, start + tile)
+        total = x_ref[:, cols].astype(f32)
+        for t in range(devices):
+            left = jnp.concatenate([first_ref[t], second_ref[t]], axis=0)
+            total = total + jnp.dot(
+                left, ws[t // 2, t % 2, :, :, cols].reshape(width, tile), preferred_element_type=f32)
+        hidden_ref[:, cols] = total
+        squares = squares + jnp.sum(total * total, axis=-1, keepdims=True)
+    scale = lax.rsqrt(squares / model + epsilon)
+    for start in range(0, model, tile):
+        cols = slice(start, start + tile)
+        normed_ref[:, cols] = (hidden_ref[:, cols] * scale * gain_ref[:, cols]).astype(bf16)
+    keep.wait()
+
+
+def attend(x, first, second, gain, pieces):
+    rows, model = x.shape
+    lines, part, _ = pieces[0].shape
+    full = (lines, 2, 4, part, model)
+    anywhere = pl.BlockSpec(memory_space=pl.ANY)
+    return pl.pallas_call(
+        attend_kernel,
+        out_shape=(
+            jax.ShapeDtypeStruct((rows, model), f32),
+            jax.ShapeDtypeStruct((rows, model), bf16),
+            jax.ShapeDtypeStruct(full, bf16),
+        ),
+        in_specs=[vmem()] * 4 + [anywhere] * 8,
+        out_specs=(vmem(), vmem(), anywhere),
+        scratch_shapes=[
+            pltpu.VMEM(full, bf16), pltpu.SemaphoreType.DMA((8,)), pltpu.SemaphoreType.DMA((1,))],
+        compiler_params=pltpu.CompilerParams(vmem_limit_bytes=32 * 2**20),
+        cost_estimate=pl.CostEstimate(flops=10**10, bytes_accessed=2 * 10**7, transcendentals=0),
+        name="attend",
+    )(x, first, second, gain, *pieces)
+
+
+def attend_back_kernel(hidden_ref, ffn_ref, grad_ref, c_ref, gain_ref, w_ref, first_ref, second_ref,
+                       result_ref, hgrad_ref, back_first, back_second, wgrad_ref, gain_out, low):
+    rows, model = hidden_ref.shape
+    half = rows // 2
+    tile = min(512, model)
+    squares, dots = 0.0, 0.0
+    for start in range(0, model, tile):
+        cols = slice(start, start + tile)
+        hidden = hidden_ref[:, cols]
+        squares = squares + jnp.sum(hidden * hidden, axis=-1, keepdims=True)
+        dots = dots + jnp.sum(hidden * grad_ref[:, cols] * gain_ref[:, cols], axis=-1, keepdims=True)
+    scale = lax.rsqrt(squares / model + epsilon)
+    pull = scale * scale * scale * (dots / model)
+    for start in range(0, model, tile):
+        cols = slice(start, start + tile)
+        hidden = hidden_ref[:, cols]
+        grad = grad_ref[:, cols]
+        result_ref[:, cols] = hidden + ffn_ref[:, cols]
+        gain_out[:, cols] = jnp.sum(grad * hidden * scale, axis=0, keepdims=True)
+        hgrad = c_ref[:, cols].astype(f32) + scale * (grad * gain_ref[:, cols]) - hidden * pull
+        hgrad_ref[:, cols] = hgrad
+        low[:, cols] = hgrad.astype(bf16)
+    devices, _, width = first_ref.shape
+
+    for t in range(devices):
+        back = lax.dot_general(
+            low[...], w_ref[t // 2, t % 2].reshape(width, model), NT, preferred_element_type=f32)
+        back_first[t] = back[:half].astype(bf16)
+        back_second[t] = back[half:].astype(bf16)
+        left = jnp.concatenate([first_ref[t], second_ref[t]], axis=0)
+        for start in range(0, model, tile):
+            cols = slice(start, start + tile)
+            wgrad_ref[t // 2, t % 2, :, :, cols] = lax.dot_general(
+                left, low[:, cols], (((0,), (0,)), ((), ())), preferred_element_type=f32
+            ).reshape(4, width // 4, tile).astype(bf16)
+
+
+def attend_back(hidden, ffn_out, normed_grad, c_rows, gain, w_full, first, second):
+    rows, model = hidden.shape
+    wide = jax.ShapeDtypeStruct((rows, model), f32)
+    return pl.pallas_call(
+        attend_back_kernel,
+        out_shape=(
+            wide, wide,
+            jax.ShapeDtypeStruct(first.shape, bf16),
+            jax.ShapeDtypeStruct(second.shape, bf16),
+            jax.ShapeDtypeStruct(w_full.shape, bf16),
+            jax.ShapeDtypeStruct((1, model), f32),
+        ),
+        in_specs=[vmem()] * 8,
+        out_specs=(vmem(),) * 6,
+        scratch_shapes=[pltpu.VMEM((rows, model), bf16)],
+        compiler_params=pltpu.CompilerParams(vmem_limit_bytes=56 * 2**20),
+        cost_estimate=pl.CostEstimate(flops=10**10, bytes_accessed=4 * 10**7, transcendentals=0),
+        name="attend_back",
+    )(hidden, ffn_out, normed_grad, c_rows, gain, w_full, first, second)
 
 
 def root_scale(row_values, gain_vector):
@@ -1068,27 +1309,18 @@
     quarter = hidden // size
     blocks = local.reshape(kinds, size, quarter, part).swapaxes(0, 1)
     own = jnp.concatenate(swap_blocks(blocks), axis=2)
-    own = own.reshape(kinds * quarter, size * part)
-    return gather(own, "z").reshape(-1, kinds, quarter, size * part)
-
-
-def plane_weight_grads(grads):
+    return own.reshape(kinds * quarter, size * part)
+
+
+def plane_weight_grads(own, kinds):
     size = lax.axis_size(DP)
-    lines, kinds, quarter, model = grads.shape
-    own = lax.psum_scatter(
-        grads.reshape(lines * kinds * quarter, model), "z", scatter_dimension=0, tiled=True)
+    quarter, model = own.shape[0] // kinds, own.shape[1]
     blocks = own.reshape(kinds * quarter, size, model // size).swapaxes(0, 1)
     pieces = [piece.reshape(kinds, quarter, -1) for piece in swap_blocks(blocks)]
     whole = jnp.concatenate(pieces, axis=1).astype(f32)
     return whole[0].T, whole[1].T, whole[2]
 
 
-def plane_rows(x):
-    for axis_name in ("x", "y", "core"):
-        x = jnp.concatenate([x, exchange(x, axis_name)])
-    return x
-
-
 def ordered_blocks(pieces):
     me = lax.axis_index(DP)
     pieces = jnp.stack(pieces)
@@ -1099,50 +1331,14 @@
     return lax.dynamic_index_in_dim(x, index, axis, keepdims=False)
 
 
-def gather_pairs(x):
-    across = exchange(x, "x")
-    return ordered_blocks([x, exchange(x, "core"), across, exchange(across, "core")])
-
-
-def sum_pairs(x):
-    core = lax.axis_index("core")
-    halves = x.reshape(2, x.shape[0] // 2, *x.shape[1:])
-    mine = pick(halves, core, 0).astype(f32)
-    mine = mine + exchange(pick(halves, 1 - core, 0).astype(bf16), "core").astype(f32)
-    low = mine.astype(bf16)
-    mine = (mine + exchange(low, "x").astype(f32)).astype(bf16)
-    theirs = exchange(mine, "core")
-    first = jnp.where(core == 0, mine, theirs)
-    second = jnp.where(core == 0, theirs, mine)
-    return first, second
-
-
-def gather_out(w_out):
-    me = lax.axis_index(DP)
-    quarters = w_out.reshape(lax.axis_size(DP), -1, w_out.shape[1])
-    column = gather(pick(quarters, me, 0)[None], TP)
-    return jnp.stack(gather_pairs(column), axis=1).reshape(-1, w_out.shape[1])
-
-
-def scatter_out(grad):
-    devices = lax.axis_size(TP)
-    grad = grad.reshape(devices, 2, 2, -1, grad.shape[1])
-    for axis_name, axis in (("core", 2), ("x", 1)):
-        me = lax.axis_index(axis_name)
-        theirs = exchange(pick(grad, 1 - me, axis), axis_name)
-        grad = (pick(grad, me, axis).astype(f32) + theirs.astype(f32)).astype(bf16)
-    own = lax.psum_scatter(grad, TP, scatter_dimension=0, tiled=True)[0]
-    return jnp.concatenate(gather_pairs(own)).astype(f32)
-
-
-def feed_forward_plane(normed, cotangents, w_gate, w_up, w_down):
-    weights = plane_weights(w_gate, w_up, w_down)
-    batches, rows, model = normed.shape
-    rows = normed.reshape(batches * rows, model)
-    count = rows.shape[0]
-    c_all = plane_rows(cotangents.reshape(1, count, model))
-    out, normed_grad, grads = ffn_plane(rows, c_all, weights)
-    return out.reshape(normed.shape), normed_grad.reshape(normed.shape), plane_weight_grads(grads)
+def after(x, *others):
+    return lax.optimization_barrier((x, *others))[0]
+
+
+def halve_sum(grad, axis_name, axis):
+    me = lax.axis_index(axis_name)
+    theirs = exchange(pick(grad, 1 - me, axis), axis_name)
+    return (pick(grad, me, axis).astype(f32) + theirs.astype(f32)).astype(bf16)
 
 
 def feed_forward_groups(normed, cotangents, w_gate, w_up, w_down):
@@ -1200,51 +1396,98 @@
     devices = lax.axis_size(TP)
     planar = all(lax.axis_size(name) == 2 for name in ("x", "core", "y"))
     w_inner = jnp.concatenate([w_query, w_key, w_value, w_gate_out], axis=1)
+    w_beta_wide = jnp.pad(w_beta, ((0, 0), (0, 128 - heads)))
     taps = conv_weight.astype(f32).reshape(-1, local_width)
     gain_heads = head_gain.astype(f32)
-    gains = gather(jnp.stack([norm_gain, ffn_gain]), DP, 1).astype(f32)
-    gain_one, gain_two = gains[0], gains[1]
+    gains = gather(jnp.stack([norm_gain, ffn_gain]), DP, 1)
+    gain_one, gain_two = gains[0].astype(f32), gains[1].astype(f32)
     rows_in = inputs.astype(f32)
     normed_one, scale_one = root_scale(rows_in, gain_one)
     normed_one = normed_one.astype(bf16)
+
+    def run_mixer(m, wide, logits):
+        low, *kept = mixer_forward(lengths[m, 0], wide, logits, taps, gain_heads, exact=False)
+        return low, kept
+
+    def back_mixer(m, wide, logits, grad, kept):
+        return mixer_backward(
+            lengths[m, 0], wide, logits, taps, gain_heads, grad, kept, exact=False)
+
     if planar:
-        gathered_one, projected, beta_logits = gather_project(normed_one, w_inner, w_beta)
-        out_full = gather_out(w_out)
+        count = rows_in.shape[0] * rows_in.shape[1]
+        model = rows_in.shape[2]
+        own_weights = plane_weights(*after((w_gate, w_up, w_down), gains))
+        c_rows = [None] * 8
+        c_rows[0] = after(cotangent.reshape(count, model), gains)
+        c_rows[1] = exchange(c_rows[0], "x")
+        c_rows[4] = exchange(c_rows[0], "core")
+        out_shares = pick(
+            w_out.reshape(lax.axis_size(DP), len(batches), -1, model), lax.axis_index(DP), 0)
+        gathered_one, out_own, projected, beta_logits = gather_project(
+            normed_one, out_shares, w_inner, w_beta_wide)
+        own_weights, early, early_x, out_own = after(
+            (own_weights, c_rows[0], c_rows[1], out_own), gathered_one)
+        weights = gather(own_weights, "z").reshape(lax.axis_size("z"), 3, -1, model)
+        c_rows[2], c_rows[3] = exchange(early, "y"), exchange(early_x, "y")
+        c_rows[5], c_rows[6], c_rows[7] = (exchange(c_rows[n], "core") for n in (1, 2, 3))
+        out_own = out_own.reshape(out_own.shape[0], -1, model)
+        out_pieces = []
+        for piece in (out_own, exchange(out_own, "y")):
+            across = exchange(piece, "x")
+            out_pieces += [piece, exchange(piece, "core"), across, exchange(across, "core")]
     else:
         gathered_one = jnp.stack([gather(normed_one[m], TP) for m in batches])
         projected = [dot(gathered_one[m], w_inner) for m in batches]
-        beta_logits = [
-            jnp.pad(dot(gathered_one[m], w_beta), ((0, 0), (0, 128 - heads))) for m in batches]
+        beta_logits = [dot(gathered_one[m], w_beta_wide) for m in batches]
         out_full = gather(w_out, TP)
     token_heads, saved = [], []
     for m in batches:
-        low, *kept = mixer_forward(lengths[m, 0], projected[m], beta_logits[m], taps, gain_heads)
+        low, kept = run_mixer(m, projected[m], beta_logits[m])
         saved.append(kept)
-        token_heads.append(lax.all_to_all(low, TP, split_axis=0, concat_axis=1, tiled=True))
-    token_heads = jnp.concatenate(token_heads)
-    hidden = rows_in + dot(token_heads, out_full).reshape(rows_in.shape)
-    normed_two, scale_two = root_scale(hidden, gain_two)
-    feed_forward = feed_forward_plane if planar else feed_forward_groups
-    ffn_out, normed_grad, (gate_share, up_share, down_share) = feed_forward(
-        normed_two.astype(bf16), cotangent, w_gate, w_up, w_down)
-    result_rows = hidden + ffn_out
-    norm_grad, gain_two_sum = norm_backward(hidden, scale_two, gain_two, normed_grad)
-    hidden_grad = cotangent.astype(f32) + norm_grad
-    attended_low = hidden_grad.astype(bf16)
-    mixed_grads = []
-    for m in batches:
-        token_grad = dot_nt(attended_low[m], out_full).astype(bf16)
-        token_grad = token_grad.reshape(-1, devices, local_width).swapaxes(0, 1)
-        mixed_grads.append(
-            lax.all_to_all(token_grad, TP, split_axis=0, concat_axis=0, tiled=True).reshape(
-                -1, local_width))
-    out_grad = dot_tn(token_heads, attended_low.reshape(token_heads.shape[0], -1)).astype(bf16)
+        token_heads.append(lax.all_to_all(
+            low.reshape(devices, -1, local_width), TP, split_axis=0, concat_axis=0, tiled=True))
+    if planar:
+        hidden, normed_two, out_full = attend(
+            inputs.reshape(count, model), *token_heads, gain_two[None], out_pieces)
+        ffn_out, normed_grad, weight_grads = ffn_plane(normed_two, weights, c_rows)
+        own_grads = lax.psum_scatter(
+            weight_grads.reshape(-1, model), "z", scatter_dimension=0, tiled=True)
+        gate_share, up_share, down_share = plane_weight_grads(own_grads, 3)
+        result_rows, hidden_grad, *mixed_grads, out_grad, gain_two_sum = attend_back(
+            hidden, ffn_out, normed_grad, c_rows[0], gain_two[None], out_full, *token_heads)
+        gain_two_sum = gain_two_sum[0]
+        result_rows = result_rows.reshape(rows_in.shape)
+        hidden_grad = hidden_grad.reshape(rows_in.shape)
+        out_grad = halve_sum(
+            out_grad.reshape(out_grad.shape[0], 2, 2, 2, *out_grad.shape[3:]), "core", 3)
+    else:
+        heads_rows = [
+            block.swapaxes(0, 1).reshape(-1, devices * local_width) for block in token_heads]
+        hidden = rows_in + jnp.stack([dot(rows, out_full) for rows in heads_rows])
+        normed_two, scale_two = root_scale(hidden, gain_two)
+        ffn_out, normed_grad, (gate_share, up_share, down_share) = feed_forward_groups(
+            normed_two.astype(bf16), cotangent, w_gate, w_up, w_down)
+        result_rows = hidden + ffn_out
+        norm_grad, gain_two_sum = norm_backward(hidden, scale_two, gain_two, normed_grad)
+        hidden_grad = cotangent.astype(f32) + norm_grad
+        attended_low = hidden_grad.astype(bf16)
+        mixed_grads = [
+            dot_nt(attended_low[m], out_full).astype(bf16)
+            .reshape(-1, devices, local_width).swapaxes(0, 1) for m in batches]
+        out_grad = dot_tn(
+            jnp.concatenate(heads_rows), jnp.concatenate(list(attended_low))).astype(bf16)
+    mixed_grads = [
+        lax.all_to_all(grad, TP, split_axis=0, concat_axis=0, tiled=True).reshape(-1, local_width)
+        for grad in mixed_grads]
+    if planar:
+        mixed_grads[0] = after(mixed_grads[0], out_grad)
+        out_grad = halve_sum(halve_sum(out_grad, "x", 2), "y", 1)
+        out_grad = out_grad.reshape(out_grad.shape[0], len(batches), -1, model)
     projected_low, beta_low = [], []
     taps_sum, heads_sum = 0.0, 0.0
     for m in batches:
-        projected_grad, beta_grad, taps_part, heads_part = mixer_backward(
-            lengths[m, 0], projected[m], beta_logits[m], taps, gain_heads, mixed_grads[m], saved[m]
-        )
+        projected_grad, beta_grad, taps_part, heads_part = back_mixer(
+            m, projected[m], beta_logits[m], mixed_grads[m], saved[m])
         taps_sum = taps_sum + taps_part
         heads_sum = heads_sum + heads_part
         projected_low.append(projected_grad)
@@ -1258,32 +1501,44 @@
         jnp.sum(inner_sum * w_inner.astype(f32), axis=1)
         + jnp.sum(beta_sum * w_beta.astype(f32), axis=1)
     ) / gain_one
-    gain_totals = lax.psum_scatter(
-        jnp.stack([gain_one_sum, gain_two_sum]), DP + TP, scatter_dimension=1, tiled=True)
+    gain_parts = jnp.stack([gain_one_sum, gain_two_sum])
     small = jnp.concatenate([part.reshape(-1) for part in (beta_sum, taps_sum, heads_sum)])
+    low_sum = inner_sum.astype(bf16)
     if planar:
-        inner_total = sum_pairs(inner_sum)
-        small = small + exchange(small, "core")
-        small = small + exchange(small, "x")
-        out_total = scatter_out(out_grad)
-        input_norm = scatter_rows(projected_low, beta_low, w_inner, w_beta)
+        ranks = lax.axis_size(DP)
+        gain_parts = gain_parts.reshape(2, ranks, devices, -1).transpose(2, 0, 1, 3)
+        chunk = gain_parts.shape[3]
+        gain_parts = gain_parts.reshape(devices, -1, 128)
+        gain_rows = gain_parts.shape[1]
+        gain_parts = jnp.pad(gain_parts, ((0, 0), (0, -gain_rows % 8), (0, 0)))
+        small = jnp.pad(small, (0, -small.size % 1024)).reshape(-1, 128)
+        input_norm, flat, out_total, inner_total = scatter_rows(
+            after(projected_low, own_grads), beta_low, out_grad,
+            low_sum.reshape(2, -1, low_sum.shape[1]), w_inner, w_beta_wide, small, gain_parts)
+        gain_totals = pick(
+            flat[small.shape[0] :][:gain_rows].reshape(2, ranks, chunk), lax.axis_index(DP), 1)
+        small = flat[: small.shape[0]].reshape(-1)
+        out_total = out_total.reshape(w_out.shape).astype(f32)
+        inner_total = inner_total.reshape(low_sum.shape)
     else:
-        inner_total = [lax.psum(inner_sum.astype(bf16), DP)]
+        gain_totals = lax.psum_scatter(gain_parts, DP + TP, scatter_dimension=1, tiled=True)
+        inner_total = lax.psum(low_sum, DP)
         small = lax.psum(small, DP)
         out_grad = lax.psum_scatter(out_grad, TP, scatter_dimension=0, tiled=True)
         out_total = lax.psum(out_grad, DP).astype(f32)
         input_norm = jnp.stack([
             scatter_sum(
-                dot_nt(projected_low[m], w_inner) + dot_nt(beta_low[m, :, :heads], w_beta), TP)
+                dot_nt(projected_low[m], w_inner) + dot_nt(beta_low[m], w_beta_wide), TP)
             for m in batches])
     norm_grad, _ = norm_backward(rows_in, scale_one, gain_one, input_norm)
     beta_total, conv_total, heads_total = (
         piece.reshape(shape) for piece, shape in zip(
-            jnp.split(small, (beta_sum.size, beta_sum.size + taps_sum.size)),
+            jnp.split(
+                small[: beta_sum.size + taps_sum.size + heads_sum.size],
+                (beta_sum.size, beta_sum.size + taps_sum.size)),
             (beta_sum.shape, conv_weight.shape, head_gain.shape)))
     columns = [
-        jnp.concatenate([part[:, n * local_width : (n + 1) * local_width] for part in inner_total])
-        .astype(f32) for n in range(4)]
+        inner_total[:, n * local_width : (n + 1) * local_width].astype(f32) for n in range(4)]
     return (
         result_rows,
         hidden_grad + norm_grad,

time: 1160 us -> 803 us (0.69)
  waiting for transfers between devices: 280 us -> 119 us
  Pallas kernels: 628 us -> 501 us
  other arithmetic: 73.4 us -> 37.9 us
  matrix products: 32.3 us -> 15 us
  blocking collectives: 19.6 us -> 6.11 us
    reduce_scatter x2 -> x1, waiting for transfers between devices: 114 us -> 0.01 us  [per_device(): lax.psum_scatter(weight_grads.reshape(-1, model), 'z', scatter_dimension=...]
    pallas_call x1, Pallas kernels: 207 us -> 107 us  [gather_project(): pl.pallas_call(gather_kernel, out_shape=(jax.ShapeDtypeStruct((batches, s...]
    ppermute x22 -> x23, waiting for transfers between devices: 143 us -> 43.5 us  [exchange(): return lax.ppermute(x, axis_name, [(i, i ^ distance) for i in range(size)])]
    pallas_call x2, Pallas kernels: 90 us -> 55.8 us  [mixer_backward(): pl.pallas_call(partial(mixer_backward_kernel, exact), out_shape=(jax.Shap...]
    all_gather x2 -> x1, waiting for transfers between devices: 0.01 us -> 31.5 us  [gather(): return lax.all_gather(x, axis_name, axis=axis, tiled=True)]
    pallas_call x2 -> x4, Pallas kernels: 262 us -> 286 us  [the longest x1 140 us: scatter_rows(): pl.pallas_call(scatter_kernel, out_shape=(jax.ShapeDtypeStruct((batches,...]
    all_to_all x4, waiting for transfers between devices: 22.4 us -> 43.6 us  [the longest x2 26.6 us: per_device(): lax.all_to_all(grad, TP, split_axis=0, concat_axis=0, tiled=True)]
    pallas_call x2, Pallas kernels: 68.3 us -> 52.5 us  [mixer_forward(): pl.pallas_call(partial(mixer_forward_kernel, exact, group), out_shape=(ja...]
  transfers between devices with their start and end apart: 31 -> 29, of which waited for: 11 -> 6; matrix products, arithmetic and copies ran while one was open for 12% -> 11% of each run, Pallas kernels for 44% -> 47%
where the time goes in v4:
time: 803 us; the launch traced here: 799 us
  Pallas kernels  501 us (62%)
  waiting for transfers between devices  119 us (15%)
  local copies, waits for them, and re-layouts  69.4 us (9%)
  other arithmetic  37.9 us (5%)
  starting transfers between devices  35.4 us (4%)
  between operations  15.1 us (2%)
  matrix products  15 us (2%)
    pallas_call x1, Pallas kernels, scatter_rows(): pl.pallas_call(scatter_kernel, out_shape=(jax.ShapeDtypeStruct((batches,...  140 us
    pallas_call x1, Pallas kernels, ffn_plane(): pl.pallas_call(ffn_call_kernel, out_shape=(jax.ShapeDtypeStruct((rows, mo...  124 us
    pallas_call x1, Pallas kernels, gather_project(): pl.pallas_call(gather_kernel, out_shape=(jax.ShapeDtypeStruct((batches, s...  107 us
    pallas_call x2, Pallas kernels, mixer_backward(): pl.pallas_call(partial(mixer_backward_kernel, exact), out_shape=(jax.Shap...  55.8 us
    pallas_call x2, Pallas kernels, mixer_forward(): pl.pallas_call(partial(mixer_forward_kernel, exact, group), out_shape=(ja...  52.5 us
    ppermute x23, waiting for transfers between devices, exchange(): return lax.ppermute(x, axis_name, [(i, i ^ distance) for i in range(size)])  43.5 us
    all_gather x1, waiting for transfers between devices, gather(): return lax.all_gather(x, axis_name, axis=axis, tiled=True)  31.5 us
    all_to_all x2, waiting for transfers between devices, per_device(): lax.all_to_all(grad, TP, split_axis=0, concat_axis=0, tiled=True)  26.6 us
  transfers between devices with their start and end apart: 29, of which 6 were waited for; matrix products, arithmetic and copies ran while one was open for 11% of the time, Pallas kernels for 47%

profile of v4, /device:TPU:0, one launch (start us, length us, event | category | flops | bytes accessed | tf_op | source)
XLA Modules:
  0.0 798.7 jit_solution(14974794278300235521)
XLA Ops:
  8.7 6.1 all_gather.6
  14.8 1.8 pad_maximum_fusion.1
  18.3 2.0 collective-permute-start.1
  20.3 1.6 collective-permute-start.3
  24.1 2.4 constant_dynamic-update-slice_fusion.2
  28.7 2.2 copy-done.9
  30.9 106.7 %gather_project.1 = (bf16[2,8,128,2048]{3,2,1,0:T(8,128)(2,1)}, bf16[4,2,32,2048]{3,2,1,0:T(8,128)(2,1)}, f32[2,8,128,1024]{3,2,1,0:T(8,128)}, f32[2,8,128,128]{3,2,1,0:T(8,128)S(1)}) custom-call(bf16[2,128,2048]{2,1,0:T(8,128)(2,1)S(1)} %fusion.4.x_ref, bf16[2,32,2048]{2,1,0:T(8,128)(2,1)S(1)} %dynamic-slice_bitcast_fusion.6.o_ref, ...), custom_call_target="tpu_custom_call" | custom-call | flops 99999997952 | bytes 40000000 | tf_op jit(solution)/shard_map/gather_project/pallas_call | solution.py:852
  137.7 1.6 pad_maximum_fusion.2
  139.5 1.6 pad_maximum_fusion.3
  143.1 9.8 %fusion.17 = (f32[1,8,128,1024]{3,2,1,0:T(8,128)}, f32[1,8,128,1024]{3,2,1,0:T(8,128)}) fusion(f32[2,8,128,1024]{3,2,1,0:T(8,128)} %get-tuple-element.65), kind=kLoop, calls=%fused_computation.87 | loop fusion | bytes 16777216 | tf_op jit(solution)/shard_map/slice | solution.py:1445
  152.9 12.1 %collective-permute-done.7.refs_4_ = bf16[4,64,2048]{2,1,0:T(8,128)(2,1)} collective-permute-done((bf16[4,64,2048]{2,1,0:T(8,128)(2,1)}, bf16[4,64,2048]{2,1,0:T(8,128)(2,1)}, u32[]{:S(2)}, u32[]{:S(2)}) %collective-permute-start.7) | collective-permute-done | bytes 1048608 | tf_op jit(solution)/shard_map/ppermute | solution.py:1292
  165.6 26.2 %mixer_forward.3 = (bf16[1024,256]{1,0:T(8,128)(2,1)}, f32[1024,256]{1,0:T(8,128)S(1)}, f32[1024,256]{1,0:T(8,128)S(1)}, f32[1024,256]{1,0:T(8,128)S(1)}, f32[16...) custom-call(s32[3]{0:T(128)S(1)} %get-tuple-element.195.lengths_ref, f32[1024,1024]{1,0:T(8,128)} %bitcast.140, ...), custom_call_target="tpu_custom_call" | custom-call | flops 10000000000 | bytes 10000000 | tf_op jit(solution)/shard_map/mixer_forward/pallas_call | solution.py:333
  195.8 3.7 all-to-all-start.1
  199.4 1.9 collective-permute-start.11
  202.1 26.2 %mixer_forward.2 = (bf16[1024,256]{1,0:T(8,128)(2,1)}, f32[1024,256]{1,0:T(8,128)S(1)}, f32[1024,256]{1,0:T(8,128)S(1)}, f32[1024,256]{1,0:T(8,128)S(1)}, f32[16...) custom-call(s32[3]{0:T(128)S(1)} %get-tuple-element.196.lengths_ref, f32[1024,1024]{1,0:T(8,128)} %bitcast.138, ...), custom_call_target="tpu_custom_call" | custom-call | flops 10000000000 | bytes 10000000 | tf_op jit(solution)/shard_map/mixer_forward/pallas_call | solution.py:333
  232.3 5.9 all-to-all-start
  238.7 14.2 %collective-permute-done.12.refs_3_ = bf16[256,2048]{1,0:T(8,128)(2,1)} collective-permute-done((bf16[256,2048]{1,0:T(8,128)(2,1)}, bf16[256,2048]{1,0:T(8,128)(2,1)}, u32[]{:S(2)}, u32[]{:S(2)}) %collective-permute-start.12) | collective-permute-done | bytes 1048608 | tf_op jit(solution)/shard_map/ppermute | solution.py:1292
  253.5 17.0 %all-to-all-done.first_ref = bf16[8,128,256]{2,1,0:T(8,128)(2,1)S(1)} async-done(((bf16[8,128,256]{2,1,0:T(8,128)(2,1)}), bf16[8,128,256]{2,1,0:T(8,128)(2,1)S(1)}, u32[]{:S(2)}, u32[]{:S(2)}) %all-to-all-start) | async-done | bytes 524320 | tf_op jit(solution)/shard_map/all_to_all | solution.py:1447
  270.5 6.8 attend.1
  277.3 3.2 copy-done.16
  282.9 31.5 %all-gather.2.cloned.1.call-done = bf16[2112,2048]{1,0:T(8,128)(2,1)} async-done(((bf16[528,2048]{1,0:T(8,128)(2,1)}), bf16[2112,2048]{1,0:T(8,128)(2,1)}) %all-gather.2.cloned.1.call-update) | async-done | bytes 8650768 | tf_op jit(solution)/shard_map/all_gather | solution.py:1269
  314.3 124.3 %ffn_plane.1 = (f32[256,2048]{1,0:T(8,128)}, f32[256,2048]{1,0:T(8,128)}, bf16[4,3,176,2048]{3,2,1,0:T(8,128)(2,1)}) custom-call(bf16[256,2048]{1,0:T(8,128)(2,1)} %copy-done.26, bf16[4,3,176,2048]{3,2,1,0:T(8,128)(2,1)} %bitcast.169, bf16[256,2048]{1,0:T(8,128)(2,1)} %bitcast.28.refs_0_.c_ref, bf16[256,2048]{1,0:T(8,128)(2,1)} %collective-permute-done.3.refs_1_, ...), custom_call_target="tpu_custom_call" | custom-call | flops 80000000000 | bytes 40000000 | tf_op jit(solution)/shard_map/ffn_plane/pallas_call | solution.py:655
  438.6 15.5 %attend_back.1 = (f32[256,2048]{1,0:T(8,128)}, f32[256,2048]{1,0:T(8,128)}, bf16[8,128,256]{2,1,0:T(8,128)(2,1)}, bf16[8,128,256]{2,1,0:T(8,128)(2,1)}, bf16[4,2...) custom-call(f32[256,2048]{1,0:T(8,128)} %copy-done.17, f32[256,2048]{1,0:T(8,128)} %get-tuple-element.80.ffn_ref, ...), custom_call_target="tpu_custom_call" | custom-call | flops 10000000000 | bytes 40000000 | tf_op jit(solution)/shard_map/attend_back/pallas_call | solution.py:1232
  454.1 6.8 constant_dynamic-slice_fusion.11
  460.9 2.4 copy.64
  463.3 2.1 collective-permute-start.17
  465.4 3.5 all-to-all-start.3
  470.2 26.6 %all-to-all-done.3 = bf16[8,128,256]{2,1,0:T(8,128)(2,1)S(1)} async-done(((bf16[8,128,256]{2,1,0:T(8,128)(2,1)}), bf16[8,128,256]{2,1,0:T(8,128)(2,1)S(1)}, u32[]{:S(2)}, u32[]{:S(2)}) %all-to-all-start.3) | async-done | bytes 524320 | tf_op jit(solution)/shard_map/all_to_all | solution.py:1480
  496.8 5.6 all-to-all-start.2
  502.4 27.9 %mixer_backward.3 = (bf16[1024,1024]{1,0:T(8,128)(2,1)}, bf16[1024,128]{1,0:T(8,128)(2,1)}, f32[12,256]{1,0:T(8,128)}, f32[2,128]{1,0:T(2,128)}) custom-call(s32[3]{0:T(128)} %copy-done.14, f32[1024,1024]{1,0:T(8,128)} %bitcast.141, f32[1024,128]{1,0:T(8,128)} %bitcast.127, f32[12,256]{1,0:T(8,128)} %copy-done.11, f32[2,128]{1,0:T(2,128)} %copy-done.15, ...), custom_call_target="tpu_custom_call" | custom-call | flops 10000000000 | bytes 10000000 | tf_op jit(solution)/shard_map/mixer_backward/pallas_call | solution.py:356
  530.3 6.5 fusion
  536.9 1.9 dynamic-slice_bitcast_fusion
  540.3 27.9 %mixer_backward.2 = (bf16[1024,1024]{1,0:T(8,128)(2,1)}, bf16[1024,128]{1,0:T(8,128)(2,1)}, f32[12,256]{1,0:T(8,128)}, f32[2,128]{1,0:T(2,128)}) custom-call(s32[3]{0:T(128)} %copy-done.13, f32[1024,1024]{1,0:T(8,128)} %bitcast.139, f32[1024,128]{1,0:T(8,128)} %bitcast.126, f32[12,256]{1,0:T(8,128)} %copy-done.11, f32[2,128]{1,0:T(2,128)} %copy-done.15, ...), custom_call_target="tpu_custom_call" | custom-call | flops 10000000000 | bytes 10000000 | tf_op jit(solution)/shard_map/mixer_backward/pallas_call | solution.py:356
  568.2 2.1 pad_maximum_fusion
  570.4 3.3 pad_maximum_fusion.6
  573.7 13.8 %multiply_reduce_fusion = (f32[2048]{0:T(1024)S(1)}, bf16[2048,1024]{1,0:T(8,128)(2,1)}) fusion(bf16[2048,1024]{1,0:T(8,128)(2,1)S(1)} %copy-done.10, bf16[2048,2048]{1,0:T(8,128)(2,1)} %bitcast.129, bf16[2048,1024]{1,0:T(8,128)(2,1)S(1)} %bitcast.136), kind=kOutput, calls=%fused_computation.2 | convolution fusion | flops 8598321152 | bytes 20979712 | tf_op jit(solution)/shard_map/tm,tn->mn/dot_general | solution.py:1287
  589.4 2.0 collective-permute-start.19
  595.1 1.8 pad_maximum_fusion.5.gb_ref
  596.9 17.2 %collective-permute-done.19 = bf16[4,64,2048]{2,1,0:T(8,128)(2,1)} collective-permute-done((bf16[4,64,2048]{2,1,0:T(8,128)(2,1)}, bf16[4,64,2048]{2,1,0:T(8,128)(2,1)}, u32[]{:S(2)}, u32[]{:S(2)}) %collective-permute-start.19) | collective-permute-done | bytes 1048608 | tf_op jit(solution)/shard_map/ppermute | solution.py:1292
  614.1 2.6 fusion.11
  616.7 4.7 reshape.266
  621.4 5.5 constant_dynamic-slice_fusion.8
  631.5 139.6 %scatter_rows.1 = (f32[2,128,2048]{2,1,0:T(8,128)}, f32[72,128]{1,0:T(8,128)}, bf16[4,64,2048]{2,1,0:T(8,128)(2,1)}, bf16[2,1024,1024]{2,1,0:T(8,128)(2,1)}) custom-call(bf16[2,8,128,1024]{3,2,1,0:T(8,128)(2,1)} %bitcast.137, bf16[2,8,128,128]{3,2,1,0:T(8,128)(2,1)} %pad_maximum_fusion.5.gb_ref, bf16[4,2,32,2048]{3,2,1,0:T(8,128)(2,1)} %bitcast.155, ...), custom_call_target="tpu_custom_call" | custom-call | flops 70000001024 | bytes 40000000 | tf_op jit(solution)/shard_map/scatter_rows/pallas_call | solution.py:1100
  771.2 5.9 slice_convert_fusion
  777.9 3.7 fusion.8
  785.4 1.6 bitcast_convert_fusion
  787.0 1.6 pad_maximum_fusion.4
  789.5 2.2 slice_bitcast_fusion
  (222 shorter events, 40.5 us)
Async XLA Ops:
  7.2 307.1 %all-gather.2.cloned.1.call-start = ((), (), s32[]{:S(2)}) async-start(), calls=%async_computation.5 | async-start | bytes 10813440 | tf_op jit(solution)/shard_map/all_gather | solution.py:1269
  18.0 119.7 %collective-permute-start = (bf16[3,176,512]{2,1,0:T(8,128)(2,1)}, bf16[3,176,512]{2,1,0:T(8,128)(2,1)}, u32[]{:S(2)}, u32[]{:S(2)}) collective-permute-start(bf16[3,176,512]{2,1,0:T(8,128)(2,1)} %get-tuple-element.188), channel_id=1, source_target_pairs={{0,8},{8,0},{16,24},{24,16},{1,9},{9,1},{17,25},{25,17},{2,10},{10... | collective-permute-start | bytes 1622024 | tf_op jit(solution)/shard_map/ppermute | solution.py:1292
  18.3 119.4 %collective-permute-start.1 = (bf16[3,176,512]{2,1,0:T(8,128)(2,1)}, bf16[3,176,512]{2,1,0:T(8,128)(2,1)}, u32[]{:S(2)}, u32[]{:S(2)}) collective-permute-start(bf16[3,176,512]{2,1,0:T(8,128)(2,1)} %get-tuple-element.187), channel_id=1, source_target_pairs={{0,16},{8,24},{16,0},{24,8},{1,17},{9,25},{17,1},{25,9},{2,18},{10... | collective-permute-start | bytes 1622024 | tf_op jit(solution)/shard_map/ppermute | solution.py:1292
  20.3 117.4 %collective-permute-start.2 = (bf16[3,176,512]{2,1,0:T(8,128)(2,1)}, bf16[3,176,512]{2,1,0:T(8,128)(2,1)}, u32[]{:S(2)}, u32[]{:S(2)}) collective-permute-start(bf16[3,176,512]{2,1,0:T(8,128)(2,1)} %get-tuple-element.186), channel_id=1, source_target_pairs={{0,24},{8,16},{16,8},{24,0},{1,25},{9,17},{17,9},{25,1},{2,26},{10... | collective-permute-start | bytes 1622024 | tf_op jit(solution)/shard_map/ppermute | solution.py:1292
  20.3 120.8 %collective-permute-start.3 = (bf16[256,2048]{1,0:T(8,128)(2,1)}, bf16[256,2048]{1,0:T(8,128)(2,1)}, u32[]{:S(2)}, u32[]{:S(2)}) collective-permute-start(bf16[256,2048]{1,0:T(8,128)(2,1)} %bitcast.28.refs_0_.c_ref), channel_id=1, source_target_pairs={{0,16},{16,0},{1,17},{17,1},{2,18},{18,2},{3,19},{19,3},{4,20},{20... | collective-permute-start | bytes 3145736 | tf_op jit(solution)/shard_map/ppermute | solution.py:1292
  21.9 248.6 %copy-start.12 = (f32[1,2048]{1,0:T(1,128)}, f32[1,2048]{1,0:T(1,128)S(1)}, u32[]{:S(2)}) copy-start(f32[1,2048]{1,0:T(1,128)S(1)} %get-tuple-element.191.gain_ref) | copy-start | bytes 24580
  30.9 106.8 %copy-start.6 = (bf16[2048,128]{1,0:T(8,128)(2,1)}, bf16[2048,128]{1,0:T(8,128)(2,1)S(1)}, u32[]{:S(2)}) copy-start(bf16[2048,128]{1,0:T(8,128)(2,1)S(1)} %pad.12.wb_ref) | copy-start | bytes 1572868
  30.9 106.8 %copy-start.32 = (bf16[1,3,176,512]{3,2,1,0:T(8,128)(2,1)S(1)}, bf16[1,3,176,512]{3,2,1,0:T(8,128)(2,1)}, u32[]{:S(2)}) copy-start(bf16[1,3,176,512]{3,2,1,0:T(8,128)(2,1)} %get-tuple-element.185) | copy-start | bytes 1622020
  141.2 23.8 %collective-permute-start.7 = (bf16[4,64,2048]{2,1,0:T(8,128)(2,1)}, bf16[4,64,2048]{2,1,0:T(8,128)(2,1)}, u32[]{:S(2)}, u32[]{:S(2)}) collective-permute-start(bf16[4,64,2048]{2,1,0:T(8,128)(2,1)} %bitcast.29.refs_0_), channel_id=1, source_target_pairs={{0,1},{1,0},{2,3},{3,2},{4,5},{5,4},{6,7},{7,6},{8,9},{9,8},{10,11... | collective-permute-start | bytes 3145736 | tf_op jit(solution)/shard_map/ppermute | solution.py:1292
  143.1 59.0 %copy-start.7 = (f32[1,8,128,128]{3,2,1,0:T(8,128)}, f32[1,8,128,128]{3,2,1,0:T(8,128)S(1)}, u32[]{:S(2)}) copy-start(f32[1,8,128,128]{3,2,1,0:T(8,128)S(1)} %get-tuple-element.190) | copy-start | bytes 1572868
  143.1 22.4 %copy-start.56 = (s32[2,1,3]{2,1,0:T(1,128)S(1)}, s32[2,1,3]{2,1,0:T(1,128)}, u32[]{:S(2)}) copy-start(s32[2,1,3]{2,1,0:T(1,128)} %param.17) | copy-start | bytes 76
  143.1 22.4 %copy-start.53 = (bf16[3,4,256]{2,1,0:T(4,128)(2,1)S(1)}, bf16[3,4,256]{2,1,0:T(4,128)(2,1)}, u32[]{:S(2)}) copy-start(bf16[3,4,256]{2,1,0:T(4,128)(2,1)} %param.25) | copy-start | bytes 18436
  143.1 22.4 %copy-start.58 = (bf16[2,128]{1,0:T(2,128)(2,1)S(1)}, bf16[2,128]{1,0:T(2,128)(2,1)}, u32[]{:S(2)}) copy-start(bf16[2,128]{1,0:T(2,128)(2,1)} %param.26) | copy-start | bytes 1540
  143.1 22.5 %copy-start.8 = (f32[1,8,128,128]{3,2,1,0:T(8,128)S(1)}, f32[1,8,128,128]{3,2,1,0:T(8,128)}, u32[]{:S(2)}) copy-start(f32[1,8,128,128]{3,2,1,0:T(8,128)} %get-tuple-element.189) | copy-start | bytes 1572868
  152.9 48.6 %collective-permute-start.5 = (bf16[4,64,2048]{2,1,0:T(8,128)(2,1)}, bf16[4,64,2048]{2,1,0:T(8,128)(2,1)}, u32[]{:S(2)}, u32[]{:S(2)}) collective-permute-start(bf16[4,64,2048]{2,1,0:T(8,128)(2,1)} %bitcast.29.refs_0_), channel_id=1, source_target_pairs={{0,16},{16,0},{1,17},{17,1},{2,18},{18,2},{3,19},{19,3},{4,20},{20... | collective-permute-start | bytes 3145736 | tf_op jit(solution)/shard_map/ppermute | solution.py:1292
  152.9 48.6 %collective-permute-start.4 = (bf16[4,64,2048]{2,1,0:T(8,128)(2,1)}, bf16[4,64,2048]{2,1,0:T(8,128)(2,1)}, u32[]{:S(2)}, u32[]{:S(2)}) collective-permute-start(bf16[4,64,2048]{2,1,0:T(8,128)(2,1)} %bitcast.29.refs_0_), channel_id=1, source_target_pairs={{0,8},{8,0},{1,9},{9,1},{2,10},{10,2},{3,11},{11,3},{4,12},{12,4},... | collective-permute-start | bytes 3145736 | tf_op jit(solution)/shard_map/ppermute | solution.py:1292
  165.0 37.1 %collective-permute-start.9 = (bf16[4,64,2048]{2,1,0:T(8,128)(2,1)}, bf16[4,64,2048]{2,1,0:T(8,128)(2,1)}, u32[]{:S(2)}, u32[]{:S(2)}) collective-permute-start(bf16[4,64,2048]{2,1,0:T(8,128)(2,1)} %collective-permute-done.7.refs_4_), channel_id=1, source_target_pairs={{0,16},{16,0},{1,17},{17,1},{2,18},{18,2},{3,19},{19,3},{4,20},{20... | collective-permute-start | bytes 3145736 | tf_op jit(solution)/shard_map/ppermute | solution.py:1292
  165.5 26.3 %copy-start.14 = (s32[3]{0:T(128)}, s32[3]{0:T(128)S(1)}, u32[]{:S(2)}) copy-start(s32[3]{0:T(128)S(1)} %get-tuple-element.195.lengths_ref) | copy-start | bytes 40
  165.5 36.6 %copy-start.13 = (s32[3]{0:T(128)}, s32[3]{0:T(128)S(1)}, u32[]{:S(2)}) copy-start(s32[3]{0:T(128)S(1)} %get-tuple-element.196.lengths_ref) | copy-start | bytes 40
  165.6 36.6 %copy-start.11 = (f32[12,256]{1,0:T(8,128)}, f32[12,256]{1,0:T(8,128)S(1)}, u32[]{:S(2)}) copy-start(f32[12,256]{1,0:T(8,128)S(1)} %reshape.273.tap_ref) | copy-start | bytes 36868
  165.6 36.6 %copy-start.15 = (f32[2,128]{1,0:T(2,128)}, f32[2,128]{1,0:T(2,128)S(1)}, u32[]{:S(2)}) copy-start(f32[2,128]{1,0:T(2,128)S(1)} %convert_element_type.103.gain_ref) | copy-start | bytes 3076
  195.8 36.5 %all-to-all-start.1 = ((bf16[8,128,256]{2,1,0:T(8,128)(2,1)}), bf16[8,128,256]{2,1,0:T(8,128)(2,1)S(1)}, u32[]{:S(2)}, u32[]{:S(2)}) async-start(bf16[8,128,256]{2,1,0:T(8,128)(2,1)} %bitcast.11), calls=%async_computation.1 | async-start | bytes 1048576 | tf_op jit(solution)/shard_map/all_to_all | solution.py:1447
  199.4 39.0 %collective-permute-start.11 = (bf16[256,2048]{1,0:T(8,128)(2,1)}, bf16[256,2048]{1,0:T(8,128)(2,1)S(1)}, u32[]{:S(2)}, u32[]{:S(2)}) collective-permute-start(bf16[256,2048]{1,0:T(8,128)(2,1)} %bitcast.28.refs_0_.c_ref), channel_id=1, source_target_pairs={{0,1},{1,0},{2,3},{3,2},{4,5},{5,4},{6,7},{7,6},{8,9},{9,8},{10,11... | collective-permute-start | bytes 3145736 | tf_op jit(solution)/shard_map/ppermute | solution.py:1292
  201.4 51.5 %collective-permute-start.12 = (bf16[256,2048]{1,0:T(8,128)(2,1)}, bf16[256,2048]{1,0:T(8,128)(2,1)}, u32[]{:S(2)}, u32[]{:S(2)}) collective-permute-start(bf16[256,2048]{1,0:T(8,128)(2,1)} %collective-permute-done.3.refs_1_), channel_id=1, source_target_pairs={{0,1},{1,0},{2,3},{3,2},{4,5},{5,4},{6,7},{7,6},{8,9},{9,8},{10,11... | collective-permute-start | bytes 3145736 | tf_op jit(solution)/shard_map/ppermute | solution.py:1292
  201.5 51.9 %collective-permute-start.8 = (bf16[4,64,2048]{2,1,0:T(8,128)(2,1)}, bf16[4,64,2048]{2,1,0:T(8,128)(2,1)}, u32[]{:S(2)}, u32[]{:S(2)}) collective-permute-start(bf16[4,64,2048]{2,1,0:T(8,128)(2,1)} %collective-permute-done.7.refs_4_), channel_id=1, source_target_pairs={{0,8},{8,0},{1,9},{9,1},{2,10},{10,2},{3,11},{11,3},{4,12},{12,4},... | collective-permute-start | bytes 3145736 | tf_op jit(solution)/shard_map/ppermute | solution.py:1292
  201.6 51.3 %collective-permute-start.6 = (bf16[4,64,2048]{2,1,0:T(8,128)(2,1)}, bf16[4,64,2048]{2,1,0:T(8,128)(2,1)}, u32[]{:S(2)}, u32[]{:S(2)}) collective-permute-start(bf16[4,64,2048]{2,1,0:T(8,128)(2,1)} %collective-permute-done.5.refs_2_), channel_id=1, source_target_pairs={{0,8},{8,0},{1,9},{9,1},{2,10},{10,2},{3,11},{11,3},{4,12},{12,4},... | collective-permute-start | bytes 3145736 | tf_op jit(solution)/shard_map/ppermute | solution.py:1292
  202.1 68.4 %collective-permute-start.10 = (bf16[4,64,2048]{2,1,0:T(8,128)(2,1)}, bf16[4,64,2048]{2,1,0:T(8,128)(2,1)}, u32[]{:S(2)}, u32[]{:S(2)}) collective-permute-start(bf16[4,64,2048]{2,1,0:T(8,128)(2,1)} %collective-permute-done.9.refs_6_), channel_id=1, source_target_pairs={{0,8},{8,0},{1,9},{9,1},{2,10},{10,2},{3,11},{11,3},{4,12},{12,4},... | collective-permute-start | bytes 3145736 | tf_op jit(solution)/shard_map/ppermute | solution.py:1292
  232.3 45.0 %copy-start.4 = (bf16[8,128,256]{2,1,0:T(8,128)(2,1)}, bf16[8,128,256]{2,1,0:T(8,128)(2,1)S(1)}, u32[]{:S(2)}) copy-start(bf16[8,128,256]{2,1,0:T(8,128)(2,1)S(1)} %all-to-all-done.1.second_ref) | copy-start | bytes 1572868
  232.3 38.2 %all-to-all-start = ((bf16[8,128,256]{2,1,0:T(8,128)(2,1)}), bf16[8,128,256]{2,1,0:T(8,128)(2,1)S(1)}, u32[]{:S(2)}, u32[]{:S(2)}) async-start(bf16[8,128,256]{2,1,0:T(8,128)(2,1)} %bitcast.7), calls=%async_computation | async-start | bytes 1048576 | tf_op jit(solution)/shard_map/all_to_all | solution.py:1447
  238.2 378.5 %reduce-scatter.2.cloned.1.call-start = ((), (), s32[]{:S(2)}) async-start(), calls=%async_computation.6 | async-start | bytes 10813440 | tf_op jit(solution)/shard_map/reduce_scatter | solution.py:1453
  238.4 38.9 %copy-start.57 = (bf16[256,2048]{1,0:T(8,128)(2,1)}, bf16[256,2048]{1,0:T(8,128)(2,1)S(1)}, u32[]{:S(2)}) copy-start(bf16[256,2048]{1,0:T(8,128)(2,1)S(1)} %collective-permute-done.11.refs_2_) | copy-start | bytes 3145732
  238.4 44.4 %collective-permute-start.13 = (bf16[256,2048]{1,0:T(8,128)(2,1)}, bf16[256,2048]{1,0:T(8,128)(2,1)}, u32[]{:S(2)}, u32[]{:S(2)}) collective-permute-start(bf16[256,2048]{1,0:T(8,128)(2,1)} %bitcast.28.refs_0_.c_ref), channel_id=1, source_target_pairs={{0,8},{8,0},{1,9},{9,1},{2,10},{10,2},{3,11},{11,3},{4,12},{12,4},... | collective-permute-start | bytes 3145736 | tf_op jit(solution)/shard_map/ppermute | solution.py:1292
  252.9 30.0 %collective-permute-start.14 = (bf16[256,2048]{1,0:T(8,128)(2,1)}, bf16[256,2048]{1,0:T(8,128)(2,1)}, u32[]{:S(2)}, u32[]{:S(2)}) collective-permute-start(bf16[256,2048]{1,0:T(8,128)(2,1)} %collective-permute-done.3.refs_1_), channel_id=1, source_target_pairs={{0,8},{8,0},{1,9},{9,1},{2,10},{10,2},{3,11},{11,3},{4,12},{12,4},... | collective-permute-start | bytes 3145736 | tf_op jit(solution)/shard_map/ppermute | solution.py:1292
  252.9 30.0 %collective-permute-start.15 = (bf16[256,2048]{1,0:T(8,128)(2,1)S(1)}, bf16[256,2048]{1,0:T(8,128)(2,1)}, u32[]{:S(2)}, u32[]{:S(2)}) collective-permute-start(bf16[256,2048]{1,0:T(8,128)(2,1)S(1)} %collective-permute-done.11.refs_2_), channel_id=1, source_target_pairs={{0,8},{8,0},{1,9},{9,1},{2,10},{10,2},{3,11},{11,3},{4,12},{12,4},... | collective-permute-start | bytes 3145736 | tf_op jit(solution)/shard_map/ppermute | solution.py:1292
  253.4 29.5 %collective-permute-start.16 = (bf16[256,2048]{1,0:T(8,128)(2,1)}, bf16[256,2048]{1,0:T(8,128)(2,1)}, u32[]{:S(2)}, u32[]{:S(2)}) collective-permute-start(bf16[256,2048]{1,0:T(8,128)(2,1)} %collective-permute-done.12.refs_3_), channel_id=1, source_target_pairs={{0,8},{8,0},{1,9},{9,1},{2,10},{10,2},{3,11},{11,3},{4,12},{12,4},... | collective-permute-start | bytes 3145736 | tf_op jit(solution)/shard_map/ppermute | solution.py:1292
  463.3 67.0 %collective-permute-start.17 = (bf16[4,2,2,64,2048]{4,3,0,1,2:T(8,128)(2,1)}, bf16[4,2,2,64,2048]{4,3,0,1,2:T(8,128)(2,1)}, u32[]{:S(2)}, u32[]{:S(2)}) collective-permute-start(bf16[4,2,2,64,2048]{4,3,0,1,2:T(8,128)(2,1)} %bitcast.118), channel_id=1, source_target_pairs={{0,8},{8,0},{1,9},{9,1},{2,10},{10,2},{3,11},{11,3},{4,12},{12,4},... | collective-permute-start | bytes 12582920 | tf_op jit(solution)/shard_map/ppermute | solution.py:1292
  465.4 31.4 %all-to-all-start.3 = ((bf16[8,128,256]{2,1,0:T(8,128)(2,1)}), bf16[8,128,256]{2,1,0:T(8,128)(2,1)S(1)}, u32[]{:S(2)}, u32[]{:S(2)}) async-start(bf16[8,128,256]{2,1,0:T(8,128)(2,1)} %get-tuple-element.94), calls=%async_computation.3 | async-start | bytes 1048576 | tf_op jit(solution)/shard_map/all_to_all | solution.py:1480
  496.8 40.1 %all-to-all-start.2 = ((bf16[8,128,256]{2,1,0:T(8,128)(2,1)}), bf16[8,128,256]{2,1,0:T(8,128)(2,1)S(1)}, u32[]{:S(2)}, u32[]{:S(2)}) async-start(bf16[8,128,256]{2,1,0:T(8,128)(2,1)} %get-tuple-element.85), calls=%async_computation.2 | async-start | bytes 1048576 | tf_op jit(solution)/shard_map/all_to_all | solution.py:1480
  502.4 27.9 %copy-start.28 = (bf16[4,2,2,1,64,2048]{5,4,3,2,1,0:T(8,128)(2,1)S(1)}, bf16[4,2,2,1,64,2048]{5,4,3,2,1,0:T(8,128)(2,1)}, u32[]{:S(2)}) copy-start(bf16[4,2,2,1,64,2048]{5,4,3,2,1,0:T(8,128)(2,1)} %get-tuple-element.162) | copy-start | bytes 12582916
  538.8 48.7 %collective-permute-start.18 = (bf16[4,2,64,2048]{3,2,0,1:T(8,128)(2,1)S(1)}, bf16[4,2,64,2048]{3,2,0,1:T(8,128)(2,1)S(1)}, u32[]{:S(2)}, u32[]{:S(2)}) collective-permute-start(bf16[4,2,64,2048]{3,2,0,1:T(8,128)(2,1)S(1)} %dynamic-slice_bitcast_fusion), channel_id=1, source_target_pairs={{0,16},{16,0},{1,17},{17,1},{2,18},{18,2},{3,19},{19,3},{4,20},{20... | collective-permute-start | bytes 6291464 | tf_op jit(solution)/shard_map/ppermute | solution.py:1292
  540.3 27.9 %copy-start.33 = (bf16[1024,1024]{1,0:T(8,128)(2,1)S(1)}, bf16[1024,1024]{1,0:T(8,128)(2,1)}, u32[]{:S(2)}) copy-start(bf16[1024,1024]{1,0:T(8,128)(2,1)} %get-tuple-element.100) | copy-start | bytes 6291460
  540.3 30.1 %copy-start.38 = (bf16[1024,128]{1,0:T(8,128)(2,1)S(1)}, bf16[1024,128]{1,0:T(8,128)(2,1)}, u32[]{:S(2)}) copy-start(bf16[1024,128]{1,0:T(8,128)(2,1)} %get-tuple-element.104) | copy-start | bytes 786436
  568.2 23.2 %slice-start = ((s8[8388608]{0:T(1024)(128)(4,1)}), s8[4194304]{0:T(1024)(128)(4,1)S(1)}, s32[]{:S(2)}) async-start(s8[8388608]{0:T(1024)(128)(4,1)} %bitcast.130), calls=%async_computation.7 | async-start | bytes 8388608
  573.7 17.7 %slice-start.1 = ((s8[8388608]{0:T(1024)(128)(4,1)}), s8[4194304]{0:T(1024)(128)(4,1)S(1)}, s32[]{:S(2)}) async-start(s8[8388608]{0:T(1024)(128)(4,1)} %bitcast.130), calls=%async_computation.8 | async-start | bytes 8388608
  589.4 24.8 %collective-permute-start.19 = (bf16[4,64,2048]{2,1,0:T(8,128)(2,1)}, bf16[4,64,2048]{2,1,0:T(8,128)(2,1)}, u32[]{:S(2)}, u32[]{:S(2)}) collective-permute-start(bf16[4,64,2048]{2,1,0:T(8,128)(2,1)} %dynamic-slice_bitcast_fusion.1), channel_id=1, source_target_pairs={{0,1},{1,0},{2,3},{3,2},{4,5},{5,4},{6,7},{7,6},{8,9},{9,8},{10,11... | collective-permute-start | bytes 3145736 | tf_op jit(solution)/shard_map/ppermute | solution.py:1292
  627.8 159.2 %collective-permute-start.20 = (bf16[528,512]{1,0:T(8,128)(2,1)}, bf16[528,512]{1,0:T(8,128)(2,1)}, u32[]{:S(2)}, u32[]{:S(2)}) collective-permute-start(bf16[528,512]{1,0:T(8,128)(2,1)} %bitcast.121), channel_id=1, source_target_pairs={{0,8},{8,0},{16,24},{24,16},{1,9},{9,1},{17,25},{25,17},{2,10},{10... | collective-permute-start | bytes 1622024 | tf_op jit(solution)/shard_map/ppermute | solution.py:1292
  628.8 158.3 %collective-permute-start.21 = (bf16[528,512]{1,0:T(8,128)(2,1)}, bf16[528,512]{1,0:T(8,128)(2,1)}, u32[]{:S(2)}, u32[]{:S(2)}) collective-permute-start(bf16[528,512]{1,0:T(8,128)(2,1)} %bitcast.120), channel_id=1, source_target_pairs={{0,16},{8,24},{16,0},{24,8},{1,17},{9,25},{17,1},{25,9},{2,18},{10... | collective-permute-start | bytes 1622024 | tf_op jit(solution)/shard_map/ppermute | solution.py:1292
  630.4 156.6 %collective-permute-start.22 = (bf16[528,512]{1,0:T(8,128)(2,1)}, bf16[528,512]{1,0:T(8,128)(2,1)}, u32[]{:S(2)}, u32[]{:S(2)}) collective-permute-start(bf16[528,512]{1,0:T(8,128)(2,1)} %bitcast.119), channel_id=1, source_target_pairs={{0,24},{8,16},{16,8},{24,0},{1,25},{9,17},{17,9},{25,1},{2,26},{10... | collective-permute-start | bytes 1622024 | tf_op jit(solution)/shard_map/ppermute | solution.py:1292
  (42 other events, 165.8 us)
Sparse Core Ops, SparseCore 0:
  141.3 173.0 all-gather.1
  438.7 164.2 reduce-scatter.1

commit v5 on v4

--- a/solution.py
+++ b/solution.py
@@ -379,18 +379,19 @@
     return {axis_name: 1 - lax.axis_index(axis_name)}
 
 
-def ffn_kernel(x_ref, w_ref, c_refs, out_ref, ngrad_ref, wgrad_ref,
-               xs, cs, ws, inner_s, gate_s, up_s, acts_t, part, crecv, drecv, nrecv, stage, ctile,
-               ag_send, ag_recv, pair_send, pair_recv, rs_send, rs_recv, c_sem, w_sem, g_sem, t_sem):
+def ffn_kernel(x_ref, w_ref, down_ref, c_refs, out_ref, ngrad_ref, wgrad_ref, down_out,
+               xs, cs, ws, gu, inner_s, gate_s, up_s, acts_t, part, crecv, drecv, nrecv, stage,
+               ag_send, ag_recv, pair_send, pair_recv, rs_send, rs_recv, c_sem, w_sem, g_sem, t_sem,
+               down_right, down_left, down_recv, down_sem, sum_sems, keep_sem, out_sem, ready):
     half = xs.shape[1] // 2
     rows = 2 * half
     model = xs.shape[2]
     hidden = ws.shape[1]
     lines = w_ref.shape[0]
-    quarter = w_ref.shape[2]
+    parts, _, quarter, width = w_ref.shape[1:]
     tile_f = 256
     tile_d = min(512, model)
-    tile_w = min(256, model)
+    tile_w = min(256, width)
 
     def remote(src, dst, send, recv, axis_name):
         return pltpu.make_async_remote_copy(
@@ -400,21 +401,50 @@
     def halves(ref, index, h):
         return ref.at[index, pl.ds(h * half, half)]
 
-    barrier = pltpu.get_barrier_semaphore()
-    for axis_name in ("core", "x", "y"):
-        pl.semaphore_signal(
-            barrier, inc=1, device_id=other(axis_name), device_id_type=pl.DeviceIdType.MESH)
-
-    weight_copies = [
-        pltpu.make_async_copy(
-            w_ref.at[line, kind], ws.at[kind, pl.ds(line * quarter, quarter)], w_sem.at[line, kind])
-        for line in range(lines) for kind in range(3)
-    ]
+    o = lax.axis_index("z")
+
+    def down_rows(z):
+        return ws.at[2, pl.ds(pl.multiple_of(z * quarter, 16), quarter)]
+
+    def down_pass(z, right):
+        send = down_right if right else down_left
+        return pltpu.make_async_remote_copy(
+            src_ref=down_rows(z), dst_ref=down_rows(z), send_sem=send.at[z], recv_sem=down_recv.at[z],
+            device_id={"z": o + 1 if right else o - 1}, device_id_type=pl.DeviceIdType.MESH)
+
+    def down_forward(z, right):
+        @pl.when(o < lines - 1 if right else o > 0)
+        def _():
+            down_pass(z, right).start()
+
+    def down_step(far):
+        for side in (-1, 1):
+            z = o + side * far
+
+            @pl.when((z >= 0) & (z < lines))
+            def _():
+                down_pass(z, side < 0).wait_recv()
+                down_forward(z, side < 0)
+
+    weight_copies, down_copies = [], []
+    for r in range(parts):
+        cols = pl.ds(r * width, width)
+        for line in range(lines):
+            weight_copies.append(pltpu.make_async_copy(
+                w_ref.at[line, r], ws.at[pl.ds(0, 2), pl.ds(line * quarter, quarter), cols],
+                w_sem.at[line, r]))
+        down_copies.append(pltpu.make_async_copy(
+            down_ref.at[r], down_rows(o).at[:, cols], down_sem.at[r]))
+    for copy in down_copies:
+        copy.start()
     for copy in weight_copies:
         copy.start()
 
+    def pair_at(turn):
+        return jnp.where(turn < 2, 3 - 2 * turn, 6 - 2 * turn)
+
     def slot_of(step):
-        return (1 - lax.rem(step, 2)) * 4 + step // 2
+        return (1 - lax.rem(step, 2)) * 4 + pair_at(step // 2)
 
     def c_copy(step, n):
         buffer = lax.rem(step, 2)
@@ -426,8 +456,8 @@
             def _():
                 c_copy(step, n).start()
 
-    c_copy(0, 4).start()
-    pl.semaphore_wait(barrier, 3)
+    c_copy(0, 7).start()
+    line_barrier(lines, [other(name) for name in ("core", "x", "y")])
 
     own_pair = remote(x_ref, xs.at[4], ag_send.at[0], ag_recv.at[0], "core")
     own_x = [remote(x_ref.at[pl.ds(h * half, half)], halves(xs, 1, h), ag_send.at[1 + h], ag_recv.at[1 + h], "x") for h in range(2)]
@@ -440,14 +470,19 @@
     own_y[1].start()
     own_x[1].start()
     own_y[0].start()
+    for copy in down_copies:
+        copy.wait()
+    down_forward(o, True)
+    down_forward(o, False)
     own_copy = pltpu.make_async_copy(x_ref, xs.at[0], t_sem.at[0, 0])
     own_copy.start()
     own_copy.wait()
     for copy in weight_copies:
         copy.wait()
 
-    def part_send(j):
-        return remote(part.at[lax.rem(j, 2)], crecv.at[j], pair_send.at[j], pair_recv.at[j], "core")
+    def part_send(turn):
+        j = pair_at(turn)
+        return remote(part.at[lax.rem(turn, 2)], crecv.at[j], pair_send.at[j], pair_recv.at[j], "core")
 
     x_sends = [[remote(crecv.at[1, a, pl.ds(h * half, half)], nrecv.at[0, a, pl.ds(h * half, half)],
                        rs_send.at[a * 2 + h], rs_recv.at[a * 2 + h], "x") for a in range(2)] for h in range(2)]
@@ -456,22 +491,28 @@
     d_sends = [[remote(crecv.at[3, a, pl.ds(h * half, half)], drecv.at[a, pl.ds(h * half, half)],
                        rs_send.at[8 + a * 2 + h], rs_recv.at[8 + a * 2 + h], ("x", "y")[h]) for a in range(2)] for h in range(2)]
 
-    @pl.loop(0, 8)
-    def _(step):
-        j = step // 2
+    def place_of(step):
+        return jnp.where(step >= 6, step - 4, lax.rem(step, 2))
+
+    def gates(step):
         slot = slot_of(step)
-        pairing = lax.rem(step, 2) == 0
-
-        @pl.when(step < 7)
-        def _():
-            c_start(step + 1)
-
-        @pl.when(step == 0)
+        for start in range(0, hidden, tile_f):
+            cols = slice(start, min(start + tile_f, hidden))
+            for kind in range(2):
+                gu[place_of(step), kind, :, cols] = lax.dot_general(
+                    xs[slot], ws[kind, cols, :], NT, preferred_element_type=f32)
+
+    @pl.loop(0, 4)
+    def _(early):
+        step = jnp.where(early < 2, 6 + early, 3 - early)
+
+        @pl.when(early == 0)
         def _():
             own_pair.wait_recv()
 
-        @pl.when(step == 2)
-        def _():
+        @pl.when(early == 2)
+        def _():
+            down_step(1)
             own_x[0].wait_recv()
             relay_y.start()
             own_y[1].wait_recv()
@@ -480,27 +521,54 @@
             pair_of[1].start()
             own_y[0].wait_recv()
             pair_of[2].start()
-            pair_of[1].wait_recv()
-
-        @pl.when(step == 4)
-        def _():
+            if lines > 2:
+                down_step(2)
             relay_y.wait_recv()
             relay_x.wait_recv()
             pair_of[3].start()
-            pair_of[2].wait_recv()
-
-        @pl.when(step == 6)
+
+        @pl.when(early == 3)
         def _():
             pair_of[3].wait_recv()
+        gates(step)
+
+    pair_of[1].wait_recv()
+    pair_of[2].wait_recv()
+    for far in range(3, lines):
+        down_step(far)
+
+    tiles = model // tile_w
+
+    def c_tile(t):
+        buffer = lax.rem(t, 2)
+        cols = pl.ds(pl.multiple_of(t * tile_w, tile_w), tile_w)
+        return [
+            pltpu.make_async_copy(
+                ref.at[:, cols], part.at[0, buffer, :, pl.ds(n * tile_w, tile_w)], t_sem.at[buffer, n])
+            for n, ref in enumerate(c_refs)]
+
+    @pl.loop(0, 8)
+    def _(step):
+        turn = step // 2
+        j = pair_at(turn)
+        slot = slot_of(step)
+        pairing = lax.rem(step, 2) == 0
+
+        @pl.when(step < 7)
+        def _():
+            c_start(step + 1)
+
+        @pl.when((step >= 2) & (step < 6))
+        def _():
+            gates(step)
 
         c_copy(step, 0).wait()
 
         for start in range(0, hidden, tile_f):
             size = min(tile_f, hidden - start)
             cols = slice(start, start + size)
-            x = xs[slot]
-            gate = lax.dot_general(x, ws[0, cols, :], NT, preferred_element_type=f32)
-            up = lax.dot_general(x, ws[1, cols, :], NT, preferred_element_type=f32)
+            gate = gu[place_of(step), 0, :, cols]
+            up = gu[place_of(step), 1, :, cols]
             grad = lax.dot_general(cs[lax.rem(step, 2)], ws[2, cols, :], NT, preferred_element_type=f32)
             sg = sigmoid(gate)
             silu = gate * sg
@@ -514,9 +582,9 @@
 
         @pl.when(pairing & (step >= 4))
         def _():
-            part_send(j - 2).wait_send()
-
-        place = jnp.where(pairing, lax.rem(j, 2), 2)
+            part_send(turn - 2).wait_send()
+
+        place = jnp.where(pairing, lax.rem(turn, 2), 2)
         for start in range(0, model, tile_d):
             cols = slice(start, start + tile_d)
             part[place, 0, :, cols] = jnp.dot(
@@ -528,11 +596,11 @@
 
         @pl.when(pairing)
         def _():
-            part_send(j).start()
+            part_send(turn).start()
 
         @pl.when(jnp.logical_not(pairing))
         def _():
-            part_send(j).wait_recv()
+            part_send(turn).wait_recv()
             for a in range(2):
                 for start in range(0, model, tile_d):
                     cols = slice(start, start + tile_d)
@@ -540,70 +608,141 @@
                         crecv[j, a, :, cols].astype(f32) + part[2, a, :, cols].astype(f32)
                     ).astype(bf16)
 
-        @pl.when(step == 3)
-        def _():
-            for copy in x_sends[0]:
-                copy.start()
-
-        @pl.when(step == 5)
-        def _():
-            for copy in y_sends[1]:
-                copy.start()
-
-        @pl.when(step == 7)
+        @pl.when(step == 1)
         def _():
             for h in range(2):
                 for copy in d_sends[h]:
                     copy.start()
 
-    tiles = model // tile_w
-
-    def c_tile(t):
-        buffer = lax.rem(t, 2)
-        cols = pl.ds(pl.multiple_of(t * tile_w, tile_w), tile_w)
-        return [
-            pltpu.make_async_copy(ref.at[:, cols], ctile.at[buffer, n], t_sem.at[buffer, n])
-            for n, ref in enumerate(c_refs)]
+        @pl.when(step == 3)
+        def _():
+            for copy in x_sends[0]:
+                copy.start()
+
+        @pl.when(step == 5)
+        def _():
+            for copy in y_sends[1]:
+                copy.start()
+
+        @pl.when(step == 6)
+        def _():
+            part_send(2).wait_send()
+            for t in range(2):
+                for copy in c_tile(t):
+                    copy.start()
 
     def grad_copy(kind, t, line):
         return pltpu.make_async_copy(
             stage.at[lax.rem(t, 2), pl.ds(line * quarter, quarter)],
-            wgrad_ref.at[line, kind, :, pl.ds(pl.multiple_of(t * tile_w, tile_w), tile_w)],
+            wgrad_ref.at[line, t * tile_w // width, kind, :,
+                         pl.ds(pl.multiple_of(lax.rem(t * tile_w, width), tile_w), tile_w)],
             g_sem.at[lax.rem(t, 2), line])
 
     def weight_grads(kind):
-        if kind == 2:
-            for copy in c_tile(0):
-                copy.start()
-
         @pl.loop(0, tiles)
         def _(t):
             if kind == 2:
-                @pl.when(t + 1 < tiles)
-                def _():
-                    for copy in c_tile(t + 1):
-                        copy.start()
                 for copy in c_tile(t):
                     copy.wait()
-                right = ctile[lax.rem(t, 2)].reshape(8 * rows, tile_w)
+                right = jnp.concatenate(
+                    [part[0, lax.rem(t, 2), :, n * tile_w : (n + 1) * tile_w] for n in range(8)])
             else:
                 right = xs[:, :, pl.ds(pl.multiple_of(t * tile_w, tile_w), tile_w)].reshape(8 * rows, tile_w)
 
-            @pl.when(t >= 2)
-            def _():
+            if kind < 2:
+                @pl.when(t >= 2)
+                def _():
+                    for line in range(lines):
+                        grad_copy(kind, t - 2, line).wait()
+
+            value = jnp.dot(acts_t[kind], right, preferred_element_type=f32).astype(bf16)
+            if kind == 2:
+                @pl.when(t + 2 < tiles)
+                def _():
+                    for copy in c_tile(t + 2):
+                        copy.start()
+            if kind < 2:
+                stage[lax.rem(t, 2)] = value
                 for line in range(lines):
-                    grad_copy(kind, t - 2, line).wait()
-
-            stage[lax.rem(t, 2)] = jnp.dot(
-                acts_t[kind], right, preferred_element_type=f32).astype(bf16)
-            for line in range(lines):
-                grad_copy(kind, t, line).start()
-
+                    grad_copy(kind, t, line).start()
+            else:
+                ws[0, :, pl.ds(pl.multiple_of(t * tile_w, tile_w), tile_w)] = value
+
+        if kind == 2:
+            return
         for t in range(max(tiles - 2, 0), tiles):
             for line in range(lines):
                 grad_copy(kind, t, line).wait()
 
-    weight_grads(0)
+    @pl.loop(0, lines)
+    def _(z):
+        @pl.when((o < lines - 1) & (z <= o))
+        def _():
+            down_pass(z, True).wait_send()
+
+        @pl.when((o > 0) & (z >= o))
+        def _():
+            down_pass(z, False).wait_send()
+
+    mesh_id = pl.DeviceIdType.MESH
+
+    @pl.when(o > 0)
+    def _():
+        pl.semaphore_signal(ready, inc=1, device_id={"z": o - 1}, device_id_type=mesh_id)
+
+    @pl.when(o < lines - 1)
+    def _():
+        pl.semaphore_signal(ready, inc=1, device_id={"z": o + 1}, device_id_type=mesh_id)
+
+    def rows_of(n, z):
+        return ws.at[n, pl.ds(pl.multiple_of(z * quarter, 16), quarter)]
+
+    def sum_pass(z, right):
+        side = 0 if right else 2
+        return pltpu.make_async_remote_copy(
+            src_ref=rows_of(0, z), dst_ref=rows_of(1 if right else 2, z),
+            send_sem=sum_sems.at[side, z], recv_sem=sum_sems.at[side + 1, z],
+            device_id={"z": o + 1 if right else o - 1}, device_id_type=mesh_id)
+
+    def sum_add(z, n):
+        at = pl.ds(pl.multiple_of(z * quarter, 16), quarter)
+        for start in range(0, model, tile_d):
+            cols = slice(start, start + tile_d)
+            ws[0, at, cols] = (ws[0, at, cols].astype(f32) + ws[n, at, cols].astype(f32)).astype(bf16)
+
+    def sum_tick(k):
+        z_right = lines - 1 - k + o
+
+        @pl.when(o <= k)
+        def _():
+            @pl.when(o > 0)
+            def _():
+                sum_pass(z_right, True).wait_recv()
+                sum_add(z_right, 1)
+
+            @pl.when(o < k)
+            def _():
+                sum_pass(z_right + 1, True).wait_send()
+            sum_pass(z_right, True).start()
+
+        back = lines - 1 - o
+        z_left = k - back
+
+        @pl.when(back <= k)
+        def _():
+            @pl.when(back > 0)
+            def _():
+                sum_pass(z_left, False).wait_recv()
+                sum_add(z_left, 2)
+
+            @pl.when(back < k)
+            def _():
+                sum_pass(z_left - 1, False).wait_send()
+            sum_pass(z_left, False).start()
+
+    weight_grads(2)
+    pl.semaphore_wait(ready, (o > 0).astype(jnp.int32) + (o < lines - 1).astype(jnp.int32))
+    sum_tick(0)
     for h in range(2):
         j = 2 - h
         for a in range(2):
@@ -613,18 +752,31 @@
                 crecv[j, a, at, :].astype(f32) + drecv[a, at, :].astype(f32)).astype(bf16)
         for copy in (y_sends, x_sends)[h][h]:
             copy.start()
+    weight_grads(0)
+    if lines > 2:
+        sum_tick(1)
     weight_grads(1)
-    weight_grads(2)
+    for k in range(2, lines - 1):
+        sum_tick(k)
+    out_copies = []
     for a, target in enumerate((out_ref, ngrad_ref)):
         for h in range(2):
             x_sends[h][a].wait_recv()
             y_sends[h][a].wait_recv()
-            at = pl.ds(h * half, half)
-            target[at, :] = (
-                crecv[0, a, at, :].astype(f32)
-                + nrecv[0, a, at, :].astype(f32)
-                + nrecv[1, a, at, :].astype(f32)
+        for n in range(model // tile_d):
+            cols = slice(n * tile_d, (n + 1) * tile_d)
+            gu[n, a, :, :tile_d] = (
+                crecv[0, a, :, cols].astype(f32)
+                + nrecv[0, a, :, cols].astype(f32)
+                + nrecv[1, a, :, cols].astype(f32)
             )
+            copy = pltpu.make_async_copy(
+                gu.at[n, a, :, pl.ds(0, tile_d)], target.at[:, pl.ds(n * tile_d, tile_d)],
+                out_sem.at[n, a])
+            copy.start()
+            out_copies.append(copy)
+    for copy in out_copies:
+        copy.wait()
     own_pair.wait_send()
     for h in range(2):
         own_x[h].wait_send()
@@ -637,19 +789,46 @@
     relay_y.wait_send()
     for j in (1, 2, 3):
         pair_of[j].wait_send()
-    part_send(2).wait_send()
     part_send(3).wait_send()
 
-
-def ffn_call_kernel(x_ref, w_ref, *refs):
-    ffn_kernel(x_ref, w_ref, refs[:8], *refs[8:])
-
-
-def ffn_plane(x_own, weights, c_rows):
+    @pl.when(o > 0)
+    def _():
+        sum_pass(o, True).wait_recv()
+        sum_add(o, 1)
+
+    @pl.when(o < lines - 1)
+    def _():
+        sum_pass(o, False).wait_recv()
+        sum_add(o, 2)
+
+    keeps = [
+        pltpu.make_async_copy(
+            rows_of(0, o).at[:, pl.ds(q * width, width)], down_out.at[q], keep_sem.at[q])
+        for q in range(parts)
+    ]
+    for copy in keeps:
+        copy.start()
+
+    @pl.when(o < lines - 1)
+    def _():
+        sum_pass(o + 1, True).wait_send()
+
+    @pl.when(o > 0)
+    def _():
+        sum_pass(o - 1, False).wait_send()
+    for copy in keeps:
+        copy.wait()
+
+
+def ffn_call_kernel(x_ref, w_ref, down_ref, *refs):
+    ffn_kernel(x_ref, w_ref, down_ref, refs[:8], *refs[8:])
+
+
+def ffn_plane(x_own, weights, down_own, c_rows):
     rows, model = x_own.shape
-    lines, _, quarter, _ = weights.shape
+    lines, parts, _, quarter, width = weights.shape
     hidden = lines * quarter
-    tile_w = min(256, model)
+    tile_w = min(256, width)
     sems = pltpu.SemaphoreType.DMA
     anywhere = pl.BlockSpec(memory_space=pl.ANY)
     return pl.pallas_call(
@@ -658,13 +837,15 @@
             jax.ShapeDtypeStruct((rows, model), f32),
             jax.ShapeDtypeStruct((rows, model), f32),
             jax.ShapeDtypeStruct(weights.shape, bf16),
+            jax.ShapeDtypeStruct((parts, quarter, width), bf16),
         ),
-        in_specs=[anywhere] * 10,
-        out_specs=(vmem(), vmem(), anywhere),
+        in_specs=[anywhere] * 11,
+        out_specs=(anywhere,) * 4,
         scratch_shapes=[
             pltpu.VMEM((8, rows, model), bf16),
             pltpu.VMEM((2, rows, model), bf16),
             pltpu.VMEM((3, hidden, model), bf16),
+            pltpu.VMEM((4, 2, rows, max(hidden, min(512, model))), f32),
             pltpu.VMEM((rows, hidden), bf16),
             pltpu.VMEM((rows, hidden), bf16),
             pltpu.VMEM((rows, hidden), bf16),
@@ -674,15 +855,16 @@
             pltpu.VMEM((2, rows, model), bf16),
             pltpu.VMEM((2, 2, rows, model), bf16),
             pltpu.VMEM((2, hidden, tile_w), bf16),
-            pltpu.VMEM((2, 8, rows, tile_w), bf16),
             sems((10,)), sems((10,)), sems((4,)), sems((4,)), sems((12,)), sems((12,)),
-            sems((2,)), sems((lines, 3)), sems((2, lines)), sems((2, 8)),
+            sems((2,)), sems((lines, parts)), sems((2, lines)), sems((2, 8)),
+            sems((lines,)), sems((lines,)), sems((lines,)), sems((parts,)),
+            sems((4, lines)), sems((parts,)), sems((4, 2)), pltpu.SemaphoreType.REGULAR,
         ],
         compiler_params=pltpu.CompilerParams(
-            collective_id=2, has_side_effects=True, vmem_limit_bytes=62 * 2**20),
+            collective_id=2, has_side_effects=True, vmem_limit_bytes=60 * 2**20),
         cost_estimate=pl.CostEstimate(flops=8 * 10**10, bytes_accessed=4 * 10**7, transcendentals=10**6),
         name="ffn_plane",
-    )(x_own, weights, *c_rows)
+    )(x_own, weights, down_own, *c_rows)
 
 
 def line_barrier(lines, others):
@@ -710,15 +892,53 @@
         device_id=target, device_id_type=pl.DeviceIdType.MESH)
 
 
-def gather_kernel(x_ref, o_ref, w_ref, wb_ref, rows_ref, outs_ref, proj_ref, beta_ref,
-                  xs, stage, beta_stage, right_send, left_send, line_recv, pair_send, pair_recv,
-                  own_sem, row_sem, outs_sem, out_sem, beta_sem):
+def pair_peers():
+    x, core = lax.axis_index("x"), lax.axis_index("core")
+    peers = [
+        (x * 2 + 1 - core, {"core": 1 - core}),
+        ((1 - x) * 2 + core, {"x": 1 - x}),
+        ((1 - x) * 2 + 1 - core, {"x": 1 - x, "core": 1 - core}),
+    ]
+    return x * 2 + core, peers
+
+
+class Swap:
+    def __init__(self, pairs, send, recv, own):
+        me, peers = pair_peers()
+        self.own = [
+            pltpu.make_async_copy(source.at[me], target(me), own.at[n])
+            for n, (source, target) in enumerate(pairs)]
+        self.away = [
+            line_copy(source.at[place], target(me), send.at[n, d], recv.at[n, d], device)
+            for n, (source, target) in enumerate(pairs) for d, (place, device) in enumerate(peers)]
+
+    def start(self):
+        for copy in self.away + self.own:
+            copy.start()
+
+    def wait(self):
+        for copy in self.own:
+            copy.wait()
+        for copy in self.away:
+            copy.wait_recv()
+            copy.wait_send()
+
+
+def gather_kernel(x_ref, o_ref, f_refs, w_refs, wb_ref, rows_ref, outs_ref, proj_refs, beta_ref,
+                  pair_ref, down_ref,
+                  xs, parts, stage, beta_stage, right_send, left_send, line_recv, pair_send, pair_recv,
+                  part_right, part_left, part_recv, own_sem, row_sem, outs_sem, out_sem, beta_sem,
+                  swap_send, swap_recv, swap_own):
     lines = xs.shape[0] // 2
     batches, rows, model = x_ref.shape
-    more = o_ref.shape[1]
     o = lax.axis_index("z")
     i = lax.axis_index("y")
-    line_barrier(lines, [other("y")])
+    line_barrier(lines, [other("y")] + [device for _, device in pair_peers()[1]])
+    swap = Swap(
+        [(f_refs[0], lambda place: pair_ref.at[place, 0]),
+         (f_refs[1], lambda place: pair_ref.at[place, 1]),
+         (f_refs[2], lambda place: down_ref.at[place])],
+        swap_send, swap_recv, swap_own)
 
     def right(z, m):
         ref = xs.at[z * 2 + i, m]
@@ -729,13 +949,19 @@
         return line_copy(ref, ref, left_send.at[z, m], line_recv.at[z, m], {"z": o - 1})
 
     def across(z, m):
-        ref = xs.at[z * 2 + i, m, pl.ds(0, rows)]
+        ref = xs.at[z * 2 + i, m]
         return line_copy(ref, ref, pair_send.at[z, m], pair_recv.at[z, m], other("y"))
 
     own = [
-        pltpu.make_async_copy(x_ref, xs.at[o * 2 + i, :, pl.ds(0, rows)], own_sem.at[0]),
-        pltpu.make_async_copy(o_ref, xs.at[o * 2 + i, :, pl.ds(rows, more)], own_sem.at[1]),
+        pltpu.make_async_copy(x_ref, xs.at[o * 2 + i], own_sem.at[0]),
+        pltpu.make_async_copy(o_ref, parts.at[o], own_sem.at[1]),
     ]
+
+    def pass_part(z):
+        ref = parts.at[z]
+        return (line_copy(ref, ref, part_right.at[z], part_recv.at[z], {"z": o + 1}),
+                line_copy(ref, ref, part_left.at[z], part_recv.at[z], {"z": o - 1}))
+
     for copy in own:
         copy.start()
     for copy in own:
@@ -745,15 +971,15 @@
         buffer = lax.rem(turn, 2)
         return [
             copy for m in range(batches) for copy in (
-                pltpu.make_async_copy(stage.at[buffer, m], proj_ref.at[m, slot], out_sem.at[buffer, m]),
+                pltpu.make_async_copy(stage.at[buffer, m], proj_refs[m].at[slot], out_sem.at[buffer, m]),
                 pltpu.make_async_copy(beta_stage.at[buffer, m], beta_ref.at[m, slot], beta_sem.at[buffer, m]))
         ]
 
     def keep(slot, m):
-        return pltpu.make_async_copy(xs.at[slot, m, pl.ds(0, rows)], rows_ref.at[m, slot], row_sem.at[slot, m])
+        return pltpu.make_async_copy(xs.at[slot, m], rows_ref.at[m, slot], row_sem.at[slot, m])
 
     def keep_outs(z):
-        return pltpu.make_async_copy(xs.at[z * 2 + i, :, pl.ds(rows, more)], outs_ref.at[z], outs_sem.at[z])
+        return pltpu.make_async_copy(parts.at[z], outs_ref.at[z], outs_sem.at[z])
 
     def project(turn, slot):
         @pl.when(turn >= 2)
@@ -762,14 +988,12 @@
                 copy.wait()
         for m in range(batches):
             keep(slot, m).start()
-        x = xs[slot, :, :rows].reshape(batches * rows, model)
+        x = xs[slot].reshape(batches * rows, model)
         buffer = lax.rem(turn, 2)
-        width = w_ref.shape[1]
-        tile = min(256, width)
-        for start in range(0, width, tile):
-            cols = slice(start, start + tile)
-            stage[buffer, :, :, cols] = jnp.dot(
-                x, w_ref[:, cols], preferred_element_type=f32).reshape(batches, rows, tile)
+        width = w_refs[0].shape[1]
+        for n, w_ref in enumerate(w_refs):
+            stage[buffer, :, :, n * width : (n + 1) * width] = jnp.dot(
+                x, w_ref[...], preferred_element_type=f32).reshape(batches, rows, width)
         beta_stage[buffer] = jnp.dot(
             x, wb_ref[...], preferred_element_type=f32).reshape(batches, rows, 128)
         for copy in outs(turn, slot):
@@ -800,11 +1024,11 @@
                     left(z, m).start()
 
                 across(z, m).start()
-            keep_outs(z).start()
             project(turn, z * 2 + i)
 
         return turn + valid.astype(jnp.int32)
 
+    swap.start()
     turn = lax.fori_loop(0, 2 * lines - 1, first, jnp.int32(0))
 
     def second(index, turn):
@@ -812,6 +1036,21 @@
 
         @pl.when(valid)
         def _():
+            to_right, to_left = pass_part(z)
+
+            @pl.when(far > 0)
+            def _():
+                to_left.wait_recv()
+
+            @pl.when((o < lines - 1) & (z <= o))
+            def _():
+                to_right.start()
+
+            @pl.when((o > 0) & (z >= o))
+            def _():
+                to_left.start()
+
+            keep_outs(z).start()
             for m in range(batches):
                 across(z, m).wait_recv()
             project(turn, z * 2 + 1 - i)
@@ -826,65 +1065,82 @@
     @pl.loop(0, lines)
     def _(z):
         keep_outs(z).wait()
+
+        @pl.when((o < lines - 1) & (z <= o))
+        def _():
+            pass_part(z)[0].wait_send()
+            for m in range(batches):
+                right(z, m).wait_send()
+
+        @pl.when((o > 0) & (z >= o))
+        def _():
+            pass_part(z)[1].wait_send()
+            for m in range(batches):
+                left(z, m).wait_send()
+
         for m in range(batches):
-            @pl.when((o < lines - 1) & (z <= o))
-            def _():
-                right(z, m).wait_send()
-
-            @pl.when((o > 0) & (z >= o))
-            def _():
-                left(z, m).wait_send()
 
             across(z, m).wait_send()
             for y in range(2):
                 keep(z * 2 + y, m).wait()
 
-
-def gather_project(x, w_out_part, w_inner, w_beta):
+    swap.wait()
+
+
+def gather_call_kernel(x_ref, o_ref, *refs):
+    gather_kernel(x_ref, o_ref, refs[:3], refs[3:7], refs[7], refs[8], refs[9], refs[10:12], *refs[12:])
+
+
+def gather_project(x, w_out_part, ffn_parts, w_inner, w_beta):
     batches, rows, model = x.shape
     more = w_out_part.shape[1]
     lines = lax.axis_size("z")
-    width = w_inner.shape[1]
+    width = sum(w.shape[1] for w in w_inner)
     slots = 2 * lines
     sems = pltpu.SemaphoreType.DMA
     anywhere = pl.BlockSpec(memory_space=pl.ANY)
     pair = sems((lines, batches))
-    gathered, outs, projected, beta = pl.pallas_call(
-        gather_kernel,
+    ranks, quarter, share = ffn_parts[0].shape
+    gathered, outs, *projected, beta, pair_parts, down_part = pl.pallas_call(
+        gather_call_kernel,
         out_shape=(
             jax.ShapeDtypeStruct((batches, slots, rows, model), bf16),
             jax.ShapeDtypeStruct((lines, batches, more, model), bf16),
-            jax.ShapeDtypeStruct((batches, slots, rows, width), f32),
+            *[jax.ShapeDtypeStruct((slots, rows, width), f32)] * batches,
             jax.ShapeDtypeStruct((batches, slots, rows, 128), f32),
+            jax.ShapeDtypeStruct((ranks, 2, quarter, share), bf16),
+            jax.ShapeDtypeStruct((ranks, quarter, share), bf16),
         ),
-        in_specs=[anywhere] * 2 + [vmem()] * 2,
-        out_specs=(anywhere,) * 4,
+        in_specs=[anywhere] * 5 + [vmem()] * 5,
+        out_specs=(anywhere,) * (5 + batches),
         scratch_shapes=[
-            pltpu.VMEM((slots, batches, rows + more, model), bf16),
+            pltpu.VMEM((slots, batches, rows, model), bf16),
+            pltpu.VMEM((lines, batches, more, model), bf16),
             pltpu.VMEM((2, batches, rows, width), f32),
             pltpu.VMEM((2, batches, rows, 128), f32),
-            pair, pair, pair, pair, pair,
+            pair, pair, pair, pair, pair, sems((lines,)), sems((lines,)), sems((lines,)),
             sems((2,)), sems((slots, batches)), sems((lines,)), sems((2, batches)), sems((2, batches)),
+            sems((3, 3)), sems((3, 3)), sems((3,)),
         ],
         compiler_params=pltpu.CompilerParams(
             collective_id=1, has_side_effects=True, vmem_limit_bytes=40 * 2**20),
         cost_estimate=pl.CostEstimate(flops=10**11, bytes_accessed=4 * 10**7, transcendentals=0),
         name="gather_project",
-    )(x, w_out_part, w_inner, w_beta)
+    )(x, w_out_part, *ffn_parts, *w_inner, w_beta)
     total = slots * rows
-    return (gathered.reshape(batches, total, model), outs, projected.reshape(batches, total, width),
-            beta.reshape(batches, total, 128))
-
-
-def scatter_kernel(g_ref, gb_ref, o_ref, inner_ref, w_ref, wb_ref, small_ref, gains_ref,
-                   out_ref, small_out, outs_ref, inner_out,
-                   gs, bs, ysend, yrecv, from_left, from_right, outs_s, inner_s, inner_r, small_s, small_r, gains_r,
+    return (gathered.reshape(batches, total, model), outs,
+            [wide.reshape(total, width) for wide in projected],
+            beta.reshape(batches, total, 128), pair_parts, down_part)
+
+
+def scatter_kernel(w_refs, g_ref, gb_ref, o_ref, inner_ref, wb_ref, small_ref, gains_ref, pair_ref, down_ref,
+                   out_ref, small_out, outs_ref, inner_out, pair_out, down_out,
+                   gs, bs, ysend, yrecv, from_left, from_right, part_sum, part_left, part_right, outs_s, inner_s, inner_r, small_s, small_r, gains_r,
                    pair_send, pair_recv, right_send, left_send, right_recv, left_recv, g_sem,
-                   sum_send, sum_recv, outs_send, outs_recv, gain_send, gain_recv, sum_sem):
+                   sum_send, sum_recv, outs_send, outs_recv, gain_send, gain_recv, part_sems, swap_send, swap_recv, swap_own, sum_sem):
     batches, rows, width = gs.shape
     lines = yrecv.shape[0]
     model = yrecv.shape[3]
-    more = yrecv.shape[2] - rows
     o = lax.axis_index("z")
     i = lax.axis_index("y")
     core = lax.axis_index("core")
@@ -921,6 +1177,10 @@
         line_copy(outs_s, outs_ref.at[me], outs_send.at[n], outs_recv.at[n], target)
         for n, target in enumerate((other("core"), other("x"), diagonal))
     ]
+    swap = Swap(
+        [(pair_ref, lambda place: pair_out.at[place]), (down_ref, lambda place: down_out.at[place])],
+        swap_send, swap_recv, swap_own)
+    swap.start()
     inner_pair.start()
     inner_own.start()
 
@@ -954,11 +1214,14 @@
             b = bs[m]
             for start in range(0, model, tile):
                 cols = slice(start, start + tile)
-                store(m, slice(0, rows), cols, lax.dot_general(g, w_ref[cols, :], NT, preferred_element_type=f32)
-                      + lax.dot_general(b, wb_ref[cols, :], NT, preferred_element_type=f32))
+                value = lax.dot_general(b, wb_ref[cols, :], NT, preferred_element_type=f32)
+                for n, w_ref in enumerate(w_refs):
+                    part = g[:, n * w_ref.shape[1] : (n + 1) * w_ref.shape[1]]
+                    value = value + lax.dot_general(part, w_ref[cols, :], NT, preferred_element_type=f32)
+                store(m, cols, value)
 
     def across(z, m):
-        return line_copy(ysend.at[z, m], yrecv.at[z, m, pl.ds(0, rows)], pair_send.at[z, m], pair_recv.at[z, m], other("y"))
+        return line_copy(ysend.at[z, m], yrecv.at[z, m], pair_send.at[z, m], pair_recv.at[z, m], other("y"))
 
     def right(z, m):
         return line_copy(yrecv.at[z, m], from_left.at[z, m], right_send.at[z, m], right_recv.at[z, m], {"z": o + 1})
@@ -966,44 +1229,106 @@
     def left(z, m):
         return line_copy(yrecv.at[z, m], from_right.at[z, m], left_send.at[z, m], left_recv.at[z, m], {"z": o - 1})
 
-    @pl.loop(0, 2 * lines)
-    def _(index):
+    def across_partial(z):
+        def store(m, cols, value):
+            ysend[z, m, :, cols] = value.astype(bf16)
+        partial_rows(z, 1 - i, store)
+
+    def pass_part(z):
+        return (line_copy(part_sum.at[z], part_left.at[z], part_sems.at[0, z], part_sems.at[1, z], {"z": o + 1}),
+                line_copy(part_sum.at[z], part_right.at[z], part_sems.at[2, z], part_sems.at[3, z], {"z": o - 1}))
+
+    def part_round():
+        @pl.loop(0, 2 * lines)
+        def _(index):
+            far, z, valid = target(index)
+
+            @pl.when(valid & (far > 0))
+            def _():
+                to_right, to_left = pass_part(z)
+
+                @pl.when((z > o) & (o > 0))
+                def _():
+                    to_right.wait_recv()
+                    add_into(part_sum.at[z], part_left.at[z])
+
+                @pl.when((z < o) & (o < lines - 1))
+                def _():
+                    to_left.wait_recv()
+                    add_into(part_sum.at[z], part_right.at[z])
+
+                @pl.when(z > o)
+                def _():
+                    to_right.start()
+
+                @pl.when(z < o)
+                def _():
+                    to_left.start()
+
+        to_right, to_left = pass_part(o)
+        outs_s[...] = part_sum[o]
+
+        @pl.when(o > 0)
+        def _():
+            to_right.wait_recv()
+            add_into(outs_s, part_left.at[o])
+
+        @pl.when(o < lines - 1)
+        def _():
+            to_left.wait_recv()
+            add_into(outs_s, part_right.at[o])
+        outs_keep.start()
+        for copy in outs_away:
+            copy.start()
+
+    def side_work():
+        for z in range(lines):
+            part_sum[z] = o_ref[z]
+        part_round()
+        inner_own.wait()
+        inner_pair.wait_recv()
+        add_into(inner_s, inner_r.at[0])
+        inner_across.start()
+        gains_r[mine] = gains_ref[mine]
+        for copy in gain_copies:
+            copy.wait_recv()
+        tail = small_ref.shape[0]
+        small_s[0, :tail] = small_ref[...]
+        small_s[0, tail:] = jnp.sum(gains_r[...], axis=0)
+        small_pair.start()
+
+    def turn(index, before):
         far, z, valid = target(index)
+        last = index == 2 * lines
+        valid = valid & (index < 2 * lines)
+        ready = (valid | last) & (before >= 0)
 
         @pl.when(valid)
         def _():
-            def store(m, at, cols, value):
-                ysend[z, m, at, cols] = value.astype(bf16)
-            partial_rows(z, 1 - i, store)
+            across_partial(z)
+
+        @pl.when(ready)
+        def _():
+            for m in range(batches):
+                across(before, m).wait_recv()
+
+        @pl.when(valid)
+        def _():
             for m in range(batches):
                 across(z, m).start()
 
-    inner_own.wait()
-    inner_pair.wait_recv()
-    add_into(inner_s, inner_r.at[0])
-    inner_across.start()
-    gains_r[mine] = gains_ref[mine]
-    for copy in gain_copies:
-        copy.wait_recv()
-    tail = small_ref.shape[0]
-    small_s[0, :tail] = small_ref[...]
-    small_s[0, tail:] = jnp.sum(gains_r[...], axis=0)
-    small_pair.start()
-
-    @pl.loop(0, 2 * lines)
-    def _(index):
-        far, z, valid = target(index)
-
-        @pl.when(valid)
-        def _():
-            for m in range(batches):
-                across(z, m).wait_recv()
-
-            def store(m, at, cols, value):
-                yrecv[z, m, at, cols] = (yrecv[z, m, at, cols].astype(f32) + value).astype(bf16)
+        @pl.when(valid & (before < 0))
+        def _():
+            side_work()
+
+        @pl.when(ready)
+        def _():
+            z = before
+
+            def store(m, cols, value):
+                yrecv[z, m, :, cols] = (yrecv[z, m, :, cols].astype(f32) + value).astype(bf16)
             partial_rows(z, i, store)
             for m in range(batches):
-                yrecv[z, m, rows:, :] = o_ref[z, m]
                 @pl.when((z > o) & (o > 0))
                 def _():
                     right(z, m).wait_recv()
@@ -1021,6 +1346,10 @@
                 @pl.when(z < o)
                 def _():
                     left(z, m).start()
+
+        return jnp.where(valid, z, before)
+
+    lax.fori_loop(0, 2 * lines + 1, turn, jnp.int32(-1))
 
     inner_across.wait_recv()
     inner_across.wait_send()
@@ -1032,29 +1361,17 @@
     small_across.start()
 
     for m in range(batches):
+        out_ref[m] = yrecv[o, m].astype(f32)
+
         @pl.when(o > 0)
         def _():
             right(o, m).wait_recv()
+            out_ref[m] += from_left[o, m].astype(f32)
 
         @pl.when(o < lines - 1)
         def _():
             left(o, m).wait_recv()
-
-        out_ref[m] = yrecv[o, m, :rows, :].astype(f32)
-        outs_s[m * more : (m + 1) * more, :] = yrecv[o, m, rows : rows + more, :]
-
-        for side_ref, exists in ((from_left, o > 0), (from_right, o < lines - 1)):
-            @pl.when(exists)
-            def _():
-                out_ref[m] += side_ref[o, m, :rows, :].astype(f32)
-                at = slice(m * more, (m + 1) * more)
-                outs_s[at, :] = (
-                    outs_s[at, :].astype(f32) + side_ref[o, m, rows : rows + more, :].astype(f32)
-                ).astype(bf16)
-
-    outs_keep.start()
-    for copy in outs_away:
-        copy.start()
+            out_ref[m] += from_right[o, m].astype(f32)
 
     @pl.loop(0, lines)
     def _(z):
@@ -1068,6 +1385,14 @@
             @pl.when(z < o)
             def _():
                 left(z, m).wait_send()
+
+        @pl.when(z > o)
+        def _():
+            pass_part(z)[0].wait_send()
+
+        @pl.when(z < o)
+        def _():
+            pass_part(z)[1].wait_send()
 
     small_across.wait_recv()
     small_out[...] = small_s[1] + small_r[1]
@@ -1080,38 +1405,47 @@
     inner_back.wait_send()
     inner_keep.wait()
     outs_keep.wait()
+    swap.wait()
     for copy in outs_away:
         copy.wait_recv()
         copy.wait_send()
 
 
-def scatter_rows(grads, beta_grads, out_grads, inner_grads, w_inner, w_beta, small, gains):
+def scatter_call_kernel(*refs):
+    scatter_kernel(refs[:4], *refs[4:])
+
+
+def scatter_rows(grads, beta_grads, out_grads, inner_grads, w_inner, w_beta, small, gains,
+                 pair_grads, down_grads):
     batches, total, width = grads.shape
-    model = w_inner.shape[0]
+    model = w_inner[0].shape[0]
     lines = lax.axis_size("z")
     slots = 2 * lines
     rows = total // slots
-    more = out_grads.shape[2]
+    more = out_grads.shape[1]
     sems = pltpu.SemaphoreType.DMA
     anywhere = pl.BlockSpec(memory_space=pl.ANY)
-    slab = pltpu.VMEM((lines, batches, rows + more, model), bf16)
+    slab = pltpu.VMEM((lines, batches, rows, model), bf16)
+    part = pltpu.VMEM((lines, more, model), bf16)
     half = inner_grads.shape[1:]
     flat = (small.shape[0] + gains.shape[1], 128)
     return pl.pallas_call(
-        scatter_kernel,
+        scatter_call_kernel,
         out_shape=(
             jax.ShapeDtypeStruct((batches, rows, model), f32),
             jax.ShapeDtypeStruct(flat, f32),
-            jax.ShapeDtypeStruct((4, batches * more, model), bf16),
+            jax.ShapeDtypeStruct((4, more, model), bf16),
             jax.ShapeDtypeStruct(inner_grads.shape, bf16),
+            jax.ShapeDtypeStruct(pair_grads.shape, bf16),
+            jax.ShapeDtypeStruct(down_grads.shape, bf16),
         ),
-        in_specs=[anywhere, anywhere, vmem(), anywhere, vmem(), vmem(), vmem(), vmem()],
-        out_specs=(vmem(), vmem(), anywhere, anywhere),
+        in_specs=[vmem()] * 4 + [anywhere, anywhere, vmem(), anywhere, vmem(), vmem(), vmem(), anywhere, anywhere],
+        out_specs=(vmem(), vmem()) + (anywhere,) * 4,
         scratch_shapes=[
             pltpu.VMEM((batches, rows, width), bf16),
             pltpu.VMEM((batches, rows, 128), bf16),
-            pltpu.VMEM((lines, batches, rows, model), bf16), slab, slab, slab,
-            pltpu.VMEM((batches * more, model), bf16),
+            slab, slab, slab, slab, part, part, part,
+            pltpu.VMEM((more, model), bf16),
             pltpu.VMEM(half, bf16),
             pltpu.VMEM((2, *half), bf16),
             pltpu.VMEM((2, *flat), f32),
@@ -1119,18 +1453,47 @@
             pltpu.VMEM(gains.shape, f32),
             sems((lines, batches)), sems((lines, batches)), sems((lines, batches)),
             sems((lines, batches)), sems((lines, batches)), sems((lines, batches)),
-            sems((2,)), sems((5,)), sems((5,)), sems((3,)), sems((3,)), sems((slots,)), sems((slots,)), sems((3,)),
+            sems((2,)), sems((5,)), sems((5,)), sems((3,)), sems((3,)), sems((slots,)), sems((slots,)), sems((4, lines)),
+            sems((2, 3)), sems((2, 3)), sems((2,)), sems((3,)),
         ],
         compiler_params=pltpu.CompilerParams(
             collective_id=3, has_side_effects=True, vmem_limit_bytes=58 * 2**20),
         cost_estimate=pl.CostEstimate(flops=7 * 10**10, bytes_accessed=4 * 10**7, transcendentals=0),
         name="scatter_rows",
-    )(grads.reshape(batches, slots, rows, width), beta_grads.reshape(batches, slots, rows, 128),
-      out_grads, inner_grads, w_inner, w_beta, small, gains)
-
-
-def attend_kernel(x_ref, first_ref, second_ref, gain_ref, *refs):
-    pieces, (hidden_ref, normed_ref, w_ref, ws, sem, w_sem) = refs[:8], refs[8:]
+    )(*w_inner, grads.reshape(batches, slots, rows, width),
+      beta_grads.reshape(batches, slots, rows, 128), out_grads, inner_grads, w_beta, small, gains,
+      pair_grads, down_grads)
+
+
+def tensor_peers(slots):
+    mine = lax.axis_index("z") * 2 + lax.axis_index("y")
+    places = [lax.rem(mine + d, slots) for d in range(1, slots)]
+    return mine, [(place, {"z": place // 2, "y": lax.rem(place, 2)}) for place in places]
+
+
+def greet(devices):
+    barrier = pltpu.get_barrier_semaphore()
+    for device in devices:
+        pl.semaphore_signal(barrier, inc=1, device_id=device, device_id_type=pl.DeviceIdType.MESH)
+    pl.semaphore_wait(barrier, len(devices))
+
+
+def attend_kernel(x_ref, low_first, low_second, gain_ref, *refs):
+    pieces, refs = refs[:8], refs[8:]
+    hidden_ref, normed_ref, w_ref, heads_ref, ws, heads, send, recv, sem, own_sem = refs
+    slots = heads.shape[1]
+    mine, peers = tensor_peers(slots)
+    greet([device for _, device in peers])
+    lows = (low_first, low_second)
+    away = [
+        line_copy(low.at[place], heads.at[m, mine], send.at[m, d], recv.at[m, d], device)
+        for d, (place, device) in enumerate(peers) for m, low in enumerate(lows)
+    ]
+    for copy in away:
+        copy.start()
+    own = [pltpu.make_async_copy(low.at[mine], heads.at[m, mine], own_sem.at[m]) for m, low in enumerate(lows)]
+    for copy in own:
+        copy.start()
     x = lax.axis_index("x")
     core = lax.axis_index("core")
     y = lax.axis_index("y")
@@ -1142,20 +1505,23 @@
         copies.append(pltpu.make_async_copy(piece, ws.at[:, column, quarter], sem.at[n]))
     for copy in copies:
         copy.start()
-    for copy in copies:
+    for copy in copies + own:
         copy.wait()
-    keep = pltpu.make_async_copy(ws, w_ref, w_sem.at[0])
+    keep = pltpu.make_async_copy(ws, w_ref, own_sem.at[2])
     keep.start()
+    for copy in away:
+        copy.wait_recv()
+    keep_heads = pltpu.make_async_copy(heads, heads_ref, own_sem.at[3])
+    keep_heads.start()
     model = x_ref.shape[1]
     tile = min(512, model)
-    devices = first_ref.shape[0]
-    width = first_ref.shape[2]
+    width = heads.shape[3]
     squares = 0.0
     for start in range(0, model, tile):
         cols = slice(start, start + tile)
         total = x_ref[:, cols].astype(f32)
-        for t in range(devices):
-            left = jnp.concatenate([first_ref[t], second_ref[t]], axis=0)
+        for t in range(slots):
+            left = jnp.concatenate([heads[0, t], heads[1, t]], axis=0)
             total = total + jnp.dot(
                 left, ws[t // 2, t % 2, :, :, cols].reshape(width, tile), preferred_element_type=f32)
         hidden_ref[:, cols] = total
@@ -1165,35 +1531,49 @@
         cols = slice(start, start + tile)
         normed_ref[:, cols] = (hidden_ref[:, cols] * scale * gain_ref[:, cols]).astype(bf16)
     keep.wait()
-
-
-def attend(x, first, second, gain, pieces):
+    keep_heads.wait()
+    for copy in away:
+        copy.wait_send()
+
+
+def attend(x, lows, gain, pieces):
     rows, model = x.shape
     lines, part, _ = pieces[0].shape
     full = (lines, 2, 4, part, model)
+    heads = (2, *lows[0].shape)
+    slots = 2 * lines
     anywhere = pl.BlockSpec(memory_space=pl.ANY)
+    sems = pltpu.SemaphoreType.DMA
     return pl.pallas_call(
         attend_kernel,
         out_shape=(
             jax.ShapeDtypeStruct((rows, model), f32),
             jax.ShapeDtypeStruct((rows, model), bf16),
             jax.ShapeDtypeStruct(full, bf16),
+            jax.ShapeDtypeStruct(heads, bf16),
         ),
-        in_specs=[vmem()] * 4 + [anywhere] * 8,
-        out_specs=(vmem(), vmem(), anywhere),
+        in_specs=[vmem(), anywhere, anywhere, vmem()] + [anywhere] * 8,
+        out_specs=(vmem(), vmem(), anywhere, anywhere),
         scratch_shapes=[
-            pltpu.VMEM(full, bf16), pltpu.SemaphoreType.DMA((8,)), pltpu.SemaphoreType.DMA((1,))],
-        compiler_params=pltpu.CompilerParams(vmem_limit_bytes=32 * 2**20),
-        cost_estimate=pl.CostEstimate(flops=10**10, bytes_accessed=2 * 10**7, transcendentals=0),
+            pltpu.VMEM(full, bf16), pltpu.VMEM(heads, bf16),
+            sems((2, slots)), sems((2, slots)), sems((8,)), sems((4,))],
+        compiler_params=pltpu.CompilerParams(
+            collective_id=4, has_side_effects=True, vmem_limit_bytes=32 * 2**20),
+        cost_estimate=pl.CostEstimate(flops=3 * 10**10, bytes_accessed=2 * 10**7, transcendentals=0),
         name="attend",
-    )(x, first, second, gain, *pieces)
-
-
-def attend_back_kernel(hidden_ref, ffn_ref, grad_ref, c_ref, gain_ref, w_ref, first_ref, second_ref,
-                       result_ref, hgrad_ref, back_first, back_second, wgrad_ref, gain_out, low):
+    )(x, *lows, gain, *pieces)
+
+
+def attend_back_kernel(hidden_ref, ffn_ref, grad_ref, c_ref, gain_ref, w_ref, heads,
+                       result_ref, hgrad_ref, back_first, back_second, left_mine, left_theirs,
+                       right_mine, right_theirs, gain_out, low, wgrad, wrecv, backs, send, recv, sem, core_sem):
     rows, model = hidden_ref.shape
     half = rows // 2
     tile = min(512, model)
+    slots = heads.shape[1]
+    width = heads.shape[3]
+    mine, peers = tensor_peers(slots)
+    greet([device for _, device in peers] + [other("core")])
     squares, dots = 0.0, 0.0
     for start in range(0, model, tile):
         cols = slice(start, start + tile)
@@ -1211,40 +1591,99 @@
         hgrad = c_ref[:, cols].astype(f32) + scale * (grad * gain_ref[:, cols]) - hidden * pull
         hgrad_ref[:, cols] = hgrad
         low[:, cols] = hgrad.astype(bf16)
-    devices, _, width = first_ref.shape
-
-    for t in range(devices):
+
+    outs = (back_first, back_second)
+
+    def away(m, d):
+        place = lax.rem(mine + d, slots)
+        return line_copy(backs.at[m, d], outs[m].at[mine], send.at[m, d], recv.at[m, d],
+                         {"z": place // 2, "y": lax.rem(place, 2)})
+
+    @pl.loop(0, slots)
+    def _(step):
+        d = slots - 1 - step
+        place = lax.rem(mine + d, slots)
         back = lax.dot_general(
-            low[...], w_ref[t // 2, t % 2].reshape(width, model), NT, preferred_element_type=f32)
-        back_first[t] = back[:half].astype(bf16)
-        back_second[t] = back[half:].astype(bf16)
-        left = jnp.concatenate([first_ref[t], second_ref[t]], axis=0)
+            low[...], w_ref[place // 2, lax.rem(place, 2)].reshape(width, model), NT,
+            preferred_element_type=f32)
+        for m in range(2):
+            backs[m, d] = back[m * half : (m + 1) * half].astype(bf16)
+
+            @pl.when(d > 0)
+            def _():
+                away(m, d).start()
+
+            @pl.when(d == 0)
+            def _():
+                pltpu.make_async_copy(backs.at[m, 0], outs[m].at[mine], sem.at[2 + m]).start()
+
+    for t in range(slots):
+        left = jnp.concatenate([heads[0, t], heads[1, t]], axis=0)
         for start in range(0, model, tile):
             cols = slice(start, start + tile)
-            wgrad_ref[t // 2, t % 2, :, :, cols] = lax.dot_general(
+            value = lax.dot_general(
                 left, low[:, cols], (((0,), (0,)), ((), ())), preferred_element_type=f32
-            ).reshape(4, width // 4, tile).astype(bf16)
-
-
-def attend_back(hidden, ffn_out, normed_grad, c_rows, gain, w_full, first, second):
+            ).astype(bf16).reshape(2, 2, width // 4, tile)
+            for c in range(2):
+                wgrad[c, :, t % 2, t // 2, :, cols] = value[:, c]
+    core = lax.axis_index("core")
+    to_pair = line_copy(wgrad.at[1 - core], wrecv, core_sem.at[0], core_sem.at[1], other("core"))
+    to_pair.start()
+    to_pair.wait_recv()
+    lines = wgrad.shape[3]
+    for far_x in range(2):
+        for far_y in range(2):
+            @pl.loop(0, lines)
+            def _(z):
+                wrecv[far_x, far_y, z] = (
+                    wrecv[far_x, far_y, z].astype(f32) + wgrad[core, far_x, far_y, z].astype(f32)
+                ).astype(bf16)
+    x, y = lax.axis_index("x"), lax.axis_index("y")
+    wide = model // 2
+    keeps = [
+        pltpu.make_async_copy(source.at[..., pl.ds(start, wide)], target, sem.at[4 + n])
+        for n, (source, start, target) in enumerate((
+            (wrecv.at[x], 0, left_mine), (wrecv.at[1 - x], 0, left_theirs),
+            (wrecv.at[:, y], wide, right_mine), (wrecv.at[:, 1 - y], wide, right_theirs)))
+    ]
+    for copy in keeps:
+        copy.start()
+    for copy in keeps:
+        copy.wait()
+    to_pair.wait_send()
+    for m in range(2):
+        pltpu.make_async_copy(backs.at[m, 0], outs[m].at[mine], sem.at[2 + m]).wait()
+        for d in range(1, slots):
+            away(m, d).wait_recv()
+            away(m, d).wait_send()
+
+
+def attend_back(hidden, ffn_out, normed_grad, c_rows, gain, w_full, heads):
     rows, model = hidden.shape
     wide = jax.ShapeDtypeStruct((rows, model), f32)
+    lines, _, _, part, _ = w_full.shape
+    share = (2, 2, lines, part, model)
+    slots = 2 * lines
+    back = jax.ShapeDtypeStruct(heads.shape[1:], bf16)
+    anywhere = pl.BlockSpec(memory_space=pl.ANY)
+    sems = pltpu.SemaphoreType.DMA
     return pl.pallas_call(
         attend_back_kernel,
         out_shape=(
-            wide, wide,
-            jax.ShapeDtypeStruct(first.shape, bf16),
-            jax.ShapeDtypeStruct(second.shape, bf16),
-            jax.ShapeDtypeStruct(w_full.shape, bf16),
+            wide, wide, back, back,
+            *[jax.ShapeDtypeStruct((2, lines, part, model // 2), bf16)] * 4,
             jax.ShapeDtypeStruct((1, model), f32),
         ),
-        in_specs=[vmem()] * 8,
-        out_specs=(vmem(),) * 6,
-        scratch_shapes=[pltpu.VMEM((rows, model), bf16)],
-        compiler_params=pltpu.CompilerParams(vmem_limit_bytes=56 * 2**20),
-        cost_estimate=pl.CostEstimate(flops=10**10, bytes_accessed=4 * 10**7, transcendentals=0),
+        in_specs=[vmem()] * 7,
+        out_specs=(vmem(),) * 2 + (anywhere,) * 6 + (vmem(),),
+        scratch_shapes=[
+            pltpu.VMEM((rows, model), bf16), pltpu.VMEM((2, *share), bf16), pltpu.VMEM(share, bf16),
+            pltpu.VMEM(heads.shape, bf16), sems((2, slots)), sems((2, slots)), sems((8,)), sems((2,))],
+        compiler_params=pltpu.CompilerParams(
+            collective_id=5, has_side_effects=True, vmem_limit_bytes=48 * 2**20),
+        cost_estimate=pl.CostEstimate(flops=3 * 10**10, bytes_accessed=4 * 10**7, transcendentals=0),
         name="attend_back",
-    )(hidden, ffn_out, normed_grad, c_rows, gain, w_full, first, second)
+    )(hidden, ffn_out, normed_grad, c_rows, gain, w_full, heads)
 
 
 def root_scale(row_values, gain_vector):
@@ -1292,41 +1731,6 @@
     return lax.ppermute(x, axis_name, [(i, i ^ distance) for i in range(size)])
 
 
-def swap_blocks(blocks):
-    size = lax.axis_size(DP)
-    me = lax.axis_index(DP)
-    pieces = []
-    for r in range(size):
-        block = lax.dynamic_index_in_dim(blocks, me ^ r, keepdims=False)
-        pieces.append(exchange(block, DP, r) if r else block)
-    return ordered_blocks(pieces)
-
-
-def plane_weights(w_gate, w_up, w_down):
-    size = lax.axis_size(DP)
-    local = jnp.stack([w_gate.T, w_up.T, w_down])
-    kinds, hidden, part = local.shape
-    quarter = hidden // size
-    blocks = local.reshape(kinds, size, quarter, part).swapaxes(0, 1)
-    own = jnp.concatenate(swap_blocks(blocks), axis=2)
-    return own.reshape(kinds * quarter, size * part)
-
-
-def plane_weight_grads(own, kinds):
-    size = lax.axis_size(DP)
-    quarter, model = own.shape[0] // kinds, own.shape[1]
-    blocks = own.reshape(kinds * quarter, size, model // size).swapaxes(0, 1)
-    pieces = [piece.reshape(kinds, quarter, -1) for piece in swap_blocks(blocks)]
-    whole = jnp.concatenate(pieces, axis=1).astype(f32)
-    return whole[0].T, whole[1].T, whole[2]
-
-
-def ordered_blocks(pieces):
-    me = lax.axis_index(DP)
-    pieces = jnp.stack(pieces)
-    return [lax.dynamic_index_in_dim(pieces, me ^ q, keepdims=False) for q in range(len(pieces))]
-
-
 def pick(x, index, axis):
     return lax.dynamic_index_in_dim(x, index, axis, keepdims=False)
 
@@ -1335,10 +1739,13 @@
     return lax.optimization_barrier((x, *others))[0]
 
 
-def halve_sum(grad, axis_name, axis):
+def add_low(x, y):
+    return (x.astype(f32) + y.astype(f32)).astype(bf16)
+
+
+def halve_sum(grad, axis_name):
     me = lax.axis_index(axis_name)
-    theirs = exchange(pick(grad, 1 - me, axis), axis_name)
-    return (pick(grad, me, axis).astype(f32) + theirs.astype(f32)).astype(bf16)
+    return add_low(pick(grad, me, 0), exchange(pick(grad, 1 - me, 0), axis_name))
 
 
 def feed_forward_groups(normed, cotangents, w_gate, w_up, w_down):
@@ -1395,7 +1802,8 @@
     heads = w_beta.shape[1]
     devices = lax.axis_size(TP)
     planar = all(lax.axis_size(name) == 2 for name in ("x", "core", "y"))
-    w_inner = jnp.concatenate([w_query, w_key, w_value, w_gate_out], axis=1)
+    w_parts = (w_query, w_key, w_value, w_gate_out)
+    w_inner = jnp.concatenate(w_parts, axis=1)
     w_beta_wide = jnp.pad(w_beta, ((0, 0), (0, 128 - heads)))
     taps = conv_weight.astype(f32).reshape(-1, local_width)
     gain_heads = head_gain.astype(f32)
@@ -1416,25 +1824,23 @@
     if planar:
         count = rows_in.shape[0] * rows_in.shape[1]
         model = rows_in.shape[2]
-        own_weights = plane_weights(*after((w_gate, w_up, w_down), gains))
+        ranks = lax.axis_size(DP)
+        ffn_parts = [
+            w.reshape(ranks, -1, w.shape[1]) for w in after((w_gate.T, w_up.T, w_down), gains)]
         c_rows = [None] * 8
         c_rows[0] = after(cotangent.reshape(count, model), gains)
-        c_rows[1] = exchange(c_rows[0], "x")
         c_rows[4] = exchange(c_rows[0], "core")
         out_shares = pick(
             w_out.reshape(lax.axis_size(DP), len(batches), -1, model), lax.axis_index(DP), 0)
-        gathered_one, out_own, projected, beta_logits = gather_project(
-            normed_one, out_shares, w_inner, w_beta_wide)
-        own_weights, early, early_x, out_own = after(
-            (own_weights, c_rows[0], c_rows[1], out_own), gathered_one)
-        weights = gather(own_weights, "z").reshape(lax.axis_size("z"), 3, -1, model)
-        c_rows[2], c_rows[3] = exchange(early, "y"), exchange(early_x, "y")
-        c_rows[5], c_rows[6], c_rows[7] = (exchange(c_rows[n], "core") for n in (1, 2, 3))
+        gathered_one, out_own, projected, beta_logits, own_weights, own_down = gather_project(
+            normed_one, out_shares, ffn_parts, w_parts, w_beta_wide)
+        early = after(c_rows[0], gathered_one)
+        c_rows[1] = exchange(early, "x")
+        weights = gather(own_weights[None], "z")
+        c_rows[2] = exchange(early, "y")
         out_own = out_own.reshape(out_own.shape[0], -1, model)
-        out_pieces = []
-        for piece in (out_own, exchange(out_own, "y")):
-            across = exchange(piece, "x")
-            out_pieces += [piece, exchange(piece, "core"), across, exchange(across, "core")]
+        out_y = exchange(out_own, "y")
+        out_x = exchange(out_own, "x")
     else:
         gathered_one = jnp.stack([gather(normed_one[m], TP) for m in batches])
         projected = [dot(gathered_one[m], w_inner) for m in batches]
@@ -1444,22 +1850,33 @@
     for m in batches:
         low, kept = run_mixer(m, projected[m], beta_logits[m])
         saved.append(kept)
-        token_heads.append(lax.all_to_all(
-            low.reshape(devices, -1, local_width), TP, split_axis=0, concat_axis=0, tiled=True))
+        if planar and m == 0:
+            out_y, c_rows[1], c_rows[2] = after((out_y, c_rows[1], c_rows[2]), low)
+            out_xy = exchange(out_y, "x")
+            c_rows[3] = exchange(c_rows[1], "y")
+            c_rows[5] = exchange(c_rows[1], "core")
+            c_rows[6] = exchange(c_rows[2], "core")
+            projected[1] = after(projected[1], out_y, c_rows[2])
+        low = low.reshape(devices, -1, local_width)
+        if not planar:
+            low = lax.all_to_all(low, TP, split_axis=0, concat_axis=0, tiled=True)
+        token_heads.append(low)
     if planar:
-        hidden, normed_two, out_full = attend(
-            inputs.reshape(count, model), *token_heads, gain_two[None], out_pieces)
-        ffn_out, normed_grad, weight_grads = ffn_plane(normed_two, weights, c_rows)
-        own_grads = lax.psum_scatter(
-            weight_grads.reshape(-1, model), "z", scatter_dimension=0, tiled=True)
-        gate_share, up_share, down_share = plane_weight_grads(own_grads, 3)
-        result_rows, hidden_grad, *mixed_grads, out_grad, gain_two_sum = attend_back(
-            hidden, ffn_out, normed_grad, c_rows[0], gain_two[None], out_full, *token_heads)
+        out_x, out_xy, c_rows[3] = after((out_x, out_xy, c_rows[3]), low)
+        out_pieces = []
+        for piece in (out_own, out_x, out_y, out_xy):
+            out_pieces += [piece, exchange(piece, "core")]
+        c_rows[7] = exchange(c_rows[3], "core")
+        hidden, normed_two, out_full, token_heads = attend(
+            inputs.reshape(count, model), token_heads, gain_two[None], out_pieces)
+        ffn_out, normed_grad, weight_grads, down_grad = ffn_plane(normed_two, weights, own_down, c_rows)
+        result_rows, hidden_grad, *mixed_grads, left, left_away, right, right_away, gain_two_sum = attend_back(
+            hidden, ffn_out, normed_grad, c_rows[0], gain_two[None], out_full, token_heads)
+        weight_grads = after(weight_grads, left)
+        own_grads = lax.psum_scatter(weight_grads, "z", scatter_dimension=0, tiled=True)
         gain_two_sum = gain_two_sum[0]
         result_rows = result_rows.reshape(rows_in.shape)
         hidden_grad = hidden_grad.reshape(rows_in.shape)
-        out_grad = halve_sum(
-            out_grad.reshape(out_grad.shape[0], 2, 2, 2, *out_grad.shape[3:]), "core", 3)
     else:
         heads_rows = [
             block.swapaxes(0, 1).reshape(-1, devices * local_width) for block in token_heads]
@@ -1476,16 +1893,19 @@
             .reshape(-1, devices, local_width).swapaxes(0, 1) for m in batches]
         out_grad = dot_tn(
             jnp.concatenate(heads_rows), jnp.concatenate(list(attended_low))).astype(bf16)
-    mixed_grads = [
-        lax.all_to_all(grad, TP, split_axis=0, concat_axis=0, tiled=True).reshape(-1, local_width)
-        for grad in mixed_grads]
+    if not planar:
+        mixed_grads = [
+            lax.all_to_all(grad, TP, split_axis=0, concat_axis=0, tiled=True)
+            for grad in mixed_grads]
+    mixed_grads = [grad.reshape(-1, local_width) for grad in mixed_grads]
     if planar:
-        mixed_grads[0] = after(mixed_grads[0], out_grad)
-        out_grad = halve_sum(halve_sum(out_grad, "x", 2), "y", 1)
-        out_grad = out_grad.reshape(out_grad.shape[0], len(batches), -1, model)
+        left = add_low(left, exchange(left_away, "x"))
+        right = add_low(right, exchange(right_away, "y"))
     projected_low, beta_low = [], []
     taps_sum, heads_sum = 0.0, 0.0
     for m in batches:
+        if planar and m > 0:
+            mixed_grads[m] = after(mixed_grads[m], left, right)
         projected_grad, beta_grad, taps_part, heads_part = back_mixer(
             m, projected[m], beta_logits[m], mixed_grads[m], saved[m])
         taps_sum = taps_sum + taps_part
@@ -1494,11 +1914,17 @@
         beta_low.append(beta_grad)
     projected_low = jnp.stack(projected_low)
     beta_low = jnp.stack(beta_low)
+    if planar:
+        left, right = halve_sum(left, "y"), halve_sum(right, "x")
+        projected_low = after(projected_low, left, right)
+        out_grad = jnp.concatenate([left, right], axis=2)
     tokens = gathered_one.reshape(-1, gathered_one.shape[2])
     inner_sum = dot_tn(tokens, projected_low.reshape(-1, 4 * local_width))
     beta_sum = dot_tn(tokens, beta_low.reshape(-1, 128)[:, :heads])
     gain_one_sum = (
-        jnp.sum(inner_sum * w_inner.astype(f32), axis=1)
+        sum(
+            jnp.sum(inner_sum[:, n * local_width : (n + 1) * local_width] * w.astype(f32), axis=1)
+            for n, w in enumerate(w_parts))
         + jnp.sum(beta_sum * w_beta.astype(f32), axis=1)
     ) / gain_one
     gain_parts = jnp.stack([gain_one_sum, gain_two_sum])
@@ -1512,9 +1938,13 @@
         gain_rows = gain_parts.shape[1]
         gain_parts = jnp.pad(gain_parts, ((0, 0), (0, -gain_rows % 8), (0, 0)))
         small = jnp.pad(small, (0, -small.size % 1024)).reshape(-1, 128)
-        input_norm, flat, out_total, inner_total = scatter_rows(
-            after(projected_low, own_grads), beta_low, out_grad,
-            low_sum.reshape(2, -1, low_sum.shape[1]), w_inner, w_beta_wide, small, gain_parts)
+        input_norm, flat, out_total, inner_total, pair_grads, down_grads = scatter_rows(
+            projected_low, beta_low, out_grad,
+            low_sum.reshape(2, -1, low_sum.shape[1]), w_parts, w_beta_wide, small, gain_parts,
+            own_grads[0], down_grad)
+        gate_share, up_share = (
+            pair_grads[:, kind].reshape(-1, pair_grads.shape[3]).astype(f32).T for kind in range(2))
+        down_share = down_grads.reshape(w_down.shape).astype(f32)
         gain_totals = pick(
             flat[small.shape[0] :][:gain_rows].reshape(2, ranks, chunk), lax.axis_index(DP), 1)
         small = flat[: small.shape[0]].reshape(-1)

time: 803 us -> 718 us (0.89)
  waiting for transfers between devices: 119 us -> 17.4 us
  Pallas kernels: 501 us -> 563 us
  local copies, waits for them, and re-layouts: 69.4 us -> 42.5 us
  starting transfers between devices: 35.4 us -> 11.4 us
    all_to_all x4 -> x0, waiting for transfers between devices: 43.6 us -> none  [the longest x2 26.6 us: per_device(): lax.all_to_all(grad, TP, split_axis=0, concat_axis=0, tiled=True)]
    pallas_call x1, Pallas kernels: 124 us -> 163 us  [ffn_plane(): pl.pallas_call(ffn_call_kernel, out_shape=(jax.ShapeDtypeStruct((rows, mo...]
    pallas_call x1, Pallas kernels: 6.79 us -> 37.7 us  [attend(): pl.pallas_call(attend_kernel, out_shape=(jax.ShapeDtypeStruct((rows, mode...]
    all_gather x1, waiting for transfers between devices: 31.5 us -> 2.42 us  [gather(): return lax.all_gather(x, axis_name, axis=axis, tiled=True)]
    ppermute x23 -> x18, waiting for transfers between devices: 43.5 us -> 14.9 us  [exchange(): return lax.ppermute(x, axis_name, [(i, i ^ distance) for i in range(size)])]
    all_to_all x4 -> x0, starting transfers between devices: 18.6 us -> none  [the longest x2 9.53 us: per_device(): lax.all_to_all(low.reshape(devices, -1, local_width), TP, split_axis=0, c...]
    dynamic_slice x5 -> x0, local copies, waits for them, and re-layouts: 10.9 us -> none  [the longest x2 9.17 us: pick(): return lax.dynamic_index_in_dim(x, index, axis, keepdims=False)]
    slice x2 -> x1, local copies, waits for them, and re-layouts: 10.7 us -> 1.08 us  [per_device(): low, kept = run_mixer(m, projected[m], beta_logits[m])]
  transfers between devices with their start and end apart: 29 -> 20, of which waited for: 6 -> 4; matrix products, arithmetic and copies ran while one was open for 11% -> 6% of each run, Pallas kernels for 47% -> 21%
where the time goes in v5:
time: 718 us; the launch traced here: 709 us
  Pallas kernels  563 us (78%)
  local copies, waits for them, and re-layouts  42.5 us (6%)
  other arithmetic  35 us (5%)
  matrix products  17.5 us (2%)
  waiting for transfers between devices  17.4 us (2%)
  between operations  15 us (2%)
  starting transfers between devices  11.4 us (2%)
    pallas_call x1, Pallas kernels, ffn_plane(): pl.pallas_call(ffn_call_kernel, out_shape=(jax.ShapeDtypeStruct((rows, mo...  163 us
    pallas_call x1, Pallas kernels, scatter_rows(): pl.pallas_call(scatter_call_kernel, out_shape=(jax.ShapeDtypeStruct((batc...  117 us
    pallas_call x1, Pallas kernels, gather_project(): pl.pallas_call(gather_call_kernel, out_shape=(jax.ShapeDtypeStruct((batch...  99.1 us
    pallas_call x2, Pallas kernels, mixer_backward(): pl.pallas_call(partial(mixer_backward_kernel, exact), out_shape=(jax.Shap...  56.9 us
    pallas_call x2, Pallas kernels, mixer_forward(): pl.pallas_call(partial(mixer_forward_kernel, exact, group), out_shape=(ja...  53 us
    pallas_call x1, Pallas kernels, attend(): pl.pallas_call(attend_kernel, out_shape=(jax.ShapeDtypeStruct((rows, mode...  37.7 us
    pallas_call x1, Pallas kernels, attend_back(): pl.pallas_call(attend_back_kernel, out_shape=(wide, wide, back, back, *[j...  36.5 us
    unnamed x141, local copies, waits for them, and re-layouts  26.8 us
  transfers between devices with their start and end apart: 20, of which 4 were waited for; matrix products, arithmetic and copies ran while one was open for 6% of the time, Pallas kernels for 21%

profile of v5, /device:TPU:0, one launch (start us, length us, event | category | flops | bytes accessed | tf_op | source)
XLA Modules:
  0.0 708.5 jit_solution(23418483291026291)
XLA Ops:
  8.8 6.1 all_gather.6
  14.9 1.5 fusion.7
  16.5 1.8 copy.40
  18.7 1.3 pad.12.refs_7_.refs_8_
  20.3 1.1 copy-done.22
  21.4 1.1 copy-done.23
  22.6 1.1 copy-done.24
  23.7 99.1 %gather_project.1 = (bf16[2,8,128,2048]{3,2,1,0:T(8,128)(2,1)}, bf16[4,2,32,2048]{3,2,1,0:T(8,128)(2,1)S(1)}, f32[8,128,1024]{2,1,0:T(8,128)}, f32[8,128,1024]{2...) custom-call(bf16[2,128,2048]{2,1,0:T(8,128)(2,1)S(1)} %fusion.2.x_re, ...), custom_call_target="tpu_custom_call" | custom-call | flops 99999997952 | bytes 40000000 | tf_op jit(solution)/shard_map/gather_project/pallas_call | solution.py:1104
  124.9 1.3 collective-permute-start.1
  126.1 1.5 collective-permute-start.2
  129.0 1.1 fusion.21
  130.2 1.1 copy-done.14
  131.3 26.7 %mixer_forward.2 = (bf16[1024,256]{1,0:T(8,128)(2,1)S(1)}, f32[1024,256]{1,0:T(8,128)S(1)}, f32[1024,256]{1,0:T(8,128)S(1)}, f32[1024,256]{1,0:T(8,128)S(1)}, f3...) custom-call(s32[3]{0:T(128)S(1)} %get-tuple-element.205.lengths_ref, f32[1024,1024]{1,0:T(8,128)} %bitcast.119, ...), custom_call_target="tpu_custom_call" | custom-call | flops 10000000000 | bytes 10000000 | tf_op jit(solution)/shard_map/mixer_forward/pallas_call | solution.py:333
  159.9 1.0 copy-done.34
  161.9 10.8 %collective-permute-done.refs_4_ = bf16[4,64,2048]{2,1,0:T(8,128)(2,1)} collective-permute-done((bf16[4,64,2048]{2,1,0:T(8,128)(2,1)}, bf16[4,64,2048]{2,1,0:T(8,128)(2,1)}, u32[]{:S(2)}, u32[]{:S(2)}) %collective-permute-start) | collective-permute-done | bytes 1048608 | tf_op jit(solution)/shard_map/ppermute | solution.py:1731
  174.4 26.3 %mixer_forward.3 = (bf16[1024,256]{1,0:T(8,128)(2,1)S(1)}, f32[1024,256]{1,0:T(8,128)S(1)}, f32[1024,256]{1,0:T(8,128)S(1)}, f32[1024,256]{1,0:T(8,128)S(1)}, f3...) custom-call(s32[3]{0:T(128)S(1)} %get-tuple-element.204.lengths_ref, f32[1024,1024]{1,0:T(8,128)} %bitcast.117, ...), custom_call_target="tpu_custom_call" | custom-call | flops 10000000000 | bytes 10000000 | tf_op jit(solution)/shard_map/mixer_forward/pallas_call | solution.py:333
  201.9 2.5 collective-permute-done.7.refs_3_
  204.5 1.6 collective-permute-done.9.refs_7_
  206.1 37.7 %attend.1 = (f32[256,2048]{1,0:T(8,128)S(1)}, bf16[256,2048]{1,0:T(8,128)(2,1)S(1)}, bf16[4,2,4,64,2048]{4,3,2,1,0:T(8,128)(2,1)}, bf16[2,8,128,256]{3,2,1,0:T(8,128)(2,1)S(1)}) custom-call(bf16[256,2048]{1,0:T(8,128)(2,1)S(1)} %bitcast.81, bf16[8,128,256]{2,1,0:T(8,128)(2,1)S(1)} %bitcast.94, bf16[8,128,256]{2,1,0:T(8,128)(2,1)S(1)} %bitcast.96, ...), custom_call_target="tpu_custom_call" | custom-call | flops 30000001024 | bytes 20000000 | tf_op jit(solution)/shard_map/attend/pallas_call | solution.py:1547
  243.9 1.3 copy-done.36
  250.1 2.4 all-gather.3.cloned.1.call-done
  252.5 163.4 %ffn_plane.1 = (f32[256,2048]{1,0:T(8,128)}, f32[256,2048]{1,0:T(8,128)}, bf16[4,4,2,176,512]{4,3,2,1,0:T(8,128)(2,1)}, bf16[4,176,512]{2,1,0:T(8,128)(2,1)}) custom-call(bf16[256,2048]{1,0:T(8,128)(2,1)} %copy-done.38, bf16[4,4,2,176,512]{4,3,2,1,0:T(8,128)(2,1)} %bitcast.115, bf16[4,176,512]{2,1,0:T(8,128)(2,1)} %copy-done.39, ...), custom_call_target="tpu_custom_call" | custom-call | flops 80000000000 | bytes 40000000 | tf_op jit(solution)/shard_map/ffn_plane/pallas_call | solution.py:834
  415.9 36.5 %attend_back.1 = (f32[256,2048]{1,0:T(8,128)}, f32[256,2048]{1,0:T(8,128)}, bf16[8,128,256]{2,1,0:T(8,128)(2,1)S(1)}, bf16[8,128,256]{2,1,0:T(8,128)(2,1)S(1)}, ...) custom-call(f32[256,2048]{1,0:T(8,128)} %copy-done.36, ...), custom_call_target="tpu_custom_call" | custom-call | flops 30000001024 | bytes 40000000 | tf_op jit(solution)/shard_map/attend_back/pallas_call | solution.py:1670
  456.9 1.8 collective-permute-start.14
  460.0 28.9 %mixer_backward.2 = (bf16[1024,1024]{1,0:T(8,128)(2,1)}, bf16[1024,128]{1,0:T(8,128)(2,1)}, f32[12,256]{1,0:T(8,128)}, f32[2,128]{1,0:T(2,128)}) custom-call(s32[3]{0:T(128)} %copy-done.17, f32[1024,1024]{1,0:T(8,128)} %bitcast.120, f32[1024,128]{1,0:T(8,128)} %bitcast.84, f32[12,256]{1,0:T(8,128)} %copy-done.15, f32[2,128]{1,0:T(2,128)} %copy-done.27, ...), custom_call_target="tpu_custom_call" | custom-call | flops 10000000000 | bytes 10000000 | tf_op jit(solution)/shard_map/mixer_backward/pallas_call | solution.py:356
  488.9 1.6 add_convert_fusion.1
  490.6 2.0 add_convert_fusion
  494.7 2.0 collective-permute-start.16
  496.7 28.0 %mixer_backward.3 = (bf16[1024,1024]{1,0:T(8,128)(2,1)}, bf16[1024,128]{1,0:T(8,128)(2,1)}, f32[12,256]{1,0:T(8,128)}, f32[2,128]{1,0:T(2,128)}) custom-call(s32[3]{0:T(128)} %copy-done.16, f32[1024,1024]{1,0:T(8,128)} %bitcast.118, f32[1024,128]{1,0:T(8,128)} %bitcast.82, f32[12,256]{1,0:T(8,128)} %copy-done.15, f32[2,128]{1,0:T(2,128)} %copy-done.27, ...), custom_call_target="tpu_custom_call" | custom-call | flops 10000000000 | bytes 10000000 | tf_op jit(solution)/shard_map/mixer_backward/pallas_call | solution.py:356
  524.7 1.0 pad_maximum_fusion.3
  525.7 4.6 multiply_reduce_fusion
  531.2 1.8 pad_maximum_fusion.2.refs_5_
  533.7 2.8 pad_maximum_fusion
  536.5 2.4 fusion.13
  539.0 2.0 fusion.14
  541.0 12.9 %fusion.22 = (bf16[2048,1024]{1,0:T(8,128)(2,1)}, f32[2048,1024]{1,0:T(8,128)S(1)}) fusion(bf16[2048,2048]{1,0:T(8,128)(2,1)} %bitcast.98, bf16[2048,1024]{1,0:T(8,128)(2,1)S(1)} %bitcast.100), kind=kOutput, calls=%fused_computation.65 | convolution fusion | flops 8592031744 | bytes 25165824 | tf_op jit(solution)/shard_map/tm,tn->mn/dot_general | solution.py:1726
  554.0 1.2 fusion.11
  556.1 2.3 pad_maximum_fusion.1.refs_6_
  558.3 116.9 %scatter_rows.1 = (f32[2,128,2048]{2,1,0:T(8,128)}, f32[72,128]{1,0:T(8,128)}, bf16[4,64,2048]{2,1,0:T(8,128)(2,1)}, bf16[2,1024,1024]{2,1,0:T(8,128)(2,1)}, bf1...) custom-call(bf16[2048,256]{1,0:T(8,128)(2,1)} %refs_0_.1, bf16[2048,256]{1,0:T(8,128)(2,1)} %refs_1_.1, ...), custom_call_target="tpu_custom_call" | custom-call | flops 70000001024 | bytes 40000000 | tf_op jit(solution)/shard_map/scatter_rows/pallas_call | solution.py:1432
  677.3 1.2 split.11
  678.5 2.3 fusion.20
  680.8 5.9 slice_convert_fusion
  687.9 1.6 bitcast_convert_fusion
  689.5 1.3 bitcast_convert_fusion.1
  690.9 1.0 reshape.243
  693.5 3.3 convert_bitcast_fusion
  696.8 2.1 fusion.6
  699.4 1.3 copy.46
  (204 shorter events, 32.7 us)
Async XLA Ops:
  7.2 11.1 %copy-start = (bf16[256,2048]{1,0:T(8,128)(2,1)S(1)}, bf16[256,2048]{1,0:T(8,128)(2,1)}, u32[]{:S(2)}) copy-start(bf16[256,2048]{1,0:T(8,128)(2,1)} %param.27) | copy-start | bytes 3145732
  7.2 11.2 %copy-start.2 = (bf16[2,128,2048]{2,1,0:T(8,128)(2,1)S(1)}, bf16[2,128,2048]{2,1,0:T(8,128)(2,1)}, u32[]{:S(2)}) copy-start(bf16[2,128,2048]{2,1,0:T(8,128)(2,1)} %param.16) | copy-start | bytes 3145732
  7.2 245.3 %all-gather.3.cloned.1.call-start = ((), (), s32[]{:S(2)}) async-start(), calls=%async_computation.2 | async-start | bytes 7208960 | tf_op jit(solution)/shard_map/all_gather | solution.py:1708
  14.9 3.8 copy-start.52
  16.4 3.6 copy-start.59
  20.0 102.7 %copy-start.12 = (bf16[2048,128]{1,0:T(8,128)(2,1)}, bf16[2048,128]{1,0:T(8,128)(2,1)S(1)}, u32[]{:S(2)}) copy-start(bf16[2048,128]{1,0:T(8,128)(2,1)S(1)} %pad.12.refs_7_.refs_8_) | copy-start | bytes 1572868
  124.6 5.5 copy-start.64
  124.6 5.5 copy-start.61
  124.6 5.5 copy-start.68
  124.6 433.7 %reduce-scatter.2.cloned.1.call-start = ((), (), s32[]{:S(2)}) async-start(), calls=%async_computation.1 | async-start | bytes 7208960 | tf_op jit(solution)/shard_map/reduce_scatter | solution.py:1876
  124.9 47.9 %collective-permute-start.1 = (bf16[256,2048]{1,0:T(8,128)(2,1)}, bf16[256,2048]{1,0:T(8,128)(2,1)}, u32[]{:S(2)}, u32[]{:S(2)}) collective-permute-start(bf16[256,2048]{1,0:T(8,128)(2,1)} %bitcast.16.refs_0_.c_ref), channel_id=1, source_target_pairs={{0,16},{16,0},{1,17},{17,1},{2,18},{18,2},{3,19},{19,3},{4,20},{20... | collective-permute-start | bytes 3145736 | tf_op jit(solution)/shard_map/ppermute | solution.py:1731
  126.1 46.6 %collective-permute-start.2 = (bf16[256,2048]{1,0:T(8,128)(2,1)}, bf16[256,2048]{1,0:T(8,128)(2,1)}, u32[]{:S(2)}, u32[]{:S(2)}) collective-permute-start(bf16[256,2048]{1,0:T(8,128)(2,1)} %bitcast.16.refs_0_.c_ref), channel_id=1, source_target_pairs={{0,1},{1,0},{2,3},{3,2},{4,5},{5,4},{6,7},{7,6},{8,9},{9,8},{10,11... | collective-permute-start | bytes 3145736 | tf_op jit(solution)/shard_map/ppermute | solution.py:1731
  127.7 45.1 %collective-permute-start = (bf16[4,64,2048]{2,1,0:T(8,128)(2,1)}, bf16[4,64,2048]{2,1,0:T(8,128)(2,1)}, u32[]{:S(2)}, u32[]{:S(2)}) collective-permute-start(bf16[4,64,2048]{2,1,0:T(8,128)(2,1)} %bitcast.86), channel_id=1, source_target_pairs={{0,1},{1,0},{2,3},{3,2},{4,5},{5,4},{6,7},{7,6},{8,9},{9,8},{10,11... | collective-permute-start | bytes 3145736 | tf_op jit(solution)/shard_map/ppermute | solution.py:1731
  128.2 72.5 %collective-permute-start.4 = (bf16[4,64,2048]{2,1,0:T(8,128)(2,1)}, bf16[4,64,2048]{2,1,0:T(8,128)(2,1)}, u32[]{:S(2)}, u32[]{:S(2)}) collective-permute-start(bf16[4,64,2048]{2,1,0:T(8,128)(2,1)} %bitcast.87), channel_id=1, source_target_pairs={{0,16},{16,0},{1,17},{17,1},{2,18},{18,2},{3,19},{19,3},{4,20},{20... | collective-permute-start | bytes 3145736 | tf_op jit(solution)/shard_map/ppermute | solution.py:1731
  130.1 27.9 %copy-start.17 = (s32[3]{0:T(128)}, s32[3]{0:T(128)S(1)}, u32[]{:S(2)}) copy-start(s32[3]{0:T(128)S(1)} %get-tuple-element.205.lengths_ref) | copy-start | bytes 40
  130.1 44.3 %copy-start.16 = (s32[3]{0:T(128)}, s32[3]{0:T(128)S(1)}, u32[]{:S(2)}) copy-start(s32[3]{0:T(128)S(1)} %get-tuple-element.204.lengths_ref) | copy-start | bytes 40
  130.1 44.3 %copy-start.15 = (f32[12,256]{1,0:T(8,128)}, f32[12,256]{1,0:T(8,128)S(1)}, u32[]{:S(2)}) copy-start(f32[12,256]{1,0:T(8,128)S(1)} %reshape.247.tap_ref) | copy-start | bytes 36868
  130.1 44.2 %copy-start.27 = (f32[2,128]{1,0:T(2,128)}, f32[2,128]{1,0:T(2,128)S(1)}, u32[]{:S(2)}) copy-start(f32[2,128]{1,0:T(2,128)S(1)} %convert_element_type.129.gain_ref) | copy-start | bytes 3076
  131.2 42.6 %copy-start.19 = (bf16[4,2,32,2048]{3,2,1,0:T(8,128)(2,1)S(1)}, bf16[4,2,32,2048]{3,2,1,0:T(8,128)(2,1)}, u32[]{:S(2)}) copy-start(bf16[4,2,32,2048]{3,2,1,0:T(8,128)(2,1)} %copy-done.18) | copy-start | bytes 3145732
  131.3 43.1 %copy-start.13 = (f32[1,8,128,128]{3,2,1,0:T(8,128)S(1)}, f32[1,8,128,128]{3,2,1,0:T(8,128)}, u32[]{:S(2)}) copy-start(f32[1,8,128,128]{3,2,1,0:T(8,128)} %get-tuple-element.198) | copy-start | bytes 1572868
  172.7 28.0 %collective-permute-start.5 = (bf16[4,64,2048]{2,1,0:T(8,128)(2,1)}, bf16[4,64,2048]{2,1,0:T(8,128)(2,1)S(1)}, u32[]{:S(2)}, u32[]{:S(2)}) collective-permute-start(bf16[4,64,2048]{2,1,0:T(8,128)(2,1)} %collective-permute-done.refs_4_), channel_id=1, source_target_pairs={{0,16},{16,0},{1,17},{17,1},{2,18},{18,2},{3,19},{19,3},{4,20},{20... | collective-permute-start | bytes 3145736 | tf_op jit(solution)/shard_map/ppermute | solution.py:1731
  173.3 27.4 %collective-permute-start.6 = (bf16[256,2048]{1,0:T(8,128)(2,1)}, bf16[256,2048]{1,0:T(8,128)(2,1)}, u32[]{:S(2)}, u32[]{:S(2)}) collective-permute-start(bf16[256,2048]{1,0:T(8,128)(2,1)} %collective-permute-done.1.refs_1_), channel_id=1, source_target_pairs={{0,1},{1,0},{2,3},{3,2},{4,5},{5,4},{6,7},{7,6},{8,9},{9,8},{10,11... | collective-permute-start | bytes 3145736 | tf_op jit(solution)/shard_map/ppermute | solution.py:1731
  173.9 27.5 %collective-permute-start.3 = (bf16[4,64,2048]{2,1,0:T(8,128)(2,1)S(1)}, bf16[4,64,2048]{2,1,0:T(8,128)(2,1)S(1)}, u32[]{:S(2)}, u32[]{:S(2)}) collective-permute-start(bf16[4,64,2048]{2,1,0:T(8,128)(2,1)S(1)} %bitcast.88), channel_id=1, source_target_pairs={{0,8},{8,0},{1,9},{9,1},{2,10},{10,2},{3,11},{11,3},{4,12},{12,4},... | collective-permute-start | bytes 3145736 | tf_op jit(solution)/shard_map/ppermute | solution.py:1731
  173.9 28.0 %collective-permute-start.8 = (bf16[4,64,2048]{2,1,0:T(8,128)(2,1)}, bf16[4,64,2048]{2,1,0:T(8,128)(2,1)S(1)}, u32[]{:S(2)}, u32[]{:S(2)}) collective-permute-start(bf16[4,64,2048]{2,1,0:T(8,128)(2,1)} %collective-permute-done.refs_4_), channel_id=1, source_target_pairs={{0,8},{8,0},{1,9},{9,1},{2,10},{10,2},{3,11},{11,3},{4,12},{12,4},... | collective-permute-start | bytes 3145736 | tf_op jit(solution)/shard_map/ppermute | solution.py:1731
  200.7 43.1 %copy-start.28 = (f32[1024,256]{1,0:T(8,128)}, f32[1024,256]{1,0:T(8,128)S(1)}, u32[]{:S(2)}) copy-start(f32[1024,256]{1,0:T(8,128)S(1)} %get-tuple-element.119.heads_ref) | copy-start | bytes 3145732
  200.7 43.1 %copy-start.29 = (f32[1024,256]{1,0:T(8,128)}, f32[1024,256]{1,0:T(8,128)S(1)}, u32[]{:S(2)}) copy-start(f32[1024,256]{1,0:T(8,128)S(1)} %get-tuple-element.120.fixed_ref) | copy-start | bytes 3145732
  200.7 43.1 %copy-start.30 = (f32[1024,256]{1,0:T(8,128)}, f32[1024,256]{1,0:T(8,128)S(1)}, u32[]{:S(2)}) copy-start(f32[1024,256]{1,0:T(8,128)S(1)} %get-tuple-element.121.delta_ref) | copy-start | bytes 3145732
  200.7 43.2 %copy-start.31 = (f32[16,128,128]{2,1,0:T(8,128)}, f32[16,128,128]{2,1,0:T(8,128)S(1)}, u32[]{:S(2)}) copy-start(f32[16,128,128]{2,1,0:T(8,128)S(1)} %get-tuple-element.122.state_ref) | copy-start | bytes 3145732
  200.7 3.7 collective-permute-start.7
  200.8 5.3 collective-permute-start.9
  201.3 45.8 %collective-permute-start.10 = (bf16[256,2048]{1,0:T(8,128)(2,1)}, bf16[256,2048]{1,0:T(8,128)(2,1)S(1)}, u32[]{:S(2)}, u32[]{:S(2)}) collective-permute-start(bf16[256,2048]{1,0:T(8,128)(2,1)} %bitcast.16.refs_0_.c_ref), channel_id=1, source_target_pairs={{0,8},{8,0},{1,9},{9,1},{2,10},{10,2},{3,11},{11,3},{4,12},{12,4},... | collective-permute-start | bytes 3145736 | tf_op jit(solution)/shard_map/ppermute | solution.py:1731
  201.4 46.7 %collective-permute-start.11 = (bf16[256,2048]{1,0:T(8,128)(2,1)}, bf16[256,2048]{1,0:T(8,128)(2,1)S(1)}, u32[]{:S(2)}, u32[]{:S(2)}) collective-permute-start(bf16[256,2048]{1,0:T(8,128)(2,1)} %collective-permute-done.1.refs_1_), channel_id=1, source_target_pairs={{0,8},{8,0},{1,9},{9,1},{2,10},{10,2},{3,11},{11,3},{4,12},{12,4},... | collective-permute-start | bytes 3145736 | tf_op jit(solution)/shard_map/ppermute | solution.py:1731
  201.8 47.2 %collective-permute-start.12 = (bf16[256,2048]{1,0:T(8,128)(2,1)}, bf16[256,2048]{1,0:T(8,128)(2,1)S(1)}, u32[]{:S(2)}, u32[]{:S(2)}) collective-permute-start(bf16[256,2048]{1,0:T(8,128)(2,1)} %collective-permute-done.2.refs_2_), channel_id=1, source_target_pairs={{0,8},{8,0},{1,9},{9,1},{2,10},{10,2},{3,11},{11,3},{4,12},{12,4},... | collective-permute-start | bytes 3145736 | tf_op jit(solution)/shard_map/ppermute | solution.py:1731
  204.4 45.7 %collective-permute-start.13 = (bf16[256,2048]{1,0:T(8,128)(2,1)}, bf16[256,2048]{1,0:T(8,128)(2,1)}, u32[]{:S(2)}, u32[]{:S(2)}) collective-permute-start(bf16[256,2048]{1,0:T(8,128)(2,1)} %collective-permute-done.6.refs_3_), channel_id=1, source_target_pairs={{0,8},{8,0},{1,9},{9,1},{2,10},{10,2},{3,11},{11,3},{4,12},{12,4},... | collective-permute-start | bytes 3145736 | tf_op jit(solution)/shard_map/ppermute | solution.py:1731
  456.9 32.0 %collective-permute-start.14 = (bf16[2,4,64,1024]{3,2,1,0:T(8,128)(2,1)}, bf16[2,4,64,1024]{3,2,1,0:T(8,128)(2,1)}, u32[]{:S(2)}, u32[]{:S(2)}) collective-permute-start(bf16[2,4,64,1024]{3,2,1,0:T(8,128)(2,1)} %copy-done.21), channel_id=1, source_target_pairs={{0,16},{16,0},{1,17},{17,1},{2,18},{18,2},{3,19},{19,3},{4,20},{20... | collective-permute-start | bytes 3145736 | tf_op jit(solution)/shard_map/ppermute | solution.py:1731
  458.7 31.8 %collective-permute-start.15 = (bf16[2,4,64,1024]{3,2,1,0:T(8,128)(2,1)}, bf16[2,4,64,1024]{3,2,1,0:T(8,128)(2,1)}, u32[]{:S(2)}, u32[]{:S(2)}) collective-permute-start(bf16[2,4,64,1024]{3,2,1,0:T(8,128)(2,1)} %copy-done.20), channel_id=1, source_target_pairs={{0,1},{1,0},{2,3},{3,2},{4,5},{5,4},{6,7},{7,6},{8,9},{9,8},{10,11... | collective-permute-start | bytes 3145736 | tf_op jit(solution)/shard_map/ppermute | solution.py:1731
  460.0 28.9 %copy-start.11 = (bf16[2,4,64,1024]{3,2,1,0:T(8,128)(2,1)S(1)}, bf16[2,4,64,1024]{3,2,1,0:T(8,128)(2,1)}, u32[]{:S(2)}) copy-start(bf16[2,4,64,1024]{3,2,1,0:T(8,128)(2,1)} %copy-done.10) | copy-start | bytes 3145732
  493.5 43.0 %collective-permute-start.17 = (bf16[4,64,1024]{2,1,0:T(8,128)(2,1)}, bf16[4,64,1024]{2,1,0:T(8,128)(2,1)}, u32[]{:S(2)}, u32[]{:S(2)}) collective-permute-start(bf16[4,64,1024]{2,1,0:T(8,128)(2,1)} %dynamic-slice_bitcast_fusion), channel_id=1, source_target_pairs={{0,16},{16,0},{1,17},{17,1},{2,18},{18,2},{3,19},{19,3},{4,20},{20... | collective-permute-start | bytes 1572872 | tf_op jit(solution)/shard_map/ppermute | solution.py:1731
  494.7 44.3 %collective-permute-start.16 = (bf16[4,64,1024]{2,1,0:T(8,128)(2,1)}, bf16[4,64,1024]{2,1,0:T(8,128)(2,1)}, u32[]{:S(2)}, u32[]{:S(2)}) collective-permute-start(bf16[4,64,1024]{2,1,0:T(8,128)(2,1)} %dynamic-slice_bitcast_fusion.1), channel_id=1, source_target_pairs={{0,1},{1,0},{2,3},{3,2},{4,5},{5,4},{6,7},{7,6},{8,9},{9,8},{10,11... | collective-permute-start | bytes 1572872 | tf_op jit(solution)/shard_map/ppermute | solution.py:1731
  496.7 28.0 %copy-start.50 = (bf16[1024,128]{1,0:T(8,128)(2,1)S(1)}, bf16[1024,128]{1,0:T(8,128)(2,1)}, u32[]{:S(2)}) copy-start(bf16[1024,128]{1,0:T(8,128)(2,1)} %get-tuple-element.126) | copy-start | bytes 786436
  496.7 29.0 %copy-start.56 = (bf16[2048,2]{0,1:T(2,128)(2,1)S(1)}, bf16[2048,2]{0,1:T(2,128)(2,1)}, u32[]{:S(2)}) copy-start(bf16[2048,2]{0,1:T(2,128)(2,1)} %param.24) | copy-start | bytes 24580
  533.7 5.3 copy-start.43
  536.5 17.4 %copy-start.46 = (bf16[2,1024,1024]{2,1,0:T(8,128)(2,1)}, bf16[2,1024,1024]{2,1,0:T(8,128)(2,1)S(1)}, u32[]{:S(2)}) copy-start(bf16[2,1024,1024]{2,1,0:T(8,128)(2,1)S(1)} %pad_maximum_fusion) | copy-start | bytes 12582916
  541.0 12.9 %copy-start.5 = (bf16[2048,256]{1,0:T(8,128)(2,1)S(1)}, bf16[2048,256]{1,0:T(8,128)(2,1)}, u32[]{:S(2)}) copy-start(bf16[2048,256]{1,0:T(8,128)(2,1)} %refs_1_.1) | copy-start | bytes 3145732
  541.0 12.9 %copy-start.7 = (bf16[2048,256]{1,0:T(8,128)(2,1)S(1)}, bf16[2048,256]{1,0:T(8,128)(2,1)}, u32[]{:S(2)}) copy-start(bf16[2048,256]{1,0:T(8,128)(2,1)} %refs_2_.1) | copy-start | bytes 3145732
  541.0 12.9 %copy-start.9 = (bf16[2048,256]{1,0:T(8,128)(2,1)S(1)}, bf16[2048,256]{1,0:T(8,128)(2,1)}, u32[]{:S(2)}) copy-start(bf16[2048,256]{1,0:T(8,128)(2,1)} %refs_3_.3) | copy-start | bytes 3145732
  680.8 5.9 copy-start.40
  680.8 5.9 copy-start.53
  (41 other events, 66.3 us)
Sparse Core Ops, SparseCore 0:
  124.8 127.6 all-gather.2
  457.0 100.4 reduce-scatter.1

commit v6 on v5

--- a/solution.py
+++ b/solution.py
@@ -380,9 +380,9 @@
 
 
 def ffn_kernel(x_ref, w_ref, down_ref, c_refs, out_ref, ngrad_ref, wgrad_ref, down_out,
-               xs, cs, ws, gu, inner_s, gate_s, up_s, acts_t, part, crecv, drecv, nrecv, stage,
+               xs, cs, ws, dsum, landed, outs, inner_s, gate_s, up_s, acts_t, part, crecv, drecv, nrecv, stage,
                ag_send, ag_recv, pair_send, pair_recv, rs_send, rs_recv, c_sem, w_sem, g_sem, t_sem,
-               down_right, down_left, down_recv, down_sem, sum_sems, keep_sem, out_sem, ready):
+               down_right, down_left, down_recv, down_sem, sum_sems, keep_sem, out_sem):
     half = xs.shape[1] // 2
     rows = 2 * half
     model = xs.shape[2]
@@ -491,20 +491,14 @@
     d_sends = [[remote(crecv.at[3, a, pl.ds(h * half, half)], drecv.at[a, pl.ds(h * half, half)],
                        rs_send.at[8 + a * 2 + h], rs_recv.at[8 + a * 2 + h], ("x", "y")[h]) for a in range(2)] for h in range(2)]
 
-    def place_of(step):
-        return jnp.where(step >= 6, step - 4, lax.rem(step, 2))
-
-    def gates(step):
-        slot = slot_of(step)
-        for start in range(0, hidden, tile_f):
-            cols = slice(start, min(start + tile_f, hidden))
-            for kind in range(2):
-                gu[place_of(step), kind, :, cols] = lax.dot_general(
-                    xs[slot], ws[kind, cols, :], NT, preferred_element_type=f32)
-
-    @pl.loop(0, 4)
+    def gates(slot, cols):
+        return [
+            lax.dot_general(xs[slot], ws[kind, cols, :], NT, preferred_element_type=f32)
+            for kind in range(2)]
+
+    @pl.loop(0, 8)
     def _(early):
-        step = jnp.where(early < 2, 6 + early, 3 - early)
+        slot = lax.rem(early + 1, 2) * 4 + early // 2
 
         @pl.when(early == 0)
         def _():
@@ -521,21 +515,26 @@
             pair_of[1].start()
             own_y[0].wait_recv()
             pair_of[2].start()
+            pair_of[1].wait_recv()
+
+        @pl.when(early == 4)
+        def _():
+            pair_of[2].wait_recv()
+
+        @pl.when(early == 6)
+        def _():
             if lines > 2:
                 down_step(2)
             relay_y.wait_recv()
             relay_x.wait_recv()
             pair_of[3].start()
-
-        @pl.when(early == 3)
-        def _():
             pair_of[3].wait_recv()
-        gates(step)
-
-    pair_of[1].wait_recv()
-    pair_of[2].wait_recv()
-    for far in range(3, lines):
-        down_step(far)
+
+        places = pl.ds(pl.multiple_of(slot * rows, rows), rows)
+        for start in range(0, hidden, tile_f):
+            cols = slice(start, min(start + tile_f, hidden))
+            gate, up = gates(slot, cols)
+            acts_t[2, cols, places] = (gate * sigmoid(gate) * up).astype(bf16).T
 
     tiles = model // tile_w
 
@@ -546,90 +545,6 @@
             pltpu.make_async_copy(
                 ref.at[:, cols], part.at[0, buffer, :, pl.ds(n * tile_w, tile_w)], t_sem.at[buffer, n])
             for n, ref in enumerate(c_refs)]
-
-    @pl.loop(0, 8)
-    def _(step):
-        turn = step // 2
-        j = pair_at(turn)
-        slot = slot_of(step)
-        pairing = lax.rem(step, 2) == 0
-
-        @pl.when(step < 7)
-        def _():
-            c_start(step + 1)
-
-        @pl.when((step >= 2) & (step < 6))
-        def _():
-            gates(step)
-
-        c_copy(step, 0).wait()
-
-        for start in range(0, hidden, tile_f):
-            size = min(tile_f, hidden - start)
-            cols = slice(start, start + size)
-            gate = gu[place_of(step), 0, :, cols]
-            up = gu[place_of(step), 1, :, cols]
-            grad = lax.dot_general(cs[lax.rem(step, 2)], ws[2, cols, :], NT, preferred_element_type=f32)
-            sg = sigmoid(gate)
-            silu = gate * sg
-            inner = (silu * up).astype(bf16)
-            gate_grad = (grad * up * sg * (1.0 + gate * (1.0 - sg))).astype(bf16)
-            up_grad = (grad * silu).astype(bf16)
-            places = pl.ds(pl.multiple_of(slot * rows, rows), rows)
-            for kind, (value, target) in enumerate(((gate_grad, gate_s), (up_grad, up_s), (inner, inner_s))):
-                target[:, cols] = value
-                acts_t[kind, cols, places] = value.T
-
-        @pl.when(pairing & (step >= 4))
-        def _():
-            part_send(turn - 2).wait_send()
-
-        place = jnp.where(pairing, lax.rem(turn, 2), 2)
-        for start in range(0, model, tile_d):
-            cols = slice(start, start + tile_d)
-            part[place, 0, :, cols] = jnp.dot(
-                inner_s[...], ws[2, :, cols], preferred_element_type=f32).astype(bf16)
-            part[place, 1, :, cols] = (
-                jnp.dot(gate_s[...], ws[0, :, cols], preferred_element_type=f32)
-                + jnp.dot(up_s[...], ws[1, :, cols], preferred_element_type=f32)
-            ).astype(bf16)
-
-        @pl.when(pairing)
-        def _():
-            part_send(turn).start()
-
-        @pl.when(jnp.logical_not(pairing))
-        def _():
-            part_send(turn).wait_recv()
-            for a in range(2):
-                for start in range(0, model, tile_d):
-                    cols = slice(start, start + tile_d)
-                    crecv[j, a, :, cols] = (
-                        crecv[j, a, :, cols].astype(f32) + part[2, a, :, cols].astype(f32)
-                    ).astype(bf16)
-
-        @pl.when(step == 1)
-        def _():
-            for h in range(2):
-                for copy in d_sends[h]:
-                    copy.start()
-
-        @pl.when(step == 3)
-        def _():
-            for copy in x_sends[0]:
-                copy.start()
-
-        @pl.when(step == 5)
-        def _():
-            for copy in y_sends[1]:
-                copy.start()
-
-        @pl.when(step == 6)
-        def _():
-            part_send(2).wait_send()
-            for t in range(2):
-                for copy in c_tile(t):
-                    copy.start()
 
     def grad_copy(kind, t, line):
         return pltpu.make_async_copy(
@@ -666,7 +581,7 @@
                 for line in range(lines):
                     grad_copy(kind, t, line).start()
             else:
-                ws[0, :, pl.ds(pl.multiple_of(t * tile_w, tile_w), tile_w)] = value
+                dsum[:, pl.ds(pl.multiple_of(t * tile_w, tile_w), tile_w)] = value
 
         if kind == 2:
             return
@@ -674,41 +589,25 @@
             for line in range(lines):
                 grad_copy(kind, t, line).wait()
 
-    @pl.loop(0, lines)
-    def _(z):
-        @pl.when((o < lines - 1) & (z <= o))
-        def _():
-            down_pass(z, True).wait_send()
-
-        @pl.when((o > 0) & (z >= o))
-        def _():
-            down_pass(z, False).wait_send()
-
     mesh_id = pl.DeviceIdType.MESH
 
-    @pl.when(o > 0)
-    def _():
-        pl.semaphore_signal(ready, inc=1, device_id={"z": o - 1}, device_id_type=mesh_id)
-
-    @pl.when(o < lines - 1)
-    def _():
-        pl.semaphore_signal(ready, inc=1, device_id={"z": o + 1}, device_id_type=mesh_id)
-
-    def rows_of(n, z):
-        return ws.at[n, pl.ds(pl.multiple_of(z * quarter, 16), quarter)]
+    def rows_of(z):
+        return dsum.at[pl.ds(pl.multiple_of(z * quarter, 16), quarter)]
 
     def sum_pass(z, right):
         side = 0 if right else 2
+        block = jnp.maximum(z - o - 1, 0) if right else jnp.minimum(lines - o + 1 + z, lines)
         return pltpu.make_async_remote_copy(
-            src_ref=rows_of(0, z), dst_ref=rows_of(1 if right else 2, z),
+            src_ref=rows_of(z), dst_ref=landed.at[block],
             send_sem=sum_sems.at[side, z], recv_sem=sum_sems.at[side + 1, z],
             device_id={"z": o + 1 if right else o - 1}, device_id_type=mesh_id)
 
-    def sum_add(z, n):
+    def sum_add(z, block):
         at = pl.ds(pl.multiple_of(z * quarter, 16), quarter)
         for start in range(0, model, tile_d):
             cols = slice(start, start + tile_d)
-            ws[0, at, cols] = (ws[0, at, cols].astype(f32) + ws[n, at, cols].astype(f32)).astype(bf16)
+            dsum[at, cols] = (
+                dsum[at, cols].astype(f32) + landed[block, :, cols].astype(f32)).astype(bf16)
 
     def sum_tick(k):
         z_right = lines - 1 - k + o
@@ -718,7 +617,7 @@
             @pl.when(o > 0)
             def _():
                 sum_pass(z_right, True).wait_recv()
-                sum_add(z_right, 1)
+                sum_add(z_right, z_right - o)
 
             @pl.when(o < k)
             def _():
@@ -733,16 +632,100 @@
             @pl.when(back > 0)
             def _():
                 sum_pass(z_left, False).wait_recv()
-                sum_add(z_left, 2)
+                sum_add(z_left, lines - o + z_left)
 
             @pl.when(back < k)
             def _():
                 sum_pass(z_left - 1, False).wait_send()
             sum_pass(z_left, False).start()
 
+    for t in range(2):
+        for copy in c_tile(t):
+            copy.start()
     weight_grads(2)
-    pl.semaphore_wait(ready, (o > 0).astype(jnp.int32) + (o < lines - 1).astype(jnp.int32))
     sum_tick(0)
+    for far in range(3, lines):
+        down_step(far)
+
+    @pl.loop(0, 8)
+    def _(step):
+        turn = step // 2
+        j = pair_at(turn)
+        slot = slot_of(step)
+        pairing = lax.rem(step, 2) == 0
+
+        @pl.when(step < 7)
+        def _():
+            c_start(step + 1)
+
+        for k in range(1, lines - 1):
+            @pl.when(step == min(1 + 3 * k, 7))
+            def _():
+                sum_tick(k)
+
+        c_copy(step, 0).wait()
+
+        for start in range(0, hidden, tile_f):
+            size = min(tile_f, hidden - start)
+            cols = slice(start, start + size)
+            gate, up = gates(slot, cols)
+            grad = lax.dot_general(cs[lax.rem(step, 2)], ws[2, cols, :], NT, preferred_element_type=f32)
+            sg = sigmoid(gate)
+            silu = gate * sg
+            inner = (silu * up).astype(bf16)
+            gate_grad = (grad * up * sg * (1.0 + gate * (1.0 - sg))).astype(bf16)
+            up_grad = (grad * silu).astype(bf16)
+            places = pl.ds(pl.multiple_of(slot * rows, rows), rows)
+            for kind, (value, target) in enumerate(((gate_grad, gate_s), (up_grad, up_s), (inner, inner_s))):
+                target[:, cols] = value
+                if kind < 2:
+                    acts_t[kind, cols, places] = value.T
+
+        @pl.when(pairing & (step >= 4))
+        def _():
+            part_send(turn - 2).wait_send()
+
+        place = jnp.where(pairing, lax.rem(turn, 2), 2)
+        for start in range(0, model, tile_d):
+            cols = slice(start, start + tile_d)
+            part[place, 0, :, cols] = jnp.dot(
+                inner_s[...], ws[2, :, cols], preferred_element_type=f32).astype(bf16)
+            part[place, 1, :, cols] = (
+                jnp.dot(gate_s[...], ws[0, :, cols], preferred_element_type=f32)
+                + jnp.dot(up_s[...], ws[1, :, cols], preferred_element_type=f32)
+            ).astype(bf16)
+
+        @pl.when(pairing)
+        def _():
+            part_send(turn).start()
+
+        @pl.when(jnp.logical_not(pairing))
+        def _():
+            part_send(turn).wait_recv()
+            for a in range(2):
+                for start in range(0, model, tile_d):
+                    cols = slice(start, start + tile_d)
+                    crecv[j, a, :, cols] = (
+                        crecv[j, a, :, cols].astype(f32) + part[2, a, :, cols].astype(f32)
+                    ).astype(bf16)
+
+        @pl.when(step == 1)
+        def _():
+            for h in range(2):
+                for copy in d_sends[h]:
+                    copy.start()
+
+        @pl.when(step == 3)
+        def _():
+            for copy in x_sends[0]:
+                copy.start()
+
+        @pl.when(step == 5)
+        def _():
+            for copy in y_sends[1]:
+                copy.start()
+
+
     for h in range(2):
         j = 2 - h
         for a in range(2):
@@ -753,11 +736,7 @@
         for copy in (y_sends, x_sends)[h][h]:
             copy.start()
     weight_grads(0)
-    if lines > 2:
-        sum_tick(1)
     weight_grads(1)
-    for k in range(2, lines - 1):
-        sum_tick(k)
     out_copies = []
     for a, target in enumerate((out_ref, ngrad_ref)):
         for h in range(2):
@@ -765,18 +744,32 @@
             y_sends[h][a].wait_recv()
         for n in range(model // tile_d):
             cols = slice(n * tile_d, (n + 1) * tile_d)
-            gu[n, a, :, :tile_d] = (
+            if n >= 2:
+                out_copies[-2].wait()
+            outs[a, n % 2] = (
                 crecv[0, a, :, cols].astype(f32)
                 + nrecv[0, a, :, cols].astype(f32)
                 + nrecv[1, a, :, cols].astype(f32)
             )
             copy = pltpu.make_async_copy(
-                gu.at[n, a, :, pl.ds(0, tile_d)], target.at[:, pl.ds(n * tile_d, tile_d)],
+                outs.at[a, n % 2], target.at[:, pl.ds(n * tile_d, tile_d)],
                 out_sem.at[n, a])
             copy.start()
             out_copies.append(copy)
-    for copy in out_copies:
-        copy.wait()
+    steps = model // tile_d
+    for a in range(2):
+        for copy in out_copies[a * steps : (a + 1) * steps][-2:]:
+            copy.wait()
+    @pl.loop(0, lines)
+    def _(z):
+        @pl.when((o < lines - 1) & (z <= o))
+        def _():
+            down_pass(z, True).wait_send()
+
+        @pl.when((o > 0) & (z >= o))
+        def _():
+            down_pass(z, False).wait_send()
+
     own_pair.wait_send()
     for h in range(2):
         own_x[h].wait_send()
@@ -789,21 +782,22 @@
     relay_y.wait_send()
     for j in (1, 2, 3):
         pair_of[j].wait_send()
+    part_send(2).wait_send()
     part_send(3).wait_send()
 
     @pl.when(o > 0)
     def _():
         sum_pass(o, True).wait_recv()
-        sum_add(o, 1)
+        sum_add(o, 0)
 
     @pl.when(o < lines - 1)
     def _():
         sum_pass(o, False).wait_recv()
-        sum_add(o, 2)
+        sum_add(o, lines)
 
     keeps = [
         pltpu.make_async_copy(
-            rows_of(0, o).at[:, pl.ds(q * width, width)], down_out.at[q], keep_sem.at[q])
+            rows_of(o).at[:, pl.ds(q * width, width)], down_out.at[q], keep_sem.at[q])
         for q in range(parts)
     ]
     for copy in keeps:
@@ -845,7 +839,9 @@
             pltpu.VMEM((8, rows, model), bf16),
             pltpu.VMEM((2, rows, model), bf16),
             pltpu.VMEM((3, hidden, model), bf16),
-            pltpu.VMEM((4, 2, rows, max(hidden, min(512, model))), f32),
+            pltpu.VMEM((hidden, model), bf16),
+            pltpu.VMEM((lines + 1, quarter, model), bf16),
+            pltpu.VMEM((2, 2, rows, min(512, model)), f32),
             pltpu.VMEM((rows, hidden), bf16),
             pltpu.VMEM((rows, hidden), bf16),
             pltpu.VMEM((rows, hidden), bf16),
@@ -858,7 +854,7 @@
             sems((10,)), sems((10,)), sems((4,)), sems((4,)), sems((12,)), sems((12,)),
             sems((2,)), sems((lines, parts)), sems((2, lines)), sems((2, 8)),
             sems((lines,)), sems((lines,)), sems((lines,)), sems((parts,)),
-            sems((4, lines)), sems((parts,)), sems((4, 2)), pltpu.SemaphoreType.REGULAR,
+            sems((4, lines)), sems((parts,)), sems((4, 2)),
         ],
         compiler_params=pltpu.CompilerParams(
             collective_id=2, has_side_effects=True, vmem_limit_bytes=60 * 2**20),

time: 718 us -> 705 us (0.982)
  Pallas kernels: 563 us -> 549 us
    pallas_call x1, Pallas kernels: 163 us -> 150 us  [ffn_plane(): pl.pallas_call(ffn_call_kernel, out_shape=(jax.ShapeDtypeStruct((rows, mo...]
where the time goes in v6:
time: 705 us; the launch traced here: 694 us
  Pallas kernels  549 us (78%)
  local copies, waits for them, and re-layouts  42.5 us (6%)
  other arithmetic  35 us (5%)
  waiting for transfers between devices  17.4 us (2%)
  matrix products  17.4 us (2%)
  between operations  15 us (2%)
  starting transfers between devices  11.5 us (2%)
    pallas_call x1, Pallas kernels, ffn_plane(): pl.pallas_call(ffn_call_kernel, out_shape=(jax.ShapeDtypeStruct((rows, mo...  150 us
    pallas_call x1, Pallas kernels, scatter_rows(): pl.pallas_call(scatter_call_kernel, out_shape=(jax.ShapeDtypeStruct((batc...  114 us
    pallas_call x1, Pallas kernels, gather_project(): pl.pallas_call(gather_call_kernel, out_shape=(jax.ShapeDtypeStruct((batch...  99.1 us
    pallas_call x2, Pallas kernels, mixer_backward(): pl.pallas_call(partial(mixer_backward_kernel, exact), out_shape=(jax.Shap...  56.9 us
    pallas_call x2, Pallas kernels, mixer_forward(): pl.pallas_call(partial(mixer_forward_kernel, exact, group), out_shape=(ja...  53 us
    pallas_call x1, Pallas kernels, attend(): pl.pallas_call(attend_kernel, out_shape=(jax.ShapeDtypeStruct((rows, mode...  37.7 us
    pallas_call x1, Pallas kernels, attend_back(): pl.pallas_call(attend_back_kernel, out_shape=(wide, wide, back, back, *[j...  37.5 us
    unnamed x141, local copies, waits for them, and re-layouts  26.8 us
  transfers between devices with their start and end apart: 20, of which 4 were waited for; matrix products, arithmetic and copies ran while one was open for 6% of the time, Pallas kernels for 21%

profile of v6, /device:TPU:0, one launch (start us, length us, event | category | flops | bytes accessed | tf_op | source)
XLA Modules:
  0.0 693.9 jit_solution(15966660129592342889)
XLA Ops:
  8.8 6.1 all_gather.6
  14.9 1.5 fusion.7
  16.5 1.8 copy.40
  18.7 1.3 pad.12.refs_7_.refs_8_
  20.3 1.1 copy-done.22
  21.4 1.1 copy-done.23
  22.6 1.1 copy-done.24
  23.7 99.1 %gather_project.1 = (bf16[2,8,128,2048]{3,2,1,0:T(8,128)(2,1)}, bf16[4,2,32,2048]{3,2,1,0:T(8,128)(2,1)S(1)}, f32[8,128,1024]{2,1,0:T(8,128)}, f32[8,128,1024]{2...) custom-call(bf16[2,128,2048]{2,1,0:T(8,128)(2,1)S(1)} %fusion.2.x_re, ...), custom_call_target="tpu_custom_call" | custom-call | flops 99999997952 | bytes 40000000 | tf_op jit(solution)/shard_map/gather_project/pallas_call | solution.py:1100
  124.9 1.3 collective-permute-start.1
  126.1 1.5 collective-permute-start.2
  129.0 1.1 fusion.21
  130.2 1.1 copy-done.14
  131.3 26.7 %mixer_forward.2 = (bf16[1024,256]{1,0:T(8,128)(2,1)S(1)}, f32[1024,256]{1,0:T(8,128)S(1)}, f32[1024,256]{1,0:T(8,128)S(1)}, f32[1024,256]{1,0:T(8,128)S(1)}, f3...) custom-call(s32[3]{0:T(128)S(1)} %get-tuple-element.205.lengths_ref, f32[1024,1024]{1,0:T(8,128)} %bitcast.119, ...), custom_call_target="tpu_custom_call" | custom-call | flops 10000000000 | bytes 10000000 | tf_op jit(solution)/shard_map/mixer_forward/pallas_call | solution.py:333
  159.9 1.0 copy-done.34
  161.9 10.8 %collective-permute-done.refs_4_ = bf16[4,64,2048]{2,1,0:T(8,128)(2,1)} collective-permute-done((bf16[4,64,2048]{2,1,0:T(8,128)(2,1)}, bf16[4,64,2048]{2,1,0:T(8,128)(2,1)}, u32[]{:S(2)}, u32[]{:S(2)}) %collective-permute-start) | collective-permute-done | bytes 1048608 | tf_op jit(solution)/shard_map/ppermute | solution.py:1727
  174.4 26.3 %mixer_forward.3 = (bf16[1024,256]{1,0:T(8,128)(2,1)S(1)}, f32[1024,256]{1,0:T(8,128)S(1)}, f32[1024,256]{1,0:T(8,128)S(1)}, f32[1024,256]{1,0:T(8,128)S(1)}, f3...) custom-call(s32[3]{0:T(128)S(1)} %get-tuple-element.204.lengths_ref, f32[1024,1024]{1,0:T(8,128)} %bitcast.117, ...), custom_call_target="tpu_custom_call" | custom-call | flops 10000000000 | bytes 10000000 | tf_op jit(solution)/shard_map/mixer_forward/pallas_call | solution.py:333
  201.9 2.5 collective-permute-done.7.refs_3_
  204.5 1.6 collective-permute-done.9.refs_7_
  206.1 37.7 %attend.1 = (f32[256,2048]{1,0:T(8,128)S(1)}, bf16[256,2048]{1,0:T(8,128)(2,1)S(1)}, bf16[4,2,4,64,2048]{4,3,2,1,0:T(8,128)(2,1)}, bf16[2,8,128,256]{3,2,1,0:T(8,128)(2,1)S(1)}) custom-call(bf16[256,2048]{1,0:T(8,128)(2,1)S(1)} %bitcast.81, bf16[8,128,256]{2,1,0:T(8,128)(2,1)S(1)} %bitcast.94, bf16[8,128,256]{2,1,0:T(8,128)(2,1)S(1)} %bitcast.96, ...), custom_call_target="tpu_custom_call" | custom-call | flops 30000001024 | bytes 20000000 | tf_op jit(solution)/shard_map/attend/pallas_call | solution.py:1543
  243.9 1.3 copy-done.36
  250.1 2.4 all-gather.3.cloned.1.call-done
  252.5 150.3 %ffn_plane.1 = (f32[256,2048]{1,0:T(8,128)}, f32[256,2048]{1,0:T(8,128)}, bf16[4,4,2,176,512]{4,3,2,1,0:T(8,128)(2,1)}, bf16[4,176,512]{2,1,0:T(8,128)(2,1)}) custom-call(bf16[256,2048]{1,0:T(8,128)(2,1)} %copy-done.38, bf16[4,4,2,176,512]{4,3,2,1,0:T(8,128)(2,1)} %bitcast.115, bf16[4,176,512]{2,1,0:T(8,128)(2,1)} %copy-done.39, ...), custom_call_target="tpu_custom_call" | custom-call | flops 80000000000 | bytes 40000000 | tf_op jit(solution)/shard_map/ffn_plane/pallas_call | solution.py:828
  402.8 37.5 %attend_back.1 = (f32[256,2048]{1,0:T(8,128)}, f32[256,2048]{1,0:T(8,128)}, bf16[8,128,256]{2,1,0:T(8,128)(2,1)S(1)}, bf16[8,128,256]{2,1,0:T(8,128)(2,1)S(1)}, ...) custom-call(f32[256,2048]{1,0:T(8,128)} %copy-done.36, ...), custom_call_target="tpu_custom_call" | custom-call | flops 30000001024 | bytes 40000000 | tf_op jit(solution)/shard_map/attend_back/pallas_call | solution.py:1666
  444.8 1.2 collective-permute-start.14
  447.2 28.8 %mixer_backward.2 = (bf16[1024,1024]{1,0:T(8,128)(2,1)}, bf16[1024,128]{1,0:T(8,128)(2,1)}, f32[12,256]{1,0:T(8,128)}, f32[2,128]{1,0:T(2,128)}) custom-call(s32[3]{0:T(128)} %copy-done.17, f32[1024,1024]{1,0:T(8,128)} %bitcast.120, f32[1024,128]{1,0:T(8,128)} %bitcast.84, f32[12,256]{1,0:T(8,128)} %copy-done.15, f32[2,128]{1,0:T(2,128)} %copy-done.27, ...), custom_call_target="tpu_custom_call" | custom-call | flops 10000000000 | bytes 10000000 | tf_op jit(solution)/shard_map/mixer_backward/pallas_call | solution.py:356
  476.1 1.6 add_convert_fusion.1
  477.8 2.0 add_convert_fusion
  482.5 2.0 collective-permute-start.16
  484.5 28.1 %mixer_backward.3 = (bf16[1024,1024]{1,0:T(8,128)(2,1)}, bf16[1024,128]{1,0:T(8,128)(2,1)}, f32[12,256]{1,0:T(8,128)}, f32[2,128]{1,0:T(2,128)}) custom-call(s32[3]{0:T(128)} %copy-done.16, f32[1024,1024]{1,0:T(8,128)} %bitcast.118, f32[1024,128]{1,0:T(8,128)} %bitcast.82, f32[12,256]{1,0:T(8,128)} %copy-done.15, f32[2,128]{1,0:T(2,128)} %copy-done.27, ...), custom_call_target="tpu_custom_call" | custom-call | flops 10000000000 | bytes 10000000 | tf_op jit(solution)/shard_map/mixer_backward/pallas_call | solution.py:356
  512.6 1.0 pad_maximum_fusion.3
  513.6 4.6 multiply_reduce_fusion
  519.2 1.8 pad_maximum_fusion.2.refs_5_
  521.6 2.8 pad_maximum_fusion
  524.4 2.4 fusion.13
  526.8 2.0 fusion.14
  528.9 12.8 %fusion.22 = (bf16[2048,1024]{1,0:T(8,128)(2,1)}, f32[2048,1024]{1,0:T(8,128)S(1)}) fusion(bf16[2048,2048]{1,0:T(8,128)(2,1)} %bitcast.98, bf16[2048,1024]{1,0:T(8,128)(2,1)S(1)} %bitcast.100), kind=kOutput, calls=%fused_computation.65 | convolution fusion | flops 8592031744 | bytes 25165824 | tf_op jit(solution)/shard_map/tm,tn->mn/dot_general | solution.py:1722
  541.7 1.2 fusion.11
  543.8 2.3 pad_maximum_fusion.1.refs_6_
  546.1 114.4 %scatter_rows.1 = (f32[2,128,2048]{2,1,0:T(8,128)}, f32[72,128]{1,0:T(8,128)}, bf16[4,64,2048]{2,1,0:T(8,128)(2,1)}, bf16[2,1024,1024]{2,1,0:T(8,128)(2,1)}, bf1...) custom-call(bf16[2048,256]{1,0:T(8,128)(2,1)} %refs_0_.1, bf16[2048,256]{1,0:T(8,128)(2,1)} %refs_1_.1, ...), custom_call_target="tpu_custom_call" | custom-call | flops 70000001024 | bytes 40000000 | tf_op jit(solution)/shard_map/scatter_rows/pallas_call | solution.py:1428
  662.6 1.2 split.11
  663.9 2.3 fusion.20
  666.2 5.9 slice_convert_fusion
  673.3 1.6 bitcast_convert_fusion
  674.9 1.3 bitcast_convert_fusion.1
  676.2 1.0 reshape.243
  678.9 3.3 convert_bitcast_fusion
  682.2 2.1 fusion.6
  684.8 1.3 copy.46
  (204 shorter events, 33.4 us)
Async XLA Ops:
  7.2 11.1 %copy-start = (bf16[256,2048]{1,0:T(8,128)(2,1)S(1)}, bf16[256,2048]{1,0:T(8,128)(2,1)}, u32[]{:S(2)}) copy-start(bf16[256,2048]{1,0:T(8,128)(2,1)} %param.27) | copy-start | bytes 3145732
  7.2 11.2 %copy-start.2 = (bf16[2,128,2048]{2,1,0:T(8,128)(2,1)S(1)}, bf16[2,128,2048]{2,1,0:T(8,128)(2,1)}, u32[]{:S(2)}) copy-start(bf16[2,128,2048]{2,1,0:T(8,128)(2,1)} %param.16) | copy-start | bytes 3145732
  7.2 245.3 %all-gather.3.cloned.1.call-start = ((), (), s32[]{:S(2)}) async-start(), calls=%async_computation.2 | async-start | bytes 7208960 | tf_op jit(solution)/shard_map/all_gather | solution.py:1704
  14.9 3.8 copy-start.52
  20.0 102.7 %copy-start.12 = (bf16[2048,128]{1,0:T(8,128)(2,1)}, bf16[2048,128]{1,0:T(8,128)(2,1)S(1)}, u32[]{:S(2)}) copy-start(bf16[2048,128]{1,0:T(8,128)(2,1)S(1)} %pad.12.refs_7_.refs_8_) | copy-start | bytes 1572868
  124.6 5.5 copy-start.64
  124.6 5.5 copy-start.61
  124.6 5.5 copy-start.68
  124.6 421.5 %reduce-scatter.2.cloned.1.call-start = ((), (), s32[]{:S(2)}) async-start(), calls=%async_computation.1 | async-start | bytes 7208960 | tf_op jit(solution)/shard_map/reduce_scatter | solution.py:1872
  124.9 47.9 %collective-permute-start.1 = (bf16[256,2048]{1,0:T(8,128)(2,1)}, bf16[256,2048]{1,0:T(8,128)(2,1)}, u32[]{:S(2)}, u32[]{:S(2)}) collective-permute-start(bf16[256,2048]{1,0:T(8,128)(2,1)} %bitcast.16.refs_0_.c_ref), channel_id=1, source_target_pairs={{0,16},{16,0},{1,17},{17,1},{2,18},{18,2},{3,19},{19,3},{4,20},{20... | collective-permute-start | bytes 3145736 | tf_op jit(solution)/shard_map/ppermute | solution.py:1727
  126.1 46.6 %collective-permute-start.2 = (bf16[256,2048]{1,0:T(8,128)(2,1)}, bf16[256,2048]{1,0:T(8,128)(2,1)}, u32[]{:S(2)}, u32[]{:S(2)}) collective-permute-start(bf16[256,2048]{1,0:T(8,128)(2,1)} %bitcast.16.refs_0_.c_ref), channel_id=1, source_target_pairs={{0,1},{1,0},{2,3},{3,2},{4,5},{5,4},{6,7},{7,6},{8,9},{9,8},{10,11... | collective-permute-start | bytes 3145736 | tf_op jit(solution)/shard_map/ppermute | solution.py:1727
  127.7 45.1 %collective-permute-start = (bf16[4,64,2048]{2,1,0:T(8,128)(2,1)}, bf16[4,64,2048]{2,1,0:T(8,128)(2,1)}, u32[]{:S(2)}, u32[]{:S(2)}) collective-permute-start(bf16[4,64,2048]{2,1,0:T(8,128)(2,1)} %bitcast.86), channel_id=1, source_target_pairs={{0,1},{1,0},{2,3},{3,2},{4,5},{5,4},{6,7},{7,6},{8,9},{9,8},{10,11... | collective-permute-start | bytes 3145736 | tf_op jit(solution)/shard_map/ppermute | solution.py:1727
  128.2 72.5 %collective-permute-start.4 = (bf16[4,64,2048]{2,1,0:T(8,128)(2,1)}, bf16[4,64,2048]{2,1,0:T(8,128)(2,1)}, u32[]{:S(2)}, u32[]{:S(2)}) collective-permute-start(bf16[4,64,2048]{2,1,0:T(8,128)(2,1)} %bitcast.87), channel_id=1, source_target_pairs={{0,16},{16,0},{1,17},{17,1},{2,18},{18,2},{3,19},{19,3},{4,20},{20... | collective-permute-start | bytes 3145736 | tf_op jit(solution)/shard_map/ppermute | solution.py:1727
  130.1 27.9 %copy-start.17 = (s32[3]{0:T(128)}, s32[3]{0:T(128)S(1)}, u32[]{:S(2)}) copy-start(s32[3]{0:T(128)S(1)} %get-tuple-element.205.lengths_ref) | copy-start | bytes 40
  130.1 44.3 %copy-start.16 = (s32[3]{0:T(128)}, s32[3]{0:T(128)S(1)}, u32[]{:S(2)}) copy-start(s32[3]{0:T(128)S(1)} %get-tuple-element.204.lengths_ref) | copy-start | bytes 40
  130.1 44.3 %copy-start.15 = (f32[12,256]{1,0:T(8,128)}, f32[12,256]{1,0:T(8,128)S(1)}, u32[]{:S(2)}) copy-start(f32[12,256]{1,0:T(8,128)S(1)} %reshape.247.tap_ref) | copy-start | bytes 36868
  130.1 44.2 %copy-start.27 = (f32[2,128]{1,0:T(2,128)}, f32[2,128]{1,0:T(2,128)S(1)}, u32[]{:S(2)}) copy-start(f32[2,128]{1,0:T(2,128)S(1)} %convert_element_type.129.gain_ref) | copy-start | bytes 3076
  131.2 42.6 %copy-start.19 = (bf16[4,2,32,2048]{3,2,1,0:T(8,128)(2,1)S(1)}, bf16[4,2,32,2048]{3,2,1,0:T(8,128)(2,1)}, u32[]{:S(2)}) copy-start(bf16[4,2,32,2048]{3,2,1,0:T(8,128)(2,1)} %copy-done.18) | copy-start | bytes 3145732
  131.3 43.1 %copy-start.13 = (f32[1,8,128,128]{3,2,1,0:T(8,128)S(1)}, f32[1,8,128,128]{3,2,1,0:T(8,128)}, u32[]{:S(2)}) copy-start(f32[1,8,128,128]{3,2,1,0:T(8,128)} %get-tuple-element.198) | copy-start | bytes 1572868
  172.7 28.0 %collective-permute-start.5 = (bf16[4,64,2048]{2,1,0:T(8,128)(2,1)}, bf16[4,64,2048]{2,1,0:T(8,128)(2,1)S(1)}, u32[]{:S(2)}, u32[]{:S(2)}) collective-permute-start(bf16[4,64,2048]{2,1,0:T(8,128)(2,1)} %collective-permute-done.refs_4_), channel_id=1, source_target_pairs={{0,16},{16,0},{1,17},{17,1},{2,18},{18,2},{3,19},{19,3},{4,20},{20... | collective-permute-start | bytes 3145736 | tf_op jit(solution)/shard_map/ppermute | solution.py:1727
  173.3 27.4 %collective-permute-start.6 = (bf16[256,2048]{1,0:T(8,128)(2,1)}, bf16[256,2048]{1,0:T(8,128)(2,1)}, u32[]{:S(2)}, u32[]{:S(2)}) collective-permute-start(bf16[256,2048]{1,0:T(8,128)(2,1)} %collective-permute-done.1.refs_1_), channel_id=1, source_target_pairs={{0,1},{1,0},{2,3},{3,2},{4,5},{5,4},{6,7},{7,6},{8,9},{9,8},{10,11... | collective-permute-start | bytes 3145736 | tf_op jit(solution)/shard_map/ppermute | solution.py:1727
  173.9 27.5 %collective-permute-start.3 = (bf16[4,64,2048]{2,1,0:T(8,128)(2,1)S(1)}, bf16[4,64,2048]{2,1,0:T(8,128)(2,1)S(1)}, u32[]{:S(2)}, u32[]{:S(2)}) collective-permute-start(bf16[4,64,2048]{2,1,0:T(8,128)(2,1)S(1)} %bitcast.88), channel_id=1, source_target_pairs={{0,8},{8,0},{1,9},{9,1},{2,10},{10,2},{3,11},{11,3},{4,12},{12,4},... | collective-permute-start | bytes 3145736 | tf_op jit(solution)/shard_map/ppermute | solution.py:1727
  173.9 28.0 %collective-permute-start.8 = (bf16[4,64,2048]{2,1,0:T(8,128)(2,1)}, bf16[4,64,2048]{2,1,0:T(8,128)(2,1)S(1)}, u32[]{:S(2)}, u32[]{:S(2)}) collective-permute-start(bf16[4,64,2048]{2,1,0:T(8,128)(2,1)} %collective-permute-done.refs_4_), channel_id=1, source_target_pairs={{0,8},{8,0},{1,9},{9,1},{2,10},{10,2},{3,11},{11,3},{4,12},{12,4},... | collective-permute-start | bytes 3145736 | tf_op jit(solution)/shard_map/ppermute | solution.py:1727
  200.7 43.1 %copy-start.28 = (f32[1024,256]{1,0:T(8,128)}, f32[1024,256]{1,0:T(8,128)S(1)}, u32[]{:S(2)}) copy-start(f32[1024,256]{1,0:T(8,128)S(1)} %get-tuple-element.119.heads_ref) | copy-start | bytes 3145732
  200.7 43.1 %copy-start.29 = (f32[1024,256]{1,0:T(8,128)}, f32[1024,256]{1,0:T(8,128)S(1)}, u32[]{:S(2)}) copy-start(f32[1024,256]{1,0:T(8,128)S(1)} %get-tuple-element.120.fixed_ref) | copy-start | bytes 3145732
  200.7 43.1 %copy-start.30 = (f32[1024,256]{1,0:T(8,128)}, f32[1024,256]{1,0:T(8,128)S(1)}, u32[]{:S(2)}) copy-start(f32[1024,256]{1,0:T(8,128)S(1)} %get-tuple-element.121.delta_ref) | copy-start | bytes 3145732
  200.7 43.2 %copy-start.31 = (f32[16,128,128]{2,1,0:T(8,128)}, f32[16,128,128]{2,1,0:T(8,128)S(1)}, u32[]{:S(2)}) copy-start(f32[16,128,128]{2,1,0:T(8,128)S(1)} %get-tuple-element.122.state_ref) | copy-start | bytes 3145732
  200.7 3.7 collective-permute-start.7
  200.8 5.3 collective-permute-start.9
  201.3 45.8 %collective-permute-start.10 = (bf16[256,2048]{1,0:T(8,128)(2,1)}, bf16[256,2048]{1,0:T(8,128)(2,1)S(1)}, u32[]{:S(2)}, u32[]{:S(2)}) collective-permute-start(bf16[256,2048]{1,0:T(8,128)(2,1)} %bitcast.16.refs_0_.c_ref), channel_id=1, source_target_pairs={{0,8},{8,0},{1,9},{9,1},{2,10},{10,2},{3,11},{11,3},{4,12},{12,4},... | collective-permute-start | bytes 3145736 | tf_op jit(solution)/shard_map/ppermute | solution.py:1727
  201.4 46.7 %collective-permute-start.11 = (bf16[256,2048]{1,0:T(8,128)(2,1)}, bf16[256,2048]{1,0:T(8,128)(2,1)S(1)}, u32[]{:S(2)}, u32[]{:S(2)}) collective-permute-start(bf16[256,2048]{1,0:T(8,128)(2,1)} %collective-permute-done.1.refs_1_), channel_id=1, source_target_pairs={{0,8},{8,0},{1,9},{9,1},{2,10},{10,2},{3,11},{11,3},{4,12},{12,4},... | collective-permute-start | bytes 3145736 | tf_op jit(solution)/shard_map/ppermute | solution.py:1727
  201.8 47.2 %collective-permute-start.12 = (bf16[256,2048]{1,0:T(8,128)(2,1)}, bf16[256,2048]{1,0:T(8,128)(2,1)S(1)}, u32[]{:S(2)}, u32[]{:S(2)}) collective-permute-start(bf16[256,2048]{1,0:T(8,128)(2,1)} %collective-permute-done.2.refs_2_), channel_id=1, source_target_pairs={{0,8},{8,0},{1,9},{9,1},{2,10},{10,2},{3,11},{11,3},{4,12},{12,4},... | collective-permute-start | bytes 3145736 | tf_op jit(solution)/shard_map/ppermute | solution.py:1727
  204.4 45.7 %collective-permute-start.13 = (bf16[256,2048]{1,0:T(8,128)(2,1)}, bf16[256,2048]{1,0:T(8,128)(2,1)}, u32[]{:S(2)}, u32[]{:S(2)}) collective-permute-start(bf16[256,2048]{1,0:T(8,128)(2,1)} %collective-permute-done.6.refs_3_), channel_id=1, source_target_pairs={{0,8},{8,0},{1,9},{9,1},{2,10},{10,2},{3,11},{11,3},{4,12},{12,4},... | collective-permute-start | bytes 3145736 | tf_op jit(solution)/shard_map/ppermute | solution.py:1727
  444.8 31.3 %collective-permute-start.14 = (bf16[2,4,64,1024]{3,2,1,0:T(8,128)(2,1)}, bf16[2,4,64,1024]{3,2,1,0:T(8,128)(2,1)}, u32[]{:S(2)}, u32[]{:S(2)}) collective-permute-start(bf16[2,4,64,1024]{3,2,1,0:T(8,128)(2,1)} %copy-done.21), channel_id=1, source_target_pairs={{0,16},{16,0},{1,17},{17,1},{2,18},{18,2},{3,19},{19,3},{4,20},{20... | collective-permute-start | bytes 3145736 | tf_op jit(solution)/shard_map/ppermute | solution.py:1727
  446.0 31.8 %collective-permute-start.15 = (bf16[2,4,64,1024]{3,2,1,0:T(8,128)(2,1)}, bf16[2,4,64,1024]{3,2,1,0:T(8,128)(2,1)}, u32[]{:S(2)}, u32[]{:S(2)}) collective-permute-start(bf16[2,4,64,1024]{3,2,1,0:T(8,128)(2,1)} %copy-done.20), channel_id=1, source_target_pairs={{0,1},{1,0},{2,3},{3,2},{4,5},{5,4},{6,7},{7,6},{8,9},{9,8},{10,11... | collective-permute-start | bytes 3145736 | tf_op jit(solution)/shard_map/ppermute | solution.py:1727
  447.2 28.9 %copy-start.11 = (bf16[2,4,64,1024]{3,2,1,0:T(8,128)(2,1)S(1)}, bf16[2,4,64,1024]{3,2,1,0:T(8,128)(2,1)}, u32[]{:S(2)}) copy-start(bf16[2,4,64,1024]{3,2,1,0:T(8,128)(2,1)} %copy-done.10) | copy-start | bytes 3145732
  477.7 3.9 copy-start.42
  480.7 43.7 %collective-permute-start.17 = (bf16[4,64,1024]{2,1,0:T(8,128)(2,1)}, bf16[4,64,1024]{2,1,0:T(8,128)(2,1)}, u32[]{:S(2)}, u32[]{:S(2)}) collective-permute-start(bf16[4,64,1024]{2,1,0:T(8,128)(2,1)} %dynamic-slice_bitcast_fusion), channel_id=1, source_target_pairs={{0,16},{16,0},{1,17},{17,1},{2,18},{18,2},{3,19},{19,3},{4,20},{20... | collective-permute-start | bytes 1572872 | tf_op jit(solution)/shard_map/ppermute | solution.py:1727
  482.5 44.3 %collective-permute-start.16 = (bf16[4,64,1024]{2,1,0:T(8,128)(2,1)}, bf16[4,64,1024]{2,1,0:T(8,128)(2,1)}, u32[]{:S(2)}, u32[]{:S(2)}) collective-permute-start(bf16[4,64,1024]{2,1,0:T(8,128)(2,1)} %dynamic-slice_bitcast_fusion.1), channel_id=1, source_target_pairs={{0,1},{1,0},{2,3},{3,2},{4,5},{5,4},{6,7},{7,6},{8,9},{9,8},{10,11... | collective-permute-start | bytes 1572872 | tf_op jit(solution)/shard_map/ppermute | solution.py:1727
  484.5 28.1 %copy-start.50 = (bf16[1024,128]{1,0:T(8,128)(2,1)S(1)}, bf16[1024,128]{1,0:T(8,128)(2,1)}, u32[]{:S(2)}) copy-start(bf16[1024,128]{1,0:T(8,128)(2,1)} %get-tuple-element.126) | copy-start | bytes 786436
  484.5 29.1 %copy-start.56 = (bf16[2048,2]{0,1:T(2,128)(2,1)S(1)}, bf16[2048,2]{0,1:T(2,128)(2,1)}, u32[]{:S(2)}) copy-start(bf16[2048,2]{0,1:T(2,128)(2,1)} %param.24) | copy-start | bytes 24580
  521.6 5.2 copy-start.43
  524.4 17.3 %copy-start.46 = (bf16[2,1024,1024]{2,1,0:T(8,128)(2,1)}, bf16[2,1024,1024]{2,1,0:T(8,128)(2,1)S(1)}, u32[]{:S(2)}) copy-start(bf16[2,1024,1024]{2,1,0:T(8,128)(2,1)S(1)} %pad_maximum_fusion) | copy-start | bytes 12582916
  528.9 12.8 %copy-start.5 = (bf16[2048,256]{1,0:T(8,128)(2,1)S(1)}, bf16[2048,256]{1,0:T(8,128)(2,1)}, u32[]{:S(2)}) copy-start(bf16[2048,256]{1,0:T(8,128)(2,1)} %refs_1_.1) | copy-start | bytes 3145732
  528.9 12.8 %copy-start.7 = (bf16[2048,256]{1,0:T(8,128)(2,1)S(1)}, bf16[2048,256]{1,0:T(8,128)(2,1)}, u32[]{:S(2)}) copy-start(bf16[2048,256]{1,0:T(8,128)(2,1)} %refs_2_.1) | copy-start | bytes 3145732
  528.9 12.8 %copy-start.9 = (bf16[2048,256]{1,0:T(8,128)(2,1)S(1)}, bf16[2048,256]{1,0:T(8,128)(2,1)}, u32[]{:S(2)}) copy-start(bf16[2048,256]{1,0:T(8,128)(2,1)} %refs_3_.3) | copy-start | bytes 3145732
  666.2 5.9 copy-start.40
  666.2 5.9 copy-start.53
  (41 other events, 67.2 us)
Sparse Core Ops, SparseCore 0:
  124.8 127.6 all-gather.2
  444.9 99.6 reduce-scatter.1

commit v7 on v6

--- a/solution.py
+++ b/solution.py
@@ -1129,12 +1129,13 @@
             beta.reshape(batches, total, 128), pair_parts, down_part)
 
 
-def scatter_kernel(w_refs, g_ref, gb_ref, o_ref, inner_ref, wb_ref, small_ref, gains_ref, pair_ref, down_ref,
+def scatter_kernel(w_refs, g_refs, gb_refs, o_refs, inner_ref, wb_ref, small_ref, gains_ref, pair_ref, down_ref,
                    out_ref, small_out, outs_ref, inner_out, pair_out, down_out,
                    gs, bs, ysend, yrecv, from_left, from_right, part_sum, part_left, part_right, outs_s, inner_s, inner_r, small_s, small_r, gains_r,
                    pair_send, pair_recv, right_send, left_send, right_recv, left_recv, g_sem,
                    sum_send, sum_recv, outs_send, outs_recv, gain_send, gain_recv, part_sems, swap_send, swap_recv, swap_own, sum_sem):
-    batches, rows, width = gs.shape
+    batches = len(g_refs)
+    rows, width = gs.shape
     lines = yrecv.shape[0]
     model = yrecv.shape[3]
     o = lax.axis_index("z")
@@ -1195,26 +1196,28 @@
         z = o + side * far
         return far, z, (z >= 0) & (z < lines) & ((far > 0) | (side > 0))
 
-    def load(z, y):
+    def load(z, y, m):
         slot = z * 2 + y
-        return (pltpu.make_async_copy(g_ref.at[:, slot], gs, g_sem.at[0]),
-                pltpu.make_async_copy(gb_ref.at[:, slot], bs, g_sem.at[1]))
-
-    def partial_rows(z, y, store):
-        for copy in load(z, y):
-            copy.start()
-        for copy in load(z, y):
+        return (pltpu.make_async_copy(g_refs[m].at[slot], gs, g_sem.at[0]),
+                pltpu.make_async_copy(gb_refs[m].at[slot], bs, g_sem.at[1]))
+
+    def partial_rows(z, y, m, store):
+        for n in range(batches):
+            @pl.when(m == n)
+            def _():
+                for copy in load(z, y, n):
+                    copy.start()
+        for copy in load(z, y, 0):
             copy.wait()
-        for m in range(batches):
-            g = gs[m]
-            b = bs[m]
-            for start in range(0, model, tile):
-                cols = slice(start, start + tile)
-                value = lax.dot_general(b, wb_ref[cols, :], NT, preferred_element_type=f32)
-                for n, w_ref in enumerate(w_refs):
-                    part = g[:, n * w_ref.shape[1] : (n + 1) * w_ref.shape[1]]
-                    value = value + lax.dot_general(part, w_ref[cols, :], NT, preferred_element_type=f32)
-                store(m, cols, value)
+        g = gs[...]
+        b = bs[...]
+        for start in range(0, model, tile):
+            cols = slice(start, start + tile)
+            value = lax.dot_general(b, wb_ref[cols, :], NT, preferred_element_type=f32)
+            for n, w_ref in enumerate(w_refs):
+                part = g[:, n * w_ref.shape[1] : (n + 1) * w_ref.shape[1]]
+                value = value + lax.dot_general(part, w_ref[cols, :], NT, preferred_element_type=f32)
+            store(cols, value)
 
     def across(z, m):
         return line_copy(ysend.at[z, m], yrecv.at[z, m], pair_send.at[z, m], pair_recv.at[z, m], other("y"))
@@ -1225,10 +1228,10 @@
     def left(z, m):
         return line_copy(yrecv.at[z, m], from_right.at[z, m], left_send.at[z, m], left_recv.at[z, m], {"z": o - 1})
 
-    def across_partial(z):
-        def store(m, cols, value):
+    def across_partial(z, m):
+        def store(cols, value):
             ysend[z, m, :, cols] = value.astype(bf16)
-        partial_rows(z, 1 - i, store)
+        partial_rows(z, 1 - i, m, store)
 
     def pass_part(z):
         return (line_copy(part_sum.at[z], part_left.at[z], part_sems.at[0, z], part_sems.at[1, z], {"z": o + 1}),
@@ -1278,8 +1281,14 @@
             copy.start()
 
     def side_work():
+        left, left_in, right, right_in = o_refs
+        column, row = lax.axis_index("y"), lax.axis_index("x")
+        wide = model // 2
         for z in range(lines):
-            part_sum[z] = o_ref[z]
+            part_sum[z, :, :wide] = (
+                left[column, z].astype(f32) + left_in[z].astype(f32)).astype(bf16)
+            part_sum[z, :, wide:] = (
+                right[row, z].astype(f32) + right_in[z].astype(f32)).astype(bf16)
         part_round()
         inner_own.wait()
         inner_pair.wait_recv()
@@ -1293,59 +1302,69 @@
         small_s[0, tail:] = jnp.sum(gains_r[...], axis=0)
         small_pair.start()
 
-    def turn(index, before):
-        far, z, valid = target(index)
-        last = index == 2 * lines
-        valid = valid & (index < 2 * lines)
-        ready = (valid | last) & (before >= 0)
+    total = 2 * lines * batches
+
+    def turn(index, carry):
+        before, earlier = carry
+        far, z, valid = target(index // batches)
+        m = lax.rem(index, batches)
+        last = index >= total
+        valid = valid & jnp.logical_not(last)
+        moves = valid | last
 
         @pl.when(valid)
         def _():
-            across_partial(z)
-
-        @pl.when(ready)
-        def _():
-            for m in range(batches):
-                across(before, m).wait_recv()
+            across_partial(z, m)
 
         @pl.when(valid)
         def _():
-            for m in range(batches):
-                across(z, m).start()
+            across(z, m).start()
+
+        @pl.when(moves & (before >= 0))
+        def _():
+            across(before // batches, lax.rem(before, batches)).wait_recv()
 
         @pl.when(valid & (before < 0))
         def _():
             side_work()
 
-        @pl.when(ready)
-        def _():
-            z = before
-
-            def store(m, cols, value):
-                yrecv[z, m, :, cols] = (yrecv[z, m, :, cols].astype(f32) + value).astype(bf16)
-            partial_rows(z, i, store)
-            for m in range(batches):
-                @pl.when((z > o) & (o > 0))
-                def _():
-                    right(z, m).wait_recv()
-                    add_into(yrecv.at[z, m], from_left.at[z, m])
-
-                @pl.when(z > o)
-                def _():
-                    right(z, m).start()
-
-                @pl.when((z < o) & (o < lines - 1))
-                def _():
-                    left(z, m).wait_recv()
-                    add_into(yrecv.at[z, m], from_right.at[z, m])
-
-                @pl.when(z < o)
-                def _():
-                    left(z, m).start()
-
-        return jnp.where(valid, z, before)
-
-    lax.fori_loop(0, 2 * lines + 1, turn, jnp.int32(-1))
+        @pl.when(moves & (before >= 0))
+        def _():
+            place, n = before // batches, lax.rem(before, batches)
+
+            def store(cols, value):
+                yrecv[place, n, :, cols] = (
+                    yrecv[place, n, :, cols].astype(f32) + value).astype(bf16)
+            partial_rows(place, i, n, store)
+
+            @pl.when((place > o) & (o == 0))
+            def _():
+                right(place, n).start()
+
+            @pl.when((place < o) & (o == lines - 1))
+            def _():
+                left(place, n).start()
+
+        @pl.when(moves & (earlier >= 0))
+        def _():
+            place, n = earlier // batches, lax.rem(earlier, batches)
+
+            @pl.when((place > o) & (o > 0))
+            def _():
+                right(place, n).wait_recv()
+                add_into(yrecv.at[place, n], from_left.at[place, n])
+                right(place, n).start()
+
+            @pl.when((place < o) & (o < lines - 1))
+            def _():
+                left(place, n).wait_recv()
+                add_into(yrecv.at[place, n], from_right.at[place, n])
+                left(place, n).start()
+
+        code = jnp.where(valid, z * batches + m, -1)
+        return jnp.where(moves, code, before), jnp.where(moves, before, earlier)
+
+    lax.fori_loop(0, total + 2, turn, (jnp.int32(-1), jnp.int32(-1)))
 
     inner_across.wait_recv()
     inner_across.wait_send()
@@ -1408,17 +1427,18 @@
 
 
 def scatter_call_kernel(*refs):
-    scatter_kernel(refs[:4], *refs[4:])
+    scatter_kernel(refs[:4], refs[4:6], refs[6:8], refs[8:12], *refs[12:])
 
 
 def scatter_rows(grads, beta_grads, out_grads, inner_grads, w_inner, w_beta, small, gains,
                  pair_grads, down_grads):
-    batches, total, width = grads.shape
+    batches = len(grads)
+    total, width = grads[0].shape
     model = w_inner[0].shape[0]
     lines = lax.axis_size("z")
     slots = 2 * lines
     rows = total // slots
-    more = out_grads.shape[1]
+    more = out_grads[1].shape[1]
     sems = pltpu.SemaphoreType.DMA
     anywhere = pl.BlockSpec(memory_space=pl.ANY)
     slab = pltpu.VMEM((lines, batches, rows, model), bf16)
@@ -1435,11 +1455,12 @@
             jax.ShapeDtypeStruct(pair_grads.shape, bf16),
             jax.ShapeDtypeStruct(down_grads.shape, bf16),
         ),
-        in_specs=[vmem()] * 4 + [anywhere, anywhere, vmem(), anywhere, vmem(), vmem(), vmem(), anywhere, anywhere],
+        in_specs=[vmem()] * 4 + [anywhere] * 4 + [vmem()] * 4
+        + [anywhere, vmem(), vmem(), vmem(), anywhere, anywhere],
         out_specs=(vmem(), vmem()) + (anywhere,) * 4,
         scratch_shapes=[
-            pltpu.VMEM((batches, rows, width), bf16),
-            pltpu.VMEM((batches, rows, 128), bf16),
+            pltpu.VMEM((rows, width), bf16),
+            pltpu.VMEM((rows, 128), bf16),
             slab, slab, slab, slab, part, part, part,
             pltpu.VMEM((more, model), bf16),
             pltpu.VMEM(half, bf16),
@@ -1456,8 +1477,9 @@
             collective_id=3, has_side_effects=True, vmem_limit_bytes=58 * 2**20),
         cost_estimate=pl.CostEstimate(flops=7 * 10**10, bytes_accessed=4 * 10**7, transcendentals=0),
         name="scatter_rows",
-    )(*w_inner, grads.reshape(batches, slots, rows, width),
-      beta_grads.reshape(batches, slots, rows, 128), out_grads, inner_grads, w_beta, small, gains,
+    )(*w_inner, *[grad.reshape(slots, rows, width) for grad in grads],
+      *[grad.reshape(slots, rows, 128) for grad in beta_grads], *out_grads,
+      inner_grads, w_beta, small, gains,
       pair_grads, down_grads)
 
 
@@ -1680,6 +1702,54 @@
         cost_estimate=pl.CostEstimate(flops=3 * 10**10, bytes_accessed=4 * 10**7, transcendentals=0),
         name="attend_back",
     )(hidden, ffn_out, normed_grad, c_rows, gain, w_full, heads)
+
+
+def inner_grads_kernel(x_ref, g_first, g_second, b_first, b_second, w0, w1, w2, w3, wb_ref,
+                       low_ref, beta_ref, gain_ref):
+    dims = (((0,), (0,)), ((), ()))
+    beta = 0.0
+    for m, b_ref in enumerate((b_first, b_second)):
+        beta = beta + lax.dot_general(x_ref[m], b_ref[...], dims, preferred_element_type=f32)
+    beta_ref[...] = beta
+    gain = jnp.sum(beta * wb_ref[...].astype(f32), axis=1, keepdims=True)
+    for n, w_ref in enumerate((w0, w1, w2, w3)):
+        width = w_ref.shape[1]
+        cols = slice(n * width, (n + 1) * width)
+        value = 0.0
+        for m, g_ref in enumerate((g_first, g_second)):
+            value = value + lax.dot_general(x_ref[m], g_ref[:, cols], dims, preferred_element_type=f32)
+        low_ref[:, cols] = value.astype(bf16)
+        gain = gain + jnp.sum(value * w_ref[...].astype(f32), axis=1, keepdims=True)
+    gain_ref[...] = jnp.broadcast_to(gain, gain_ref.shape)
+
+
+def inner_grads(tokens, grads, beta_grads, w_inner, w_beta):
+    _, total, model = tokens.shape
+    wide = grads[0].shape[1]
+    width = w_inner[0].shape[1]
+    tile = 256
+
+    def whole(columns):
+        return pl.BlockSpec((total, columns), lambda n: (0, 0))
+
+    def rows(columns):
+        return pl.BlockSpec((tile, columns), lambda n: (n, 0))
+
+    return pl.pallas_call(
+        inner_grads_kernel,
+        out_shape=(
+            jax.ShapeDtypeStruct((model, wide), bf16),
+            jax.ShapeDtypeStruct((model, 128), f32),
+            jax.ShapeDtypeStruct((model, 128), f32),
+        ),
+        grid=(model // tile,),
+        in_specs=[pl.BlockSpec((2, total, tile), lambda n: (0, 0, n))]
+        + [whole(wide)] * 2 + [whole(128)] * 2 + [rows(width)] * 4 + [rows(128)],
+        out_specs=(rows(wide), rows(128), rows(128)),
+        compiler_params=pltpu.CompilerParams(vmem_limit_bytes=40 * 2**20),
+        cost_estimate=pl.CostEstimate(flops=10**10, bytes_accessed=2 * 10**7, transcendentals=0),
+        name="inner_grads",
+    )(tokens, *grads, *beta_grads, *w_inner, w_beta)
 
 
 def root_scale(row_values, gain_vector):
@@ -1908,24 +1978,26 @@
         heads_sum = heads_sum + heads_part
         projected_low.append(projected_grad)
         beta_low.append(beta_grad)
-    projected_low = jnp.stack(projected_low)
-    beta_low = jnp.stack(beta_low)
     if planar:
-        left, right = halve_sum(left, "y"), halve_sum(right, "x")
-        projected_low = after(projected_low, left, right)
-        out_grad = jnp.concatenate([left, right], axis=2)
-    tokens = gathered_one.reshape(-1, gathered_one.shape[2])
-    inner_sum = dot_tn(tokens, projected_low.reshape(-1, 4 * local_width))
-    beta_sum = dot_tn(tokens, beta_low.reshape(-1, 128)[:, :heads])
-    gain_one_sum = (
-        sum(
-            jnp.sum(inner_sum[:, n * local_width : (n + 1) * local_width] * w.astype(f32), axis=1)
-            for n, w in enumerate(w_parts))
-        + jnp.sum(beta_sum * w_beta.astype(f32), axis=1)
-    ) / gain_one
+        left_in = exchange(pick(left, 1 - lax.axis_index("y"), 0), "y")
+        right_in = exchange(pick(right, 1 - lax.axis_index("x"), 0), "x")
+        low_sum, beta_sum, gain_rows = inner_grads(
+            gathered_one, projected_low, beta_low, w_parts, w_beta_wide)
+        beta_sum = beta_sum[:, :heads]
+        gain_one_sum = gain_rows[:, 0] / gain_one
+    else:
+        tokens = gathered_one.reshape(-1, gathered_one.shape[2])
+        inner_sum = dot_tn(tokens, jnp.concatenate(projected_low))
+        beta_sum = dot_tn(tokens, jnp.concatenate(beta_low)[:, :heads])
+        gain_one_sum = (
+            jnp.sum(inner_sum * w_inner.astype(f32), axis=1)
+            + jnp.sum(beta_sum * w_beta.astype(f32), axis=1)
+        ) / gain_one
+        low_sum = inner_sum.astype(bf16)
     gain_parts = jnp.stack([gain_one_sum, gain_two_sum])
-    small = jnp.concatenate([part.reshape(-1) for part in (beta_sum, taps_sum, heads_sum)])
-    low_sum = inner_sum.astype(bf16)
+    sums = [part.reshape(-1, 128) for part in (beta_sum.T, taps_sum, heads_sum)]
+    marks = [sums[0].shape[0], sums[0].shape[0] + sums[1].shape[0], sum(part.shape[0] for part in sums)]
+    small = jnp.concatenate(sums)
     if planar:
         ranks = lax.axis_size(DP)
         gain_parts = gain_parts.reshape(2, ranks, devices, -1).transpose(2, 0, 1, 3)
@@ -1933,9 +2005,9 @@
         gain_parts = gain_parts.reshape(devices, -1, 128)
         gain_rows = gain_parts.shape[1]
         gain_parts = jnp.pad(gain_parts, ((0, 0), (0, -gain_rows % 8), (0, 0)))
-        small = jnp.pad(small, (0, -small.size % 1024)).reshape(-1, 128)
+        small = jnp.pad(small, ((0, -small.shape[0] % 8), (0, 0)))
         input_norm, flat, out_total, inner_total, pair_grads, down_grads = scatter_rows(
-            projected_low, beta_low, out_grad,
+            projected_low, beta_low, (left, left_in, right, right_in),
             low_sum.reshape(2, -1, low_sum.shape[1]), w_parts, w_beta_wide, small, gain_parts,
             own_grads[0], down_grad)
         gate_share, up_share = (
@@ -1943,7 +2015,7 @@
         down_share = down_grads.reshape(w_down.shape).astype(f32)
         gain_totals = pick(
             flat[small.shape[0] :][:gain_rows].reshape(2, ranks, chunk), lax.axis_index(DP), 1)
-        small = flat[: small.shape[0]].reshape(-1)
+        small = flat[: small.shape[0]]
         out_total = out_total.reshape(w_out.shape).astype(f32)
         inner_total = inner_total.reshape(low_sum.shape)
     else:
@@ -1957,12 +2029,9 @@
                 dot_nt(projected_low[m], w_inner) + dot_nt(beta_low[m], w_beta_wide), TP)
             for m in batches])
     norm_grad, _ = norm_backward(rows_in, scale_one, gain_one, input_norm)
-    beta_total, conv_total, heads_total = (
-        piece.reshape(shape) for piece, shape in zip(
-            jnp.split(
-                small[: beta_sum.size + taps_sum.size + heads_sum.size],
-                (beta_sum.size, beta_sum.size + taps_sum.size)),
-            (beta_sum.shape, conv_weight.shape, head_gain.shape)))
+    beta_total = small[: marks[0]].reshape(heads, -1).T
+    conv_total = small[marks[0] : marks[1]].reshape(conv_weight.shape)
+    heads_total = small[marks[1] : marks[2]].reshape(head_gain.shape)
     columns = [
         inner_total[:, n * local_width : (n + 1) * local_width].astype(f32) for n in range(4)]
     return (

time: 705 us -> 702 us (level)
  Pallas kernels: 549 us -> 570 us
  matrix products: 17.4 us -> 0 us
  waiting for transfers between devices: 17.4 us -> 31.2 us
  other arithmetic: 35 us -> 21.8 us
    dot_general x2 -> x0, matrix products: 17.4 us -> none  [dot_tn(): return jnp.einsum('tm,tn->mn', a, b, preferred_element_type=f32)]
    pallas_call x0 -> x1, Pallas kernels: none -> 15.7 us  [inner_grads(): pl.pallas_call(inner_grads_kernel, out_shape=(jax.ShapeDtypeStruct((model...]
    ppermute x18, waiting for transfers between devices: 14.9 us -> 27.7 us  [exchange(): return lax.ppermute(x, axis_name, [(i, i ^ distance) for i in range(size)])]
    pallas_call x1, Pallas kernels: 114 us -> 122 us  [scatter_rows(): pl.pallas_call(scatter_call_kernel, out_shape=(jax.ShapeDtypeStruct((batc...]
    unnamed x141 -> x132, local copies, waits for them, and re-layouts: 26.8 us -> 26.2 us
  transfers between devices with their start and end apart: 20 -> 20, of which waited for: 4 -> 6; matrix products, arithmetic and copies ran while one was open for 6% -> 2% of each run, Pallas kernels for 21% -> 23%
where the time goes in v7:
time: 702 us; the launch traced here: 697 us
  Pallas kernels  570 us (81%)
  local copies, waits for them, and re-layouts  40.6 us (6%)
  waiting for transfers between devices  31.2 us (4%)
  other arithmetic  21.8 us (3%)
  between operations  15.2 us (2%)
  starting transfers between devices  12 us (2%)
    pallas_call x1, Pallas kernels, ffn_plane(): pl.pallas_call(ffn_call_kernel, out_shape=(jax.ShapeDtypeStruct((rows, mo...  150 us
    pallas_call x1, Pallas kernels, scatter_rows(): pl.pallas_call(scatter_call_kernel, out_shape=(jax.ShapeDtypeStruct((batc...  122 us
    pallas_call x1, Pallas kernels, gather_project(): pl.pallas_call(gather_call_kernel, out_shape=(jax.ShapeDtypeStruct((batch...  99.1 us
    pallas_call x2, Pallas kernels, mixer_backward(): pl.pallas_call(partial(mixer_backward_kernel, exact), out_shape=(jax.Shap...  56.5 us
    pallas_call x2, Pallas kernels, mixer_forward(): pl.pallas_call(partial(mixer_forward_kernel, exact, group), out_shape=(ja...  53.5 us
    pallas_call x1, Pallas kernels, attend_back(): pl.pallas_call(attend_back_kernel, out_shape=(wide, wide, back, back, *[j...  37.6 us
    pallas_call x1, Pallas kernels, attend(): pl.pallas_call(attend_kernel, out_shape=(jax.ShapeDtypeStruct((rows, mode...  35.9 us
    ppermute x18, waiting for transfers between devices, exchange(): return lax.ppermute(x, axis_name, [(i, i ^ distance) for i in range(size)])  27.7 us
  transfers between devices with their start and end apart: 20, of which 6 were waited for; matrix products, arithmetic and copies ran while one was open for 2% of the time, Pallas kernels for 23%

profile of v7, /device:TPU:0, one launch (start us, length us, event | category | flops | bytes accessed | tf_op | source)
XLA Modules:
  0.0 696.9 jit_solution(5308120149857611711)
XLA Ops:
  8.8 6.1 all_gather.6
  14.9 1.5 fusion.7
  16.5 1.8 copy.39
  18.7 1.3 pad.12.refs_7_.wb_ref.refs_13_
  20.3 1.1 copy-done.22
  21.4 1.1 copy-done.23
  22.6 1.1 copy-done.24
  23.7 99.1 %gather_project.1 = (bf16[2,8,128,2048]{3,2,1,0:T(8,128)(2,1)}, bf16[4,2,32,2048]{3,2,1,0:T(8,128)(2,1)S(1)}, f32[8,128,1024]{2,1,0:T(8,128)}, f32[8,128,1024]{2...) custom-call(bf16[2,128,2048]{2,1,0:T(8,128)(2,1)S(1)} %fusion.2.x_re, ...), custom_call_target="tpu_custom_call" | custom-call | flops 99999997952 | bytes 40000000 | tf_op jit(solution)/shard_map/gather_project/pallas_call | solution.py:1100
  125.0 1.3 collective-permute-start.1
  126.3 1.5 collective-permute-start.2
  129.4 26.8 %mixer_forward.2 = (bf16[1024,256]{1,0:T(8,128)(2,1)S(1)}, f32[1024,256]{1,0:T(8,128)S(1)}, f32[1024,256]{1,0:T(8,128)S(1)}, f32[1024,256]{1,0:T(8,128)S(1)}, f3...) custom-call(s32[3]{0:T(128)S(1)} %get-tuple-element.162.lengths_ref, f32[1024,1024]{1,0:T(8,128)} %bitcast.99, ...), custom_call_target="tpu_custom_call" | custom-call | flops 10000000000 | bytes 10000000 | tf_op jit(solution)/shard_map/mixer_forward/pallas_call | solution.py:333
  156.2 1.0 copy-done.32
  157.2 1.0 copy-done.33
  158.1 1.0 copy-done.34
  159.1 1.0 copy-done.35
  160.1 12.8 %collective-permute-done.refs_4_ = bf16[4,64,2048]{2,1,0:T(8,128)(2,1)} collective-permute-done((bf16[4,64,2048]{2,1,0:T(8,128)(2,1)}, bf16[4,64,2048]{2,1,0:T(8,128)(2,1)}, u32[]{:S(2)}, u32[]{:S(2)}) %collective-permute-start) | collective-permute-done | bytes 1048608 | tf_op jit(solution)/shard_map/ppermute | solution.py:1797
  174.5 26.6 %mixer_forward.3 = (bf16[1024,256]{1,0:T(8,128)(2,1)S(1)}, f32[1024,256]{1,0:T(8,128)S(1)}, f32[1024,256]{1,0:T(8,128)S(1)}, f32[1024,256]{1,0:T(8,128)S(1)}, f3...) custom-call(s32[3]{0:T(128)S(1)} %get-tuple-element.161.lengths_ref, f32[1024,1024]{1,0:T(8,128)} %bitcast.97, ...), custom_call_target="tpu_custom_call" | custom-call | flops 10000000000 | bytes 10000000 | tf_op jit(solution)/shard_map/mixer_forward/pallas_call | solution.py:333
  202.3 2.5 collective-permute-done.7.refs_3_
  204.9 3.1 collective-permute-done.9.refs_7_
  208.0 35.9 %attend.1 = (f32[256,2048]{1,0:T(8,128)S(1)}, bf16[256,2048]{1,0:T(8,128)(2,1)S(1)}, bf16[4,2,4,64,2048]{4,3,2,1,0:T(8,128)(2,1)}, bf16[2,8,128,256]{3,2,1,0:T(8,128)(2,1)S(1)}) custom-call(bf16[256,2048]{1,0:T(8,128)(2,1)S(1)} %bitcast.66, bf16[8,128,256]{2,1,0:T(8,128)(2,1)S(1)} %bitcast.81, bf16[8,128,256]{2,1,0:T(8,128)(2,1)S(1)} %bitcast.83, ...), custom_call_target="tpu_custom_call" | custom-call | flops 30000001024 | bytes 20000000 | tf_op jit(solution)/shard_map/attend/pallas_call | solution.py:1565
  244.0 1.3 copy-done.40
  245.3 1.0 copy-done.41
  246.2 1.0 copy-done.42
  247.2 3.4 all-gather.3.cloned.1.call-done
  250.7 150.3 %ffn_plane.1 = (f32[256,2048]{1,0:T(8,128)}, f32[256,2048]{1,0:T(8,128)}, bf16[4,4,2,176,512]{4,3,2,1,0:T(8,128)(2,1)}, bf16[4,176,512]{2,1,0:T(8,128)(2,1)}) custom-call(bf16[256,2048]{1,0:T(8,128)(2,1)} %copy-done.42, bf16[4,4,2,176,512]{4,3,2,1,0:T(8,128)(2,1)} %bitcast.94, bf16[4,176,512]{2,1,0:T(8,128)(2,1)} %copy-done.43, ...), custom_call_target="tpu_custom_call" | custom-call | flops 80000000000 | bytes 40000000 | tf_op jit(solution)/shard_map/ffn_plane/pallas_call | solution.py:828
  401.0 37.6 %attend_back.1 = (f32[256,2048]{1,0:T(8,128)}, f32[256,2048]{1,0:T(8,128)}, bf16[8,128,256]{2,1,0:T(8,128)(2,1)S(1)}, bf16[8,128,256]{2,1,0:T(8,128)(2,1)S(1)}, ...) custom-call(f32[256,2048]{1,0:T(8,128)} %copy-done.40, ...), custom_call_target="tpu_custom_call" | custom-call | flops 30000001024 | bytes 40000000 | tf_op jit(solution)/shard_map/attend_back/pallas_call | solution.py:1688
  439.5 1.0 copy-done.21
  442.1 2.2 collective-permute-start.14
  445.6 28.6 %mixer_backward.2 = (bf16[1024,1024]{1,0:T(8,128)(2,1)}, bf16[1024,128]{1,0:T(8,128)(2,1)}, f32[12,256]{1,0:T(8,128)}, f32[2,128]{1,0:T(2,128)}) custom-call(s32[3]{0:T(128)} %copy-done.9, f32[1024,1024]{1,0:T(8,128)} %bitcast.100, f32[1024,128]{1,0:T(8,128)} %bitcast.70, f32[12,256]{1,0:T(8,128)} %copy-done.7, f32[2,128]{1,0:T(2,128)} %copy-done.31, ...), custom_call_target="tpu_custom_call" | custom-call | flops 10000000000 | bytes 10000000 | tf_op jit(solution)/shard_map/mixer_backward/pallas_call | solution.py:356
  474.2 2.6 add_convert_fusion.1.refs_8_
  476.8 2.6 add_convert_fusion.refs_10_
  479.5 27.9 %mixer_backward.3 = (bf16[1024,1024]{1,0:T(8,128)(2,1)}, bf16[1024,128]{1,0:T(8,128)(2,1)}, f32[12,256]{1,0:T(8,128)}, f32[2,128]{1,0:T(2,128)}) custom-call(s32[3]{0:T(128)} %copy-done.8, f32[1024,1024]{1,0:T(8,128)} %bitcast.98, f32[1024,128]{1,0:T(8,128)} %bitcast.68, f32[12,256]{1,0:T(8,128)} %copy-done.7, f32[2,128]{1,0:T(2,128)} %copy-done.31, ...), custom_call_target="tpu_custom_call" | custom-call | flops 10000000000 | bytes 10000000 | tf_op jit(solution)/shard_map/mixer_backward/pallas_call | solution.py:356
  507.4 1.6 copy-done.25
  509.0 1.6 copy-done.26
  511.6 15.7 %inner_grads.1 = (bf16[2048,1024]{1,0:T(8,128)(2,1)}, f32[2048,128]{1,0:T(8,128)S(1)}, f32[2048,128]{1,0:T(8,128)S(1)}) custom-call(bf16[2,1024,2048]{2,1,0:T(8,128)(2,1)} %bitcast.96, bf16[1024,1024]{1,0:T(8,128)(2,1)S(1)} %copy-done.25, bf16[1024,1024]{1,0:T(8,128)(2,1)S(1)} %copy-done.26, bf16[1024,128]{1,0:T(8,128)(2,1)S(1)} %copy-done.29, ...), custom_call_target="tpu_custom_call" | custom-call | flops 10000000000 | bytes 20000000 | tf_op jit(solution)/shard_map/inner_grads/pallas_call | solution.py:1738
  527.9 1.9 dynamic-slice_bitcast_fusion
  531.0 2.0 collective-permute-start.16
  534.7 8.5 %collective-permute-done.17.refs_11_ = bf16[4,64,1024]{2,1,0:T(8,128)(2,1)} collective-permute-done((bf16[4,64,1024]{2,1,0:T(8,128)(2,1)}, bf16[4,64,1024]{2,1,0:T(8,128)(2,1)}, u32[]{:S(2)}, u32[]{:S(2)}) %collective-permute-start.17) | collective-permute-done | bytes 524320 | tf_op jit(solution)/shard_map/ppermute | solution.py:1797
  544.1 121.5 %scatter_rows.1 = (f32[2,128,2048]{2,1,0:T(8,128)}, f32[72,128]{1,0:T(8,128)}, bf16[4,64,2048]{2,1,0:T(8,128)(2,1)}, bf16[2,1024,1024]{2,1,0:T(8,128)(2,1)}, bf1...) custom-call(bf16[2048,256]{1,0:T(8,128)(2,1)} %refs_0_.1, bf16[2048,256]{1,0:T(8,128)(2,1)} %refs_1_.1, ...), custom_call_target="tpu_custom_call" | custom-call | flops 70000001024 | bytes 40000000 | tf_op jit(solution)/shard_map/scatter_rows/pallas_call | solution.py:1448
  667.7 1.2 slice.91
  669.0 1.4 fusion.11
  670.4 5.9 slice_convert_fusion
  677.5 1.6 bitcast_convert_fusion
  679.2 1.3 bitcast_convert_fusion.1
  681.8 2.1 convert_bitcast_fusion
  683.9 1.2 copy-done.47
  685.1 2.1 fusion.6
  687.7 1.3 copy.44
  (188 shorter events, 23.8 us)
Async XLA Ops:
  7.2 11.1 %copy-start = (bf16[256,2048]{1,0:T(8,128)(2,1)S(1)}, bf16[256,2048]{1,0:T(8,128)(2,1)}, u32[]{:S(2)}) copy-start(bf16[256,2048]{1,0:T(8,128)(2,1)} %param.27) | copy-start | bytes 3145732
  7.2 11.2 %copy-start.2 = (bf16[2,128,2048]{2,1,0:T(8,128)(2,1)S(1)}, bf16[2,128,2048]{2,1,0:T(8,128)(2,1)}, u32[]{:S(2)}) copy-start(bf16[2,128,2048]{2,1,0:T(8,128)(2,1)} %param.16) | copy-start | bytes 3145732
  7.2 243.5 %all-gather.3.cloned.1.call-start = ((), (), s32[]{:S(2)}) async-start(), calls=%async_computation.2 | async-start | bytes 7208960 | tf_op jit(solution)/shard_map/all_gather | solution.py:1774
  20.0 102.7 %copy-start.3 = (bf16[2048,128]{1,0:T(8,128)(2,1)}, bf16[2048,128]{1,0:T(8,128)(2,1)S(1)}, u32[]{:S(2)}) copy-start(bf16[2048,128]{1,0:T(8,128)(2,1)S(1)} %pad.12.refs_7_.wb_ref.refs_13_) | copy-start | bytes 1572868
  124.6 4.6 copy-start.62
  124.6 4.6 copy-start.59
  124.6 4.7 copy-start.64
  124.7 419.4 %reduce-scatter.2.cloned.1.call-start = ((), (), s32[]{:S(2)}) async-start(), calls=%async_computation.1 | async-start | bytes 7208960 | tf_op jit(solution)/shard_map/reduce_scatter | solution.py:1942
  125.0 35.1 %collective-permute-start.1 = (bf16[256,2048]{1,0:T(8,128)(2,1)}, bf16[256,2048]{1,0:T(8,128)(2,1)}, u32[]{:S(2)}, u32[]{:S(2)}) collective-permute-start(bf16[256,2048]{1,0:T(8,128)(2,1)} %bitcast.16.refs_0_.c_ref), channel_id=1, source_target_pairs={{0,16},{16,0},{1,17},{17,1},{2,18},{18,2},{3,19},{19,3},{4,20},{20... | collective-permute-start | bytes 3145736 | tf_op jit(solution)/shard_map/ppermute | solution.py:1797
  126.3 33.8 %collective-permute-start.2 = (bf16[256,2048]{1,0:T(8,128)(2,1)}, bf16[256,2048]{1,0:T(8,128)(2,1)}, u32[]{:S(2)}, u32[]{:S(2)}) collective-permute-start(bf16[256,2048]{1,0:T(8,128)(2,1)} %bitcast.16.refs_0_.c_ref), channel_id=1, source_target_pairs={{0,1},{1,0},{2,3},{3,2},{4,5},{5,4},{6,7},{7,6},{8,9},{9,8},{10,11... | collective-permute-start | bytes 3145736 | tf_op jit(solution)/shard_map/ppermute | solution.py:1797
  127.8 45.1 %collective-permute-start = (bf16[4,64,2048]{2,1,0:T(8,128)(2,1)}, bf16[4,64,2048]{2,1,0:T(8,128)(2,1)}, u32[]{:S(2)}, u32[]{:S(2)}) collective-permute-start(bf16[4,64,2048]{2,1,0:T(8,128)(2,1)} %bitcast.71), channel_id=1, source_target_pairs={{0,1},{1,0},{2,3},{3,2},{4,5},{5,4},{6,7},{7,6},{8,9},{9,8},{10,11... | collective-permute-start | bytes 3145736 | tf_op jit(solution)/shard_map/ppermute | solution.py:1797
  128.3 72.8 %collective-permute-start.4 = (bf16[4,64,2048]{2,1,0:T(8,128)(2,1)}, bf16[4,64,2048]{2,1,0:T(8,128)(2,1)}, u32[]{:S(2)}, u32[]{:S(2)}) collective-permute-start(bf16[4,64,2048]{2,1,0:T(8,128)(2,1)} %bitcast.72), channel_id=1, source_target_pairs={{0,16},{16,0},{1,17},{17,1},{2,18},{18,2},{3,19},{19,3},{4,20},{20... | collective-permute-start | bytes 3145736 | tf_op jit(solution)/shard_map/ppermute | solution.py:1797
  129.2 27.0 %copy-start.6 = (f32[1,8,128,128]{3,2,1,0:T(8,128)}, f32[1,8,128,128]{3,2,1,0:T(8,128)S(1)}, u32[]{:S(2)}) copy-start(f32[1,8,128,128]{3,2,1,0:T(8,128)S(1)} %get-tuple-element.156) | copy-start | bytes 1572868
  129.2 45.2 %copy-start.5 = (f32[1,8,128,128]{3,2,1,0:T(8,128)}, f32[1,8,128,128]{3,2,1,0:T(8,128)S(1)}, u32[]{:S(2)}) copy-start(f32[1,8,128,128]{3,2,1,0:T(8,128)S(1)} %get-tuple-element.155) | copy-start | bytes 1572868
  129.3 26.9 %copy-start.9 = (s32[3]{0:T(128)}, s32[3]{0:T(128)S(1)}, u32[]{:S(2)}) copy-start(s32[3]{0:T(128)S(1)} %get-tuple-element.162.lengths_ref) | copy-start | bytes 40
  129.3 45.2 %copy-start.8 = (s32[3]{0:T(128)}, s32[3]{0:T(128)S(1)}, u32[]{:S(2)}) copy-start(s32[3]{0:T(128)S(1)} %get-tuple-element.161.lengths_ref) | copy-start | bytes 40
  129.3 45.2 %copy-start.7 = (f32[12,256]{1,0:T(8,128)}, f32[12,256]{1,0:T(8,128)S(1)}, u32[]{:S(2)}) copy-start(f32[12,256]{1,0:T(8,128)S(1)} %reshape.193.tap_ref) | copy-start | bytes 36868
  129.3 45.1 %copy-start.31 = (f32[2,128]{1,0:T(2,128)}, f32[2,128]{1,0:T(2,128)S(1)}, u32[]{:S(2)}) copy-start(f32[2,128]{1,0:T(2,128)S(1)} %convert_element_type.87.gain_ref) | copy-start | bytes 3076
  129.3 44.6 %copy-start.19 = (bf16[4,2,32,2048]{3,2,1,0:T(8,128)(2,1)S(1)}, bf16[4,2,32,2048]{3,2,1,0:T(8,128)(2,1)}, u32[]{:S(2)}) copy-start(bf16[4,2,32,2048]{3,2,1,0:T(8,128)(2,1)} %copy-done.18) | copy-start | bytes 3145732
  172.8 28.3 %collective-permute-start.5 = (bf16[4,64,2048]{2,1,0:T(8,128)(2,1)}, bf16[4,64,2048]{2,1,0:T(8,128)(2,1)S(1)}, u32[]{:S(2)}, u32[]{:S(2)}) collective-permute-start(bf16[4,64,2048]{2,1,0:T(8,128)(2,1)} %collective-permute-done.refs_4_), channel_id=1, source_target_pairs={{0,16},{16,0},{1,17},{17,1},{2,18},{18,2},{3,19},{19,3},{4,20},{20... | collective-permute-start | bytes 3145736 | tf_op jit(solution)/shard_map/ppermute | solution.py:1797
  173.5 27.7 %collective-permute-start.6 = (bf16[256,2048]{1,0:T(8,128)(2,1)}, bf16[256,2048]{1,0:T(8,128)(2,1)}, u32[]{:S(2)}, u32[]{:S(2)}) collective-permute-start(bf16[256,2048]{1,0:T(8,128)(2,1)} %collective-permute-done.1.refs_1_), channel_id=1, source_target_pairs={{0,1},{1,0},{2,3},{3,2},{4,5},{5,4},{6,7},{7,6},{8,9},{9,8},{10,11... | collective-permute-start | bytes 3145736 | tf_op jit(solution)/shard_map/ppermute | solution.py:1797
  174.0 27.8 %collective-permute-start.3 = (bf16[4,64,2048]{2,1,0:T(8,128)(2,1)S(1)}, bf16[4,64,2048]{2,1,0:T(8,128)(2,1)S(1)}, u32[]{:S(2)}, u32[]{:S(2)}) collective-permute-start(bf16[4,64,2048]{2,1,0:T(8,128)(2,1)S(1)} %bitcast.73), channel_id=1, source_target_pairs={{0,8},{8,0},{1,9},{9,1},{2,10},{10,2},{3,11},{11,3},{4,12},{12,4},... | collective-permute-start | bytes 3145736 | tf_op jit(solution)/shard_map/ppermute | solution.py:1797
  174.0 28.3 %collective-permute-start.8 = (bf16[4,64,2048]{2,1,0:T(8,128)(2,1)}, bf16[4,64,2048]{2,1,0:T(8,128)(2,1)S(1)}, u32[]{:S(2)}, u32[]{:S(2)}) collective-permute-start(bf16[4,64,2048]{2,1,0:T(8,128)(2,1)} %collective-permute-done.refs_4_), channel_id=1, source_target_pairs={{0,8},{8,0},{1,9},{9,1},{2,10},{10,2},{3,11},{11,3},{4,12},{12,4},... | collective-permute-start | bytes 3145736 | tf_op jit(solution)/shard_map/ppermute | solution.py:1797
  201.1 42.8 %copy-start.36 = (f32[1024,256]{1,0:T(8,128)}, f32[1024,256]{1,0:T(8,128)S(1)}, u32[]{:S(2)}) copy-start(f32[1024,256]{1,0:T(8,128)S(1)} %get-tuple-element.124.heads_ref) | copy-start | bytes 3145732
  201.1 42.8 %copy-start.37 = (f32[1024,256]{1,0:T(8,128)}, f32[1024,256]{1,0:T(8,128)S(1)}, u32[]{:S(2)}) copy-start(f32[1024,256]{1,0:T(8,128)S(1)} %get-tuple-element.125.fixed_ref) | copy-start | bytes 3145732
  201.1 42.8 %copy-start.38 = (f32[1024,256]{1,0:T(8,128)}, f32[1024,256]{1,0:T(8,128)S(1)}, u32[]{:S(2)}) copy-start(f32[1024,256]{1,0:T(8,128)S(1)} %get-tuple-element.126.delta_ref) | copy-start | bytes 3145732
  201.1 42.8 %copy-start.39 = (f32[16,128,128]{2,1,0:T(8,128)}, f32[16,128,128]{2,1,0:T(8,128)S(1)}, u32[]{:S(2)}) copy-start(f32[16,128,128]{2,1,0:T(8,128)S(1)} %get-tuple-element.127.state_ref) | copy-start | bytes 3145732
  201.1 3.7 collective-permute-start.7
  201.3 6.8 collective-permute-start.9
  201.7 45.5 %collective-permute-start.10 = (bf16[256,2048]{1,0:T(8,128)(2,1)}, bf16[256,2048]{1,0:T(8,128)(2,1)S(1)}, u32[]{:S(2)}, u32[]{:S(2)}) collective-permute-start(bf16[256,2048]{1,0:T(8,128)(2,1)} %bitcast.16.refs_0_.c_ref), channel_id=1, source_target_pairs={{0,8},{8,0},{1,9},{9,1},{2,10},{10,2},{3,11},{11,3},{4,12},{12,4},... | collective-permute-start | bytes 3145736 | tf_op jit(solution)/shard_map/ppermute | solution.py:1797
  201.8 45.4 %collective-permute-start.11 = (bf16[256,2048]{1,0:T(8,128)(2,1)}, bf16[256,2048]{1,0:T(8,128)(2,1)}, u32[]{:S(2)}, u32[]{:S(2)}) collective-permute-start(bf16[256,2048]{1,0:T(8,128)(2,1)} %collective-permute-done.1.refs_1_), channel_id=1, source_target_pairs={{0,8},{8,0},{1,9},{9,1},{2,10},{10,2},{3,11},{11,3},{4,12},{12,4},... | collective-permute-start | bytes 3145736 | tf_op jit(solution)/shard_map/ppermute | solution.py:1797
  202.2 45.0 %collective-permute-start.12 = (bf16[256,2048]{1,0:T(8,128)(2,1)}, bf16[256,2048]{1,0:T(8,128)(2,1)}, u32[]{:S(2)}, u32[]{:S(2)}) collective-permute-start(bf16[256,2048]{1,0:T(8,128)(2,1)} %collective-permute-done.2.refs_2_), channel_id=1, source_target_pairs={{0,8},{8,0},{1,9},{9,1},{2,10},{10,2},{3,11},{11,3},{4,12},{12,4},... | collective-permute-start | bytes 3145736 | tf_op jit(solution)/shard_map/ppermute | solution.py:1797
  204.8 42.4 %collective-permute-start.13 = (bf16[256,2048]{1,0:T(8,128)(2,1)}, bf16[256,2048]{1,0:T(8,128)(2,1)}, u32[]{:S(2)}, u32[]{:S(2)}) collective-permute-start(bf16[256,2048]{1,0:T(8,128)(2,1)} %collective-permute-done.6.refs_3_), channel_id=1, source_target_pairs={{0,8},{8,0},{1,9},{9,1},{2,10},{10,2},{3,11},{11,3},{4,12},{12,4},... | collective-permute-start | bytes 3145736 | tf_op jit(solution)/shard_map/ppermute | solution.py:1797
  442.1 32.1 %collective-permute-start.14 = (bf16[2,4,64,1024]{3,2,1,0:T(8,128)(2,1)}, bf16[2,4,64,1024]{3,2,1,0:T(8,128)(2,1)}, u32[]{:S(2)}, u32[]{:S(2)}) collective-permute-start(bf16[2,4,64,1024]{3,2,1,0:T(8,128)(2,1)} %copy-done.21), channel_id=1, source_target_pairs={{0,16},{16,0},{1,17},{17,1},{2,18},{18,2},{3,19},{19,3},{4,20},{20... | collective-permute-start | bytes 3145736 | tf_op jit(solution)/shard_map/ppermute | solution.py:1797
  444.3 32.5 %collective-permute-start.15 = (bf16[2,4,64,1024]{3,2,1,0:T(8,128)(2,1)}, bf16[2,4,64,1024]{3,2,1,0:T(8,128)(2,1)}, u32[]{:S(2)}, u32[]{:S(2)}) collective-permute-start(bf16[2,4,64,1024]{3,2,1,0:T(8,128)(2,1)} %copy-done.20), channel_id=1, source_target_pairs={{0,1},{1,0},{2,3},{3,2},{4,5},{5,4},{6,7},{7,6},{8,9},{9,8},{10,11... | collective-permute-start | bytes 3145736 | tf_op jit(solution)/shard_map/ppermute | solution.py:1797
  479.5 27.9 %copy-start.4 = (bf16[2048,128]{1,0:T(8,128)(2,1)S(1)}, bf16[2048,128]{1,0:T(8,128)(2,1)}, u32[]{:S(2)}) copy-start(bf16[2048,128]{1,0:T(8,128)(2,1)} %copy-done.3) | copy-start | bytes 1572868
  479.5 27.9 %copy-start.11 = (bf16[2048,256]{1,0:T(8,128)(2,1)S(1)}, bf16[2048,256]{1,0:T(8,128)(2,1)}, u32[]{:S(2)}) copy-start(bf16[2048,256]{1,0:T(8,128)(2,1)} %refs_0_.1) | copy-start | bytes 3145732
  479.5 27.9 %copy-start.13 = (bf16[2048,256]{1,0:T(8,128)(2,1)S(1)}, bf16[2048,256]{1,0:T(8,128)(2,1)}, u32[]{:S(2)}) copy-start(bf16[2048,256]{1,0:T(8,128)(2,1)} %refs_1_.1) | copy-start | bytes 3145732
  479.5 27.9 %copy-start.15 = (bf16[2048,256]{1,0:T(8,128)(2,1)S(1)}, bf16[2048,256]{1,0:T(8,128)(2,1)}, u32[]{:S(2)}) copy-start(bf16[2048,256]{1,0:T(8,128)(2,1)} %refs_2_.1) | copy-start | bytes 3145732
  479.5 27.9 %copy-start.17 = (bf16[2048,256]{1,0:T(8,128)(2,1)S(1)}, bf16[2048,256]{1,0:T(8,128)(2,1)}, u32[]{:S(2)}) copy-start(bf16[2048,256]{1,0:T(8,128)(2,1)} %refs_3_.3) | copy-start | bytes 3145732
  479.5 27.9 %copy-start.29 = (bf16[1024,128]{1,0:T(8,128)(2,1)S(1)}, bf16[1024,128]{1,0:T(8,128)(2,1)}, u32[]{:S(2)}) copy-start(bf16[1024,128]{1,0:T(8,128)(2,1)} %get-tuple-element.130.b_first) | copy-start | bytes 786436
  511.6 16.1 %copy-start.54 = (bf16[2,2048]{1,0:T(2,128)(2,1)S(1)}, bf16[2,2048]{1,0:T(2,128)(2,1)}, u32[]{:S(2)}) copy-start(bf16[2,2048]{1,0:T(2,128)(2,1)} %copy-done.53) | copy-start | bytes 24580
  529.8 4.3 copy-start.60
  529.8 4.3 copy-start.61
  529.8 13.4 %collective-permute-start.17 = (bf16[4,64,1024]{2,1,0:T(8,128)(2,1)}, bf16[4,64,1024]{2,1,0:T(8,128)(2,1)}, u32[]{:S(2)}, u32[]{:S(2)}) collective-permute-start(bf16[4,64,1024]{2,1,0:T(8,128)(2,1)} %dynamic-slice_bitcast_fusion), channel_id=1, source_target_pairs={{0,16},{16,0},{1,17},{17,1},{2,18},{18,2},{3,19},{19,3},{4,20},{20... | collective-permute-start | bytes 1572872 | tf_op jit(solution)/shard_map/ppermute | solution.py:1797
  531.0 13.1 %collective-permute-start.16 = (bf16[4,64,1024]{2,1,0:T(8,128)(2,1)}, bf16[4,64,1024]{2,1,0:T(8,128)(2,1)}, u32[]{:S(2)}, u32[]{:S(2)}) collective-permute-start(bf16[4,64,1024]{2,1,0:T(8,128)(2,1)} %dynamic-slice_bitcast_fusion.1), channel_id=1, source_target_pairs={{0,1},{1,0},{2,3},{3,2},{4,5},{5,4},{6,7},{7,6},{8,9},{9,8},{10,11... | collective-permute-start | bytes 1572872 | tf_op jit(solution)/shard_map/ppermute | solution.py:1797
  670.4 5.9 copy-start.44
  670.4 5.9 copy-start.52
  (37 other events, 68.6 us)
Sparse Core Ops, SparseCore 0:
  124.8 125.8 all-gather.2
  442.2 100.3 reduce-scatter.1

commit v8 on v7

--- a/solution.py
+++ b/solution.py
@@ -1135,7 +1135,7 @@
                    pair_send, pair_recv, right_send, left_send, right_recv, left_recv, g_sem,
                    sum_send, sum_recv, outs_send, outs_recv, gain_send, gain_recv, part_sems, swap_send, swap_recv, swap_own, sum_sem):
     batches = len(g_refs)
-    rows, width = gs.shape
+    rows, width = gs.shape[2:]
     lines = yrecv.shape[0]
     model = yrecv.shape[3]
     o = lax.axis_index("z")
@@ -1144,6 +1144,12 @@
     me = lax.axis_index("x") * 2 + core
     tile = min(512, model)
     diagonal = {"x": 1 - lax.axis_index("x"), "core": 1 - core}
+    loads = [
+        pltpu.make_async_copy(source, target.at[m], g_sem.at[n, m])
+        for n, (sources, target) in enumerate(((g_refs, gs), (gb_refs, bs)))
+        for m, source in enumerate(sources)]
+    for copy in loads:
+        copy.start()
     slots = 2 * lines
     mine = o * 2 + i
     peers = []
@@ -1180,6 +1186,8 @@
     swap.start()
     inner_pair.start()
     inner_own.start()
+    for copy in loads:
+        copy.wait()
 
     def add_into(target, other_ref):
         height = target.shape[0]
@@ -1196,21 +1204,9 @@
         z = o + side * far
         return far, z, (z >= 0) & (z < lines) & ((far > 0) | (side > 0))
 
-    def load(z, y, m):
-        slot = z * 2 + y
-        return (pltpu.make_async_copy(g_refs[m].at[slot], gs, g_sem.at[0]),
-                pltpu.make_async_copy(gb_refs[m].at[slot], bs, g_sem.at[1]))
-
     def partial_rows(z, y, m, store):
-        for n in range(batches):
-            @pl.when(m == n)
-            def _():
-                for copy in load(z, y, n):
-                    copy.start()
-        for copy in load(z, y, 0):
-            copy.wait()
-        g = gs[...]
-        b = bs[...]
+        g = gs[m, z * 2 + y]
+        b = bs[m, z * 2 + y]
         for start in range(0, model, tile):
             cols = slice(start, start + tile)
             value = lax.dot_general(b, wb_ref[cols, :], NT, preferred_element_type=f32)
@@ -1328,6 +1324,17 @@
         def _():
             side_work()
 
+        @pl.when(index == (2 * lines - 2) * batches)
+        def _():
+            inner_across.wait_recv()
+            inner_across.wait_send()
+            add_into(inner_s, inner_r.at[1])
+            inner_back.start()
+            inner_keep.start()
+            small_pair.wait_recv()
+            small_s[1] = small_s[0] + small_r[0]
+            small_across.start()
+
         @pl.when(moves & (before >= 0))
         def _():
             place, n = before // batches, lax.rem(before, batches)
@@ -1366,14 +1373,6 @@
 
     lax.fori_loop(0, total + 2, turn, (jnp.int32(-1), jnp.int32(-1)))
 
-    inner_across.wait_recv()
-    inner_across.wait_send()
-    add_into(inner_s, inner_r.at[1])
-    inner_back.start()
-    inner_keep.start()
-    small_pair.wait_recv()
-    small_s[1] = small_s[0] + small_r[0]
-    small_across.start()
 
     for m in range(batches):
         out_ref[m] = yrecv[o, m].astype(f32)
@@ -1459,8 +1458,8 @@
         + [anywhere, vmem(), vmem(), vmem(), anywhere, anywhere],
         out_specs=(vmem(), vmem()) + (anywhere,) * 4,
         scratch_shapes=[
-            pltpu.VMEM((rows, width), bf16),
-            pltpu.VMEM((rows, 128), bf16),
+            pltpu.VMEM((batches, slots, rows, width), bf16),
+            pltpu.VMEM((batches, slots, rows, 128), bf16),
             slab, slab, slab, slab, part, part, part,
             pltpu.VMEM((more, model), bf16),
             pltpu.VMEM(half, bf16),
@@ -1470,7 +1469,7 @@
             pltpu.VMEM(gains.shape, f32),
             sems((lines, batches)), sems((lines, batches)), sems((lines, batches)),
             sems((lines, batches)), sems((lines, batches)), sems((lines, batches)),
-            sems((2,)), sems((5,)), sems((5,)), sems((3,)), sems((3,)), sems((slots,)), sems((slots,)), sems((4, lines)),
+            sems((2, batches)), sems((5,)), sems((5,)), sems((3,)), sems((3,)), sems((slots,)), sems((slots,)), sems((4, lines)),
             sems((2, 3)), sems((2, 3)), sems((2,)), sems((3,)),
         ],
         compiler_params=pltpu.CompilerParams(

time: 702 us -> 694 us (0.989)
    pallas_call x1, Pallas kernels: 122 us -> 114 us  [scatter_rows(): pl.pallas_call(scatter_call_kernel, out_shape=(jax.ShapeDtypeStruct((batc...]
where the time goes in v8:
time: 694 us; the launch traced here: 690 us
  Pallas kernels  563 us (81%)
  local copies, waits for them, and re-layouts  40.6 us (6%)
  waiting for transfers between devices  31.2 us (4%)
  other arithmetic  21.8 us (3%)
  between operations  15.2 us (2%)
  starting transfers between devices  12 us (2%)
    pallas_call x1, Pallas kernels, ffn_plane(): pl.pallas_call(ffn_call_kernel, out_shape=(jax.ShapeDtypeStruct((rows, mo...  150 us
    pallas_call x1, Pallas kernels, scatter_rows(): pl.pallas_call(scatter_call_kernel, out_shape=(jax.ShapeDtypeStruct((batc...  114 us
    pallas_call x1, Pallas kernels, gather_project(): pl.pallas_call(gather_call_kernel, out_shape=(jax.ShapeDtypeStruct((batch...  99.1 us
    pallas_call x2, Pallas kernels, mixer_backward(): pl.pallas_call(partial(mixer_backward_kernel, exact), out_shape=(jax.Shap...  56.5 us
    pallas_call x2, Pallas kernels, mixer_forward(): pl.pallas_call(partial(mixer_forward_kernel, exact, group), out_shape=(ja...  53.5 us
    pallas_call x1, Pallas kernels, attend_back(): pl.pallas_call(attend_back_kernel, out_shape=(wide, wide, back, back, *[j...  37.6 us
    pallas_call x1, Pallas kernels, attend(): pl.pallas_call(attend_kernel, out_shape=(jax.ShapeDtypeStruct((rows, mode...  35.9 us
    ppermute x18, waiting for transfers between devices, exchange(): return lax.ppermute(x, axis_name, [(i, i ^ distance) for i in range(size)])  27.7 us
  transfers between devices with their start and end apart: 20, of which 6 were waited for; matrix products, arithmetic and copies ran while one was open for 2% of the time, Pallas kernels for 23%

profile of v8, /device:TPU:0, one launch (start us, length us, event | category | flops | bytes accessed | tf_op | source)
XLA Modules:
  0.0 689.6 jit_solution(8848622143969255762)
XLA Ops:
  8.8 6.1 all_gather.6
  14.9 1.5 fusion.7
  16.5 1.8 copy.39
  18.7 1.3 pad.12.refs_7_.wb_ref.refs_13_
  20.3 1.1 copy-done.22
  21.4 1.1 copy-done.23
  22.6 1.1 copy-done.24
  23.7 99.1 %gather_project.1 = (bf16[2,8,128,2048]{3,2,1,0:T(8,128)(2,1)}, bf16[4,2,32,2048]{3,2,1,0:T(8,128)(2,1)S(1)}, f32[8,128,1024]{2,1,0:T(8,128)}, f32[8,128,1024]{2...) custom-call(bf16[2,128,2048]{2,1,0:T(8,128)(2,1)S(1)} %fusion.2.x_re, ...), custom_call_target="tpu_custom_call" | custom-call | flops 99999997952 | bytes 40000000 | tf_op jit(solution)/shard_map/gather_project/pallas_call | solution.py:1100
  125.0 1.3 collective-permute-start.1
  126.3 1.5 collective-permute-start.2
  129.4 26.8 %mixer_forward.2 = (bf16[1024,256]{1,0:T(8,128)(2,1)S(1)}, f32[1024,256]{1,0:T(8,128)S(1)}, f32[1024,256]{1,0:T(8,128)S(1)}, f32[1024,256]{1,0:T(8,128)S(1)}, f3...) custom-call(s32[3]{0:T(128)S(1)} %get-tuple-element.162.lengths_ref, f32[1024,1024]{1,0:T(8,128)} %bitcast.99, ...), custom_call_target="tpu_custom_call" | custom-call | flops 10000000000 | bytes 10000000 | tf_op jit(solution)/shard_map/mixer_forward/pallas_call | solution.py:333
  156.2 1.0 copy-done.32
  157.2 1.0 copy-done.33
  158.1 1.0 copy-done.34
  159.1 1.0 copy-done.35
  160.1 12.8 %collective-permute-done.refs_4_ = bf16[4,64,2048]{2,1,0:T(8,128)(2,1)} collective-permute-done((bf16[4,64,2048]{2,1,0:T(8,128)(2,1)}, bf16[4,64,2048]{2,1,0:T(8,128)(2,1)}, u32[]{:S(2)}, u32[]{:S(2)}) %collective-permute-start) | collective-permute-done | bytes 1048608 | tf_op jit(solution)/shard_map/ppermute | solution.py:1796
  174.5 26.6 %mixer_forward.3 = (bf16[1024,256]{1,0:T(8,128)(2,1)S(1)}, f32[1024,256]{1,0:T(8,128)S(1)}, f32[1024,256]{1,0:T(8,128)S(1)}, f32[1024,256]{1,0:T(8,128)S(1)}, f3...) custom-call(s32[3]{0:T(128)S(1)} %get-tuple-element.161.lengths_ref, f32[1024,1024]{1,0:T(8,128)} %bitcast.97, ...), custom_call_target="tpu_custom_call" | custom-call | flops 10000000000 | bytes 10000000 | tf_op jit(solution)/shard_map/mixer_forward/pallas_call | solution.py:333
  202.3 2.5 collective-permute-done.7.refs_3_
  204.9 3.1 collective-permute-done.9.refs_7_
  208.0 35.9 %attend.1 = (f32[256,2048]{1,0:T(8,128)S(1)}, bf16[256,2048]{1,0:T(8,128)(2,1)S(1)}, bf16[4,2,4,64,2048]{4,3,2,1,0:T(8,128)(2,1)}, bf16[2,8,128,256]{3,2,1,0:T(8,128)(2,1)S(1)}) custom-call(bf16[256,2048]{1,0:T(8,128)(2,1)S(1)} %bitcast.66, bf16[8,128,256]{2,1,0:T(8,128)(2,1)S(1)} %bitcast.81, bf16[8,128,256]{2,1,0:T(8,128)(2,1)S(1)} %bitcast.83, ...), custom_call_target="tpu_custom_call" | custom-call | flops 30000001024 | bytes 20000000 | tf_op jit(solution)/shard_map/attend/pallas_call | solution.py:1564
  244.0 1.3 copy-done.40
  245.3 1.0 copy-done.41
  246.2 1.0 copy-done.42
  247.2 3.4 all-gather.3.cloned.1.call-done
  250.7 150.3 %ffn_plane.1 = (f32[256,2048]{1,0:T(8,128)}, f32[256,2048]{1,0:T(8,128)}, bf16[4,4,2,176,512]{4,3,2,1,0:T(8,128)(2,1)}, bf16[4,176,512]{2,1,0:T(8,128)(2,1)}) custom-call(bf16[256,2048]{1,0:T(8,128)(2,1)} %copy-done.42, bf16[4,4,2,176,512]{4,3,2,1,0:T(8,128)(2,1)} %bitcast.94, bf16[4,176,512]{2,1,0:T(8,128)(2,1)} %copy-done.43, ...), custom_call_target="tpu_custom_call" | custom-call | flops 80000000000 | bytes 40000000 | tf_op jit(solution)/shard_map/ffn_plane/pallas_call | solution.py:828
  401.0 37.6 %attend_back.1 = (f32[256,2048]{1,0:T(8,128)}, f32[256,2048]{1,0:T(8,128)}, bf16[8,128,256]{2,1,0:T(8,128)(2,1)S(1)}, bf16[8,128,256]{2,1,0:T(8,128)(2,1)S(1)}, ...) custom-call(f32[256,2048]{1,0:T(8,128)} %copy-done.40, ...), custom_call_target="tpu_custom_call" | custom-call | flops 30000001024 | bytes 40000000 | tf_op jit(solution)/shard_map/attend_back/pallas_call | solution.py:1687
  439.5 1.0 copy-done.21
  442.1 2.2 collective-permute-start.14
  445.6 28.6 %mixer_backward.2 = (bf16[1024,1024]{1,0:T(8,128)(2,1)}, bf16[1024,128]{1,0:T(8,128)(2,1)}, f32[12,256]{1,0:T(8,128)}, f32[2,128]{1,0:T(2,128)}) custom-call(s32[3]{0:T(128)} %copy-done.9, f32[1024,1024]{1,0:T(8,128)} %bitcast.100, f32[1024,128]{1,0:T(8,128)} %bitcast.70, f32[12,256]{1,0:T(8,128)} %copy-done.7, f32[2,128]{1,0:T(2,128)} %copy-done.31, ...), custom_call_target="tpu_custom_call" | custom-call | flops 10000000000 | bytes 10000000 | tf_op jit(solution)/shard_map/mixer_backward/pallas_call | solution.py:356
  474.2 2.6 add_convert_fusion.1.refs_8_
  476.8 2.6 add_convert_fusion.refs_10_
  479.5 27.9 %mixer_backward.3 = (bf16[1024,1024]{1,0:T(8,128)(2,1)}, bf16[1024,128]{1,0:T(8,128)(2,1)}, f32[12,256]{1,0:T(8,128)}, f32[2,128]{1,0:T(2,128)}) custom-call(s32[3]{0:T(128)} %copy-done.8, f32[1024,1024]{1,0:T(8,128)} %bitcast.98, f32[1024,128]{1,0:T(8,128)} %bitcast.68, f32[12,256]{1,0:T(8,128)} %copy-done.7, f32[2,128]{1,0:T(2,128)} %copy-done.31, ...), custom_call_target="tpu_custom_call" | custom-call | flops 10000000000 | bytes 10000000 | tf_op jit(solution)/shard_map/mixer_backward/pallas_call | solution.py:356
  507.4 1.6 copy-done.25
  509.0 1.6 copy-done.26
  511.6 15.7 %inner_grads.1 = (bf16[2048,1024]{1,0:T(8,128)(2,1)}, f32[2048,128]{1,0:T(8,128)S(1)}, f32[2048,128]{1,0:T(8,128)S(1)}) custom-call(bf16[2,1024,2048]{2,1,0:T(8,128)(2,1)} %bitcast.96, bf16[1024,1024]{1,0:T(8,128)(2,1)S(1)} %copy-done.25, bf16[1024,1024]{1,0:T(8,128)(2,1)S(1)} %copy-done.26, bf16[1024,128]{1,0:T(8,128)(2,1)S(1)} %copy-done.29, ...), custom_call_target="tpu_custom_call" | custom-call | flops 10000000000 | bytes 20000000 | tf_op jit(solution)/shard_map/inner_grads/pallas_call | solution.py:1737
  527.9 1.9 dynamic-slice_bitcast_fusion
  531.0 2.0 collective-permute-start.16
  534.7 8.5 %collective-permute-done.17.refs_11_ = bf16[4,64,1024]{2,1,0:T(8,128)(2,1)} collective-permute-done((bf16[4,64,1024]{2,1,0:T(8,128)(2,1)}, bf16[4,64,1024]{2,1,0:T(8,128)(2,1)}, u32[]{:S(2)}, u32[]{:S(2)}) %collective-permute-start.17) | collective-permute-done | bytes 524320 | tf_op jit(solution)/shard_map/ppermute | solution.py:1796
  544.1 114.3 %scatter_rows.1 = (f32[2,128,2048]{2,1,0:T(8,128)}, f32[72,128]{1,0:T(8,128)}, bf16[4,64,2048]{2,1,0:T(8,128)(2,1)}, bf16[2,1024,1024]{2,1,0:T(8,128)(2,1)}, bf1...) custom-call(bf16[2048,256]{1,0:T(8,128)(2,1)} %refs_0_.1, bf16[2048,256]{1,0:T(8,128)(2,1)} %refs_1_.1, ...), custom_call_target="tpu_custom_call" | custom-call | flops 70000001024 | bytes 40000000 | tf_op jit(solution)/shard_map/scatter_rows/pallas_call | solution.py:1447
  660.4 1.2 slice.91
  661.7 1.4 fusion.11
  663.2 5.9 slice_convert_fusion
  670.3 1.6 bitcast_convert_fusion
  671.9 1.3 bitcast_convert_fusion.1
  674.5 2.1 convert_bitcast_fusion
  676.6 1.2 copy-done.47
  677.8 2.1 fusion.6
  680.4 1.3 copy.44
  (188 shorter events, 23.8 us)
Async XLA Ops:
  7.2 11.1 %copy-start = (bf16[256,2048]{1,0:T(8,128)(2,1)S(1)}, bf16[256,2048]{1,0:T(8,128)(2,1)}, u32[]{:S(2)}) copy-start(bf16[256,2048]{1,0:T(8,128)(2,1)} %param.27) | copy-start | bytes 3145732
  7.2 11.2 %copy-start.2 = (bf16[2,128,2048]{2,1,0:T(8,128)(2,1)S(1)}, bf16[2,128,2048]{2,1,0:T(8,128)(2,1)}, u32[]{:S(2)}) copy-start(bf16[2,128,2048]{2,1,0:T(8,128)(2,1)} %param.16) | copy-start | bytes 3145732
  7.2 243.5 %all-gather.3.cloned.1.call-start = ((), (), s32[]{:S(2)}) async-start(), calls=%async_computation.2 | async-start | bytes 7208960 | tf_op jit(solution)/shard_map/all_gather | solution.py:1773
  20.0 102.7 %copy-start.3 = (bf16[2048,128]{1,0:T(8,128)(2,1)}, bf16[2048,128]{1,0:T(8,128)(2,1)S(1)}, u32[]{:S(2)}) copy-start(bf16[2048,128]{1,0:T(8,128)(2,1)S(1)} %pad.12.refs_7_.wb_ref.refs_13_) | copy-start | bytes 1572868
  124.6 4.6 copy-start.62
  124.6 4.6 copy-start.59
  124.6 4.7 copy-start.64
  124.7 419.4 %reduce-scatter.2.cloned.1.call-start = ((), (), s32[]{:S(2)}) async-start(), calls=%async_computation.1 | async-start | bytes 7208960 | tf_op jit(solution)/shard_map/reduce_scatter | solution.py:1941
  125.0 35.1 %collective-permute-start.1 = (bf16[256,2048]{1,0:T(8,128)(2,1)}, bf16[256,2048]{1,0:T(8,128)(2,1)}, u32[]{:S(2)}, u32[]{:S(2)}) collective-permute-start(bf16[256,2048]{1,0:T(8,128)(2,1)} %bitcast.16.refs_0_.c_ref), channel_id=1, source_target_pairs={{0,16},{16,0},{1,17},{17,1},{2,18},{18,2},{3,19},{19,3},{4,20},{20... | collective-permute-start | bytes 3145736 | tf_op jit(solution)/shard_map/ppermute | solution.py:1796
  126.3 33.8 %collective-permute-start.2 = (bf16[256,2048]{1,0:T(8,128)(2,1)}, bf16[256,2048]{1,0:T(8,128)(2,1)}, u32[]{:S(2)}, u32[]{:S(2)}) collective-permute-start(bf16[256,2048]{1,0:T(8,128)(2,1)} %bitcast.16.refs_0_.c_ref), channel_id=1, source_target_pairs={{0,1},{1,0},{2,3},{3,2},{4,5},{5,4},{6,7},{7,6},{8,9},{9,8},{10,11... | collective-permute-start | bytes 3145736 | tf_op jit(solution)/shard_map/ppermute | solution.py:1796
  127.8 45.1 %collective-permute-start = (bf16[4,64,2048]{2,1,0:T(8,128)(2,1)}, bf16[4,64,2048]{2,1,0:T(8,128)(2,1)}, u32[]{:S(2)}, u32[]{:S(2)}) collective-permute-start(bf16[4,64,2048]{2,1,0:T(8,128)(2,1)} %bitcast.71), channel_id=1, source_target_pairs={{0,1},{1,0},{2,3},{3,2},{4,5},{5,4},{6,7},{7,6},{8,9},{9,8},{10,11... | collective-permute-start | bytes 3145736 | tf_op jit(solution)/shard_map/ppermute | solution.py:1796
  128.3 72.8 %collective-permute-start.4 = (bf16[4,64,2048]{2,1,0:T(8,128)(2,1)}, bf16[4,64,2048]{2,1,0:T(8,128)(2,1)}, u32[]{:S(2)}, u32[]{:S(2)}) collective-permute-start(bf16[4,64,2048]{2,1,0:T(8,128)(2,1)} %bitcast.72), channel_id=1, source_target_pairs={{0,16},{16,0},{1,17},{17,1},{2,18},{18,2},{3,19},{19,3},{4,20},{20... | collective-permute-start | bytes 3145736 | tf_op jit(solution)/shard_map/ppermute | solution.py:1796
  129.2 27.0 %copy-start.6 = (f32[1,8,128,128]{3,2,1,0:T(8,128)}, f32[1,8,128,128]{3,2,1,0:T(8,128)S(1)}, u32[]{:S(2)}) copy-start(f32[1,8,128,128]{3,2,1,0:T(8,128)S(1)} %get-tuple-element.156) | copy-start | bytes 1572868
  129.2 45.2 %copy-start.5 = (f32[1,8,128,128]{3,2,1,0:T(8,128)}, f32[1,8,128,128]{3,2,1,0:T(8,128)S(1)}, u32[]{:S(2)}) copy-start(f32[1,8,128,128]{3,2,1,0:T(8,128)S(1)} %get-tuple-element.155) | copy-start | bytes 1572868
  129.3 26.9 %copy-start.9 = (s32[3]{0:T(128)}, s32[3]{0:T(128)S(1)}, u32[]{:S(2)}) copy-start(s32[3]{0:T(128)S(1)} %get-tuple-element.162.lengths_ref) | copy-start | bytes 40
  129.3 45.2 %copy-start.8 = (s32[3]{0:T(128)}, s32[3]{0:T(128)S(1)}, u32[]{:S(2)}) copy-start(s32[3]{0:T(128)S(1)} %get-tuple-element.161.lengths_ref) | copy-start | bytes 40
  129.3 45.2 %copy-start.7 = (f32[12,256]{1,0:T(8,128)}, f32[12,256]{1,0:T(8,128)S(1)}, u32[]{:S(2)}) copy-start(f32[12,256]{1,0:T(8,128)S(1)} %reshape.193.tap_ref) | copy-start | bytes 36868
  129.3 45.1 %copy-start.31 = (f32[2,128]{1,0:T(2,128)}, f32[2,128]{1,0:T(2,128)S(1)}, u32[]{:S(2)}) copy-start(f32[2,128]{1,0:T(2,128)S(1)} %convert_element_type.87.gain_ref) | copy-start | bytes 3076
  129.3 44.6 %copy-start.19 = (bf16[4,2,32,2048]{3,2,1,0:T(8,128)(2,1)S(1)}, bf16[4,2,32,2048]{3,2,1,0:T(8,128)(2,1)}, u32[]{:S(2)}) copy-start(bf16[4,2,32,2048]{3,2,1,0:T(8,128)(2,1)} %copy-done.18) | copy-start | bytes 3145732
  172.8 28.3 %collective-permute-start.5 = (bf16[4,64,2048]{2,1,0:T(8,128)(2,1)}, bf16[4,64,2048]{2,1,0:T(8,128)(2,1)S(1)}, u32[]{:S(2)}, u32[]{:S(2)}) collective-permute-start(bf16[4,64,2048]{2,1,0:T(8,128)(2,1)} %collective-permute-done.refs_4_), channel_id=1, source_target_pairs={{0,16},{16,0},{1,17},{17,1},{2,18},{18,2},{3,19},{19,3},{4,20},{20... | collective-permute-start | bytes 3145736 | tf_op jit(solution)/shard_map/ppermute | solution.py:1796
  173.5 27.7 %collective-permute-start.6 = (bf16[256,2048]{1,0:T(8,128)(2,1)}, bf16[256,2048]{1,0:T(8,128)(2,1)}, u32[]{:S(2)}, u32[]{:S(2)}) collective-permute-start(bf16[256,2048]{1,0:T(8,128)(2,1)} %collective-permute-done.1.refs_1_), channel_id=1, source_target_pairs={{0,1},{1,0},{2,3},{3,2},{4,5},{5,4},{6,7},{7,6},{8,9},{9,8},{10,11... | collective-permute-start | bytes 3145736 | tf_op jit(solution)/shard_map/ppermute | solution.py:1796
  174.0 27.8 %collective-permute-start.3 = (bf16[4,64,2048]{2,1,0:T(8,128)(2,1)S(1)}, bf16[4,64,2048]{2,1,0:T(8,128)(2,1)S(1)}, u32[]{:S(2)}, u32[]{:S(2)}) collective-permute-start(bf16[4,64,2048]{2,1,0:T(8,128)(2,1)S(1)} %bitcast.73), channel_id=1, source_target_pairs={{0,8},{8,0},{1,9},{9,1},{2,10},{10,2},{3,11},{11,3},{4,12},{12,4},... | collective-permute-start | bytes 3145736 | tf_op jit(solution)/shard_map/ppermute | solution.py:1796
  174.0 28.3 %collective-permute-start.8 = (bf16[4,64,2048]{2,1,0:T(8,128)(2,1)}, bf16[4,64,2048]{2,1,0:T(8,128)(2,1)S(1)}, u32[]{:S(2)}, u32[]{:S(2)}) collective-permute-start(bf16[4,64,2048]{2,1,0:T(8,128)(2,1)} %collective-permute-done.refs_4_), channel_id=1, source_target_pairs={{0,8},{8,0},{1,9},{9,1},{2,10},{10,2},{3,11},{11,3},{4,12},{12,4},... | collective-permute-start | bytes 3145736 | tf_op jit(solution)/shard_map/ppermute | solution.py:1796
  201.1 42.8 %copy-start.36 = (f32[1024,256]{1,0:T(8,128)}, f32[1024,256]{1,0:T(8,128)S(1)}, u32[]{:S(2)}) copy-start(f32[1024,256]{1,0:T(8,128)S(1)} %get-tuple-element.124.heads_ref) | copy-start | bytes 3145732
  201.1 42.8 %copy-start.37 = (f32[1024,256]{1,0:T(8,128)}, f32[1024,256]{1,0:T(8,128)S(1)}, u32[]{:S(2)}) copy-start(f32[1024,256]{1,0:T(8,128)S(1)} %get-tuple-element.125.fixed_ref) | copy-start | bytes 3145732
  201.1 42.8 %copy-start.38 = (f32[1024,256]{1,0:T(8,128)}, f32[1024,256]{1,0:T(8,128)S(1)}, u32[]{:S(2)}) copy-start(f32[1024,256]{1,0:T(8,128)S(1)} %get-tuple-element.126.delta_ref) | copy-start | bytes 3145732
  201.1 42.8 %copy-start.39 = (f32[16,128,128]{2,1,0:T(8,128)}, f32[16,128,128]{2,1,0:T(8,128)S(1)}, u32[]{:S(2)}) copy-start(f32[16,128,128]{2,1,0:T(8,128)S(1)} %get-tuple-element.127.state_ref) | copy-start | bytes 3145732
  201.1 3.7 collective-permute-start.7
  201.3 6.8 collective-permute-start.9
  201.7 45.5 %collective-permute-start.10 = (bf16[256,2048]{1,0:T(8,128)(2,1)}, bf16[256,2048]{1,0:T(8,128)(2,1)S(1)}, u32[]{:S(2)}, u32[]{:S(2)}) collective-permute-start(bf16[256,2048]{1,0:T(8,128)(2,1)} %bitcast.16.refs_0_.c_ref), channel_id=1, source_target_pairs={{0,8},{8,0},{1,9},{9,1},{2,10},{10,2},{3,11},{11,3},{4,12},{12,4},... | collective-permute-start | bytes 3145736 | tf_op jit(solution)/shard_map/ppermute | solution.py:1796
  201.8 45.4 %collective-permute-start.11 = (bf16[256,2048]{1,0:T(8,128)(2,1)}, bf16[256,2048]{1,0:T(8,128)(2,1)}, u32[]{:S(2)}, u32[]{:S(2)}) collective-permute-start(bf16[256,2048]{1,0:T(8,128)(2,1)} %collective-permute-done.1.refs_1_), channel_id=1, source_target_pairs={{0,8},{8,0},{1,9},{9,1},{2,10},{10,2},{3,11},{11,3},{4,12},{12,4},... | collective-permute-start | bytes 3145736 | tf_op jit(solution)/shard_map/ppermute | solution.py:1796
  202.2 45.0 %collective-permute-start.12 = (bf16[256,2048]{1,0:T(8,128)(2,1)}, bf16[256,2048]{1,0:T(8,128)(2,1)}, u32[]{:S(2)}, u32[]{:S(2)}) collective-permute-start(bf16[256,2048]{1,0:T(8,128)(2,1)} %collective-permute-done.2.refs_2_), channel_id=1, source_target_pairs={{0,8},{8,0},{1,9},{9,1},{2,10},{10,2},{3,11},{11,3},{4,12},{12,4},... | collective-permute-start | bytes 3145736 | tf_op jit(solution)/shard_map/ppermute | solution.py:1796
  204.8 42.4 %collective-permute-start.13 = (bf16[256,2048]{1,0:T(8,128)(2,1)}, bf16[256,2048]{1,0:T(8,128)(2,1)}, u32[]{:S(2)}, u32[]{:S(2)}) collective-permute-start(bf16[256,2048]{1,0:T(8,128)(2,1)} %collective-permute-done.6.refs_3_), channel_id=1, source_target_pairs={{0,8},{8,0},{1,9},{9,1},{2,10},{10,2},{3,11},{11,3},{4,12},{12,4},... | collective-permute-start | bytes 3145736 | tf_op jit(solution)/shard_map/ppermute | solution.py:1796
  442.1 32.1 %collective-permute-start.14 = (bf16[2,4,64,1024]{3,2,1,0:T(8,128)(2,1)}, bf16[2,4,64,1024]{3,2,1,0:T(8,128)(2,1)}, u32[]{:S(2)}, u32[]{:S(2)}) collective-permute-start(bf16[2,4,64,1024]{3,2,1,0:T(8,128)(2,1)} %copy-done.21), channel_id=1, source_target_pairs={{0,16},{16,0},{1,17},{17,1},{2,18},{18,2},{3,19},{19,3},{4,20},{20... | collective-permute-start | bytes 3145736 | tf_op jit(solution)/shard_map/ppermute | solution.py:1796
  444.3 32.5 %collective-permute-start.15 = (bf16[2,4,64,1024]{3,2,1,0:T(8,128)(2,1)}, bf16[2,4,64,1024]{3,2,1,0:T(8,128)(2,1)}, u32[]{:S(2)}, u32[]{:S(2)}) collective-permute-start(bf16[2,4,64,1024]{3,2,1,0:T(8,128)(2,1)} %copy-done.20), channel_id=1, source_target_pairs={{0,1},{1,0},{2,3},{3,2},{4,5},{5,4},{6,7},{7,6},{8,9},{9,8},{10,11... | collective-permute-start | bytes 3145736 | tf_op jit(solution)/shard_map/ppermute | solution.py:1796
  479.5 27.9 %copy-start.4 = (bf16[2048,128]{1,0:T(8,128)(2,1)S(1)}, bf16[2048,128]{1,0:T(8,128)(2,1)}, u32[]{:S(2)}) copy-start(bf16[2048,128]{1,0:T(8,128)(2,1)} %copy-done.3) | copy-start | bytes 1572868
  479.5 27.9 %copy-start.11 = (bf16[2048,256]{1,0:T(8,128)(2,1)S(1)}, bf16[2048,256]{1,0:T(8,128)(2,1)}, u32[]{:S(2)}) copy-start(bf16[2048,256]{1,0:T(8,128)(2,1)} %refs_0_.1) | copy-start | bytes 3145732
  479.5 27.9 %copy-start.13 = (bf16[2048,256]{1,0:T(8,128)(2,1)S(1)}, bf16[2048,256]{1,0:T(8,128)(2,1)}, u32[]{:S(2)}) copy-start(bf16[2048,256]{1,0:T(8,128)(2,1)} %refs_1_.1) | copy-start | bytes 3145732
  479.5 27.9 %copy-start.15 = (bf16[2048,256]{1,0:T(8,128)(2,1)S(1)}, bf16[2048,256]{1,0:T(8,128)(2,1)}, u32[]{:S(2)}) copy-start(bf16[2048,256]{1,0:T(8,128)(2,1)} %refs_2_.1) | copy-start | bytes 3145732
  479.5 27.9 %copy-start.17 = (bf16[2048,256]{1,0:T(8,128)(2,1)S(1)}, bf16[2048,256]{1,0:T(8,128)(2,1)}, u32[]{:S(2)}) copy-start(bf16[2048,256]{1,0:T(8,128)(2,1)} %refs_3_.3) | copy-start | bytes 3145732
  479.5 27.9 %copy-start.29 = (bf16[1024,128]{1,0:T(8,128)(2,1)S(1)}, bf16[1024,128]{1,0:T(8,128)(2,1)}, u32[]{:S(2)}) copy-start(bf16[1024,128]{1,0:T(8,128)(2,1)} %get-tuple-element.130.b_first) | copy-start | bytes 786436
  511.6 16.1 %copy-start.54 = (bf16[2,2048]{1,0:T(2,128)(2,1)S(1)}, bf16[2,2048]{1,0:T(2,128)(2,1)}, u32[]{:S(2)}) copy-start(bf16[2,2048]{1,0:T(2,128)(2,1)} %copy-done.53) | copy-start | bytes 24580
  529.8 4.3 copy-start.60
  529.8 4.3 copy-start.61
  529.8 13.4 %collective-permute-start.17 = (bf16[4,64,1024]{2,1,0:T(8,128)(2,1)}, bf16[4,64,1024]{2,1,0:T(8,128)(2,1)}, u32[]{:S(2)}, u32[]{:S(2)}) collective-permute-start(bf16[4,64,1024]{2,1,0:T(8,128)(2,1)} %dynamic-slice_bitcast_fusion), channel_id=1, source_target_pairs={{0,16},{16,0},{1,17},{17,1},{2,18},{18,2},{3,19},{19,3},{4,20},{20... | collective-permute-start | bytes 1572872 | tf_op jit(solution)/shard_map/ppermute | solution.py:1796
  531.0 13.1 %collective-permute-start.16 = (bf16[4,64,1024]{2,1,0:T(8,128)(2,1)}, bf16[4,64,1024]{2,1,0:T(8,128)(2,1)}, u32[]{:S(2)}, u32[]{:S(2)}) collective-permute-start(bf16[4,64,1024]{2,1,0:T(8,128)(2,1)} %dynamic-slice_bitcast_fusion.1), channel_id=1, source_target_pairs={{0,1},{1,0},{2,3},{3,2},{4,5},{5,4},{6,7},{7,6},{8,9},{9,8},{10,11... | collective-permute-start | bytes 1572872 | tf_op jit(solution)/shard_map/ppermute | solution.py:1796
  663.1 5.9 copy-start.44
  663.2 5.9 copy-start.52
  (37 other events, 68.6 us)
Sparse Core Ops, SparseCore 0:
  124.8 125.8 all-gather.2
  442.2 100.3 reduce-scatter.1

commit v9 on v8

--- a/solution.py
+++ b/solution.py
@@ -920,11 +920,11 @@
             copy.wait_send()
 
 
-def gather_kernel(x_ref, o_ref, f_refs, w_refs, wb_ref, rows_ref, outs_ref, proj_refs, beta_ref,
-                  pair_ref, down_ref,
+def gather_kernel(x_ref, gain_ref, o_ref, f_refs, w_refs, wb_ref, rows_ref, outs_ref, proj_refs, beta_ref,
+                  pair_ref, down_ref, gain_out,
                   xs, parts, stage, beta_stage, right_send, left_send, line_recv, pair_send, pair_recv,
                   part_right, part_left, part_recv, own_sem, row_sem, outs_sem, out_sem, beta_sem,
-                  swap_send, swap_recv, swap_own):
+                  swap_send, swap_recv, swap_own, gains, gain_send, gain_recv, gain_own):
     lines = xs.shape[0] // 2
     batches, rows, model = x_ref.shape
     o = lax.axis_index("z")
@@ -949,7 +949,6 @@
         return line_copy(ref, ref, pair_send.at[z, m], pair_recv.at[z, m], other("y"))
 
     own = [
-        pltpu.make_async_copy(x_ref, xs.at[o * 2 + i], own_sem.at[0]),
         pltpu.make_async_copy(o_ref, parts.at[o], own_sem.at[1]),
     ]
 
@@ -960,6 +959,23 @@
 
     for copy in own:
         copy.start()
+    me, peers = pair_peers()
+    share = gain_ref.shape[1]
+    gain_place = gains.at[:, pl.ds(pl.multiple_of(me * share, 128), share)]
+    gain_away = [
+        line_copy(gain_ref, gain_place, gain_send.at[d], gain_recv.at[d], device)
+        for d, (_, device) in enumerate(peers)]
+    gain_keep = pltpu.make_async_copy(gain_ref, gain_place, gain_own.at[0])
+    gain_keep.start()
+    for copy in gain_away:
+        copy.start()
+    gain_keep.wait()
+    for copy in gain_away:
+        copy.wait_recv()
+    for m in range(batches):
+        value = x_ref[m].astype(f32)
+        scale = lax.rsqrt(jnp.mean(value * value, axis=-1, keepdims=True) + epsilon)
+        xs[o * 2 + i, m] = (value * scale * gains[0:1, :]).astype(bf16)
     for copy in own:
         copy.wait()
 
@@ -1081,13 +1097,17 @@
                 keep(z * 2 + y, m).wait()
 
     swap.wait()
-
-
-def gather_call_kernel(x_ref, o_ref, *refs):
-    gather_kernel(x_ref, o_ref, refs[:3], refs[3:7], refs[7], refs[8], refs[9], refs[10:12], *refs[12:])
-
-
-def gather_project(x, w_out_part, ffn_parts, w_inner, w_beta):
+    gain_out[...] = gains[...]
+    for copy in gain_away:
+        copy.wait_send()
+
+
+def gather_call_kernel(x_ref, gain_ref, o_ref, *refs):
+    gather_kernel(x_ref, gain_ref, o_ref, refs[:3], refs[3:7], refs[7], refs[8], refs[9], refs[10:12],
+                  *refs[12:])
+
+
+def gather_project(x, gains, w_out_part, ffn_parts, w_inner, w_beta):
     batches, rows, model = x.shape
     more = w_out_part.shape[1]
     lines = lax.axis_size("z")
@@ -1097,7 +1117,7 @@
     anywhere = pl.BlockSpec(memory_space=pl.ANY)
     pair = sems((lines, batches))
     ranks, quarter, share = ffn_parts[0].shape
-    gathered, outs, *projected, beta, pair_parts, down_part = pl.pallas_call(
+    gathered, outs, *projected, beta, pair_parts, down_part, gains_all = pl.pallas_call(
         gather_call_kernel,
         out_shape=(
             jax.ShapeDtypeStruct((batches, slots, rows, model), bf16),
@@ -1106,9 +1126,10 @@
             jax.ShapeDtypeStruct((batches, slots, rows, 128), f32),
             jax.ShapeDtypeStruct((ranks, 2, quarter, share), bf16),
             jax.ShapeDtypeStruct((ranks, quarter, share), bf16),
+            jax.ShapeDtypeStruct((gains.shape[0], model), f32),
         ),
-        in_specs=[anywhere] * 5 + [vmem()] * 5,
-        out_specs=(anywhere,) * (5 + batches),
+        in_specs=[vmem()] * 2 + [anywhere] * 4 + [vmem()] * 5,
+        out_specs=(anywhere,) * (5 + batches) + (vmem(),),
         scratch_shapes=[
             pltpu.VMEM((slots, batches, rows, model), bf16),
             pltpu.VMEM((lines, batches, more, model), bf16),
@@ -1117,16 +1138,17 @@
             pair, pair, pair, pair, pair, sems((lines,)), sems((lines,)), sems((lines,)),
             sems((2,)), sems((slots, batches)), sems((lines,)), sems((2, batches)), sems((2, batches)),
             sems((3, 3)), sems((3, 3)), sems((3,)),
+            pltpu.VMEM((gains.shape[0], model), f32), sems((3,)), sems((3,)), sems((1,)),
         ],
         compiler_params=pltpu.CompilerParams(
             collective_id=1, has_side_effects=True, vmem_limit_bytes=40 * 2**20),
         cost_estimate=pl.CostEstimate(flops=10**11, bytes_accessed=4 * 10**7, transcendentals=0),
         name="gather_project",
-    )(x, w_out_part, *ffn_parts, *w_inner, w_beta)
+    )(x, gains, w_out_part, *ffn_parts, *w_inner, w_beta)
     total = slots * rows
     return (gathered.reshape(batches, total, model), outs,
             [wide.reshape(total, width) for wide in projected],
-            beta.reshape(batches, total, 128), pair_parts, down_part)
+            beta.reshape(batches, total, 128), pair_parts, down_part, gains_all)
 
 
 def scatter_kernel(w_refs, g_refs, gb_refs, o_refs, inner_ref, wb_ref, small_ref, gains_ref, pair_ref, down_ref,
@@ -1872,11 +1894,8 @@
     w_beta_wide = jnp.pad(w_beta, ((0, 0), (0, 128 - heads)))
     taps = conv_weight.astype(f32).reshape(-1, local_width)
     gain_heads = head_gain.astype(f32)
-    gains = gather(jnp.stack([norm_gain, ffn_gain]), DP, 1)
-    gain_one, gain_two = gains[0].astype(f32), gains[1].astype(f32)
+    gains = jnp.stack([norm_gain, ffn_gain])
     rows_in = inputs.astype(f32)
-    normed_one, scale_one = root_scale(rows_in, gain_one)
-    normed_one = normed_one.astype(bf16)
 
     def run_mixer(m, wide, logits):
         low, *kept = mixer_forward(lengths[m, 0], wide, logits, taps, gain_heads, exact=False)
@@ -1891,14 +1910,17 @@
         model = rows_in.shape[2]
         ranks = lax.axis_size(DP)
         ffn_parts = [
-            w.reshape(ranks, -1, w.shape[1]) for w in after((w_gate.T, w_up.T, w_down), gains)]
+            w.reshape(ranks, -1, w.shape[1]) for w in (w_gate.T, w_up.T, w_down)]
         c_rows = [None] * 8
-        c_rows[0] = after(cotangent.reshape(count, model), gains)
+        c_rows[0] = cotangent.reshape(count, model)
         c_rows[4] = exchange(c_rows[0], "core")
         out_shares = pick(
             w_out.reshape(lax.axis_size(DP), len(batches), -1, model), lax.axis_index(DP), 0)
-        gathered_one, out_own, projected, beta_logits, own_weights, own_down = gather_project(
-            normed_one, out_shares, ffn_parts, w_parts, w_beta_wide)
+        gains = jnp.pad(gains.astype(f32), ((0, 6), (0, 0)))
+        gathered_one, out_own, projected, beta_logits, own_weights, own_down, gains = gather_project(
+            inputs, gains, out_shares, ffn_parts, w_parts, w_beta_wide)
+        gain_one, gain_two = gains[0], gains[1]
+        _, scale_one = root_scale(rows_in, gain_one)
         early = after(c_rows[0], gathered_one)
         c_rows[1] = exchange(early, "x")
         weights = gather(own_weights[None], "z")
@@ -1907,6 +1929,10 @@
         out_y = exchange(out_own, "y")
         out_x = exchange(out_own, "x")
     else:
+        gains = gather(gains, DP, 1).astype(f32)
+        gain_one, gain_two = gains[0], gains[1]
+        normed_one, scale_one = root_scale(rows_in, gain_one)
+        normed_one = normed_one.astype(bf16)
         gathered_one = jnp.stack([gather(normed_one[m], TP) for m in batches])
         projected = [dot(gathered_one[m], w_inner) for m in batches]
         beta_logits = [dot(gathered_one[m], w_beta_wide) for m in batches]

time: 694 us -> 692 us (level)
    unnamed x132 -> x124, local copies, waits for them, and re-layouts: 26.2 us -> 28.4 us
  transfers between devices with their start and end apart: 20 -> 20, of which waited for: 6 -> 6; matrix products, arithmetic and copies ran while one was open for 2% -> 2% of each run, Pallas kernels for 23% -> 24%
where the time goes in v9:
time: 692 us; the launch traced here: 687 us
  Pallas kernels  565 us (82%)
  local copies, waits for them, and re-layouts  42.5 us (6%)
  waiting for transfers between devices  29.8 us (4%)
  other arithmetic  20.9 us (3%)
  between operations  15.1 us (2%)
  starting transfers between devices  12.9 us (2%)
    pallas_call x1, Pallas kernels, ffn_plane(): pl.pallas_call(ffn_call_kernel, out_shape=(jax.ShapeDtypeStruct((rows, mo...  149 us
    pallas_call x1, Pallas kernels, scatter_rows(): pl.pallas_call(scatter_call_kernel, out_shape=(jax.ShapeDtypeStruct((batc...  113 us
    pallas_call x1, Pallas kernels, gather_project(): pl.pallas_call(gather_call_kernel, out_shape=(jax.ShapeDtypeStruct((batch...  104 us
    pallas_call x2, Pallas kernels, mixer_backward(): pl.pallas_call(partial(mixer_backward_kernel, exact), out_shape=(jax.Shap...  56.5 us
    pallas_call x2, Pallas kernels, mixer_forward(): pl.pallas_call(partial(mixer_forward_kernel, exact, group), out_shape=(ja...  53.6 us
    pallas_call x1, Pallas kernels, attend_back(): pl.pallas_call(attend_back_kernel, out_shape=(wide, wide, back, back, *[j...  37.6 us
    pallas_call x1, Pallas kernels, attend(): pl.pallas_call(attend_kernel, out_shape=(jax.ShapeDtypeStruct((rows, mode...  36.3 us
    unnamed x124, local copies, waits for them, and re-layouts  28.4 us
  transfers between devices with their start and end apart: 20, of which 6 were waited for; matrix products, arithmetic and copies ran while one was open for 2% of the time, Pallas kernels for 24%

profile of v9, /device:TPU:0, one launch (start us, length us, event | category | flops | bytes accessed | tf_op | source)
XLA Modules:
  0.0 686.7 jit_solution(1878880810992972738)
XLA Ops:
  7.3 1.9 copy.39
  10.6 1.1 pad.20.refs_7_.wb_ref.refs_13_
  11.8 1.4 copy-done.13
  13.2 1.2 copy-done.15
  14.4 1.2 copy-done.17
  15.6 1.1 copy-done.23
  16.7 1.1 copy-done.24
  17.8 1.1 copy-done.25
  18.9 104.0 %gather_project.1 = (bf16[2,8,128,2048]{3,2,1,0:T(8,128)(2,1)}, bf16[4,2,32,2048]{3,2,1,0:T(8,128)(2,1)S(1)}, f32[8,128,1024]{2,1,0:T(8,128)}, f32[8,128,1024]{2...) custom-call(bf16[2,128,2048]{2,1,0:T(8,128)(2,1)S(1)} %copy-done.2, ...), custom_call_target="tpu_custom_call" | custom-call | flops 99999997952 | bytes 40000000 | tf_op jit(solution)/shard_map/gather_project/pallas_call | solution.py:1120
  125.8 1.5 collective-permute-start.2
  127.8 1.5 collective-permute-start.4
  129.5 26.9 %mixer_forward.2 = (bf16[1024,256]{1,0:T(8,128)(2,1)S(1)}, f32[1024,256]{1,0:T(8,128)S(1)}, f32[1024,256]{1,0:T(8,128)S(1)}, f32[1024,256]{1,0:T(8,128)S(1)}, f3...) custom-call(s32[3]{0:T(128)S(1)} %get-tuple-element.158.lengths_ref, f32[1024,1024]{1,0:T(8,128)} %bitcast.105, ...), custom_call_target="tpu_custom_call" | custom-call | flops 10000000000 | bytes 10000000 | tf_op jit(solution)/shard_map/mixer_forward/pallas_call | solution.py:333
  157.4 1.0 copy-done.34
  158.4 1.0 copy-done.35
  159.4 1.0 copy-done.36
  160.4 11.6 %collective-permute-done.refs_4_ = bf16[4,64,2048]{2,1,0:T(8,128)(2,1)} collective-permute-done((bf16[4,64,2048]{2,1,0:T(8,128)(2,1)}, bf16[4,64,2048]{2,1,0:T(8,128)(2,1)}, u32[]{:S(2)}, u32[]{:S(2)}) %collective-permute-start) | collective-permute-done | bytes 1048608 | tf_op jit(solution)/shard_map/ppermute | solution.py:1818
  171.9 1.5 collective-permute-start.5
  174.4 26.7 %mixer_forward.3 = (bf16[1024,256]{1,0:T(8,128)(2,1)S(1)}, f32[1024,256]{1,0:T(8,128)S(1)}, f32[1024,256]{1,0:T(8,128)S(1)}, f32[1024,256]{1,0:T(8,128)S(1)}, f3...) custom-call(s32[3]{0:T(128)S(1)} %get-tuple-element.157.lengths_ref, f32[1024,1024]{1,0:T(8,128)} %bitcast.103, ...), custom_call_target="tpu_custom_call" | custom-call | flops 10000000000 | bytes 10000000 | tf_op jit(solution)/shard_map/mixer_forward/pallas_call | solution.py:333
  202.5 2.4 collective-permute-done.7.refs_3_
  205.0 1.6 collective-permute-done.9.refs_7_
  206.6 36.3 %attend.1 = (f32[256,2048]{1,0:T(8,128)S(1)}, bf16[256,2048]{1,0:T(8,128)(2,1)S(1)}, bf16[4,2,4,64,2048]{4,3,2,1,0:T(8,128)(2,1)}, bf16[2,8,128,256]{3,2,1,0:T(8,128)(2,1)S(1)}) custom-call(bf16[256,2048]{1,0:T(8,128)(2,1)S(1)} %bitcast.68, bf16[8,128,256]{2,1,0:T(8,128)(2,1)S(1)} %bitcast.83, bf16[8,128,256]{2,1,0:T(8,128)(2,1)S(1)} %bitcast.85, ...), custom_call_target="tpu_custom_call" | custom-call | flops 30000001024 | bytes 20000000 | tf_op jit(solution)/shard_map/attend/pallas_call | solution.py:1586
  243.0 1.3 copy-done.41
  244.3 1.0 copy-done.42
  245.2 1.0 copy-done.43
  246.2 4.9 all-gather.3.cloned.1.call-done
  251.2 148.9 %ffn_plane.1 = (f32[256,2048]{1,0:T(8,128)}, f32[256,2048]{1,0:T(8,128)}, bf16[4,4,2,176,512]{4,3,2,1,0:T(8,128)(2,1)}, bf16[4,176,512]{2,1,0:T(8,128)(2,1)}) custom-call(bf16[256,2048]{1,0:T(8,128)(2,1)} %copy-done.43, bf16[4,4,2,176,512]{4,3,2,1,0:T(8,128)(2,1)} %bitcast.95, bf16[4,176,512]{2,1,0:T(8,128)(2,1)} %copy-done.44, bf16[256,2048]{1,0:T(8,128)(2,1)} %bitcast.99, ...), custom_call_target="tpu_custom_call" | custom-call | flops 80000000000 | bytes 40000000 | tf_op jit(solution)/shard_map/ffn_plane/pallas_call | solution.py:828
  400.1 37.6 %attend_back.1 = (f32[256,2048]{1,0:T(8,128)}, f32[256,2048]{1,0:T(8,128)}, bf16[8,128,256]{2,1,0:T(8,128)(2,1)S(1)}, bf16[8,128,256]{2,1,0:T(8,128)(2,1)S(1)}, ...) custom-call(f32[256,2048]{1,0:T(8,128)} %copy-done.41, ...), custom_call_target="tpu_custom_call" | custom-call | flops 30000001024 | bytes 40000000 | tf_op jit(solution)/shard_map/attend_back/pallas_call | solution.py:1709
  440.2 1.0 copy-done.22
  441.2 2.2 collective-permute-start.14
  444.6 28.7 %mixer_backward.2 = (bf16[1024,1024]{1,0:T(8,128)(2,1)}, bf16[1024,128]{1,0:T(8,128)(2,1)}, f32[12,256]{1,0:T(8,128)}, f32[2,128]{1,0:T(2,128)}) custom-call(s32[3]{0:T(128)} %copy-done.10, f32[1024,1024]{1,0:T(8,128)} %bitcast.106, f32[1024,128]{1,0:T(8,128)} %bitcast.72, f32[12,256]{1,0:T(8,128)} %copy-done.7, f32[2,128]{1,0:T(2,128)} %copy-done.32, ...), custom_call_target="tpu_custom_call" | custom-call | flops 10000000000 | bytes 10000000 | tf_op jit(solution)/shard_map/mixer_backward/pallas_call | solution.py:356
  473.3 2.6 add_convert_fusion.1.refs_8_
  475.9 2.6 add_convert_fusion.refs_10_
  478.5 27.9 %mixer_backward.3 = (bf16[1024,1024]{1,0:T(8,128)(2,1)}, bf16[1024,128]{1,0:T(8,128)(2,1)}, f32[12,256]{1,0:T(8,128)}, f32[2,128]{1,0:T(2,128)}) custom-call(s32[3]{0:T(128)} %copy-done.9, f32[1024,1024]{1,0:T(8,128)} %bitcast.104, f32[1024,128]{1,0:T(8,128)} %bitcast.70, f32[12,256]{1,0:T(8,128)} %copy-done.7, f32[2,128]{1,0:T(2,128)} %copy-done.32, ...), custom_call_target="tpu_custom_call" | custom-call | flops 10000000000 | bytes 10000000 | tf_op jit(solution)/shard_map/mixer_backward/pallas_call | solution.py:356
  506.5 1.6 copy-done.26
  508.1 1.6 copy-done.27
  510.6 15.7 %inner_grads.1 = (bf16[2048,1024]{1,0:T(8,128)(2,1)}, f32[2048,128]{1,0:T(8,128)S(1)}, f32[2048,128]{1,0:T(8,128)S(1)}) custom-call(bf16[2,1024,2048]{2,1,0:T(8,128)(2,1)} %bitcast.102, bf16[1024,1024]{1,0:T(8,128)(2,1)S(1)} %copy-done.26, bf16[1024,1024]{1,0:T(8,128)(2,1)S(1)} %copy-done.27, bf16[1024,128]{1,0:T(8,128)(2,1)S(1)} %copy-done.30, ...), custom_call_target="tpu_custom_call" | custom-call | flops 10000000000 | bytes 20000000 | tf_op jit(solution)/shard_map/inner_grads/pallas_call | solution.py:1759
  527.8 1.9 dynamic-slice_bitcast_fusion
  530.8 2.0 collective-permute-start.16
  534.6 8.5 %collective-permute-done.17.refs_11_ = bf16[4,64,1024]{2,1,0:T(8,128)(2,1)} collective-permute-done((bf16[4,64,1024]{2,1,0:T(8,128)(2,1)}, bf16[4,64,1024]{2,1,0:T(8,128)(2,1)}, u32[]{:S(2)}, u32[]{:S(2)}) %collective-permute-start.17) | collective-permute-done | bytes 524320 | tf_op jit(solution)/shard_map/ppermute | solution.py:1818
  543.9 112.9 %scatter_rows.1 = (f32[2,128,2048]{2,1,0:T(8,128)}, f32[72,128]{1,0:T(8,128)}, bf16[4,64,2048]{2,1,0:T(8,128)(2,1)}, bf16[2,1024,1024]{2,1,0:T(8,128)(2,1)}, bf1...) custom-call(bf16[2048,256]{1,0:T(8,128)(2,1)} %refs_0_.1, bf16[2048,256]{1,0:T(8,128)(2,1)} %refs_1_.1, ...), custom_call_target="tpu_custom_call" | custom-call | flops 70000001024 | bytes 40000000 | tf_op jit(solution)/shard_map/scatter_rows/pallas_call | solution.py:1469
  658.9 1.2 slice.91
  660.1 1.4 fusion.13
  661.6 5.8 slice_convert_fusion
  667.4 1.6 bitcast_convert_fusion
  669.0 1.3 bitcast_convert_fusion.1
  671.7 2.1 convert_bitcast_fusion
  675.4 2.1 fusion.5
  677.4 1.3 copy.44
  (176 shorter events, 24.0 us)
Async XLA Ops:
  7.2 4.5 copy-start.2
  7.2 4.5 copy-start.11
  7.2 244.0 %all-gather.3.cloned.1.call-start = ((), (), s32[]{:S(2)}) async-start(), calls=%async_computation.2 | async-start | bytes 7208960 | tf_op jit(solution)/shard_map/all_gather | solution.py:1795
  11.7 111.2 %copy-start.3 = (bf16[2048,128]{1,0:T(8,128)(2,1)}, bf16[2048,128]{1,0:T(8,128)(2,1)S(1)}, u32[]{:S(2)}) copy-start(bf16[2048,128]{1,0:T(8,128)(2,1)S(1)} %pad.20.refs_7_.wb_ref.refs_13_) | copy-start | bytes 1572868
  124.8 77.1 %copy-start.8 = (f32[8,2048]{1,0:T(8,128)}, f32[8,2048]{1,0:T(8,128)S(1)}, u32[]{:S(2)}) copy-start(f32[8,2048]{1,0:T(8,128)S(1)} %get-tuple-element.90) | copy-start | bytes 196612
  124.8 4.6 copy-start.56
  124.8 4.6 copy-start.53
  124.8 4.7 copy-start.60
  124.8 419.1 %reduce-scatter.2.cloned.1.call-start = ((), (), s32[]{:S(2)}) async-start(), calls=%async_computation.1 | async-start | bytes 7208960 | tf_op jit(solution)/shard_map/reduce_scatter | solution.py:1967
  125.2 35.2 %collective-permute-start.1 = (bf16[256,2048]{1,0:T(8,128)(2,1)}, bf16[256,2048]{1,0:T(8,128)(2,1)}, u32[]{:S(2)}, u32[]{:S(2)}) collective-permute-start(bf16[256,2048]{1,0:T(8,128)(2,1)} %bitcast.97), channel_id=1, source_target_pairs={{0,16},{16,0},{1,17},{17,1},{2,18},{18,2},{3,19},{19,3},{4,20},{20... | collective-permute-start | bytes 3145736 | tf_op jit(solution)/shard_map/ppermute | solution.py:1818
  125.8 34.6 %collective-permute-start.2 = (bf16[256,2048]{1,0:T(8,128)(2,1)}, bf16[256,2048]{1,0:T(8,128)(2,1)}, u32[]{:S(2)}, u32[]{:S(2)}) collective-permute-start(bf16[256,2048]{1,0:T(8,128)(2,1)} %bitcast.98), channel_id=1, source_target_pairs={{0,1},{1,0},{2,3},{3,2},{4,5},{5,4},{6,7},{7,6},{8,9},{9,8},{10,11... | collective-permute-start | bytes 3145736 | tf_op jit(solution)/shard_map/ppermute | solution.py:1818
  127.2 44.7 %collective-permute-start = (bf16[4,64,2048]{2,1,0:T(8,128)(2,1)}, bf16[4,64,2048]{2,1,0:T(8,128)(2,1)}, u32[]{:S(2)}, u32[]{:S(2)}) collective-permute-start(bf16[4,64,2048]{2,1,0:T(8,128)(2,1)} %bitcast.73), channel_id=1, source_target_pairs={{0,1},{1,0},{2,3},{3,2},{4,5},{5,4},{6,7},{7,6},{8,9},{9,8},{10,11... | collective-permute-start | bytes 3145736 | tf_op jit(solution)/shard_map/ppermute | solution.py:1818
  127.8 73.4 %collective-permute-start.4 = (bf16[4,64,2048]{2,1,0:T(8,128)(2,1)}, bf16[4,64,2048]{2,1,0:T(8,128)(2,1)}, u32[]{:S(2)}, u32[]{:S(2)}) collective-permute-start(bf16[4,64,2048]{2,1,0:T(8,128)(2,1)} %bitcast.74), channel_id=1, source_target_pairs={{0,16},{16,0},{1,17},{17,1},{2,18},{18,2},{3,19},{19,3},{4,20},{20... | collective-permute-start | bytes 3145736 | tf_op jit(solution)/shard_map/ppermute | solution.py:1818
  129.4 27.1 %copy-start.6 = (f32[1,8,128,128]{3,2,1,0:T(8,128)}, f32[1,8,128,128]{3,2,1,0:T(8,128)S(1)}, u32[]{:S(2)}) copy-start(f32[1,8,128,128]{3,2,1,0:T(8,128)S(1)} %get-tuple-element.152) | copy-start | bytes 1572868
  129.4 45.0 %copy-start.5 = (f32[1,8,128,128]{3,2,1,0:T(8,128)}, f32[1,8,128,128]{3,2,1,0:T(8,128)S(1)}, u32[]{:S(2)}) copy-start(f32[1,8,128,128]{3,2,1,0:T(8,128)S(1)} %get-tuple-element.151) | copy-start | bytes 1572868
  129.4 27.0 %copy-start.10 = (s32[3]{0:T(128)}, s32[3]{0:T(128)S(1)}, u32[]{:S(2)}) copy-start(s32[3]{0:T(128)S(1)} %get-tuple-element.158.lengths_ref) | copy-start | bytes 40
  129.4 45.0 %copy-start.9 = (s32[3]{0:T(128)}, s32[3]{0:T(128)S(1)}, u32[]{:S(2)}) copy-start(s32[3]{0:T(128)S(1)} %get-tuple-element.157.lengths_ref) | copy-start | bytes 40
  129.5 45.0 %copy-start.7 = (f32[12,256]{1,0:T(8,128)}, f32[12,256]{1,0:T(8,128)S(1)}, u32[]{:S(2)}) copy-start(f32[12,256]{1,0:T(8,128)S(1)} %reshape.186.tap_ref) | copy-start | bytes 36868
  129.5 44.9 %copy-start.32 = (f32[2,128]{1,0:T(2,128)}, f32[2,128]{1,0:T(2,128)S(1)}, u32[]{:S(2)}) copy-start(f32[2,128]{1,0:T(2,128)S(1)} %convert_element_type.66.gain_ref) | copy-start | bytes 3076
  129.5 44.4 %copy-start.20 = (bf16[4,2,32,2048]{3,2,1,0:T(8,128)(2,1)S(1)}, bf16[4,2,32,2048]{3,2,1,0:T(8,128)(2,1)}, u32[]{:S(2)}) copy-start(bf16[4,2,32,2048]{3,2,1,0:T(8,128)(2,1)} %copy-done.19) | copy-start | bytes 3145732
  171.9 29.2 %collective-permute-start.5 = (bf16[4,64,2048]{2,1,0:T(8,128)(2,1)}, bf16[4,64,2048]{2,1,0:T(8,128)(2,1)S(1)}, u32[]{:S(2)}, u32[]{:S(2)}) collective-permute-start(bf16[4,64,2048]{2,1,0:T(8,128)(2,1)} %collective-permute-done.refs_4_), channel_id=1, source_target_pairs={{0,16},{16,0},{1,17},{17,1},{2,18},{18,2},{3,19},{19,3},{4,20},{20... | collective-permute-start | bytes 3145736 | tf_op jit(solution)/shard_map/ppermute | solution.py:1818
  173.4 27.8 %collective-permute-start.6 = (bf16[256,2048]{1,0:T(8,128)(2,1)}, bf16[256,2048]{1,0:T(8,128)(2,1)S(1)}, u32[]{:S(2)}, u32[]{:S(2)}) collective-permute-start(bf16[256,2048]{1,0:T(8,128)(2,1)} %collective-permute-done.1.refs_1_), channel_id=1, source_target_pairs={{0,1},{1,0},{2,3},{3,2},{4,5},{5,4},{6,7},{7,6},{8,9},{9,8},{10,11... | collective-permute-start | bytes 3145736 | tf_op jit(solution)/shard_map/ppermute | solution.py:1818
  173.9 28.0 %collective-permute-start.3 = (bf16[4,64,2048]{2,1,0:T(8,128)(2,1)S(1)}, bf16[4,64,2048]{2,1,0:T(8,128)(2,1)S(1)}, u32[]{:S(2)}, u32[]{:S(2)}) collective-permute-start(bf16[4,64,2048]{2,1,0:T(8,128)(2,1)S(1)} %bitcast.75), channel_id=1, source_target_pairs={{0,8},{8,0},{1,9},{9,1},{2,10},{10,2},{3,11},{11,3},{4,12},{12,4},... | collective-permute-start | bytes 3145736 | tf_op jit(solution)/shard_map/ppermute | solution.py:1818
  173.9 28.5 %collective-permute-start.8 = (bf16[4,64,2048]{2,1,0:T(8,128)(2,1)}, bf16[4,64,2048]{2,1,0:T(8,128)(2,1)S(1)}, u32[]{:S(2)}, u32[]{:S(2)}) collective-permute-start(bf16[4,64,2048]{2,1,0:T(8,128)(2,1)} %collective-permute-done.refs_4_), channel_id=1, source_target_pairs={{0,8},{8,0},{1,9},{9,1},{2,10},{10,2},{3,11},{11,3},{4,12},{12,4},... | collective-permute-start | bytes 3145736 | tf_op jit(solution)/shard_map/ppermute | solution.py:1818
  174.4 27.4 %copy-start.57 = (bf16[2,128,2048]{2,1,0:T(8,128)(2,1)S(1)}, bf16[2,128,2048]{2,1,0:T(8,128)(2,1)}, u32[]{:S(2)}) copy-start(bf16[2,128,2048]{2,1,0:T(8,128)(2,1)} %param.31) | copy-start | bytes 3145732
  201.2 41.7 %copy-start.37 = (f32[1024,256]{1,0:T(8,128)}, f32[1024,256]{1,0:T(8,128)S(1)}, u32[]{:S(2)}) copy-start(f32[1024,256]{1,0:T(8,128)S(1)} %get-tuple-element.118.heads_ref) | copy-start | bytes 3145732
  201.2 41.8 %copy-start.38 = (f32[1024,256]{1,0:T(8,128)}, f32[1024,256]{1,0:T(8,128)S(1)}, u32[]{:S(2)}) copy-start(f32[1024,256]{1,0:T(8,128)S(1)} %get-tuple-element.119.fixed_ref) | copy-start | bytes 3145732
  201.2 41.8 %copy-start.39 = (f32[1024,256]{1,0:T(8,128)}, f32[1024,256]{1,0:T(8,128)S(1)}, u32[]{:S(2)}) copy-start(f32[1024,256]{1,0:T(8,128)S(1)} %get-tuple-element.120.delta_ref) | copy-start | bytes 3145732
  201.2 41.8 %copy-start.40 = (f32[16,128,128]{2,1,0:T(8,128)}, f32[16,128,128]{2,1,0:T(8,128)S(1)}, u32[]{:S(2)}) copy-start(f32[16,128,128]{2,1,0:T(8,128)S(1)} %get-tuple-element.121.state_ref) | copy-start | bytes 3145732
  201.2 41.7 %copy-start.58 = (bf16[256,2048]{1,0:T(8,128)(2,1)}, bf16[256,2048]{1,0:T(8,128)(2,1)S(1)}, u32[]{:S(2)}) copy-start(bf16[256,2048]{1,0:T(8,128)(2,1)S(1)} %collective-permute-done.6.refs_3_) | copy-start | bytes 3145732
  201.2 3.7 collective-permute-start.7
  201.3 5.3 collective-permute-start.9
  201.8 44.4 %collective-permute-start.10 = (bf16[256,2048]{1,0:T(8,128)(2,1)S(1)}, bf16[256,2048]{1,0:T(8,128)(2,1)S(1)}, u32[]{:S(2)}, u32[]{:S(2)}) collective-permute-start(bf16[256,2048]{1,0:T(8,128)(2,1)S(1)} %bitcast.101), channel_id=1, source_target_pairs={{0,8},{8,0},{1,9},{9,1},{2,10},{10,2},{3,11},{11,3},{4,12},{12,4},... | collective-permute-start | bytes 3145736 | tf_op jit(solution)/shard_map/ppermute | solution.py:1818
  201.9 44.3 %collective-permute-start.11 = (bf16[256,2048]{1,0:T(8,128)(2,1)}, bf16[256,2048]{1,0:T(8,128)(2,1)}, u32[]{:S(2)}, u32[]{:S(2)}) collective-permute-start(bf16[256,2048]{1,0:T(8,128)(2,1)} %collective-permute-done.1.refs_1_), channel_id=1, source_target_pairs={{0,8},{8,0},{1,9},{9,1},{2,10},{10,2},{3,11},{11,3},{4,12},{12,4},... | collective-permute-start | bytes 3145736 | tf_op jit(solution)/shard_map/ppermute | solution.py:1818
  202.4 43.8 %collective-permute-start.12 = (bf16[256,2048]{1,0:T(8,128)(2,1)}, bf16[256,2048]{1,0:T(8,128)(2,1)}, u32[]{:S(2)}, u32[]{:S(2)}) collective-permute-start(bf16[256,2048]{1,0:T(8,128)(2,1)} %collective-permute-done.2.refs_2_), channel_id=1, source_target_pairs={{0,8},{8,0},{1,9},{9,1},{2,10},{10,2},{3,11},{11,3},{4,12},{12,4},... | collective-permute-start | bytes 3145736 | tf_op jit(solution)/shard_map/ppermute | solution.py:1818
  204.9 41.4 %collective-permute-start.13 = (bf16[256,2048]{1,0:T(8,128)(2,1)S(1)}, bf16[256,2048]{1,0:T(8,128)(2,1)}, u32[]{:S(2)}, u32[]{:S(2)}) collective-permute-start(bf16[256,2048]{1,0:T(8,128)(2,1)S(1)} %collective-permute-done.6.refs_3_), channel_id=1, source_target_pairs={{0,8},{8,0},{1,9},{9,1},{2,10},{10,2},{3,11},{11,3},{4,12},{12,4},... | collective-permute-start | bytes 3145736 | tf_op jit(solution)/shard_map/ppermute | solution.py:1818
  246.2 5.0 copy-start.59
  441.2 32.1 %collective-permute-start.14 = (bf16[2,4,64,1024]{3,2,1,0:T(8,128)(2,1)}, bf16[2,4,64,1024]{3,2,1,0:T(8,128)(2,1)}, u32[]{:S(2)}, u32[]{:S(2)}) collective-permute-start(bf16[2,4,64,1024]{3,2,1,0:T(8,128)(2,1)} %copy-done.22), channel_id=1, source_target_pairs={{0,16},{16,0},{1,17},{17,1},{2,18},{18,2},{3,19},{19,3},{4,20},{20... | collective-permute-start | bytes 3145736 | tf_op jit(solution)/shard_map/ppermute | solution.py:1818
  443.4 32.5 %collective-permute-start.15 = (bf16[2,4,64,1024]{3,2,1,0:T(8,128)(2,1)}, bf16[2,4,64,1024]{3,2,1,0:T(8,128)(2,1)}, u32[]{:S(2)}, u32[]{:S(2)}) collective-permute-start(bf16[2,4,64,1024]{3,2,1,0:T(8,128)(2,1)} %copy-done.21), channel_id=1, source_target_pairs={{0,1},{1,0},{2,3},{3,2},{4,5},{5,4},{6,7},{7,6},{8,9},{9,8},{10,11... | collective-permute-start | bytes 3145736 | tf_op jit(solution)/shard_map/ppermute | solution.py:1818
  478.5 27.9 %copy-start.4 = (bf16[2048,128]{1,0:T(8,128)(2,1)S(1)}, bf16[2048,128]{1,0:T(8,128)(2,1)}, u32[]{:S(2)}) copy-start(bf16[2048,128]{1,0:T(8,128)(2,1)} %copy-done.3) | copy-start | bytes 1572868
  478.5 27.9 %copy-start.12 = (bf16[2048,256]{1,0:T(8,128)(2,1)S(1)}, bf16[2048,256]{1,0:T(8,128)(2,1)}, u32[]{:S(2)}) copy-start(bf16[2048,256]{1,0:T(8,128)(2,1)} %refs_0_.1) | copy-start | bytes 3145732
  478.5 27.9 %copy-start.14 = (bf16[2048,256]{1,0:T(8,128)(2,1)S(1)}, bf16[2048,256]{1,0:T(8,128)(2,1)}, u32[]{:S(2)}) copy-start(bf16[2048,256]{1,0:T(8,128)(2,1)} %refs_1_.1) | copy-start | bytes 3145732
  478.5 27.9 %copy-start.16 = (bf16[2048,256]{1,0:T(8,128)(2,1)S(1)}, bf16[2048,256]{1,0:T(8,128)(2,1)}, u32[]{:S(2)}) copy-start(bf16[2048,256]{1,0:T(8,128)(2,1)} %refs_2_.1) | copy-start | bytes 3145732
  478.5 27.9 %copy-start.18 = (bf16[2048,256]{1,0:T(8,128)(2,1)S(1)}, bf16[2048,256]{1,0:T(8,128)(2,1)}, u32[]{:S(2)}) copy-start(bf16[2048,256]{1,0:T(8,128)(2,1)} %refs_3_.3) | copy-start | bytes 3145732
  478.5 27.9 %copy-start.30 = (bf16[1024,128]{1,0:T(8,128)(2,1)S(1)}, bf16[1024,128]{1,0:T(8,128)(2,1)}, u32[]{:S(2)}) copy-start(bf16[1024,128]{1,0:T(8,128)(2,1)} %get-tuple-element.124.b_first) | copy-start | bytes 786436
  529.6 13.4 %collective-permute-start.17 = (bf16[4,64,1024]{2,1,0:T(8,128)(2,1)}, bf16[4,64,1024]{2,1,0:T(8,128)(2,1)}, u32[]{:S(2)}, u32[]{:S(2)}) collective-permute-start(bf16[4,64,1024]{2,1,0:T(8,128)(2,1)} %dynamic-slice_bitcast_fusion), channel_id=1, source_target_pairs={{0,16},{16,0},{1,17},{17,1},{2,18},{18,2},{3,19},{19,3},{4,20},{20... | collective-permute-start | bytes 1572872 | tf_op jit(solution)/shard_map/ppermute | solution.py:1818
  530.8 13.1 %collective-permute-start.16 = (bf16[4,64,1024]{2,1,0:T(8,128)(2,1)}, bf16[4,64,1024]{2,1,0:T(8,128)(2,1)}, u32[]{:S(2)}, u32[]{:S(2)}) collective-permute-start(bf16[4,64,1024]{2,1,0:T(8,128)(2,1)} %dynamic-slice_bitcast_fusion.1), channel_id=1, source_target_pairs={{0,1},{1,0},{2,3},{3,2},{4,5},{5,4},{6,7},{7,6},{8,9},{9,8},{10,11... | collective-permute-start | bytes 1572872 | tf_op jit(solution)/shard_map/ppermute | solution.py:1818
  661.6 5.8 copy-start.49
  (33 other events, 56.2 us)
Sparse Core Ops, SparseCore 0:
  124.9 126.2 all-gather.2
  441.3 100.3 reduce-scatter.1

commit v10 on v9

--- a/solution.py
+++ b/solution.py
@@ -663,6 +663,18 @@
             def _():
                 sum_tick(k)
 
+        @pl.when(step == 7)
+        def _():
+            for h in range(2):
+                n = 2 - h
+                for a in range(2):
+                    d_sends[h][a].wait_recv()
+                    at = pl.ds(h * half, half)
+                    crecv[n, a, at, :] = (
+                        crecv[n, a, at, :].astype(f32) + drecv[a, at, :].astype(f32)).astype(bf16)
+                for copy in (y_sends, x_sends)[h][h]:
+                    copy.start()
+
         c_copy(step, 0).wait()
 
         for start in range(0, hidden, tile_f):
@@ -726,15 +738,6 @@
                 copy.start()
 
 
-    for h in range(2):
-        j = 2 - h
-        for a in range(2):
-            d_sends[h][a].wait_recv()
-            at = pl.ds(h * half, half)
-            crecv[j, a, at, :] = (
-                crecv[j, a, at, :].astype(f32) + drecv[a, at, :].astype(f32)).astype(bf16)
-        for copy in (y_sends, x_sends)[h][h]:
-            copy.start()
     weight_grads(0)
     weight_grads(1)
     out_copies = []

time: 692 us -> 692 us (level)
  no operation moved by 1% of the time
where the time goes in v10:
time: 692 us; the launch traced here: 687 us
  Pallas kernels  565 us (82%)
  local copies, waits for them, and re-layouts  42.5 us (6%)
  waiting for transfers between devices  29.8 us (4%)
  other arithmetic  20.9 us (3%)
  between operations  15.1 us (2%)
  starting transfers between devices  12.9 us (2%)
    pallas_call x1, Pallas kernels, ffn_plane(): pl.pallas_call(ffn_call_kernel, out_shape=(jax.ShapeDtypeStruct((rows, mo...  149 us
    pallas_call x1, Pallas kernels, scatter_rows(): pl.pallas_call(scatter_call_kernel, out_shape=(jax.ShapeDtypeStruct((batc...  113 us
    pallas_call x1, Pallas kernels, gather_project(): pl.pallas_call(gather_call_kernel, out_shape=(jax.ShapeDtypeStruct((batch...  104 us
    pallas_call x2, Pallas kernels, mixer_backward(): pl.pallas_call(partial(mixer_backward_kernel, exact), out_shape=(jax.Shap...  56.5 us
    pallas_call x2, Pallas kernels, mixer_forward(): pl.pallas_call(partial(mixer_forward_kernel, exact, group), out_shape=(ja...  53.6 us
    pallas_call x1, Pallas kernels, attend_back(): pl.pallas_call(attend_back_kernel, out_shape=(wide, wide, back, back, *[j...  37.6 us
    pallas_call x1, Pallas kernels, attend(): pl.pallas_call(attend_kernel, out_shape=(jax.ShapeDtypeStruct((rows, mode...  36.3 us
    unnamed x124, local copies, waits for them, and re-layouts  28.4 us
  transfers between devices with their start and end apart: 20, of which 6 were waited for; matrix products, arithmetic and copies ran while one was open for 2% of the time, Pallas kernels for 24%

profile of v10, /device:TPU:0, one launch (start us, length us, event | category | flops | bytes accessed | tf_op | source)
XLA Modules:
  0.0 686.7 jit_solution(7616987366819978742)
XLA Ops:
  7.3 1.9 copy.39
  10.6 1.1 pad.20.refs_7_.wb_ref.refs_13_
  11.8 1.4 copy-done.13
  13.2 1.2 copy-done.15
  14.4 1.2 copy-done.17
  15.6 1.1 copy-done.23
  16.7 1.1 copy-done.24
  17.8 1.1 copy-done.25
  18.9 104.0 %gather_project.1 = (bf16[2,8,128,2048]{3,2,1,0:T(8,128)(2,1)}, bf16[4,2,32,2048]{3,2,1,0:T(8,128)(2,1)S(1)}, f32[8,128,1024]{2,1,0:T(8,128)}, f32[8,128,1024]{2...) custom-call(bf16[2,128,2048]{2,1,0:T(8,128)(2,1)S(1)} %copy-done.2, ...), custom_call_target="tpu_custom_call" | custom-call | flops 99999997952 | bytes 40000000 | tf_op jit(solution)/shard_map/gather_project/pallas_call | solution.py:1123
  125.8 1.5 collective-permute-start.2
  127.8 1.5 collective-permute-start.4
  129.5 26.9 %mixer_forward.2 = (bf16[1024,256]{1,0:T(8,128)(2,1)S(1)}, f32[1024,256]{1,0:T(8,128)S(1)}, f32[1024,256]{1,0:T(8,128)S(1)}, f32[1024,256]{1,0:T(8,128)S(1)}, f3...) custom-call(s32[3]{0:T(128)S(1)} %get-tuple-element.158.lengths_ref, f32[1024,1024]{1,0:T(8,128)} %bitcast.105, ...), custom_call_target="tpu_custom_call" | custom-call | flops 10000000000 | bytes 10000000 | tf_op jit(solution)/shard_map/mixer_forward/pallas_call | solution.py:333
  157.4 1.0 copy-done.34
  158.4 1.0 copy-done.35
  159.4 1.0 copy-done.36
  160.4 11.6 %collective-permute-done.refs_4_ = bf16[4,64,2048]{2,1,0:T(8,128)(2,1)} collective-permute-done((bf16[4,64,2048]{2,1,0:T(8,128)(2,1)}, bf16[4,64,2048]{2,1,0:T(8,128)(2,1)}, u32[]{:S(2)}, u32[]{:S(2)}) %collective-permute-start) | collective-permute-done | bytes 1048608 | tf_op jit(solution)/shard_map/ppermute | solution.py:1821
  171.9 1.5 collective-permute-start.5
  174.4 26.7 %mixer_forward.3 = (bf16[1024,256]{1,0:T(8,128)(2,1)S(1)}, f32[1024,256]{1,0:T(8,128)S(1)}, f32[1024,256]{1,0:T(8,128)S(1)}, f32[1024,256]{1,0:T(8,128)S(1)}, f3...) custom-call(s32[3]{0:T(128)S(1)} %get-tuple-element.157.lengths_ref, f32[1024,1024]{1,0:T(8,128)} %bitcast.103, ...), custom_call_target="tpu_custom_call" | custom-call | flops 10000000000 | bytes 10000000 | tf_op jit(solution)/shard_map/mixer_forward/pallas_call | solution.py:333
  202.5 2.4 collective-permute-done.7.refs_3_
  205.0 1.6 collective-permute-done.9.refs_7_
  206.6 36.3 %attend.1 = (f32[256,2048]{1,0:T(8,128)S(1)}, bf16[256,2048]{1,0:T(8,128)(2,1)S(1)}, bf16[4,2,4,64,2048]{4,3,2,1,0:T(8,128)(2,1)}, bf16[2,8,128,256]{3,2,1,0:T(8,128)(2,1)S(1)}) custom-call(bf16[256,2048]{1,0:T(8,128)(2,1)S(1)} %bitcast.68, bf16[8,128,256]{2,1,0:T(8,128)(2,1)S(1)} %bitcast.83, bf16[8,128,256]{2,1,0:T(8,128)(2,1)S(1)} %bitcast.85, ...), custom_call_target="tpu_custom_call" | custom-call | flops 30000001024 | bytes 20000000 | tf_op jit(solution)/shard_map/attend/pallas_call | solution.py:1589
  243.0 1.3 copy-done.41
  244.3 1.0 copy-done.42
  245.2 1.0 copy-done.43
  246.2 4.9 all-gather.3.cloned.1.call-done
  251.2 148.9 %ffn_plane.1 = (f32[256,2048]{1,0:T(8,128)}, f32[256,2048]{1,0:T(8,128)}, bf16[4,4,2,176,512]{4,3,2,1,0:T(8,128)(2,1)}, bf16[4,176,512]{2,1,0:T(8,128)(2,1)}) custom-call(bf16[256,2048]{1,0:T(8,128)(2,1)} %copy-done.43, bf16[4,4,2,176,512]{4,3,2,1,0:T(8,128)(2,1)} %bitcast.95, bf16[4,176,512]{2,1,0:T(8,128)(2,1)} %copy-done.44, bf16[256,2048]{1,0:T(8,128)(2,1)} %bitcast.99, ...), custom_call_target="tpu_custom_call" | custom-call | flops 80000000000 | bytes 40000000 | tf_op jit(solution)/shard_map/ffn_plane/pallas_call | solution.py:831
  400.1 37.6 %attend_back.1 = (f32[256,2048]{1,0:T(8,128)}, f32[256,2048]{1,0:T(8,128)}, bf16[8,128,256]{2,1,0:T(8,128)(2,1)S(1)}, bf16[8,128,256]{2,1,0:T(8,128)(2,1)S(1)}, ...) custom-call(f32[256,2048]{1,0:T(8,128)} %copy-done.41, ...), custom_call_target="tpu_custom_call" | custom-call | flops 30000001024 | bytes 40000000 | tf_op jit(solution)/shard_map/attend_back/pallas_call | solution.py:1712
  440.2 1.0 copy-done.22
  441.2 2.2 collective-permute-start.14
  444.6 28.7 %mixer_backward.2 = (bf16[1024,1024]{1,0:T(8,128)(2,1)}, bf16[1024,128]{1,0:T(8,128)(2,1)}, f32[12,256]{1,0:T(8,128)}, f32[2,128]{1,0:T(2,128)}) custom-call(s32[3]{0:T(128)} %copy-done.10, f32[1024,1024]{1,0:T(8,128)} %bitcast.106, f32[1024,128]{1,0:T(8,128)} %bitcast.72, f32[12,256]{1,0:T(8,128)} %copy-done.7, f32[2,128]{1,0:T(2,128)} %copy-done.32, ...), custom_call_target="tpu_custom_call" | custom-call | flops 10000000000 | bytes 10000000 | tf_op jit(solution)/shard_map/mixer_backward/pallas_call | solution.py:356
  473.3 2.6 add_convert_fusion.1.refs_8_
  475.9 2.6 add_convert_fusion.refs_10_
  478.5 27.9 %mixer_backward.3 = (bf16[1024,1024]{1,0:T(8,128)(2,1)}, bf16[1024,128]{1,0:T(8,128)(2,1)}, f32[12,256]{1,0:T(8,128)}, f32[2,128]{1,0:T(2,128)}) custom-call(s32[3]{0:T(128)} %copy-done.9, f32[1024,1024]{1,0:T(8,128)} %bitcast.104, f32[1024,128]{1,0:T(8,128)} %bitcast.70, f32[12,256]{1,0:T(8,128)} %copy-done.7, f32[2,128]{1,0:T(2,128)} %copy-done.32, ...), custom_call_target="tpu_custom_call" | custom-call | flops 10000000000 | bytes 10000000 | tf_op jit(solution)/shard_map/mixer_backward/pallas_call | solution.py:356
  506.5 1.6 copy-done.26
  508.1 1.6 copy-done.27
  510.6 15.7 %inner_grads.1 = (bf16[2048,1024]{1,0:T(8,128)(2,1)}, f32[2048,128]{1,0:T(8,128)S(1)}, f32[2048,128]{1,0:T(8,128)S(1)}) custom-call(bf16[2,1024,2048]{2,1,0:T(8,128)(2,1)} %bitcast.102, bf16[1024,1024]{1,0:T(8,128)(2,1)S(1)} %copy-done.26, bf16[1024,1024]{1,0:T(8,128)(2,1)S(1)} %copy-done.27, bf16[1024,128]{1,0:T(8,128)(2,1)S(1)} %copy-done.30, ...), custom_call_target="tpu_custom_call" | custom-call | flops 10000000000 | bytes 20000000 | tf_op jit(solution)/shard_map/inner_grads/pallas_call | solution.py:1762
  527.8 1.9 dynamic-slice_bitcast_fusion
  530.8 2.0 collective-permute-start.16
  534.6 8.5 %collective-permute-done.17.refs_11_ = bf16[4,64,1024]{2,1,0:T(8,128)(2,1)} collective-permute-done((bf16[4,64,1024]{2,1,0:T(8,128)(2,1)}, bf16[4,64,1024]{2,1,0:T(8,128)(2,1)}, u32[]{:S(2)}, u32[]{:S(2)}) %collective-permute-start.17) | collective-permute-done | bytes 524320 | tf_op jit(solution)/shard_map/ppermute | solution.py:1821
  543.9 112.9 %scatter_rows.1 = (f32[2,128,2048]{2,1,0:T(8,128)}, f32[72,128]{1,0:T(8,128)}, bf16[4,64,2048]{2,1,0:T(8,128)(2,1)}, bf16[2,1024,1024]{2,1,0:T(8,128)(2,1)}, bf1...) custom-call(bf16[2048,256]{1,0:T(8,128)(2,1)} %refs_0_.1, bf16[2048,256]{1,0:T(8,128)(2,1)} %refs_1_.1, ...), custom_call_target="tpu_custom_call" | custom-call | flops 70000001024 | bytes 40000000 | tf_op jit(solution)/shard_map/scatter_rows/pallas_call | solution.py:1472
  658.9 1.2 slice.91
  660.1 1.4 fusion.13
  661.6 5.8 slice_convert_fusion
  667.4 1.6 bitcast_convert_fusion
  669.0 1.3 bitcast_convert_fusion.1
  671.7 2.1 convert_bitcast_fusion
  675.4 2.1 fusion.5
  677.4 1.3 copy.44
  (176 shorter events, 24.0 us)
Async XLA Ops:
  7.2 4.5 copy-start.2
  7.2 4.5 copy-start.11
  7.2 244.0 %all-gather.3.cloned.1.call-start = ((), (), s32[]{:S(2)}) async-start(), calls=%async_computation.2 | async-start | bytes 7208960 | tf_op jit(solution)/shard_map/all_gather | solution.py:1798
  11.7 111.2 %copy-start.3 = (bf16[2048,128]{1,0:T(8,128)(2,1)}, bf16[2048,128]{1,0:T(8,128)(2,1)S(1)}, u32[]{:S(2)}) copy-start(bf16[2048,128]{1,0:T(8,128)(2,1)S(1)} %pad.20.refs_7_.wb_ref.refs_13_) | copy-start | bytes 1572868
  124.8 77.1 %copy-start.8 = (f32[8,2048]{1,0:T(8,128)}, f32[8,2048]{1,0:T(8,128)S(1)}, u32[]{:S(2)}) copy-start(f32[8,2048]{1,0:T(8,128)S(1)} %get-tuple-element.90) | copy-start | bytes 196612
  124.8 4.6 copy-start.56
  124.8 4.6 copy-start.53
  124.8 4.7 copy-start.60
  124.8 419.1 %reduce-scatter.2.cloned.1.call-start = ((), (), s32[]{:S(2)}) async-start(), calls=%async_computation.1 | async-start | bytes 7208960 | tf_op jit(solution)/shard_map/reduce_scatter | solution.py:1970
  125.2 35.2 %collective-permute-start.1 = (bf16[256,2048]{1,0:T(8,128)(2,1)}, bf16[256,2048]{1,0:T(8,128)(2,1)}, u32[]{:S(2)}, u32[]{:S(2)}) collective-permute-start(bf16[256,2048]{1,0:T(8,128)(2,1)} %bitcast.97), channel_id=1, source_target_pairs={{0,16},{16,0},{1,17},{17,1},{2,18},{18,2},{3,19},{19,3},{4,20},{20... | collective-permute-start | bytes 3145736 | tf_op jit(solution)/shard_map/ppermute | solution.py:1821
  125.8 34.6 %collective-permute-start.2 = (bf16[256,2048]{1,0:T(8,128)(2,1)}, bf16[256,2048]{1,0:T(8,128)(2,1)}, u32[]{:S(2)}, u32[]{:S(2)}) collective-permute-start(bf16[256,2048]{1,0:T(8,128)(2,1)} %bitcast.98), channel_id=1, source_target_pairs={{0,1},{1,0},{2,3},{3,2},{4,5},{5,4},{6,7},{7,6},{8,9},{9,8},{10,11... | collective-permute-start | bytes 3145736 | tf_op jit(solution)/shard_map/ppermute | solution.py:1821
  127.2 44.7 %collective-permute-start = (bf16[4,64,2048]{2,1,0:T(8,128)(2,1)}, bf16[4,64,2048]{2,1,0:T(8,128)(2,1)}, u32[]{:S(2)}, u32[]{:S(2)}) collective-permute-start(bf16[4,64,2048]{2,1,0:T(8,128)(2,1)} %bitcast.73), channel_id=1, source_target_pairs={{0,1},{1,0},{2,3},{3,2},{4,5},{5,4},{6,7},{7,6},{8,9},{9,8},{10,11... | collective-permute-start | bytes 3145736 | tf_op jit(solution)/shard_map/ppermute | solution.py:1821
  127.8 73.4 %collective-permute-start.4 = (bf16[4,64,2048]{2,1,0:T(8,128)(2,1)}, bf16[4,64,2048]{2,1,0:T(8,128)(2,1)}, u32[]{:S(2)}, u32[]{:S(2)}) collective-permute-start(bf16[4,64,2048]{2,1,0:T(8,128)(2,1)} %bitcast.74), channel_id=1, source_target_pairs={{0,16},{16,0},{1,17},{17,1},{2,18},{18,2},{3,19},{19,3},{4,20},{20... | collective-permute-start | bytes 3145736 | tf_op jit(solution)/shard_map/ppermute | solution.py:1821
  129.4 27.1 %copy-start.6 = (f32[1,8,128,128]{3,2,1,0:T(8,128)}, f32[1,8,128,128]{3,2,1,0:T(8,128)S(1)}, u32[]{:S(2)}) copy-start(f32[1,8,128,128]{3,2,1,0:T(8,128)S(1)} %get-tuple-element.152) | copy-start | bytes 1572868
  129.4 45.0 %copy-start.5 = (f32[1,8,128,128]{3,2,1,0:T(8,128)}, f32[1,8,128,128]{3,2,1,0:T(8,128)S(1)}, u32[]{:S(2)}) copy-start(f32[1,8,128,128]{3,2,1,0:T(8,128)S(1)} %get-tuple-element.151) | copy-start | bytes 1572868
  129.4 27.0 %copy-start.10 = (s32[3]{0:T(128)}, s32[3]{0:T(128)S(1)}, u32[]{:S(2)}) copy-start(s32[3]{0:T(128)S(1)} %get-tuple-element.158.lengths_ref) | copy-start | bytes 40
  129.4 45.0 %copy-start.9 = (s32[3]{0:T(128)}, s32[3]{0:T(128)S(1)}, u32[]{:S(2)}) copy-start(s32[3]{0:T(128)S(1)} %get-tuple-element.157.lengths_ref) | copy-start | bytes 40
  129.5 45.0 %copy-start.7 = (f32[12,256]{1,0:T(8,128)}, f32[12,256]{1,0:T(8,128)S(1)}, u32[]{:S(2)}) copy-start(f32[12,256]{1,0:T(8,128)S(1)} %reshape.186.tap_ref) | copy-start | bytes 36868
  129.5 44.9 %copy-start.32 = (f32[2,128]{1,0:T(2,128)}, f32[2,128]{1,0:T(2,128)S(1)}, u32[]{:S(2)}) copy-start(f32[2,128]{1,0:T(2,128)S(1)} %convert_element_type.66.gain_ref) | copy-start | bytes 3076
  129.5 44.4 %copy-start.20 = (bf16[4,2,32,2048]{3,2,1,0:T(8,128)(2,1)S(1)}, bf16[4,2,32,2048]{3,2,1,0:T(8,128)(2,1)}, u32[]{:S(2)}) copy-start(bf16[4,2,32,2048]{3,2,1,0:T(8,128)(2,1)} %copy-done.19) | copy-start | bytes 3145732
  171.9 29.2 %collective-permute-start.5 = (bf16[4,64,2048]{2,1,0:T(8,128)(2,1)}, bf16[4,64,2048]{2,1,0:T(8,128)(2,1)S(1)}, u32[]{:S(2)}, u32[]{:S(2)}) collective-permute-start(bf16[4,64,2048]{2,1,0:T(8,128)(2,1)} %collective-permute-done.refs_4_), channel_id=1, source_target_pairs={{0,16},{16,0},{1,17},{17,1},{2,18},{18,2},{3,19},{19,3},{4,20},{20... | collective-permute-start | bytes 3145736 | tf_op jit(solution)/shard_map/ppermute | solution.py:1821
  173.4 27.8 %collective-permute-start.6 = (bf16[256,2048]{1,0:T(8,128)(2,1)}, bf16[256,2048]{1,0:T(8,128)(2,1)S(1)}, u32[]{:S(2)}, u32[]{:S(2)}) collective-permute-start(bf16[256,2048]{1,0:T(8,128)(2,1)} %collective-permute-done.1.refs_1_), channel_id=1, source_target_pairs={{0,1},{1,0},{2,3},{3,2},{4,5},{5,4},{6,7},{7,6},{8,9},{9,8},{10,11... | collective-permute-start | bytes 3145736 | tf_op jit(solution)/shard_map/ppermute | solution.py:1821
  173.9 28.0 %collective-permute-start.3 = (bf16[4,64,2048]{2,1,0:T(8,128)(2,1)S(1)}, bf16[4,64,2048]{2,1,0:T(8,128)(2,1)S(1)}, u32[]{:S(2)}, u32[]{:S(2)}) collective-permute-start(bf16[4,64,2048]{2,1,0:T(8,128)(2,1)S(1)} %bitcast.75), channel_id=1, source_target_pairs={{0,8},{8,0},{1,9},{9,1},{2,10},{10,2},{3,11},{11,3},{4,12},{12,4},... | collective-permute-start | bytes 3145736 | tf_op jit(solution)/shard_map/ppermute | solution.py:1821
  173.9 28.5 %collective-permute-start.8 = (bf16[4,64,2048]{2,1,0:T(8,128)(2,1)}, bf16[4,64,2048]{2,1,0:T(8,128)(2,1)S(1)}, u32[]{:S(2)}, u32[]{:S(2)}) collective-permute-start(bf16[4,64,2048]{2,1,0:T(8,128)(2,1)} %collective-permute-done.refs_4_), channel_id=1, source_target_pairs={{0,8},{8,0},{1,9},{9,1},{2,10},{10,2},{3,11},{11,3},{4,12},{12,4},... | collective-permute-start | bytes 3145736 | tf_op jit(solution)/shard_map/ppermute | solution.py:1821
  174.4 27.4 %copy-start.57 = (bf16[2,128,2048]{2,1,0:T(8,128)(2,1)S(1)}, bf16[2,128,2048]{2,1,0:T(8,128)(2,1)}, u32[]{:S(2)}) copy-start(bf16[2,128,2048]{2,1,0:T(8,128)(2,1)} %param.31) | copy-start | bytes 3145732
  201.2 41.7 %copy-start.37 = (f32[1024,256]{1,0:T(8,128)}, f32[1024,256]{1,0:T(8,128)S(1)}, u32[]{:S(2)}) copy-start(f32[1024,256]{1,0:T(8,128)S(1)} %get-tuple-element.118.heads_ref) | copy-start | bytes 3145732
  201.2 41.8 %copy-start.38 = (f32[1024,256]{1,0:T(8,128)}, f32[1024,256]{1,0:T(8,128)S(1)}, u32[]{:S(2)}) copy-start(f32[1024,256]{1,0:T(8,128)S(1)} %get-tuple-element.119.fixed_ref) | copy-start | bytes 3145732
  201.2 41.8 %copy-start.39 = (f32[1024,256]{1,0:T(8,128)}, f32[1024,256]{1,0:T(8,128)S(1)}, u32[]{:S(2)}) copy-start(f32[1024,256]{1,0:T(8,128)S(1)} %get-tuple-element.120.delta_ref) | copy-start | bytes 3145732
  201.2 41.8 %copy-start.40 = (f32[16,128,128]{2,1,0:T(8,128)}, f32[16,128,128]{2,1,0:T(8,128)S(1)}, u32[]{:S(2)}) copy-start(f32[16,128,128]{2,1,0:T(8,128)S(1)} %get-tuple-element.121.state_ref) | copy-start | bytes 3145732
  201.2 41.7 %copy-start.58 = (bf16[256,2048]{1,0:T(8,128)(2,1)}, bf16[256,2048]{1,0:T(8,128)(2,1)S(1)}, u32[]{:S(2)}) copy-start(bf16[256,2048]{1,0:T(8,128)(2,1)S(1)} %collective-permute-done.6.refs_3_) | copy-start | bytes 3145732
  201.2 3.7 collective-permute-start.7
  201.3 5.3 collective-permute-start.9
  201.8 44.4 %collective-permute-start.10 = (bf16[256,2048]{1,0:T(8,128)(2,1)S(1)}, bf16[256,2048]{1,0:T(8,128)(2,1)S(1)}, u32[]{:S(2)}, u32[]{:S(2)}) collective-permute-start(bf16[256,2048]{1,0:T(8,128)(2,1)S(1)} %bitcast.101), channel_id=1, source_target_pairs={{0,8},{8,0},{1,9},{9,1},{2,10},{10,2},{3,11},{11,3},{4,12},{12,4},... | collective-permute-start | bytes 3145736 | tf_op jit(solution)/shard_map/ppermute | solution.py:1821
  201.9 44.3 %collective-permute-start.11 = (bf16[256,2048]{1,0:T(8,128)(2,1)}, bf16[256,2048]{1,0:T(8,128)(2,1)}, u32[]{:S(2)}, u32[]{:S(2)}) collective-permute-start(bf16[256,2048]{1,0:T(8,128)(2,1)} %collective-permute-done.1.refs_1_), channel_id=1, source_target_pairs={{0,8},{8,0},{1,9},{9,1},{2,10},{10,2},{3,11},{11,3},{4,12},{12,4},... | collective-permute-start | bytes 3145736 | tf_op jit(solution)/shard_map/ppermute | solution.py:1821
  202.4 43.8 %collective-permute-start.12 = (bf16[256,2048]{1,0:T(8,128)(2,1)}, bf16[256,2048]{1,0:T(8,128)(2,1)}, u32[]{:S(2)}, u32[]{:S(2)}) collective-permute-start(bf16[256,2048]{1,0:T(8,128)(2,1)} %collective-permute-done.2.refs_2_), channel_id=1, source_target_pairs={{0,8},{8,0},{1,9},{9,1},{2,10},{10,2},{3,11},{11,3},{4,12},{12,4},... | collective-permute-start | bytes 3145736 | tf_op jit(solution)/shard_map/ppermute | solution.py:1821
  204.9 41.4 %collective-permute-start.13 = (bf16[256,2048]{1,0:T(8,128)(2,1)S(1)}, bf16[256,2048]{1,0:T(8,128)(2,1)}, u32[]{:S(2)}, u32[]{:S(2)}) collective-permute-start(bf16[256,2048]{1,0:T(8,128)(2,1)S(1)} %collective-permute-done.6.refs_3_), channel_id=1, source_target_pairs={{0,8},{8,0},{1,9},{9,1},{2,10},{10,2},{3,11},{11,3},{4,12},{12,4},... | collective-permute-start | bytes 3145736 | tf_op jit(solution)/shard_map/ppermute | solution.py:1821
  246.2 5.0 copy-start.59
  441.2 32.1 %collective-permute-start.14 = (bf16[2,4,64,1024]{3,2,1,0:T(8,128)(2,1)}, bf16[2,4,64,1024]{3,2,1,0:T(8,128)(2,1)}, u32[]{:S(2)}, u32[]{:S(2)}) collective-permute-start(bf16[2,4,64,1024]{3,2,1,0:T(8,128)(2,1)} %copy-done.22), channel_id=1, source_target_pairs={{0,16},{16,0},{1,17},{17,1},{2,18},{18,2},{3,19},{19,3},{4,20},{20... | collective-permute-start | bytes 3145736 | tf_op jit(solution)/shard_map/ppermute | solution.py:1821
  443.4 32.5 %collective-permute-start.15 = (bf16[2,4,64,1024]{3,2,1,0:T(8,128)(2,1)}, bf16[2,4,64,1024]{3,2,1,0:T(8,128)(2,1)}, u32[]{:S(2)}, u32[]{:S(2)}) collective-permute-start(bf16[2,4,64,1024]{3,2,1,0:T(8,128)(2,1)} %copy-done.21), channel_id=1, source_target_pairs={{0,1},{1,0},{2,3},{3,2},{4,5},{5,4},{6,7},{7,6},{8,9},{9,8},{10,11... | collective-permute-start | bytes 3145736 | tf_op jit(solution)/shard_map/ppermute | solution.py:1821
  478.5 27.9 %copy-start.4 = (bf16[2048,128]{1,0:T(8,128)(2,1)S(1)}, bf16[2048,128]{1,0:T(8,128)(2,1)}, u32[]{:S(2)}) copy-start(bf16[2048,128]{1,0:T(8,128)(2,1)} %copy-done.3) | copy-start | bytes 1572868
  478.5 27.9 %copy-start.12 = (bf16[2048,256]{1,0:T(8,128)(2,1)S(1)}, bf16[2048,256]{1,0:T(8,128)(2,1)}, u32[]{:S(2)}) copy-start(bf16[2048,256]{1,0:T(8,128)(2,1)} %refs_0_.1) | copy-start | bytes 3145732
  478.5 27.9 %copy-start.14 = (bf16[2048,256]{1,0:T(8,128)(2,1)S(1)}, bf16[2048,256]{1,0:T(8,128)(2,1)}, u32[]{:S(2)}) copy-start(bf16[2048,256]{1,0:T(8,128)(2,1)} %refs_1_.1) | copy-start | bytes 3145732
  478.5 27.9 %copy-start.16 = (bf16[2048,256]{1,0:T(8,128)(2,1)S(1)}, bf16[2048,256]{1,0:T(8,128)(2,1)}, u32[]{:S(2)}) copy-start(bf16[2048,256]{1,0:T(8,128)(2,1)} %refs_2_.1) | copy-start | bytes 3145732
  478.5 27.9 %copy-start.18 = (bf16[2048,256]{1,0:T(8,128)(2,1)S(1)}, bf16[2048,256]{1,0:T(8,128)(2,1)}, u32[]{:S(2)}) copy-start(bf16[2048,256]{1,0:T(8,128)(2,1)} %refs_3_.3) | copy-start | bytes 3145732
  478.5 27.9 %copy-start.30 = (bf16[1024,128]{1,0:T(8,128)(2,1)S(1)}, bf16[1024,128]{1,0:T(8,128)(2,1)}, u32[]{:S(2)}) copy-start(bf16[1024,128]{1,0:T(8,128)(2,1)} %get-tuple-element.124.b_first) | copy-start | bytes 786436
  529.6 13.4 %collective-permute-start.17 = (bf16[4,64,1024]{2,1,0:T(8,128)(2,1)}, bf16[4,64,1024]{2,1,0:T(8,128)(2,1)}, u32[]{:S(2)}, u32[]{:S(2)}) collective-permute-start(bf16[4,64,1024]{2,1,0:T(8,128)(2,1)} %dynamic-slice_bitcast_fusion), channel_id=1, source_target_pairs={{0,16},{16,0},{1,17},{17,1},{2,18},{18,2},{3,19},{19,3},{4,20},{20... | collective-permute-start | bytes 1572872 | tf_op jit(solution)/shard_map/ppermute | solution.py:1821
  530.8 13.1 %collective-permute-start.16 = (bf16[4,64,1024]{2,1,0:T(8,128)(2,1)}, bf16[4,64,1024]{2,1,0:T(8,128)(2,1)}, u32[]{:S(2)}, u32[]{:S(2)}) collective-permute-start(bf16[4,64,1024]{2,1,0:T(8,128)(2,1)} %dynamic-slice_bitcast_fusion.1), channel_id=1, source_target_pairs={{0,1},{1,0},{2,3},{3,2},{4,5},{5,4},{6,7},{7,6},{8,9},{9,8},{10,11... | collective-permute-start | bytes 1572872 | tf_op jit(solution)/shard_map/ppermute | solution.py:1821
  661.6 5.8 copy-start.49
  (33 other events, 56.2 us)
Sparse Core Ops, SparseCore 0:
  124.9 126.2 all-gather.2
  441.3 100.3 reduce-scatter.1
